TPU v7x, 512 devices: a whole 4x8x8 slice. The times are simulated.
512 devices in a mesh: gx: 8 (over z), gy: 4 (over x), gz: 16 (over y, core).
Axes of the slice: x: 4, y: 8, z: 8, core: 2. Of those that a mesh axis runs over, the one named last changes fastest.
Arguments:
- initial_edge_intensity: float32 [3, 128, 64, 2048], P(None, 'gx', 'gy', 'gz'), may hold values from -3 to 3
- source_amperage: float32 [3, 128, 64, 2048], P(None, 'gx', 'gy', 'gz'), may hold values from -24 to 24
- electric_sigma: float32 [128, 64, 2048], P('gx', 'gy', 'gz'), may hold values from 0.1 to 3
- earlier_warmth: float32 [128, 64, 2048], P('gx', 'gy', 'gz'), may hold values from -6 to 6
- storage_coefficient: float32 [128, 64, 2048], P('gx', 'gy', 'gz'), may hold values from 0.5 to 4
- receiving_partition_rank: int32 [8, 4, 16, 256, 1], P('gx', 'gy', 'gz'), may hold values from 0 to 63; in each aligned block of 256 rows (0 to 255, 256 to 511, ..., all dimensions but the last counted through in order) at most 8 rows name the same one
- receiving_node_column: int32 [8, 4, 16, 256], P('gx', 'gy', 'gz'), may hold values from 0 to 255
Outputs:
- final_edge_intensity: float32 [3, 128, 64, 2048], P(None, 'gx', 'gy', 'gz')
- updated_warmth: float32 [128, 64, 2048], P('gx', 'gy', 'gz')
Inputs may be any that keep to these rules, and one draw needn't show every extreme that they name: `receiving_partition_rank`: in the 256 element columns of one device no thermal partition is named more than 8 times, and in every draw one is named exactly 8 times in some device's columns.
All inputs are finite; a program needn't handle non-finite values.
Results may differ from a plain program's by a relative error of at most 0.00027.
Values sent between devices are 32-bit elements; how exact they have to be, the bound alone decides.
No kernel may reach another device: no remote copies, remote signals or barrier semaphores. Data moves between devices by JAX's collectives and lax.ppermute only.
A program may use at most 64 MiB of HBM per device.

v0:
```python
import math

import jax
import jax.numpy as jnp
from jax import lax
from jax.sharding import PartitionSpec as P

EM_SWEEPS = 4
HEAT_SWEEPS = 2


em_lower = 0.02
em_upper = 3.0
heat_lower = 0.07
heat_upper = 2.0
edge_offsets = (
    ((0, 0, 0), (0, 1, 0), (0, 0, 1), (0, 1, 1)),
    ((0, 0, 0), (1, 0, 0), (0, 0, 1), (1, 0, 1)),
    ((0, 0, 0), (1, 0, 0), (0, 1, 0), (1, 1, 0)),
)


def padded(array, sides, width):
    for axis, dim in sides:
        devices, length = (lax.axis_size(axis), array.shape[dim])
        up = [(i, (i + 1) % devices) for i in range(devices - 1)]
        down = [(j, i) for i, j in up]
        last = lax.slice_in_dim(array, length - width, length, axis=dim)
        initial = lax.slice_in_dim(array, 0, width, axis=dim)
        before = lax.ppermute(last, axis, up)
        after = lax.ppermute(initial, axis, down)
        array = jnp.concatenate([before, array, after], axis=dim)
    return array


def chebyshev_weights(lower_end, upper_end, sweep_count):
    middle = 0.5 * (upper_end + lower_end)
    radius = 0.5 * (upper_end - lower_end)
    return [
        1.0 / (middle + radius * math.cos(math.pi * (2 * number + 1) / (2 * sweep_count)))
        for number in range(sweep_count)
    ]


def step_up(values, dimension):
    shifted = [slice(0, -1), slice(0, -1), slice(0, -1)]
    shifted[dimension] = slice(1, None)
    return values[tuple(shifted)] - values[:-1, :-1, :-1]


def step_down(values, dimension):
    shifted = [slice(1, None), slice(1, None), slice(1, None)]
    shifted[dimension] = slice(0, -1)
    return values[1:, 1:, 1:] - values[tuple(shifted)]


def curl_curl(bordered_entries):
    field_x, field_y, field_z = (bordered_entries[0], bordered_entries[1], bordered_entries[2])
    curl_x = step_up(field_z, 1) - step_up(field_y, 2)
    curl_y = step_up(field_x, 2) - step_up(field_z, 0)
    curl_z = step_up(field_y, 0) - step_up(field_x, 1)
    back_x = step_down(curl_z, 1) - step_down(curl_y, 2)
    back_y = step_down(curl_x, 2) - step_down(curl_z, 0)
    back_z = step_down(curl_y, 0) - step_down(curl_x, 1)
    return jnp.stack([back_x, back_y, back_z])


def corner_cut(values, offsets):
    extent = values.shape
    return values[
        1 + offsets[0] : extent[0] - 1 + offsets[0],
        1 + offsets[1] : extent[1] - 1 + offsets[1],
        1 + offsets[2] : extent[2] - 1 + offsets[2],
    ]


def joule_heat(bordered_entries, electric_sigma):
    summed = jnp.zeros(electric_sigma.shape, jnp.float32)
    for component in range(3):
        squares = bordered_entries[component] * bordered_entries[component]
        for offsets in edge_offsets[component]:
            summed = summed + corner_cut(squares, offsets)
    return electric_sigma * (0.25 * summed)


def neighbour_total(bordered_entries):
    summed = bordered_entries[2:, 1:-1, 1:-1] + bordered_entries[:-2, 1:-1, 1:-1]
    summed = summed + bordered_entries[1:-1, 2:, 1:-1] + bordered_entries[1:-1, :-2, 1:-1]
    summed = summed + bordered_entries[1:-1, 1:-1, 2:] + bordered_entries[1:-1, 1:-1, :-2]
    return summed


def field_rim(values):
    return padded(values, (("gx", 1), ("gy", 2), ("gz", 3)), 1)


def local(
    initial_edge_intensity,
    source_amperage,
    electric_sigma,
    earlier_warmth,
    storage_coefficient,
    receiving_partition_rank,
    receiving_node_column,
):
    cells_x, cells_y, cells_z = electric_sigma.shape
    relax_list = chebyshev_weights(em_lower, em_upper, EM_SWEEPS)
    diagonal = 4.0 + electric_sigma
    final_edge_intensity = initial_edge_intensity
    for relaxing_factor in relax_list:
        bordered_entries = field_rim(final_edge_intensity)
        driving_excitation = curl_curl(bordered_entries) + electric_sigma * final_edge_intensity
        final_edge_intensity = (
            final_edge_intensity
            + relaxing_factor * (source_amperage - driving_excitation) / diagonal
        )
    cell_heat = joule_heat(field_rim(final_edge_intensity), electric_sigma)
    lines = cells_x * cells_y
    heat_rows = cell_heat.reshape(lines, cells_z)
    owners = receiving_partition_rank.reshape(lines)
    slots = receiving_node_column.reshape(lines)
    groups_y = lax.axis_size("gy")
    groups_z = lax.axis_size("gz")
    groups = groups_y * groups_z
    capacity_slots = max(2, 2 * lines // groups)
    member = (owners[:, None] == jnp.arange(groups, dtype=jnp.int32)[None, :]).astype(jnp.int32)
    before = jnp.cumsum(member, 0) - member
    ranking = jnp.sum(before * member, 1)
    position = owners * capacity_slots + ranking
    placing = (
        position[None, :] == jnp.arange(groups * capacity_slots, dtype=jnp.int32)[:, None]
    ).astype(jnp.float32)
    send_heat = jnp.dot(placing, heat_rows, precision=lax.Precision.HIGHEST)
    send_slot = jnp.dot(placing, (slots + 1).astype(jnp.float32), precision=lax.Precision.HIGHEST)
    got_heat, got_slot = (
        lax.all_to_all(
            send_heat.reshape(groups, capacity_slots, cells_z),
            ("gy", "gz"),
            split_axis=0,
            concat_axis=0,
            tiled=True,
        ),
        lax.all_to_all(
            send_slot.reshape(groups, capacity_slots),
            ("gy", "gz"),
            split_axis=0,
            concat_axis=0,
            tiled=True,
        ),
    )
    flat_slot = got_slot.reshape(-1)
    collect = (flat_slot[None, :] == (jnp.arange(lines, dtype=jnp.float32) + 1.0)[:, None]).astype(
        jnp.float32
    )
    dissipated_power = jnp.dot(
        collect, got_heat.reshape(-1, cells_z), precision=lax.Precision.HIGHEST
    ).reshape(cells_x, cells_y, cells_z)
    warmth_matrix_pivot = 6.0 + storage_coefficient
    linear_forcing_vector = storage_coefficient * earlier_warmth + dissipated_power
    updated_warmth = earlier_warmth
    for relaxing_factor in chebyshev_weights(heat_lower, heat_upper, HEAT_SWEEPS):
        bordered_entries = padded(updated_warmth, (("gx", 0), ("gy", 1), ("gz", 2)), 1)
        driving_excitation = warmth_matrix_pivot * updated_warmth - neighbour_total(
            bordered_entries
        )
        updated_warmth = (
            updated_warmth
            + relaxing_factor * (linear_forcing_vector - driving_excitation) / warmth_matrix_pivot
        )
    return (final_edge_intensity, updated_warmth)


def solution(mesh):
    in_specs = (
        P(None, "gx", "gy", "gz"),
        P(None, "gx", "gy", "gz"),
        P("gx", "gy", "gz"),
        P("gx", "gy", "gz"),
        P("gx", "gy", "gz"),
        P("gx", "gy", "gz", None, None),
        P("gx", "gy", "gz", None),
    )
    out_specs = (P(None, "gx", "gy", "gz"), P("gx", "gy", "gz"))
    return jax.shard_map(local, mesh=mesh, in_specs=in_specs, out_specs=out_specs, check_vma=False)
```

profile of v0, /device:TPU:38, one launch (start us, length us, event | category | flops | bytes accessed | tf_op | source)
XLA Modules:
  0.0 228.6 jit_solution(3429977298492914007)
XLA Ops:
  1.4 4.3 %collective-permute-start = (f32[3,1,16,128]{3,2,1,0:T(8,128)S(1)}, f32[3,1,16,128]{3,2,1,0:T(8,128)S(1)}, u32[]{:S(2)}, u32[]{:S(2)}) collective-permute-start(f32[3,1,16,128]{3,2,1,0:T(8,128)S(1)} %get-tuple-element.72), channel_id=1, source_target_pairs={{0,64},{64,128},{128,192},{192,256},{256,320},{320,384},{384,448},... | collective-permute-start | bytes 73736 | tf_op jit(solution)/shard_map/ppermute | solution.py:30
  5.7 1.3 collective-permute-start.1
  7.2 1.0 constant_dynamic-update-slice_fusion.1
  8.2 3.5 %collective-permute-done.1 = f32[3,1,16,128]{3,2,1,0:T(8,128)S(1)} collective-permute-done((f32[3,1,16,128]{3,2,1,0:T(8,128)S(1)}, f32[3,1,16,128]{3,2,1,0:T(8,128)S(1)}, u32[]{:S(2)}, u32[]{:S(2)}) %collective-permute-start.1) | collective-permute-done | bytes 24608 | tf_op jit(solution)/shard_map/ppermute | solution.py:31
  11.8 1.3 collective-permute-start.2
  13.1 4.5 %collective-permute-start.3 = (f32[3,18,1,128]{3,2,1,0:T(1,128)S(1)}, f32[3,18,1,128]{3,2,1,0:T(1,128)S(1)}, u32[]{:S(2)}, u32[]{:S(2)}) collective-permute-start(f32[3,18,1,128]{3,2,1,0:T(1,128)S(1)} %get-tuple-element.50), channel_id=1, source_target_pairs={{16,0},{32,16},{48,32},{17,1},{33,17},{49,33},{18,2},{34,18},{50,3... | collective-permute-start | bytes 82952 | tf_op jit(solution)/shard_map/ppermute | solution.py:31
  17.7 1.5 collective-permute-done.3
  20.0 1.9 collective-permute-start.4
  22.3 4.8 %collective-permute-start.5 = (f32[3,18,18,1]{2,3,1,0:T(1,128)S(1)}, f32[3,18,18,1]{2,3,1,0:T(1,128)S(1)}, u32[]{:S(2)}, u32[]{:S(2)}) collective-permute-start(f32[3,18,18,1]{2,3,1,0:T(1,128)S(1)} %copy.30), channel_id=1, source_target_pairs={{1,0},{2,1},{3,2},{4,3},{5,4},{6,5},{7,6},{8,7},{9,8},{10,9},{11,1... | collective-permute-start | bytes 11672 | tf_op jit(solution)/shard_map/ppermute | solution.py:31
  27.6 1.0 collective-permute-done.5
  31.6 4.3 %collective-permute-start.6 = (f32[3,1,16,128]{3,2,1,0:T(8,128)S(1)}, f32[3,1,16,128]{3,2,1,0:T(8,128)S(1)}, u32[]{:S(2)}, u32[]{:S(2)}) collective-permute-start(f32[3,1,16,128]{3,2,1,0:T(8,128)S(1)} %get-tuple-element.69), channel_id=1, source_target_pairs={{0,64},{64,128},{128,192},{192,256},{256,320},{320,384},{384,448},... | collective-permute-start | bytes 73736 | tf_op jit(solution)/shard_map/ppermute | solution.py:30
  35.9 1.3 collective-permute-start.7
  37.4 5.8 %collective-permute-done.7 = f32[3,1,16,128]{3,2,1,0:T(8,128)S(1)} collective-permute-done((f32[3,1,16,128]{3,2,1,0:T(8,128)S(1)}, f32[3,1,16,128]{3,2,1,0:T(8,128)S(1)}, u32[]{:S(2)}, u32[]{:S(2)}) %collective-permute-start.7) | collective-permute-done | bytes 24608 | tf_op jit(solution)/shard_map/ppermute | solution.py:31
  43.2 1.3 collective-permute-start.8
  44.5 4.8 %collective-permute-start.9 = (f32[3,18,1,128]{3,2,1,0:T(1,128)S(1)}, f32[3,18,1,128]{3,2,1,0:T(1,128)S(1)}, u32[]{:S(2)}, u32[]{:S(2)}) collective-permute-start(f32[3,18,1,128]{3,2,1,0:T(1,128)S(1)} %get-tuple-element.45), channel_id=1, source_target_pairs={{16,0},{32,16},{48,32},{17,1},{33,17},{49,33},{18,2},{34,18},{50,3... | collective-permute-start | bytes 82952 | tf_op jit(solution)/shard_map/ppermute | solution.py:31
  49.4 1.5 collective-permute-done.9
  51.6 1.9 collective-permute-start.10
  54.0 4.8 %collective-permute-start.11 = (f32[3,18,18,1]{2,3,1,0:T(1,128)S(1)}, f32[3,18,18,1]{2,3,1,0:T(1,128)S(1)}, u32[]{:S(2)}, u32[]{:S(2)}) collective-permute-start(f32[3,18,18,1]{2,3,1,0:T(1,128)S(1)} %copy.34), channel_id=1, source_target_pairs={{1,0},{2,1},{3,2},{4,3},{5,4},{6,5},{7,6},{8,7},{9,8},{10,9},{11,1... | collective-permute-start | bytes 11672 | tf_op jit(solution)/shard_map/ppermute | solution.py:31
  58.9 5.1 %collective-permute-start.31 = (f32[1,16,128]{2,1,0:T(8,128)S(1)}, f32[1,16,128]{2,1,0:T(8,128)S(1)}, u32[]{:S(2)}, u32[]{:S(2)}) collective-permute-start(f32[1,16,128]{2,1,0:T(8,128)S(1)} %get-tuple-element.84), channel_id=1, source_target_pairs={{0,64},{64,128},{128,192},{192,256},{256,320},{320,384},{384,448},... | collective-permute-start | bytes 24584 | tf_op jit(solution)/shard_map/ppermute | solution.py:30
  64.0 1.3 collective-permute-start.30
  67.9 4.6 %collective-permute-start.12 = (f32[3,1,16,128]{3,2,1,0:T(8,128)S(1)}, f32[3,1,16,128]{3,2,1,0:T(8,128)S(1)}, u32[]{:S(2)}, u32[]{:S(2)}) collective-permute-start(f32[3,1,16,128]{3,2,1,0:T(8,128)S(1)} %get-tuple-element.67), channel_id=1, source_target_pairs={{0,64},{64,128},{128,192},{192,256},{256,320},{320,384},{384,448},... | collective-permute-start | bytes 73736 | tf_op jit(solution)/shard_map/ppermute | solution.py:30
  72.4 1.3 collective-permute-start.13
  74.4 3.8 %collective-permute-done.13 = f32[3,1,16,128]{3,2,1,0:T(8,128)S(1)} collective-permute-done((f32[3,1,16,128]{3,2,1,0:T(8,128)S(1)}, f32[3,1,16,128]{3,2,1,0:T(8,128)S(1)}, u32[]{:S(2)}, u32[]{:S(2)}) %collective-permute-start.13) | collective-permute-done | bytes 24608 | tf_op jit(solution)/shard_map/ppermute | solution.py:31
  78.2 1.3 collective-permute-start.14
  79.5 4.8 %collective-permute-start.15 = (f32[3,18,1,128]{3,2,1,0:T(1,128)S(1)}, f32[3,18,1,128]{3,2,1,0:T(1,128)S(1)}, u32[]{:S(2)}, u32[]{:S(2)}) collective-permute-start(f32[3,18,1,128]{3,2,1,0:T(1,128)S(1)} %get-tuple-element.40), channel_id=1, source_target_pairs={{16,0},{32,16},{48,32},{17,1},{33,17},{49,33},{18,2},{34,18},{50,3... | collective-permute-start | bytes 82952 | tf_op jit(solution)/shard_map/ppermute | solution.py:31
  84.6 1.3 collective-permute-done.15
  86.7 1.9 collective-permute-start.16
  89.0 4.8 %collective-permute-start.17 = (f32[3,18,18,1]{2,3,1,0:T(1,128)S(1)}, f32[3,18,18,1]{2,3,1,0:T(1,128)S(1)}, u32[]{:S(2)}, u32[]{:S(2)}) collective-permute-start(f32[3,18,18,1]{2,3,1,0:T(1,128)S(1)} %copy.38), channel_id=1, source_target_pairs={{1,0},{2,1},{3,2},{4,3},{5,4},{6,5},{7,6},{8,7},{9,8},{10,9},{11,1... | collective-permute-start | bytes 11672 | tf_op jit(solution)/shard_map/ppermute | solution.py:31
  97.5 3.9 %collective-permute-start.18 = (f32[3,1,16,128]{3,2,1,0:T(8,128)S(1)}, f32[3,1,16,128]{3,2,1,0:T(8,128)S(1)}, u32[]{:S(2)}, u32[]{:S(2)}) collective-permute-start(f32[3,1,16,128]{3,2,1,0:T(8,128)S(1)} %get-tuple-element.65), channel_id=1, source_target_pairs={{0,64},{64,128},{128,192},{192,256},{256,320},{320,384},{384,448},... | collective-permute-start | bytes 73736 | tf_op jit(solution)/shard_map/ppermute | solution.py:30
  101.4 1.3 collective-permute-start.19
  102.9 4.2 %collective-permute-done.19 = f32[3,1,16,128]{3,2,1,0:T(8,128)S(1)} collective-permute-done((f32[3,1,16,128]{3,2,1,0:T(8,128)S(1)}, f32[3,1,16,128]{3,2,1,0:T(8,128)S(1)}, u32[]{:S(2)}, u32[]{:S(2)}) %collective-permute-start.19) | collective-permute-done | bytes 24608 | tf_op jit(solution)/shard_map/ppermute | solution.py:31
  107.2 1.3 collective-permute-start.20
  108.5 4.8 %collective-permute-start.21 = (f32[3,18,1,128]{3,2,1,0:T(1,128)S(1)}, f32[3,18,1,128]{3,2,1,0:T(1,128)S(1)}, u32[]{:S(2)}, u32[]{:S(2)}) collective-permute-start(f32[3,18,1,128]{3,2,1,0:T(1,128)S(1)} %get-tuple-element.35), channel_id=1, source_target_pairs={{16,0},{32,16},{48,32},{17,1},{33,17},{49,33},{18,2},{34,18},{50,3... | collective-permute-start | bytes 82952 | tf_op jit(solution)/shard_map/ppermute | solution.py:31
  113.4 1.5 collective-permute-done.21
  115.7 1.9 collective-permute-start.22
  118.0 5.0 %collective-permute-start.23 = (f32[3,18,18,1]{2,3,1,0:T(1,128)S(1)}, f32[3,18,18,1]{2,3,1,0:T(1,128)S(1)}, u32[]{:S(2)}, u32[]{:S(2)}) collective-permute-start(f32[3,18,18,1]{2,3,1,0:T(1,128)S(1)} %copy.42), channel_id=1, source_target_pairs={{1,0},{2,1},{3,2},{4,3},{5,4},{6,5},{7,6},{8,7},{9,8},{10,9},{11,1... | collective-permute-start | bytes 11672 | tf_op jit(solution)/shard_map/ppermute | solution.py:31
  123.0 2.5 %convolution_bitcast_fusion = f32[64,1,8]{2,1,0:T(1,128)} fusion(s32[64,8]{1,0:T(8,128)S(1)} %multiply_add_fusion, s32[256]{0:T(256)S(1)} %multiply_add_fusion.1, s32[1,1,1,256]{3,2,1,0:T(1,128)S(1)} %copy-done.8), kind=kOutput, calls=%fused_computation.6 | convolution fusion | flops 1704448 | bytes 6144 | tf_op jit(solution)/shard_map/dot_general | solution.py:134
  125.6 12.4 %all-to-all-start = ((f32[64,1,8]{2,1,0:T(1,128)}), f32[64,1,8]{2,1,0:T(1,128)S(1)}, u32[]{:S(2)}, u32[]{:S(2)}) async-start(f32[64,1,8]{2,1,0:T(1,128)} %convolution_bitcast_fusion), calls=%async_computation | async-start | bytes 65536 | tf_op jit(solution)/shard_map/all_to_all | solution.py:143
  140.6 4.1 %collective-permute-start.24 = (f32[3,1,16,128]{3,2,1,0:T(8,128)S(1)}, f32[3,1,16,128]{3,2,1,0:T(8,128)S(1)}, u32[]{:S(2)}, u32[]{:S(2)}) collective-permute-start(f32[3,1,16,128]{3,2,1,0:T(8,128)S(1)} %get-tuple-element.63), channel_id=1, source_target_pairs={{0,64},{64,128},{128,192},{192,256},{256,320},{320,384},{384,448},... | collective-permute-start | bytes 73736 | tf_op jit(solution)/shard_map/ppermute | solution.py:30
  144.6 1.3 collective-permute-start.25
  146.1 4.2 %collective-permute-done.25 = f32[3,1,16,128]{3,2,1,0:T(8,128)S(1)} collective-permute-done((f32[3,1,16,128]{3,2,1,0:T(8,128)S(1)}, f32[3,1,16,128]{3,2,1,0:T(8,128)S(1)}, u32[]{:S(2)}, u32[]{:S(2)}) %collective-permute-start.25) | collective-permute-done | bytes 24608 | tf_op jit(solution)/shard_map/ppermute | solution.py:31
  150.4 1.3 collective-permute-start.26
  151.7 4.5 %collective-permute-start.27 = (f32[3,18,1,128]{3,2,1,0:T(1,128)S(1)}, f32[3,18,1,128]{3,2,1,0:T(1,128)S(1)}, u32[]{:S(2)}, u32[]{:S(2)}) collective-permute-start(f32[3,18,1,128]{3,2,1,0:T(1,128)S(1)} %get-tuple-element.30), channel_id=1, source_target_pairs={{16,0},{32,16},{48,32},{17,1},{33,17},{49,33},{18,2},{34,18},{50,3... | collective-permute-start | bytes 82952 | tf_op jit(solution)/shard_map/ppermute | solution.py:31
  156.3 1.5 collective-permute-done.27
  158.6 1.9 collective-permute-start.28
  161.1 4.8 %collective-permute-start.29 = (f32[3,18,18,1]{2,1,3,0:T(8,128)S(1)}, f32[3,18,18,1]{2,1,3,0:T(8,128)S(1)}, u32[]{:S(2)}, u32[]{:S(2)}) collective-permute-start(f32[3,18,18,1]{2,1,3,0:T(8,128)S(1)} %copy.47), channel_id=1, source_target_pairs={{1,0},{2,1},{3,2},{4,3},{5,4},{6,5},{7,6},{8,7},{9,8},{10,9},{11,1... | collective-permute-start | bytes 11672 | tf_op jit(solution)/shard_map/ppermute | solution.py:31
  166.4 1.1 collective-permute-done.29
  169.4 1.1 fusion
  170.6 12.2 %all-to-all-start.1 = ((f32[64,8,128]{2,1,0:T(8,128)}), f32[64,8,128]{2,1,0:T(8,128)S(1)}, u32[]{:S(2)}, u32[]{:S(2)}) async-start(f32[64,8,128]{2,1,0:T(8,128)} %fusion), calls=%async_computation.1 | async-start | bytes 524288 | tf_op jit(solution)/shard_map/all_to_all | solution.py:136
  182.8 2.7 %collective-permute-start.32 = (f32[18,1,128]{2,1,0:T(1,128)S(1)}, f32[18,1,128]{2,1,0:T(1,128)S(1)}, u32[]{:S(2)}, u32[]{:S(2)}) collective-permute-start(f32[18,1,128]{2,1,0:T(1,128)S(1)} %get-tuple-element.80), channel_id=1, source_target_pairs={{16,0},{32,16},{48,32},{17,1},{33,17},{49,33},{18,2},{34,18},{50,3... | collective-permute-start | bytes 27656 | tf_op jit(solution)/shard_map/ppermute | solution.py:31
  185.4 1.3 collective-permute-start.33
  186.8 4.2 %collective-permute-done.33 = f32[18,1,128]{2,1,0:T(1,128)S(1)} collective-permute-done((f32[18,1,128]{2,1,0:T(1,128)S(1)}, f32[18,1,128]{2,1,0:T(1,128)S(1)}, u32[]{:S(2)}, u32[]{:S(2)}) %collective-permute-start.33) | collective-permute-done | bytes 9248 | tf_op jit(solution)/shard_map/ppermute | solution.py:30
  191.2 1.9 collective-permute-start.34
  193.1 2.4 %collective-permute-start.35 = (f32[18,18,1]{2,1,0:T(8,128)S(1)}, f32[18,18,1]{2,1,0:T(8,128)S(1)}, u32[]{:S(2)}, u32[]{:S(2)}) collective-permute-start(f32[18,18,1]{2,1,0:T(8,128)S(1)} %get-tuple-element.76), channel_id=1, source_target_pairs={{0,1},{1,2},{2,3},{3,4},{4,5},{5,6},{6,7},{7,8},{8,9},{9,10},{10,1... | collective-permute-start | bytes 3896 | tf_op jit(solution)/shard_map/ppermute | solution.py:30
  196.9 4.7 %collective-permute-done.35 = f32[18,18,1]{2,1,0:T(8,128)S(1)} collective-permute-done((f32[18,18,1]{2,1,0:T(8,128)S(1)}, f32[18,18,1]{2,1,0:T(8,128)S(1)}, u32[]{:S(2)}, u32[]{:S(2)}) %collective-permute-start.35) | collective-permute-done | bytes 1328 | tf_op jit(solution)/shard_map/ppermute | solution.py:30
  202.0 1.3 collective-permute-start.36
  203.3 4.5 %collective-permute-start.37 = (f32[1,16,128]{2,1,0:T(8,128)S(1)}, f32[1,16,128]{2,1,0:T(8,128)S(1)}, u32[]{:S(2)}, u32[]{:S(2)}) collective-permute-start(f32[1,16,128]{2,1,0:T(8,128)S(1)} %get-tuple-element.81), channel_id=1, source_target_pairs={{0,64},{64,128},{128,192},{192,256},{256,320},{320,384},{384,448},... | collective-permute-start | bytes 24584 | tf_op jit(solution)/shard_map/ppermute | solution.py:30
  207.9 1.3 collective-permute-done.37
  209.2 2.4 %collective-permute-start.38 = (f32[18,1,128]{2,1,0:T(1,128)S(1)}, f32[18,1,128]{2,1,0:T(1,128)S(1)}, u32[]{:S(2)}, u32[]{:S(2)}) collective-permute-start(f32[18,1,128]{2,1,0:T(1,128)S(1)} %get-tuple-element.78), channel_id=1, source_target_pairs={{16,0},{32,16},{48,32},{17,1},{33,17},{49,33},{18,2},{34,18},{50,3... | collective-permute-start | bytes 27656 | tf_op jit(solution)/shard_map/ppermute | solution.py:31
  211.6 1.3 collective-permute-start.39
  213.0 4.2 %collective-permute-done.39 = f32[18,1,128]{2,1,0:T(1,128)S(1)} collective-permute-done((f32[18,1,128]{2,1,0:T(1,128)S(1)}, f32[18,1,128]{2,1,0:T(1,128)S(1)}, u32[]{:S(2)}, u32[]{:S(2)}) %collective-permute-start.39) | collective-permute-done | bytes 9248 | tf_op jit(solution)/shard_map/ppermute | solution.py:30
  217.3 1.9 collective-permute-start.40
  219.3 2.4 %collective-permute-start.41 = (f32[18,18,1]{2,1,0:T(8,128)S(1)}, f32[18,18,1]{2,1,0:T(8,128)S(1)}, u32[]{:S(2)}, u32[]{:S(2)}) collective-permute-start(f32[18,18,1]{2,1,0:T(8,128)S(1)} %get-tuple-element.74), channel_id=1, source_target_pairs={{0,1},{1,2},{2,3},{3,4},{4,5},{5,6},{6,7},{7,8},{8,9},{9,10},{10,1... | collective-permute-start | bytes 3896 | tf_op jit(solution)/shard_map/ppermute | solution.py:30
  222.7 5.0 %collective-permute-done.41 = f32[18,18,1]{2,1,0:T(8,128)S(1)} collective-permute-done((f32[18,18,1]{2,1,0:T(8,128)S(1)}, f32[18,18,1]{2,1,0:T(8,128)S(1)}, u32[]{:S(2)}, u32[]{:S(2)}) %collective-permute-start.41) | collective-permute-done | bytes 1328 | tf_op jit(solution)/shard_map/ppermute | solution.py:30
  (137 shorter events, 27.2 us)
Async XLA Ops:
  1.4 5.8 %collective-permute-start = (f32[3,1,16,128]{3,2,1,0:T(8,128)S(1)}, f32[3,1,16,128]{3,2,1,0:T(8,128)S(1)}, u32[]{:S(2)}, u32[]{:S(2)}) collective-permute-start(f32[3,1,16,128]{3,2,1,0:T(8,128)S(1)} %get-tuple-element.72), channel_id=1, source_target_pairs={{0,64},{64,128},{128,192},{192,256},{256,320},{320,384},{384,448},... | collective-permute-start | bytes 73736 | tf_op jit(solution)/shard_map/ppermute | solution.py:30
  5.7 6.1 %collective-permute-start.1 = (f32[3,1,16,128]{3,2,1,0:T(8,128)S(1)}, f32[3,1,16,128]{3,2,1,0:T(8,128)S(1)}, u32[]{:S(2)}, u32[]{:S(2)}) collective-permute-start(f32[3,1,16,128]{3,2,1,0:T(8,128)S(1)} %get-tuple-element.71), channel_id=1, source_target_pairs={{64,0},{128,64},{192,128},{256,192},{320,256},{384,320},{448,384},... | collective-permute-start | bytes 73736 | tf_op jit(solution)/shard_map/ppermute | solution.py:31
  11.8 5.9 %collective-permute-start.2 = (f32[3,18,1,128]{3,2,1,0:T(1,128)S(1)}, f32[3,18,1,128]{3,2,1,0:T(1,128)S(1)}, u32[]{:S(2)}, u32[]{:S(2)}) collective-permute-start(f32[3,18,1,128]{3,2,1,0:T(1,128)S(1)} %get-tuple-element.49), channel_id=1, source_target_pairs={{0,16},{16,32},{32,48},{1,17},{17,33},{33,49},{2,18},{18,34},{34,5... | collective-permute-start | bytes 82952 | tf_op jit(solution)/shard_map/ppermute | solution.py:30
  13.1 6.1 %collective-permute-start.3 = (f32[3,18,1,128]{3,2,1,0:T(1,128)S(1)}, f32[3,18,1,128]{3,2,1,0:T(1,128)S(1)}, u32[]{:S(2)}, u32[]{:S(2)}) collective-permute-start(f32[3,18,1,128]{3,2,1,0:T(1,128)S(1)} %get-tuple-element.50), channel_id=1, source_target_pairs={{16,0},{32,16},{48,32},{17,1},{33,17},{49,33},{18,2},{34,18},{50,3... | collective-permute-start | bytes 82952 | tf_op jit(solution)/shard_map/ppermute | solution.py:31
  19.5 7.6 %copy-start.2 = (f32[16,16,128]{2,1,0:T(8,128)S(1)}, f32[16,16,128]{2,1,0:T(8,128)}, u32[]{:S(2)}) copy-start(f32[16,16,128]{2,1,0:T(8,128)} %param.9) | copy-start | bytes 393220
  20.0 7.2 %collective-permute-start.4 = (f32[3,18,18,1]{2,3,1,0:T(1,128)S(1)}, f32[3,18,18,1]{2,3,1,0:T(1,128)S(1)}, u32[]{:S(2)}, u32[]{:S(2)}) collective-permute-start(f32[3,18,18,1]{2,3,1,0:T(1,128)S(1)} %copy.29), channel_id=1, source_target_pairs={{0,1},{1,2},{2,3},{3,4},{4,5},{5,6},{6,7},{7,8},{8,9},{9,10},{10,1... | collective-permute-start | bytes 11672 | tf_op jit(solution)/shard_map/ppermute | solution.py:30
  22.3 6.4 %collective-permute-start.5 = (f32[3,18,18,1]{2,3,1,0:T(1,128)S(1)}, f32[3,18,18,1]{2,3,1,0:T(1,128)S(1)}, u32[]{:S(2)}, u32[]{:S(2)}) collective-permute-start(f32[3,18,18,1]{2,3,1,0:T(1,128)S(1)} %copy.30), channel_id=1, source_target_pairs={{1,0},{2,1},{3,2},{4,3},{5,4},{6,5},{7,6},{8,7},{9,8},{10,9},{11,1... | collective-permute-start | bytes 11672 | tf_op jit(solution)/shard_map/ppermute | solution.py:31
  30.3 1.0 copy-start.1
  30.3 1.1 copy-start.3
  31.6 5.8 %collective-permute-start.6 = (f32[3,1,16,128]{3,2,1,0:T(8,128)S(1)}, f32[3,1,16,128]{3,2,1,0:T(8,128)S(1)}, u32[]{:S(2)}, u32[]{:S(2)}) collective-permute-start(f32[3,1,16,128]{3,2,1,0:T(8,128)S(1)} %get-tuple-element.69), channel_id=1, source_target_pairs={{0,64},{64,128},{128,192},{192,256},{256,320},{320,384},{384,448},... | collective-permute-start | bytes 73736 | tf_op jit(solution)/shard_map/ppermute | solution.py:30
  35.9 7.3 %collective-permute-start.7 = (f32[3,1,16,128]{3,2,1,0:T(8,128)S(1)}, f32[3,1,16,128]{3,2,1,0:T(8,128)S(1)}, u32[]{:S(2)}, u32[]{:S(2)}) collective-permute-start(f32[3,1,16,128]{3,2,1,0:T(8,128)S(1)} %get-tuple-element.70), channel_id=1, source_target_pairs={{64,0},{128,64},{192,128},{256,192},{320,256},{384,320},{448,384},... | collective-permute-start | bytes 73736 | tf_op jit(solution)/shard_map/ppermute | solution.py:31
  43.2 6.2 %collective-permute-start.8 = (f32[3,18,1,128]{3,2,1,0:T(1,128)S(1)}, f32[3,18,1,128]{3,2,1,0:T(1,128)S(1)}, u32[]{:S(2)}, u32[]{:S(2)}) collective-permute-start(f32[3,18,1,128]{3,2,1,0:T(1,128)S(1)} %get-tuple-element.44), channel_id=1, source_target_pairs={{0,16},{16,32},{32,48},{1,17},{17,33},{33,49},{2,18},{18,34},{34,5... | collective-permute-start | bytes 82952 | tf_op jit(solution)/shard_map/ppermute | solution.py:30
  44.5 6.4 %collective-permute-start.9 = (f32[3,18,1,128]{3,2,1,0:T(1,128)S(1)}, f32[3,18,1,128]{3,2,1,0:T(1,128)S(1)}, u32[]{:S(2)}, u32[]{:S(2)}) collective-permute-start(f32[3,18,1,128]{3,2,1,0:T(1,128)S(1)} %get-tuple-element.45), channel_id=1, source_target_pairs={{16,0},{32,16},{48,32},{17,1},{33,17},{49,33},{18,2},{34,18},{50,3... | collective-permute-start | bytes 82952 | tf_op jit(solution)/shard_map/ppermute | solution.py:31
  51.2 7.6 %copy-start.4 = (f32[16,16,128]{2,1,0:T(8,128)S(1)}, f32[16,16,128]{2,1,0:T(8,128)}, u32[]{:S(2)}) copy-start(f32[16,16,128]{2,1,0:T(8,128)} %param.10) | copy-start | bytes 393220
  51.6 13.7 %collective-permute-start.10 = (f32[3,18,18,1]{2,3,1,0:T(1,128)S(1)}, f32[3,18,18,1]{2,3,1,0:T(1,128)S(1)}, u32[]{:S(2)}, u32[]{:S(2)}) collective-permute-start(f32[3,18,18,1]{2,3,1,0:T(1,128)S(1)} %copy.33), channel_id=1, source_target_pairs={{0,1},{1,2},{2,3},{3,4},{4,5},{5,6},{6,7},{7,8},{8,9},{9,10},{10,1... | collective-permute-start | bytes 11672 | tf_op jit(solution)/shard_map/ppermute | solution.py:30
  54.0 11.8 %collective-permute-start.11 = (f32[3,18,18,1]{2,3,1,0:T(1,128)S(1)}, f32[3,18,18,1]{2,3,1,0:T(1,128)S(1)}, u32[]{:S(2)}, u32[]{:S(2)}) collective-permute-start(f32[3,18,18,1]{2,3,1,0:T(1,128)S(1)} %copy.34), channel_id=1, source_target_pairs={{1,0},{2,1},{3,2},{4,3},{5,4},{6,5},{7,6},{8,7},{9,8},{10,9},{11,1... | collective-permute-start | bytes 11672 | tf_op jit(solution)/shard_map/ppermute | solution.py:31
  58.9 87.1 %collective-permute-start.31 = (f32[1,16,128]{2,1,0:T(8,128)S(1)}, f32[1,16,128]{2,1,0:T(8,128)S(1)}, u32[]{:S(2)}, u32[]{:S(2)}) collective-permute-start(f32[1,16,128]{2,1,0:T(8,128)S(1)} %get-tuple-element.84), channel_id=1, source_target_pairs={{0,64},{64,128},{128,192},{192,256},{256,320},{320,384},{384,448},... | collective-permute-start | bytes 24584 | tf_op jit(solution)/shard_map/ppermute | solution.py:30
  64.0 101.9 %collective-permute-start.30 = (f32[1,16,128]{2,1,0:T(8,128)S(1)}, f32[1,16,128]{2,1,0:T(8,128)S(1)}, u32[]{:S(2)}, u32[]{:S(2)}) collective-permute-start(f32[1,16,128]{2,1,0:T(8,128)S(1)} %get-tuple-element.83), channel_id=1, source_target_pairs={{64,0},{128,64},{192,128},{256,192},{320,256},{384,320},{448,384},... | collective-permute-start | bytes 24584 | tf_op jit(solution)/shard_map/ppermute | solution.py:31
  67.8 6.0 %copy-start.6 = (s32[1,1,1,256,1]{3,4,2,1,0:T(1,128)S(1)}, s32[1,1,1,256,1]{3,4,2,1,0:T(1,128)}, u32[]{:S(2)}) copy-start(s32[1,1,1,256,1]{3,4,2,1,0:T(1,128)} %param.12) | copy-start | bytes 3076
  67.9 6.5 %collective-permute-start.12 = (f32[3,1,16,128]{3,2,1,0:T(8,128)S(1)}, f32[3,1,16,128]{3,2,1,0:T(8,128)S(1)}, u32[]{:S(2)}, u32[]{:S(2)}) collective-permute-start(f32[3,1,16,128]{3,2,1,0:T(8,128)S(1)} %get-tuple-element.67), channel_id=1, source_target_pairs={{0,64},{64,128},{128,192},{192,256},{256,320},{320,384},{384,448},... | collective-permute-start | bytes 73736 | tf_op jit(solution)/shard_map/ppermute | solution.py:30
  72.4 5.7 %collective-permute-start.13 = (f32[3,1,16,128]{3,2,1,0:T(8,128)S(1)}, f32[3,1,16,128]{3,2,1,0:T(8,128)S(1)}, u32[]{:S(2)}, u32[]{:S(2)}) collective-permute-start(f32[3,1,16,128]{3,2,1,0:T(8,128)S(1)} %get-tuple-element.68), channel_id=1, source_target_pairs={{64,0},{128,64},{192,128},{256,192},{320,256},{384,320},{448,384},... | collective-permute-start | bytes 73736 | tf_op jit(solution)/shard_map/ppermute | solution.py:31
  78.2 6.4 %collective-permute-start.14 = (f32[3,18,1,128]{3,2,1,0:T(1,128)S(1)}, f32[3,18,1,128]{3,2,1,0:T(1,128)S(1)}, u32[]{:S(2)}, u32[]{:S(2)}) collective-permute-start(f32[3,18,1,128]{3,2,1,0:T(1,128)S(1)} %get-tuple-element.39), channel_id=1, source_target_pairs={{0,16},{16,32},{32,48},{1,17},{17,33},{33,49},{2,18},{18,34},{34,5... | collective-permute-start | bytes 82952 | tf_op jit(solution)/shard_map/ppermute | solution.py:30
  79.5 6.4 %collective-permute-start.15 = (f32[3,18,1,128]{3,2,1,0:T(1,128)S(1)}, f32[3,18,1,128]{3,2,1,0:T(1,128)S(1)}, u32[]{:S(2)}, u32[]{:S(2)}) collective-permute-start(f32[3,18,1,128]{3,2,1,0:T(1,128)S(1)} %get-tuple-element.40), channel_id=1, source_target_pairs={{16,0},{32,16},{48,32},{17,1},{33,17},{49,33},{18,2},{34,18},{50,3... | collective-permute-start | bytes 82952 | tf_op jit(solution)/shard_map/ppermute | solution.py:31
  84.6 1.7 copy-start.7
  86.2 7.6 %slice-start = ((s32[64,3]{0,1:T(4,128)}), s32[64,2]{0,1:T(2,128)S(1)}, s32[]{:S(2)}) async-start(s32[64,3]{0,1:T(4,128)} %copy-done.7), calls=%async_computation.2 | async-start | bytes 2048 | tf_op jit(solution)/shard_map/slice.1
  86.7 7.3 %collective-permute-start.16 = (f32[3,18,18,1]{2,3,1,0:T(1,128)S(1)}, f32[3,18,18,1]{2,3,1,0:T(1,128)S(1)}, u32[]{:S(2)}, u32[]{:S(2)}) collective-permute-start(f32[3,18,18,1]{2,3,1,0:T(1,128)S(1)} %copy.37), channel_id=1, source_target_pairs={{0,1},{1,2},{2,3},{3,4},{4,5},{5,6},{6,7},{7,8},{8,9},{9,10},{10,1... | collective-permute-start | bytes 11672 | tf_op jit(solution)/shard_map/ppermute | solution.py:30
  89.0 6.4 %collective-permute-start.17 = (f32[3,18,18,1]{2,3,1,0:T(1,128)S(1)}, f32[3,18,18,1]{2,3,1,0:T(1,128)S(1)}, u32[]{:S(2)}, u32[]{:S(2)}) collective-permute-start(f32[3,18,18,1]{2,3,1,0:T(1,128)S(1)} %copy.38), channel_id=1, source_target_pairs={{1,0},{2,1},{3,2},{4,3},{5,4},{6,5},{7,6},{8,7},{9,8},{10,9},{11,1... | collective-permute-start | bytes 11672 | tf_op jit(solution)/shard_map/ppermute | solution.py:31
  97.5 5.4 %collective-permute-start.18 = (f32[3,1,16,128]{3,2,1,0:T(8,128)S(1)}, f32[3,1,16,128]{3,2,1,0:T(8,128)S(1)}, u32[]{:S(2)}, u32[]{:S(2)}) collective-permute-start(f32[3,1,16,128]{3,2,1,0:T(8,128)S(1)} %get-tuple-element.65), channel_id=1, source_target_pairs={{0,64},{64,128},{128,192},{192,256},{256,320},{320,384},{384,448},... | collective-permute-start | bytes 73736 | tf_op jit(solution)/shard_map/ppermute | solution.py:30
  101.4 5.7 %collective-permute-start.19 = (f32[3,1,16,128]{3,2,1,0:T(8,128)S(1)}, f32[3,1,16,128]{3,2,1,0:T(8,128)S(1)}, u32[]{:S(2)}, u32[]{:S(2)}) collective-permute-start(f32[3,1,16,128]{3,2,1,0:T(8,128)S(1)} %get-tuple-element.66), channel_id=1, source_target_pairs={{64,0},{128,64},{192,128},{256,192},{320,256},{384,320},{448,384},... | collective-permute-start | bytes 73736 | tf_op jit(solution)/shard_map/ppermute | solution.py:31
  107.2 6.2 %collective-permute-start.20 = (f32[3,18,1,128]{3,2,1,0:T(1,128)S(1)}, f32[3,18,1,128]{3,2,1,0:T(1,128)S(1)}, u32[]{:S(2)}, u32[]{:S(2)}) collective-permute-start(f32[3,18,1,128]{3,2,1,0:T(1,128)S(1)} %get-tuple-element.34), channel_id=1, source_target_pairs={{0,16},{16,32},{32,48},{1,17},{17,33},{33,49},{2,18},{18,34},{34,5... | collective-permute-start | bytes 82952 | tf_op jit(solution)/shard_map/ppermute | solution.py:30
  108.5 6.4 %collective-permute-start.21 = (f32[3,18,1,128]{3,2,1,0:T(1,128)S(1)}, f32[3,18,1,128]{3,2,1,0:T(1,128)S(1)}, u32[]{:S(2)}, u32[]{:S(2)}) collective-permute-start(f32[3,18,1,128]{3,2,1,0:T(1,128)S(1)} %get-tuple-element.35), channel_id=1, source_target_pairs={{16,0},{32,16},{48,32},{17,1},{33,17},{49,33},{18,2},{34,18},{50,3... | collective-permute-start | bytes 82952 | tf_op jit(solution)/shard_map/ppermute | solution.py:31
  115.2 7.8 %copy-start.8 = (s32[1,1,1,256]{3,2,1,0:T(1,128)S(1)}, s32[1,1,1,256]{3,2,1,0:T(1,128)}, u32[]{:S(2)}) copy-start(s32[1,1,1,256]{3,2,1,0:T(1,128)} %param.13) | copy-start | bytes 3076
  115.7 22.3 %collective-permute-start.22 = (f32[3,18,18,1]{2,3,1,0:T(1,128)S(1)}, f32[3,18,18,1]{2,3,1,0:T(1,128)S(1)}, u32[]{:S(2)}, u32[]{:S(2)}) collective-permute-start(f32[3,18,18,1]{2,3,1,0:T(1,128)S(1)} %copy.41), channel_id=1, source_target_pairs={{0,1},{1,2},{2,3},{3,4},{4,5},{5,6},{6,7},{7,8},{8,9},{9,10},{10,1... | collective-permute-start | bytes 11672 | tf_op jit(solution)/shard_map/ppermute | solution.py:30
  118.0 20.4 %collective-permute-start.23 = (f32[3,18,18,1]{2,3,1,0:T(1,128)S(1)}, f32[3,18,18,1]{2,3,1,0:T(1,128)S(1)}, u32[]{:S(2)}, u32[]{:S(2)}) collective-permute-start(f32[3,18,18,1]{2,3,1,0:T(1,128)S(1)} %copy.42), channel_id=1, source_target_pairs={{1,0},{2,1},{3,2},{4,3},{5,4},{6,5},{7,6},{8,7},{9,8},{10,9},{11,1... | collective-permute-start | bytes 11672 | tf_op jit(solution)/shard_map/ppermute | solution.py:31
  125.6 45.0 %all-to-all-start = ((f32[64,1,8]{2,1,0:T(1,128)}), f32[64,1,8]{2,1,0:T(1,128)S(1)}, u32[]{:S(2)}, u32[]{:S(2)}) async-start(f32[64,1,8]{2,1,0:T(1,128)} %convolution_bitcast_fusion), calls=%async_computation | async-start | bytes 65536 | tf_op jit(solution)/shard_map/all_to_all | solution.py:143
  140.5 27.5 %copy-start = (f32[3,16,16,128]{3,2,1,0:T(8,128)}, f32[3,16,16,128]{3,2,1,0:T(8,128)S(1)}, u32[]{:S(2)}) copy-start(f32[3,16,16,128]{3,2,1,0:T(8,128)S(1)} %fusion.34) | copy-start | bytes 1179652
  140.6 5.6 %collective-permute-start.24 = (f32[3,1,16,128]{3,2,1,0:T(8,128)S(1)}, f32[3,1,16,128]{3,2,1,0:T(8,128)S(1)}, u32[]{:S(2)}, u32[]{:S(2)}) collective-permute-start(f32[3,1,16,128]{3,2,1,0:T(8,128)S(1)} %get-tuple-element.63), channel_id=1, source_target_pairs={{0,64},{64,128},{128,192},{192,256},{256,320},{320,384},{384,448},... | collective-permute-start | bytes 73736 | tf_op jit(solution)/shard_map/ppermute | solution.py:30
  144.6 5.7 %collective-permute-start.25 = (f32[3,1,16,128]{3,2,1,0:T(8,128)S(1)}, f32[3,1,16,128]{3,2,1,0:T(8,128)S(1)}, u32[]{:S(2)}, u32[]{:S(2)}) collective-permute-start(f32[3,1,16,128]{3,2,1,0:T(8,128)S(1)} %get-tuple-element.64), channel_id=1, source_target_pairs={{64,0},{128,64},{192,128},{256,192},{320,256},{384,320},{448,384},... | collective-permute-start | bytes 73736 | tf_op jit(solution)/shard_map/ppermute | solution.py:31
  150.4 5.9 %collective-permute-start.26 = (f32[3,18,1,128]{3,2,1,0:T(1,128)S(1)}, f32[3,18,1,128]{3,2,1,0:T(1,128)S(1)}, u32[]{:S(2)}, u32[]{:S(2)}) collective-permute-start(f32[3,18,1,128]{3,2,1,0:T(1,128)S(1)} %get-tuple-element.29), channel_id=1, source_target_pairs={{0,16},{16,32},{32,48},{1,17},{17,33},{33,49},{2,18},{18,34},{34,5... | collective-permute-start | bytes 82952 | tf_op jit(solution)/shard_map/ppermute | solution.py:30
  151.7 6.1 %collective-permute-start.27 = (f32[3,18,1,128]{3,2,1,0:T(1,128)S(1)}, f32[3,18,1,128]{3,2,1,0:T(1,128)S(1)}, u32[]{:S(2)}, u32[]{:S(2)}) collective-permute-start(f32[3,18,1,128]{3,2,1,0:T(1,128)S(1)} %get-tuple-element.30), channel_id=1, source_target_pairs={{16,0},{32,16},{48,32},{17,1},{33,17},{49,33},{18,2},{34,18},{50,3... | collective-permute-start | bytes 82952 | tf_op jit(solution)/shard_map/ppermute | solution.py:31
  158.6 7.3 %collective-permute-start.28 = (f32[3,18,18,1]{2,1,3,0:T(8,128)S(1)}, f32[3,18,18,1]{2,1,3,0:T(8,128)S(1)}, u32[]{:S(2)}, u32[]{:S(2)}) collective-permute-start(f32[3,18,18,1]{2,1,3,0:T(8,128)S(1)} %copy.46), channel_id=1, source_target_pairs={{0,1},{1,2},{2,3},{3,4},{4,5},{5,6},{6,7},{7,8},{8,9},{9,10},{10,1... | collective-permute-start | bytes 11672 | tf_op jit(solution)/shard_map/ppermute | solution.py:30
  161.1 6.5 %collective-permute-start.29 = (f32[3,18,18,1]{2,1,3,0:T(8,128)S(1)}, f32[3,18,18,1]{2,1,3,0:T(8,128)S(1)}, u32[]{:S(2)}, u32[]{:S(2)}) collective-permute-start(f32[3,18,18,1]{2,1,3,0:T(8,128)S(1)} %copy.47), channel_id=1, source_target_pairs={{1,0},{2,1},{3,2},{4,3},{5,4},{6,5},{7,6},{8,7},{9,8},{10,9},{11,1... | collective-permute-start | bytes 11672 | tf_op jit(solution)/shard_map/ppermute | solution.py:31
  169.4 32.1 %copy-start.5 = (f32[16,16,128]{2,1,0:T(8,128)S(1)}, f32[16,16,128]{2,1,0:T(8,128)}, u32[]{:S(2)}) copy-start(f32[16,16,128]{2,1,0:T(8,128)} %param.11) | copy-start | bytes 393220
  170.6 31.0 %all-to-all-start.1 = ((f32[64,8,128]{2,1,0:T(8,128)}), f32[64,8,128]{2,1,0:T(8,128)S(1)}, u32[]{:S(2)}, u32[]{:S(2)}) async-start(f32[64,8,128]{2,1,0:T(8,128)} %fusion), calls=%async_computation.1 | async-start | bytes 524288 | tf_op jit(solution)/shard_map/all_to_all | solution.py:136
  182.8 4.0 %collective-permute-start.32 = (f32[18,1,128]{2,1,0:T(1,128)S(1)}, f32[18,1,128]{2,1,0:T(1,128)S(1)}, u32[]{:S(2)}, u32[]{:S(2)}) collective-permute-start(f32[18,1,128]{2,1,0:T(1,128)S(1)} %get-tuple-element.80), channel_id=1, source_target_pairs={{16,0},{32,16},{48,32},{17,1},{33,17},{49,33},{18,2},{34,18},{50,3... | collective-permute-start | bytes 27656 | tf_op jit(solution)/shard_map/ppermute | solution.py:31
  185.4 5.6 %collective-permute-start.33 = (f32[18,1,128]{2,1,0:T(1,128)S(1)}, f32[18,1,128]{2,1,0:T(1,128)S(1)}, u32[]{:S(2)}, u32[]{:S(2)}) collective-permute-start(f32[18,1,128]{2,1,0:T(1,128)S(1)} %get-tuple-element.79), channel_id=1, source_target_pairs={{0,16},{16,32},{32,48},{1,17},{17,33},{33,49},{2,18},{18,34},{34,5... | collective-permute-start | bytes 27656 | tf_op jit(solution)/shard_map/ppermute | solution.py:30
  191.2 5.7 %collective-permute-start.34 = (f32[18,18,1]{2,1,0:T(8,128)S(1)}, f32[18,18,1]{2,1,0:T(8,128)S(1)}, u32[]{:S(2)}, u32[]{:S(2)}) collective-permute-start(f32[18,18,1]{2,1,0:T(8,128)S(1)} %get-tuple-element.75), channel_id=1, source_target_pairs={{1,0},{2,1},{3,2},{4,3},{5,4},{6,5},{7,6},{8,7},{9,8},{10,9},{11,1... | collective-permute-start | bytes 3896 | tf_op jit(solution)/shard_map/ppermute | solution.py:31
  193.1 8.5 %collective-permute-start.35 = (f32[18,18,1]{2,1,0:T(8,128)S(1)}, f32[18,18,1]{2,1,0:T(8,128)S(1)}, u32[]{:S(2)}, u32[]{:S(2)}) collective-permute-start(f32[18,18,1]{2,1,0:T(8,128)S(1)} %get-tuple-element.76), channel_id=1, source_target_pairs={{0,1},{1,2},{2,3},{3,4},{4,5},{5,6},{6,7},{7,8},{8,9},{9,10},{10,1... | collective-permute-start | bytes 3896 | tf_op jit(solution)/shard_map/ppermute | solution.py:30
  202.0 5.9 %collective-permute-start.36 = (f32[1,16,128]{2,1,0:T(8,128)S(1)}, f32[1,16,128]{2,1,0:T(8,128)S(1)}, u32[]{:S(2)}, u32[]{:S(2)}) collective-permute-start(f32[1,16,128]{2,1,0:T(8,128)S(1)} %get-tuple-element.82), channel_id=1, source_target_pairs={{64,0},{128,64},{192,128},{256,192},{320,256},{384,320},{448,384},... | collective-permute-start | bytes 24584 | tf_op jit(solution)/shard_map/ppermute | solution.py:31
  203.3 5.9 %collective-permute-start.37 = (f32[1,16,128]{2,1,0:T(8,128)S(1)}, f32[1,16,128]{2,1,0:T(8,128)S(1)}, u32[]{:S(2)}, u32[]{:S(2)}) collective-permute-start(f32[1,16,128]{2,1,0:T(8,128)S(1)} %get-tuple-element.81), channel_id=1, source_target_pairs={{0,64},{64,128},{128,192},{192,256},{256,320},{320,384},{384,448},... | collective-permute-start | bytes 24584 | tf_op jit(solution)/shard_map/ppermute | solution.py:30
  209.2 3.7 %collective-permute-start.38 = (f32[18,1,128]{2,1,0:T(1,128)S(1)}, f32[18,1,128]{2,1,0:T(1,128)S(1)}, u32[]{:S(2)}, u32[]{:S(2)}) collective-permute-start(f32[18,1,128]{2,1,0:T(1,128)S(1)} %get-tuple-element.78), channel_id=1, source_target_pairs={{16,0},{32,16},{48,32},{17,1},{33,17},{49,33},{18,2},{34,18},{50,3... | collective-permute-start | bytes 27656 | tf_op jit(solution)/shard_map/ppermute | solution.py:31
  211.6 5.6 %collective-permute-start.39 = (f32[18,1,128]{2,1,0:T(1,128)S(1)}, f32[18,1,128]{2,1,0:T(1,128)S(1)}, u32[]{:S(2)}, u32[]{:S(2)}) collective-permute-start(f32[18,1,128]{2,1,0:T(1,128)S(1)} %get-tuple-element.77), channel_id=1, source_target_pairs={{0,16},{16,32},{32,48},{1,17},{17,33},{33,49},{2,18},{18,34},{34,5... | collective-permute-start | bytes 27656 | tf_op jit(solution)/shard_map/ppermute | solution.py:30
  217.3 5.4 %collective-permute-start.40 = (f32[18,18,1]{2,1,0:T(8,128)S(1)}, f32[18,18,1]{2,1,0:T(8,128)S(1)}, u32[]{:S(2)}, u32[]{:S(2)}) collective-permute-start(f32[18,18,1]{2,1,0:T(8,128)S(1)} %get-tuple-element.73), channel_id=1, source_target_pairs={{1,0},{2,1},{3,2},{4,3},{5,4},{6,5},{7,6},{8,7},{9,8},{10,9},{11,1... | collective-permute-start | bytes 3896 | tf_op jit(solution)/shard_map/ppermute | solution.py:31
  219.3 8.5 %collective-permute-start.41 = (f32[18,18,1]{2,1,0:T(8,128)S(1)}, f32[18,18,1]{2,1,0:T(8,128)S(1)}, u32[]{:S(2)}, u32[]{:S(2)}) collective-permute-start(f32[18,18,1]{2,1,0:T(8,128)S(1)} %get-tuple-element.74), channel_id=1, source_target_pairs={{0,1},{1,2},{2,3},{3,4},{4,5},{5,6},{6,7},{7,8},{8,9},{9,10},{10,1... | collective-permute-start | bytes 3896 | tf_op jit(solution)/shard_map/ppermute | solution.py:30
where the time goes:
time: 230 us; the launch traced here: 229 us
  starting transfers between devices  145 us (63%)
  waiting for transfers between devices  53.4 us (23%)
  local copies, waits for them, and re-layouts  14.2 us (6%)
  other arithmetic  10.7 us (5%)
  matrix products  4.12 us (2%)
    ppermute x21, starting transfers between devices, padded(): after = lax.ppermute(initial, axis, down)  65.9 us
    ppermute x21, starting transfers between devices, padded(): before = lax.ppermute(last, axis, up)  54.2 us
    ppermute x21, waiting for transfers between devices, padded(): after = lax.ppermute(initial, axis, down)  33.2 us
    ppermute x21, waiting for transfers between devices, padded(): before = lax.ppermute(last, axis, up)  20.3 us
    all_to_all x1, starting transfers between devices, local(): lax.all_to_all(send_slot.reshape(groups, capacity_slots), ('gy', 'gz'), s...  12.4 us
    all_to_all x1, starting transfers between devices, local(): lax.all_to_all(send_heat.reshape(groups, capacity_slots, cells_z), ('gy',...  12.2 us
    concatenate x13, other arithmetic, padded(): array = jnp.concatenate([before, array, after], axis=dim)  4.68 us
  transfers between devices with their start and end apart: 44, of which 25 were waited for; matrix products, arithmetic and copies ran while one was open for 10% of the time, Pallas kernels for 0%

commit v1 on v0

v1 whole, which is shorter than its diff:
```python
import math

import jax
import jax.numpy as jnp
from jax import lax
from jax.experimental import pallas as pl
from jax.experimental.pallas import tpu as pltpu
from jax.sharding import PartitionSpec as P

EM_SWEEPS = 4
HEAT_SWEEPS = 2
CAP = 8
LOW, HIGH = 4, 5
F32 = jnp.float32

em_lower = 0.02
em_upper = 3.0
heat_lower = 0.07
heat_upper = 2.0

UP_LAYERS = ((0, 12, 4), (1, 12, 4), (2, 12, 4), (3, 13, 3), (4, 13, 3), (5, 13, 3), (6, 13, 3), (7, 15, 1))
DOWN_LAYERS = ((0, 0, 4), (1, 0, 5), (2, 0, 5), (3, 0, 3), (4, 0, 4), (5, 0, 4), (6, 0, 4), (7, 0, 1))


def spots(layers, shift):
    where, at = {}, 0
    for field, first, count in layers:
        for x in range(first, first + count):
            where[field, x + shift] = at
            at += 1
    return where, at


UP_AT, UP_COUNT = spots(UP_LAYERS, -16)
DOWN_AT, DOWN_COUNT = spots(DOWN_LAYERS, 16)
X_LAYERS = max(UP_COUNT, DOWN_COUNT)


def chebyshev_weights(lower_end, upper_end, sweep_count):
    middle = 0.5 * (upper_end + lower_end)
    radius = 0.5 * (upper_end - lower_end)
    return [
        1.0 / (middle + radius * math.cos(math.pi * (2 * number + 1) / (2 * sweep_count)))
        for number in range(sweep_count)
    ]


EM_WEIGHTS = chebyshev_weights(em_lower, em_upper, EM_SWEEPS)
HEAT_WEIGHTS = chebyshev_weights(heat_lower, heat_upper, HEAT_SWEEPS)


def on_first_core():
    return lax.rem(lax.axis_index("gz"), 2) == 0


def lanes(shape):
    return lax.broadcasted_iota(jnp.int32, shape, len(shape) - 1)


def rows(shape):
    return lax.broadcasted_iota(jnp.int32, shape, len(shape) - 2)


def roll(values, by, axis):
    size = values.shape[axis]
    by = by % size
    return values if by == 0 else pltpu.roll(values, by, axis)


def call(body, out_shapes, scratch=(), name=None):
    return pl.pallas_call(
        body,
        out_shape=[jax.ShapeDtypeStruct(s, F32) for s in out_shapes],
        scratch_shapes=[pltpu.VMEM(s, F32) for s in scratch],
        compiler_params=pltpu.CompilerParams(vmem_limit_bytes=40 << 20),
        name=name,
    )


def swap_store(first, fwd, bwd, at, up, down):
    fwd[at] = jnp.where(first, up, down)
    bwd[at] = jnp.where(first, down, up)


def pack_x(field, source, sigma, warmth, fwd, bwd, scaled):
    first = on_first_core()
    inverse = 1.0 / (4.0 + sigma[...])
    scaled[3] = inverse
    for c in range(3):
        scaled[c] = source[c] * inverse

    def layer(f, x):
        if f < 3:
            return field[f, x]
        return warmth[x] if f == 7 else scaled[f - 3, x]

    ups = [(f, x) for f, start, n in UP_LAYERS for x in range(start, start + n)]
    downs = [(f, x) for f, start, n in DOWN_LAYERS for x in range(start, start + n)]
    for at in range(X_LAYERS):
        up = layer(*ups[min(at, len(ups) - 1)])
        down = layer(*downs[min(at, len(downs) - 1)])
        swap_store(first, fwd, bwd, at, up, down)


class Slabs:
    def __init__(self, field, scaled, warmth, got_fwd, got_bwd):
        self.field, self.scaled, self.warmth = field, scaled, warmth
        self.got_fwd, self.got_bwd = got_fwd, got_bwd
        self.first = on_first_core()
        gx = lax.axis_index("gx")
        self.below, self.above = gx > 0, gx < lax.axis_size("gx") - 1

    def own(self, f, x):
        if f < 3:
            return self.field[f, x]
        return self.warmth[x] if f == 7 else self.scaled[f - 3, x]

    def beside(self, f, x):
        fwd, bwd = self.got_fwd, self.got_bwd
        if x < 0:
            at = UP_AT.get((f, x))
            if at is None:
                return None
            value = jnp.where(self.first, fwd[at], bwd[at])
            return jnp.where(self.below, value, 0.0)
        at = DOWN_AT.get((f, x))
        if at is None:
            return None
        value = jnp.where(self.first, bwd[at], fwd[at])
        return jnp.where(self.above, value, 0.0)

    def every(self, emit):
        zero = jnp.zeros((16, 128), F32)
        for x in list(range(-LOW, 0)) + list(range(16, 16 + HIGH)):
            values = [self.beside(f, x) for f in range(7)]
            emit(x + LOW, [zero if v is None else v for v in values] + [zero])

        def step(x, carry):
            emit(x + LOW, [self.own(f, x) for f in range(8)])
            return carry

        lax.fori_loop(0, 16, step, 0)


def pack_y(field, scaled, warmth, got_fwd, got_bwd, fwd, bwd):
    slabs = Slabs(field, scaled, warmth, got_fwd, got_bwd)
    row = rows((8, 128))
    low_half = row < 4

    def emit(at, v):
        tops = [a[8:16] for a in v]
        ends = [a[0:8] for a in v]
        for pair in range(4):
            a, b = 2 * pair, 2 * pair + 1
            up = jnp.where(low_half, roll(tops[b], 4, 0), tops[a])
            down = jnp.where(low_half, ends[a], roll(ends[b], 4, 0))
            if pair == 3:
                down = jnp.where(row == 5, roll(ends[0], 1, 0), down)
                down = jnp.where(row == 6, roll(ends[2], 2, 0), down)
            part = pl.ds(8 * pair, 8)
            fwd[at, part] = jnp.where(slabs.first, up, down)
            bwd[at, part] = jnp.where(slabs.first, down, up)

    slabs.every(emit)


def y_halo(first, got_fwd, got_bwd, at, pair):
    gy = lax.axis_index("gy")
    part = pl.ds(8 * pair, 8)
    f, b = got_fwd[at, part], got_bwd[at, part]
    lower = jnp.where(gy > 0, jnp.where(first, f, b), 0.0)
    upper = jnp.where(gy < lax.axis_size("gy") - 1, jnp.where(first, b, f), 0.0)
    return lower, upper


X_ALL = LOW + 16 + HIGH
X_PAIRS = (X_ALL + 1) // 2


def pack_z(field, scaled, warmth, xf, xb, yf, yb, whole, up, down, packed):
    slabs = Slabs(field, scaled, warmth, xf, xb)
    first = slabs.first
    low_half = rows((8, 128)) < 4
    window = lanes((24, 128)) // 16

    def emit(at, v):
        acc = None
        for pair in range(4):
            lower, upper = y_halo(first, yf, yb, at, pair)
            last = []
            last.append(jnp.where(low_half, upper, lower))
            if pair < 3:
                last.append(roll(jnp.where(low_half, lower, upper), 4, 0))
            else:
                last.append(roll(upper, 3, 0))
            for f, tile in zip((2 * pair, 2 * pair + 1), last):
                slab = jnp.concatenate([v[f], tile], axis=0)
                if f < 7:
                    whole[f, at] = slab
                moved = roll(slab, 16 * f + 8, 1)
                acc = moved if acc is None else jnp.where(window == f, moved, acc)
        packed[at] = acc

    slabs.every(emit)
    packed[X_ALL] = jnp.zeros((24, 128), F32)
    half = (lanes((24, 128)) // 8) % 2 == 0

    def pair_up(k, carry):
        a, b = packed[2 * k], packed[2 * k + 1]
        up[k] = jnp.where(half, a, roll(b, 8, 1))
        down[k] = jnp.where(half, roll(a, -8, 1), b)
        return carry

    lax.fori_loop(0, X_PAIRS, pair_up, 0)


def up_z(main, tail):
    last = lanes(main.shape) == 127
    a, b = roll(main, -1, 1), roll(tail, -1, 1)
    return jnp.where(last, b, a), jnp.where(last, a, b)


def down_z(main, tail):
    start = lanes(main.shape) == 0
    a, b = roll(main, 1, 1), roll(tail, 1, 1)
    return jnp.where(start, b, a), jnp.where(start, a, b)


def both(function, *pairs):
    return tuple(function(*parts) for parts in zip(*pairs))


def relax(
    whole, xf, xb, yf, yb, below_z, above_z, sigma, warmth, storage, position, nodes,
    out, send, partial, main, tail, heat, extra,
):
    first = on_first_core()
    gx, gz = lax.axis_index("gx"), lax.axis_index("gz")
    lane = lanes((24, 128))
    row = rows((24, 128))
    half = (lane // 8) % 2 == 0
    edge = (lane < 8) | (lane >= 120)
    has_below, has_above = gz > 0, gz < lax.axis_size("gz") - 1

    def unpack_one(at, packed):
        for f in range(7):
            tail[f, at] = jnp.where(edge, roll(packed, -(16 * f + 8), 1), 0.0)
        tail[7, at] = roll(packed, 8, 1)
        _, upper = y_halo(first, yf, yb, at, 3)
        for n, place in enumerate((5, 6)):
            extra[n, at, 0:8] = jnp.broadcast_to(upper[place : place + 1], (8, 128))
            extra[n, at, 8:16] = jnp.broadcast_to(tail[7, at, 16 + n : 17 + n, :], (8, 128))
        for f in range(3):
            main[f, at] = whole[f, at]

    def unpack(k, carry):
        lower = jnp.where(has_below, below_z[k], 0.0)
        upper = jnp.where(has_above, above_z[k], 0.0)
        unpack_one(2 * k, jnp.where(half, lower, roll(upper, 8, 1)))
        second = jnp.where(half, roll(lower, -8, 1), upper)

        @pl.when(2 * k + 1 < X_ALL)
        def _():
            unpack_one(2 * k + 1, second)

        return carry

    lax.fori_loop(0, X_PAIRS, unpack, 0)

    def up_y(v):
        return roll(v, -1, 0)

    def down_y(v):
        return roll(v, 1, 0)

    def load(f, at):
        return main[f, at], tail[f, at]

    def up_y_edge(v, n, at):
        moved = both(up_y, v)
        edges = (extra[n, at, 0:8], extra[n, at, 8:16])
        return tuple(
            jnp.where(row == 19, jnp.concatenate([e, e, e], axis=0), m)
            for m, e in zip(moved, edges)
        )

    def curls(at, ahead, e, outer):
        ex, ey, ez = e
        ey_ahead, ez_ahead = ahead
        if outer:
            ex_up, ez_up = up_y_edge(ex, 0, at), up_y_edge(ez, 1, at)
        else:
            ex_up, ez_up = both(up_y, ex), both(up_y, ez)
        cx = both(lambda a, b, c, d: (a - b) - (c - d), ez_up, ez, up_z(*ey), ey)
        cy = both(lambda a, b, c, d: (a - b) - (c - d), up_z(*ex), ex, ez_ahead, ez)
        cz = both(lambda a, b, c, d: (a - b) - (c - d), ey_ahead, ey, ex_up, ex)
        return cx, cy, cz

    for number, weight in enumerate(EM_WEIGHTS):
        begin = 1 + number
        outer = number == 0

        def curls_at(at, outer=outer):
            e = [load(f, at) for f in range(3)]
            ahead = (load(1, at + 1), load(2, at + 1))
            return e, curls(at, ahead, e, outer)

        def step(at, carry, weight=weight, curls_at=curls_at):
            cy_before, cz_before = carry
            e, (cx, cy, cz) = curls_at(at)
            kx = both(
                lambda a, b, c, d: (a - b) - (c - d), cz, both(down_y, cz), cy, down_z(*cy)
            )
            ky = both(lambda a, b, c, d: (a - b) - (c - d), cx, down_z(*cx), cz, cz_before)
            kz = both(
                lambda a, b, c, d: (a - b) - (c - d), cy, cy_before, cx, both(down_y, cx)
            )
            g = (whole[6, at] * weight, tail[6, at] * weight)
            keep = both(lambda v: (1.0 - weight) + 4.0 * v, g)
            for f, k in enumerate((kx, ky, kz)):
                h = (whole[3 + f, at], tail[3 + f, at])
                new = both(
                    lambda p, v, s, w, d: p * v + weight * s - w * d, keep, e[f], h, g, k
                )
                main[f, at], tail[f, at] = new
            return cy, cz

        _, (_, cy, cz) = curls_at(begin - 1)
        lax.fori_loop(begin, X_ALL - begin, step, (cy, cz))

    def joule(x, carry):
        at = x + LOW
        ex, ey, ez = (both(lambda v: v * v, load(f, at)) for f in range(3))
        ey_ahead, ez_ahead = (both(lambda v: v * v, load(f, at + 1)) for f in (1, 2))
        a = both(lambda v: v + up_y(v), ex)
        c = both(lambda p, q, r: p + (q + r), a, ey, ey_ahead)
        c = c[0] + up_z(*c)[0]
        d = ez[0] + ez_ahead[0]
        s = c + (d + up_y(d))
        heat[x] = sigma[x] * (0.25 * s[0:16])
        for f in range(3):
            out[f, x] = main[f, at, 0:16, :]
        return carry

    lax.fori_loop(0, 16, joule, 0)

    count = send.shape[0]
    spread = (rows((count, 256)) == position[...]).astype(jnp.bfloat16)
    left = heat[...].reshape(256, 128)
    total = nodes[...]
    for _ in range(3):
        piece = left.astype(jnp.bfloat16)
        left = left - piece.astype(F32)
        total = total + jnp.dot(spread, piece, preferred_element_type=F32)
    send[...] = total

    row16 = rows((16, 128))
    low_at, high_at = UP_AT[7, -1], DOWN_AT[7, 16]
    under = jnp.where(gx > 0, jnp.where(first, xf[low_at], xb[low_at]), 0.0)
    over = jnp.where(
        gx < lax.axis_size("gx") - 1, jnp.where(first, xb[high_at], xf[high_at]), 0.0
    )
    for x in range(16):
        t = warmth[x]
        ends = tail[7, x + LOW, 0:16, :]
        lower, upper = y_halo(first, yf, yb, x + LOW, 3)
        total = (warmth[x - 1] if x else under) + (warmth[x + 1] if x < 15 else over)
        total = total + jnp.where(row16 == 0, lower[3:4], roll(t, 1, 0))
        total = total + jnp.where(row16 == 15, upper[4:5], roll(t, -1, 0))
        total = total + up_z(t, ends)[0] + down_z(t, ends)[0]
        partial[x] = t + HEAT_WEIGHTS[0] * (total - 6.0 * t) / (6.0 + storage[x])


def place(owners, columns, position, nodes):
    groups = lax.axis_size("gy") * lax.axis_size("gz")
    owner, column = owners[...], columns[...]
    member = rows((groups, 256)) == owner
    earlier = (rows((256, 256)) < lanes((256, 256))).astype(jnp.bfloat16)
    before = jnp.dot(member.astype(jnp.bfloat16), earlier, preferred_element_type=F32)
    rank = jnp.sum(jnp.where(member, before, 0.0), axis=0, keepdims=True).astype(jnp.int32)
    position[...] = owner * (CAP + 1) + rank
    count = nodes.shape[0]
    spread = (rows((count, 256)) == owner * (CAP + 1) + CAP).astype(jnp.bfloat16)
    listed = jnp.where(rows((128, 256)) == rank, column + 1, 0).astype(F32).astype(jnp.bfloat16)
    nodes[...] = lax.dot_general(
        spread, listed, (((1,), (1,)), ((), ())), preferred_element_type=F32
    )


def warm(got, partial, warmth, storage, xf, xb, yf, yb, up, down, rest, heat, mid):
    first = on_first_core()
    groups = got.shape[0] // (CAP + 1)
    ids = got[pl.ds(CAP, groups, stride=CAP + 1), :]
    lane = lanes((groups, 256))
    total = None
    for r in range(CAP):
        hit = (ids[:, r : r + 1] == (lane + 1).astype(F32)).astype(jnp.bfloat16)
        left = got[pl.ds(r, groups, stride=CAP + 1), :]
        for _ in range(3):
            piece = left.astype(jnp.bfloat16)
            left = left - piece.astype(F32)
            term = lax.dot_general(
                hit, piece, (((0,), (0,)), ((), ())), preferred_element_type=F32
            )
            total = term if total is None else total + term
    heat[...] = total.reshape(16, 16, 128)
    lane = lanes((16, 128))
    row = rows((16, 128))
    for x in range(16):
        mid[x] = partial[x] + HEAT_WEIGHTS[0] * heat[x] / (6.0 + storage[x])
    xf[...] = jnp.where(first, mid[15], mid[0])
    xb[...] = jnp.where(first, mid[0], mid[15])
    ups = downs = jnp.zeros((16, 128), F32)
    for x in range(16):
        t = mid[x]
        top, end = t[15:16], t[0:1]
        yf[x : x + 1] = jnp.where(first, top, end)
        yb[x : x + 1] = jnp.where(first, end, top)
        ups = jnp.where(lane == 8 * x, roll(t, 8 * x + 1, 1), ups)
        downs = jnp.where(lane == 8 * x, roll(t, 8 * x, 1), downs)
        near = jnp.where(row == 0, 0.0, roll(t, 1, 0)) + jnp.where(row == 15, 0.0, roll(t, -1, 0))
        near = near + jnp.where(lane == 0, 0.0, roll(t, 1, 1))
        near = near + jnp.where(lane == 127, 0.0, roll(t, -1, 1))
        if x > 0:
            near = near + mid[x - 1]
        if x < 15:
            near = near + mid[x + 1]
        s = storage[x]
        push = s * warmth[x] + heat[x] - (6.0 + s) * t + near
        rest[x] = t + HEAT_WEIGHTS[1] * push / (6.0 + s)
    up[...] = ups
    down[...] = downs


def finish(rest, storage, xf, xb, yf, yb, from_below, from_above, out):
    first = on_first_core()
    gx, gy, gz = (lax.axis_index(a) for a in ("gx", "gy", "gz"))
    ends = [a > 0 for a in (gx, gy, gz)]
    tops = [a < lax.axis_size(n) - 1 for a, n in ((gx, "gx"), (gy, "gy"), (gz, "gz"))]
    f, b = xf[...], xb[...]
    x_low = jnp.where(ends[0], jnp.where(first, f, b), 0.0)
    x_high = jnp.where(tops[0], jnp.where(first, b, f), 0.0)
    f, b = yf[...], yb[...]
    y_low = jnp.where(ends[1], jnp.where(first, f, b), 0.0)
    y_high = jnp.where(tops[1], jnp.where(first, b, f), 0.0)
    z_low = jnp.where(ends[2], from_below[...], 0.0)
    z_high = jnp.where(tops[2], from_above[...], 0.0)
    lane = lanes((16, 128))
    row = rows((16, 128))
    for x in range(16):
        near = jnp.where(row == 0, y_low[x : x + 1], 0.0)
        near = near + jnp.where(row == 15, y_high[x : x + 1], 0.0)
        near = near + jnp.where(lane == 0, roll(z_low, -8 * x, 1), 0.0)
        near = near + jnp.where(lane == 127, roll(z_high, 127 - 8 * x, 1), 0.0)
        if x == 0:
            near = near + x_low
        if x == 15:
            near = near + x_high
        out[x] = rest[x] + HEAT_WEIGHTS[1] * near / (6.0 + storage[x])


def around(axis):
    n, m = lax.axis_size(axis), lax.axis_size("gz")

    def target(a, c):
        to = a + (1 if c % 2 == 0 else -1)
        return (to, c) if 0 <= to < n else (a, c ^ 1)

    forward = []
    for a in range(n):
        for c in range(m):
            to = target(a, c)
            forward.append((a * m + c, to[0] * m + to[1]))
    return forward, [(j, i) for i, j in forward]


def exchange(axis, fwd, bwd):
    forward, backward = around(axis)
    names = (axis, "gz")
    return lax.ppermute(fwd, names, forward), lax.ppermute(bwd, names, backward)


def exchange_z(up, down):
    m = lax.axis_size("gz")
    ring = [(i, (i + 1) % m) for i in range(m)]
    return lax.ppermute(up, "gz", ring), lax.ppermute(down, "gz", [(j, i) for i, j in ring])


def local(field, source, sigma, warmth, storage, partition, column):
    groups = lax.axis_size("gy") * lax.axis_size("gz")
    count = groups * (CAP + 1)
    cube = (16, 16, 128)
    face = (16, 128)
    fwd, bwd, scaled = call(
        pack_x, [(X_LAYERS, 16, 128), (X_LAYERS, 16, 128), (4, 16, 16, 128)], name="pack_x"
    )(field, source, sigma, warmth)
    xf, xb = exchange("gx", fwd, bwd)
    position, nodes = pl.pallas_call(
        place,
        out_shape=[
            jax.ShapeDtypeStruct((1, 256), jnp.int32),
            jax.ShapeDtypeStruct((count, 128), F32),
        ],
        name="place",
    )(partition.reshape(1, 256), column.reshape(1, 256))
    fwd, bwd = call(pack_y, [(X_ALL, 32, 128), (X_ALL, 32, 128)], name="pack_y")(
        field, scaled, warmth, xf, xb
    )
    yf, yb = exchange("gy", fwd, bwd)
    whole, up, down = call(
        pack_z,
        [(7, X_ALL, 24, 128), (X_PAIRS, 24, 128), (X_PAIRS, 24, 128)],
        [(X_ALL + 1, 24, 128)],
        name="pack_z",
    )(field, scaled, warmth, xf, xb, yf, yb)
    below_z, above_z = exchange_z(up, down)
    out, send, partial = call(
        relax,
        [(3, *cube), (count, 128), cube],
        [(3, X_ALL, 24, 128), (8, X_ALL, 24, 128), cube, (2, X_ALL, 16, 128)],
        name="relax",
    )(whole, xf, xb, yf, yb, below_z, above_z, sigma, warmth, storage, position, nodes)
    got = lax.all_to_all(
        send.reshape(count, 1, 128), ("gy", "gz"), split_axis=0, concat_axis=0, tiled=True
    ).reshape(count, 128)
    xf, xb, yf, yb, up, down, rest = call(
        warm, [face, face, face, face, face, face, cube], [cube, cube], name="warm"
    )(got, partial, warmth, storage)
    xf, xb = exchange("gx", xf, xb)
    yf, yb = exchange("gy", yf, yb)
    below_z, above_z = exchange_z(up, down)
    (updated,) = call(finish, [cube], name="finish")(
        rest, storage, xf, xb, yf, yb, below_z, above_z
    )
    return out, updated


def solution(mesh):
    in_specs = (
        P(None, "gx", "gy", "gz"),
        P(None, "gx", "gy", "gz"),
        P("gx", "gy", "gz"),
        P("gx", "gy", "gz"),
        P("gx", "gy", "gz"),
        P("gx", "gy", "gz", None, None),
        P("gx", "gy", "gz", None),
    )
    out_specs = (P(None, "gx", "gy", "gz"), P("gx", "gy", "gz"))
    return jax.shard_map(local, mesh=mesh, in_specs=in_specs, out_specs=out_specs, check_vma=False)
```

time: 230 us -> 93.5 us (0.41)
  the two profiles are of different devices: /device:TPU:38 before, /device:TPU:197 now
where the time goes in v1:
time: 93.5 us; the launch traced here: 93.1 us
  Pallas kernels  27.8 us (30%)
  blocking collectives  22.7 us (24%)
  waiting for transfers between devices  17.5 us (19%)
  starting transfers between devices  17 us (18%)
  local copies, waits for them, and re-layouts  7.34 us (8%)
    all_to_all x1, blocking collectives, local(): lax.all_to_all(send.reshape(count, 1, 128), ('gy', 'gz'), split_axis=0, c...  22.7 us
    pallas_call x1, Pallas kernels, local(): call(relax, [(3, *cube), (count, 128), cube], [(3, X_ALL, 24, 128), (8, X...  20.5 us
    ppermute x4, waiting for transfers between devices, exchange(): lax.ppermute(fwd, names, forward)  9.19 us
    ppermute x4, starting transfers between devices, exchange(): lax.ppermute(bwd, names, backward)  8.59 us
    ppermute x2, starting transfers between devices, exchange_z(): lax.ppermute(up, 'gz', ring)  7.89 us
    unnamed x24, local copies, waits for them, and re-layouts  7.34 us
    ppermute x2, waiting for transfers between devices, exchange_z(): lax.ppermute(down, 'gz', [(j, i) for i, j in ring])  5.05 us
    pallas_call x1, Pallas kernels, local(): call(pack_z, [(7, X_ALL, 24, 128), (X_PAIRS, 24, 128), (X_PAIRS, 24, 128)...  3.46 us
  transfers between devices with their start and end apart: 12, of which 8 were waited for; matrix products, arithmetic and copies ran while one was open for 0% of the time, Pallas kernels for 2%

profile of v1, /device:TPU:197, one launch (start us, length us, event | category | flops | bytes accessed | tf_op | source)
XLA Modules:
  0.0 93.1 jit_solution(13892000587684842865)
XLA Ops:
  0.6 0.0 copy-start
  0.6 1.0 %copy-done = f32[3,16,16,128]{3,2,1,0:T(8,128)S(1)} copy-done((f32[3,16,16,128]{3,2,1,0:T(8,128)S(1)}, f32[3,16,16,128]{3,2,1,0:T(8,128)}, u32[]{:S(2)}) %copy-start) | copy-done | bytes 393240
  1.6 0.0 copy-start.1
  1.6 0.9 copy-done.1
  2.5 0.0 copy-start.7
  2.5 0.9 copy-done.7
  3.4 0.0 copy-start.9
  3.4 1.0 %copy-done.9 = f32[3,16,16,128]{3,2,1,0:T(8,128)S(1)} copy-done((f32[3,16,16,128]{3,2,1,0:T(8,128)S(1)}, f32[3,16,16,128]{3,2,1,0:T(8,128)}, u32[]{:S(2)}) %copy-start.9) | copy-done | bytes 393240
  4.4 0.0 copy-start.3
  4.4 0.0 copy-start.6
  4.4 0.0 copy-start.8
  4.4 0.1 pack_x.1
  4.5 0.0 collective-permute-start
  4.5 3.3 %collective-permute-start.1 = (f32[30,16,128]{2,1,0:T(8,128)S(1)}, f32[30,16,128]{2,1,0:T(8,128)S(1)}, u32[]{:S(2)}, u32[]{:S(2)}) collective-permute-start(f32[30,16,128]{2,1,0:T(8,128)S(1)} %get-tuple-element.24), channel_id=1, source_target_pairs={{64,0},{0,1},{66,2},{2,3},{68,4},{4,5},{70,6},{6,7},{72,8},{8,9},{... | collective-permute-start | bytes 737288 | tf_op jit(solution)/shard_map/ppermute | solution.py:480
  7.9 3.6 %collective-permute-done.got_fwd.xf = f32[30,16,128]{2,1,0:T(8,128)S(1)} collective-permute-done((f32[30,16,128]{2,1,0:T(8,128)S(1)}, f32[30,16,128]{2,1,0:T(8,128)S(1)}, u32[]{:S(2)}, u32[]{:S(2)}) %collective-permute-start) | collective-permute-done | bytes 245792 | tf_op jit(solution)/shard_map/ppermute | solution.py:480
  11.4 1.1 %collective-permute-done.1.got_bwd.xb = f32[30,16,128]{2,1,0:T(8,128)S(1)} collective-permute-done((f32[30,16,128]{2,1,0:T(8,128)S(1)}, f32[30,16,128]{2,1,0:T(8,128)S(1)}, u32[]{:S(2)}, u32[]{:S(2)}) %collective-permute-start.1) | collective-permute-done | bytes 245792 | tf_op jit(solution)/shard_map/ppermute | solution.py:480
  12.5 0.0 copy-start.2
  12.5 0.9 copy-done.2
  13.4 0.2 pack_y.1
  13.6 0.3 collective-permute-start.2
  13.9 1.2 %collective-permute-start.3 = (f32[25,32,128]{2,1,0:T(8,128)S(1)}, f32[25,32,128]{2,1,0:T(8,128)S(1)}, u32[]{:S(2)}, u32[]{:S(2)}) collective-permute-start(f32[25,32,128]{2,1,0:T(8,128)S(1)} %get-tuple-element.26), channel_id=1, source_target_pairs={{16,0},{0,1},{18,2},{2,3},{20,4},{4,5},{22,6},{6,7},{24,8},{8,9},{... | collective-permute-start | bytes 1228808 | tf_op jit(solution)/shard_map/ppermute | solution.py:480
  15.1 5.6 %collective-permute-done.2.yf = f32[25,32,128]{2,1,0:T(8,128)S(1)} collective-permute-done((f32[25,32,128]{2,1,0:T(8,128)S(1)}, f32[25,32,128]{2,1,0:T(8,128)S(1)}, u32[]{:S(2)}, u32[]{:S(2)}) %collective-permute-start.2) | collective-permute-done | bytes 409632 | tf_op jit(solution)/shard_map/ppermute | solution.py:480
  20.7 0.7 collective-permute-done.3.yb
  21.4 0.0 copy-start.4
  21.4 3.5 %pack_z.1 = (f32[7,25,24,128]{3,2,1,0:T(8,128)S(1)}, f32[13,24,128]{2,1,0:T(8,128)}, f32[13,24,128]{2,1,0:T(8,128)}) custom-call(f32[3,16,16,128]{3,2,1,0:T(8,128)S(1)} %copy-done, f32[4,16,16,128]{3,2,1,0:T(8,128)S(1)} %get-tuple-element.22.scaled, f32[16,16,128]{2,1,0:T(8,128)S(1)} %copy-done.2, f32[30,16,128]{2,1,0:T(8,128)S(1)} %collective-permute-done.got_fwd.xf, ...), custom_call_target="tpu_custom_call" | custom-call | tf_op jit(solution)/shard_map/pack_z/pallas_call | solution.py:510
  24.9 0.0 copy-done.4
  24.9 6.2 %collective-permute-start.4 = (f32[13,24,128]{2,1,0:T(8,128)}, f32[13,24,128]{2,1,0:T(8,128)}, u32[]{:S(2)}, u32[]{:S(2)}) collective-permute-start(f32[13,24,128]{2,1,0:T(8,128)} %get-tuple-element.28), channel_id=1, source_target_pairs={{0,1},{1,2},{2,3},{3,4},{4,5},{5,6},{6,7},{7,8},{8,9},{9,10},{10,1... | collective-permute-start | bytes 479240 | tf_op jit(solution)/shard_map/ppermute | solution.py:486
  31.1 0.0 collective-permute-start.5
  31.1 1.8 %place.1 = (s32[1,256]{1,0:T(1,128)}, f32[576,128]{1,0:T(8,128)}) custom-call(s32[1,256]{1,0:T(1,128)} %bitcast.8, s32[1,256]{1,0:T(1,128)} %bitcast.9), custom_call_target="tpu_custom_call" | custom-call | tf_op jit(solution)/shard_map/place/pallas_call | solution.py:498
  33.0 0.7 collective-permute-done.4.below_z
  33.7 2.5 %collective-permute-done.5.above_z = f32[13,24,128]{2,1,0:T(8,128)} collective-permute-done((f32[13,24,128]{2,1,0:T(8,128)}, f32[13,24,128]{2,1,0:T(8,128)}, u32[]{:S(2)}, u32[]{:S(2)}) %collective-permute-start.5) | collective-permute-done | bytes 159776 | tf_op jit(solution)/shard_map/ppermute | solution.py:486
  36.1 0.0 copy-done.3
  36.1 0.0 copy-done.6
  36.1 0.0 copy-done.8
  36.1 0.0 copy-start.5
  36.2 1.0 %copy-done.5 = f32[25,32,128]{2,1,0:T(8,128)S(1)} copy-done((f32[25,32,128]{2,1,0:T(8,128)S(1)}, f32[25,32,128]{2,1,0:T(8,128)}, u32[]{:S(2)}) %copy-start.5) | copy-done | bytes 409624
  37.2 0.0 copy-start.10
  37.2 1.0 %copy-done.10 = f32[576,128]{1,0:T(8,128)S(1)} copy-done((f32[576,128]{1,0:T(8,128)S(1)}, f32[576,128]{1,0:T(8,128)}, u32[]{:S(2)}) %copy-start.10) | copy-done | bytes 294936
  38.1 0.0 copy-start.11
  38.1 0.7 copy-done.11
  38.8 20.5 %relax.1 = (f32[3,16,16,128]{3,2,1,0:T(8,128)}, f32[576,128]{1,0:T(8,128)S(1)}, f32[16,16,128]{2,1,0:T(8,128)S(1)}) custom-call(f32[7,25,24,128]{3,2,1,0:T(8,128)S(1)} %get-tuple-element.27.whole, f32[30,16,128]{2,1,0:T(8,128)S(1)} %collective-permute-done.got_fwd.xf, f32[30,16,128]{2,1,0:T(8,128)S(1)} %collective-permute-done.1.got_bwd.xb, ...), custom_call_target="tpu_custom_call" | custom-call | tf_op jit(solution)/shard_map/relax/pallas_call | solution.py:517
  59.3 22.7 %all_to_all.5 = f32[576,1,128]{2,1,0:T(1,128)S(1)} all-to-all(f32[576,1,128]{2,1,0:T(1,128)S(1)} %bitcast.7), channel_id=1, replica_groups=mesh['gx'=8,'gy'=4,'gz'=16] {'gy','gz'}, dimensions={0} | all-to-all | bytes 589824 | tf_op jit(solution)/shard_map/all_to_all | solution.py:523
  82.0 1.0 %warm.1 = (f32[16,128]{1,0:T(8,128)S(1)}, f32[16,128]{1,0:T(8,128)S(1)}, f32[16,128]{1,0:T(8,128)S(1)}, f32[16,128]{1,0:T(8,128)S(1)}, f32[16,128]{1,0:T(8,128)S...) custom-call(f32[576,128]{1,0:T(8,128)S(1)} %bitcast.6, f32[16,16,128]{2,1,0:T(8,128)S(1)} %get-tuple-element.34.partial, ...), custom_call_target="tpu_custom_call" | custom-call | tf_op jit(solution)/shard_map/warm/pallas_call | solution.py:526
  83.0 0.0 collective-permute-start.6
  83.0 2.8 %collective-permute-start.7 = (f32[16,128]{1,0:T(8,128)S(1)}, f32[16,128]{1,0:T(8,128)S(1)}, u32[]{:S(2)}, u32[]{:S(2)}) collective-permute-start(f32[16,128]{1,0:T(8,128)S(1)} %get-tuple-element.37), channel_id=1, source_target_pairs={{64,0},{0,1},{66,2},{2,3},{68,4},{4,5},{70,6},{6,7},{72,8},{8,9},{... | collective-permute-start | bytes 24584 | tf_op jit(solution)/shard_map/ppermute | solution.py:480
  85.8 0.2 collective-permute-start.8
  86.0 1.3 %collective-permute-start.9 = (f32[16,128]{1,0:T(8,128)S(1)}, f32[16,128]{1,0:T(8,128)S(1)}, u32[]{:S(2)}, u32[]{:S(2)}) collective-permute-start(f32[16,128]{1,0:T(8,128)S(1)} %get-tuple-element.39), channel_id=1, source_target_pairs={{16,0},{0,1},{18,2},{2,3},{20,4},{4,5},{22,6},{6,7},{24,8},{8,9},{... | collective-permute-start | bytes 24584 | tf_op jit(solution)/shard_map/ppermute | solution.py:480
  87.3 1.7 %collective-permute-start.10 = (f32[16,128]{1,0:T(8,128)S(1)}, f32[16,128]{1,0:T(8,128)S(1)}, u32[]{:S(2)}, u32[]{:S(2)}) collective-permute-start(f32[16,128]{1,0:T(8,128)S(1)} %get-tuple-element.40), channel_id=1, source_target_pairs={{0,1},{1,2},{2,3},{3,4},{4,5},{5,6},{6,7},{7,8},{8,9},{9,10},{10,1... | collective-permute-start | bytes 24584 | tf_op jit(solution)/shard_map/ppermute | solution.py:486
  88.9 0.0 collective-permute-done.6.xf
  88.9 0.0 collective-permute-start.11
  88.9 0.0 collective-permute-done.7.xb
  88.9 0.0 collective-permute-done.8.yf
  89.0 0.0 collective-permute-done.9.yb
  89.0 0.8 collective-permute-done.10.from_below
  89.7 2.6 %collective-permute-done.11.from_above = f32[16,128]{1,0:T(8,128)S(1)} collective-permute-done((f32[16,128]{1,0:T(8,128)S(1)}, f32[16,128]{1,0:T(8,128)S(1)}, u32[]{:S(2)}, u32[]{:S(2)}) %collective-permute-start.11) | collective-permute-done | bytes 8224 | tf_op jit(solution)/shard_map/ppermute | solution.py:486
  92.3 0.8 finish.1
Async XLA Ops:
  0.6 1.0 %copy-start = (f32[3,16,16,128]{3,2,1,0:T(8,128)S(1)}, f32[3,16,16,128]{3,2,1,0:T(8,128)}, u32[]{:S(2)}) copy-start(f32[3,16,16,128]{3,2,1,0:T(8,128)} %field.5) | copy-start | bytes 1179652
  1.6 0.9 copy-start.1
  2.5 0.9 copy-start.7
  3.4 1.0 %copy-start.9 = (f32[3,16,16,128]{3,2,1,0:T(8,128)S(1)}, f32[3,16,16,128]{3,2,1,0:T(8,128)}, u32[]{:S(2)}) copy-start(f32[3,16,16,128]{3,2,1,0:T(8,128)} %source.1) | copy-start | bytes 1179652
  4.4 31.7 %copy-start.3 = (f32[16,16,128]{2,1,0:T(8,128)S(1)}, f32[16,16,128]{2,1,0:T(8,128)}, u32[]{:S(2)}) copy-start(f32[16,16,128]{2,1,0:T(8,128)} %warmth.9) | copy-start | bytes 393220
  4.4 31.7 %copy-start.6 = (f32[16,16,128]{2,1,0:T(8,128)S(1)}, f32[16,16,128]{2,1,0:T(8,128)}, u32[]{:S(2)}) copy-start(f32[16,16,128]{2,1,0:T(8,128)} %storage.5) | copy-start | bytes 393220
  4.4 31.7 %copy-start.8 = (f32[16,16,128]{2,1,0:T(8,128)S(1)}, f32[16,16,128]{2,1,0:T(8,128)}, u32[]{:S(2)}) copy-start(f32[16,16,128]{2,1,0:T(8,128)} %sigma.3) | copy-start | bytes 393220
  4.5 6.9 %collective-permute-start = (f32[30,16,128]{2,1,0:T(8,128)S(1)}, f32[30,16,128]{2,1,0:T(8,128)S(1)}, u32[]{:S(2)}, u32[]{:S(2)}) collective-permute-start(f32[30,16,128]{2,1,0:T(8,128)S(1)} %get-tuple-element.23), channel_id=1, source_target_pairs={{0,64},{1,0},{2,66},{3,2},{4,68},{5,4},{6,70},{7,6},{8,72},{9,8},{... | collective-permute-start | bytes 737288 | tf_op jit(solution)/shard_map/ppermute | solution.py:480
  4.5 8.0 %collective-permute-start.1 = (f32[30,16,128]{2,1,0:T(8,128)S(1)}, f32[30,16,128]{2,1,0:T(8,128)S(1)}, u32[]{:S(2)}, u32[]{:S(2)}) collective-permute-start(f32[30,16,128]{2,1,0:T(8,128)S(1)} %get-tuple-element.24), channel_id=1, source_target_pairs={{64,0},{0,1},{66,2},{2,3},{68,4},{4,5},{70,6},{6,7},{72,8},{8,9},{... | collective-permute-start | bytes 737288 | tf_op jit(solution)/shard_map/ppermute | solution.py:480
  12.5 0.9 copy-start.2
  13.6 7.1 %collective-permute-start.2 = (f32[25,32,128]{2,1,0:T(8,128)S(1)}, f32[25,32,128]{2,1,0:T(8,128)S(1)}, u32[]{:S(2)}, u32[]{:S(2)}) collective-permute-start(f32[25,32,128]{2,1,0:T(8,128)S(1)} %get-tuple-element.25), channel_id=1, source_target_pairs={{0,16},{1,0},{2,18},{3,2},{4,20},{5,4},{6,22},{7,6},{8,24},{9,8},{... | collective-permute-start | bytes 1228808 | tf_op jit(solution)/shard_map/ppermute | solution.py:480
  13.9 7.5 %collective-permute-start.3 = (f32[25,32,128]{2,1,0:T(8,128)S(1)}, f32[25,32,128]{2,1,0:T(8,128)S(1)}, u32[]{:S(2)}, u32[]{:S(2)}) collective-permute-start(f32[25,32,128]{2,1,0:T(8,128)S(1)} %get-tuple-element.26), channel_id=1, source_target_pairs={{16,0},{0,1},{18,2},{2,3},{20,4},{4,5},{22,6},{6,7},{24,8},{8,9},{... | collective-permute-start | bytes 1228808 | tf_op jit(solution)/shard_map/ppermute | solution.py:480
  21.4 3.5 %copy-start.4 = (f32[25,32,128]{2,1,0:T(8,128)}, f32[25,32,128]{2,1,0:T(8,128)S(1)}, u32[]{:S(2)}) copy-start(f32[25,32,128]{2,1,0:T(8,128)S(1)} %collective-permute-done.3.yb) | copy-start | bytes 1228804
  24.9 8.8 %collective-permute-start.4 = (f32[13,24,128]{2,1,0:T(8,128)}, f32[13,24,128]{2,1,0:T(8,128)}, u32[]{:S(2)}, u32[]{:S(2)}) collective-permute-start(f32[13,24,128]{2,1,0:T(8,128)} %get-tuple-element.28), channel_id=1, source_target_pairs={{0,1},{1,2},{2,3},{3,4},{4,5},{5,6},{6,7},{7,8},{8,9},{9,10},{10,1... | collective-permute-start | bytes 479240 | tf_op jit(solution)/shard_map/ppermute | solution.py:486
  31.1 5.0 %collective-permute-start.5 = (f32[13,24,128]{2,1,0:T(8,128)}, f32[13,24,128]{2,1,0:T(8,128)}, u32[]{:S(2)}, u32[]{:S(2)}) collective-permute-start(f32[13,24,128]{2,1,0:T(8,128)} %get-tuple-element.29), channel_id=1, source_target_pairs={{1,0},{2,1},{3,2},{4,3},{5,4},{6,5},{7,6},{8,7},{9,8},{10,9},{11,1... | collective-permute-start | bytes 479240 | tf_op jit(solution)/shard_map/ppermute | solution.py:486
  36.1 1.0 %copy-start.5 = (f32[25,32,128]{2,1,0:T(8,128)S(1)}, f32[25,32,128]{2,1,0:T(8,128)}, u32[]{:S(2)}) copy-start(f32[25,32,128]{2,1,0:T(8,128)} %copy-done.4) | copy-start | bytes 1228804
  37.2 1.0 %copy-start.10 = (f32[576,128]{1,0:T(8,128)S(1)}, f32[576,128]{1,0:T(8,128)}, u32[]{:S(2)}) copy-start(f32[576,128]{1,0:T(8,128)} %get-tuple-element.31.nodes) | copy-start | bytes 884740
  38.1 0.7 copy-start.11
  83.0 5.9 %collective-permute-start.6 = (f32[16,128]{1,0:T(8,128)S(1)}, f32[16,128]{1,0:T(8,128)S(1)}, u32[]{:S(2)}, u32[]{:S(2)}) collective-permute-start(f32[16,128]{1,0:T(8,128)S(1)} %get-tuple-element.36), channel_id=1, source_target_pairs={{0,64},{1,0},{2,66},{3,2},{4,68},{5,4},{6,70},{7,6},{8,72},{9,8},{... | collective-permute-start | bytes 24584 | tf_op jit(solution)/shard_map/ppermute | solution.py:480
  83.0 5.9 %collective-permute-start.7 = (f32[16,128]{1,0:T(8,128)S(1)}, f32[16,128]{1,0:T(8,128)S(1)}, u32[]{:S(2)}, u32[]{:S(2)}) collective-permute-start(f32[16,128]{1,0:T(8,128)S(1)} %get-tuple-element.37), channel_id=1, source_target_pairs={{64,0},{0,1},{66,2},{2,3},{68,4},{4,5},{70,6},{6,7},{72,8},{8,9},{... | collective-permute-start | bytes 24584 | tf_op jit(solution)/shard_map/ppermute | solution.py:480
  85.8 3.2 %collective-permute-start.8 = (f32[16,128]{1,0:T(8,128)S(1)}, f32[16,128]{1,0:T(8,128)S(1)}, u32[]{:S(2)}, u32[]{:S(2)}) collective-permute-start(f32[16,128]{1,0:T(8,128)S(1)} %get-tuple-element.38), channel_id=1, source_target_pairs={{0,16},{1,0},{2,18},{3,2},{4,20},{5,4},{6,22},{7,6},{8,24},{9,8},{... | collective-permute-start | bytes 24584 | tf_op jit(solution)/shard_map/ppermute | solution.py:480
  86.0 3.0 %collective-permute-start.9 = (f32[16,128]{1,0:T(8,128)S(1)}, f32[16,128]{1,0:T(8,128)S(1)}, u32[]{:S(2)}, u32[]{:S(2)}) collective-permute-start(f32[16,128]{1,0:T(8,128)S(1)} %get-tuple-element.39), channel_id=1, source_target_pairs={{16,0},{0,1},{18,2},{2,3},{20,4},{4,5},{22,6},{6,7},{24,8},{8,9},{... | collective-permute-start | bytes 24584 | tf_op jit(solution)/shard_map/ppermute | solution.py:480
  87.3 2.5 %collective-permute-start.10 = (f32[16,128]{1,0:T(8,128)S(1)}, f32[16,128]{1,0:T(8,128)S(1)}, u32[]{:S(2)}, u32[]{:S(2)}) collective-permute-start(f32[16,128]{1,0:T(8,128)S(1)} %get-tuple-element.40), channel_id=1, source_target_pairs={{0,1},{1,2},{2,3},{3,4},{4,5},{5,6},{6,7},{7,8},{8,9},{9,10},{10,1... | collective-permute-start | bytes 24584 | tf_op jit(solution)/shard_map/ppermute | solution.py:486
  88.9 3.4 %collective-permute-start.11 = (f32[16,128]{1,0:T(8,128)S(1)}, f32[16,128]{1,0:T(8,128)S(1)}, u32[]{:S(2)}, u32[]{:S(2)}) collective-permute-start(f32[16,128]{1,0:T(8,128)S(1)} %get-tuple-element.41), channel_id=1, source_target_pairs={{1,0},{2,1},{3,2},{4,3},{5,4},{6,5},{7,6},{8,7},{9,8},{10,9},{11,1... | collective-permute-start | bytes 24584 | tf_op jit(solution)/shard_map/ppermute | solution.py:486

commit v2 on v1

--- a/solution.py
+++ b/solution.py
@@ -67,13 +67,14 @@
     return values if by == 0 else pltpu.roll(values, by, axis)
 
 
-def call(body, out_shapes, scratch=(), name=None):
+def call(body, out_shapes, scratch=(), name=None, **options):
     return pl.pallas_call(
         body,
         out_shape=[jax.ShapeDtypeStruct(s, F32) for s in out_shapes],
-        scratch_shapes=[pltpu.VMEM(s, F32) for s in scratch],
+        scratch_shapes=[pltpu.VMEM(s, F32) if isinstance(s, tuple) else s for s in scratch],
         compiler_params=pltpu.CompilerParams(vmem_limit_bytes=40 << 20),
         name=name,
+        **options,
     )
 
 
@@ -82,7 +83,16 @@
     bwd[at] = jnp.where(first, down, up)
 
 
-def pack_x(field, source, sigma, warmth, fwd, bwd, scaled):
+def pack_x(*refs):
+    far, (fwd, bwd, scaled, field, sigma, warmth, storage, source, arrived) = refs[:5], refs[5:]
+    near = (field, source, sigma, warmth, storage)
+    copies = [
+        pltpu.make_async_copy(a, b, arrived.at[n]) for n, (a, b) in enumerate(zip(far, near))
+    ]
+    for copy in copies:
+        copy.start()
+    for copy in copies:
+        copy.wait()
     first = on_first_core()
     inverse = 1.0 / (4.0 + sigma[...])
     scaled[3] = inverse
@@ -129,7 +139,7 @@
         value = jnp.where(self.first, bwd[at], fwd[at])
         return jnp.where(self.above, value, 0.0)
 
-    def every(self, emit):
+    def every(self, emit, unroll=4):
         zero = jnp.zeros((16, 128), F32)
         for x in list(range(-LOW, 0)) + list(range(16, 16 + HIGH)):
             values = [self.beside(f, x) for f in range(7)]
@@ -139,7 +149,7 @@
             emit(x + LOW, [self.own(f, x) for f in range(8)])
             return carry
 
-        lax.fori_loop(0, 16, step, 0)
+        lax.fori_loop(0, 16, step, 0, unroll=unroll)
 
 
 def pack_y(field, scaled, warmth, got_fwd, got_bwd, fwd, bwd):
@@ -211,7 +221,7 @@
         down[k] = jnp.where(half, roll(a, -8, 1), b)
         return carry
 
-    lax.fori_loop(0, X_PAIRS, pair_up, 0)
+    lax.fori_loop(0, X_PAIRS, pair_up, 0, unroll=True)
 
 
 def up_z(main, tail):
@@ -232,7 +242,7 @@
 
 def relax(
     whole, xf, xb, yf, yb, below_z, above_z, sigma, warmth, storage, position, nodes,
-    out, send, partial, main, tail, heat, extra,
+    out, send, partial, main, tail, other, far, heat, extra,
 ):
     first = on_first_core()
     gx, gz = lax.axis_index("gx"), lax.axis_index("gz")
@@ -250,8 +260,6 @@
         for n, place in enumerate((5, 6)):
             extra[n, at, 0:8] = jnp.broadcast_to(upper[place : place + 1], (8, 128))
             extra[n, at, 8:16] = jnp.broadcast_to(tail[7, at, 16 + n : 17 + n, :], (8, 128))
-        for f in range(3):
-            main[f, at] = whole[f, at]
 
     def unpack(k, carry):
         lower = jnp.where(has_below, below_z[k], 0.0)
@@ -259,13 +267,13 @@
         unpack_one(2 * k, jnp.where(half, lower, roll(upper, 8, 1)))
         second = jnp.where(half, roll(lower, -8, 1), upper)
 
-        @pl.when(2 * k + 1 < X_ALL)
-        def _():
-            unpack_one(2 * k + 1, second)
-
+        unpack_one(2 * k + 1, second)
         return carry
 
-    lax.fori_loop(0, X_PAIRS, unpack, 0)
+    lax.fori_loop(0, X_ALL // 2, unpack, 0, unroll=4)
+    lower = jnp.where(has_below, below_z[X_PAIRS - 1], 0.0)
+    upper = jnp.where(has_above, above_z[X_PAIRS - 1], 0.0)
+    unpack_one(X_ALL - 1, jnp.where(half, lower, roll(upper, 8, 1)))
 
     def up_y(v):
         return roll(v, -1, 0)
@@ -273,8 +281,10 @@
     def down_y(v):
         return roll(v, 1, 0)
 
-    def load(f, at):
-        return main[f, at], tail[f, at]
+    buffers = [(whole, tail), (main, far), (other, tail), (main, far), (other, tail)]
+
+    def load(number, f, at):
+        return buffers[number][0][f, at], buffers[number][1][f, at]
 
     def up_y_edge(v, n, at):
         moved = both(up_y, v)
@@ -300,12 +310,12 @@
         begin = 1 + number
         outer = number == 0
 
-        def curls_at(at, outer=outer):
-            e = [load(f, at) for f in range(3)]
-            ahead = (load(1, at + 1), load(2, at + 1))
+        def curls_at(at, number=number, outer=outer):
+            e = [load(number, f, at) for f in range(3)]
+            ahead = (load(number, 1, at + 1), load(number, 2, at + 1))
             return e, curls(at, ahead, e, outer)
 
-        def step(at, carry, weight=weight, curls_at=curls_at):
+        def step(at, carry, number=number, weight=weight, curls_at=curls_at):
             cy_before, cz_before = carry
             e, (cx, cy, cz) = curls_at(at)
             kx = both(
@@ -322,16 +332,16 @@
                 new = both(
                     lambda p, v, s, w, d: p * v + weight * s - w * d, keep, e[f], h, g, k
                 )
-                main[f, at], tail[f, at] = new
+                buffers[number + 1][0][f, at], buffers[number + 1][1][f, at] = new
             return cy, cz
 
         _, (_, cy, cz) = curls_at(begin - 1)
-        lax.fori_loop(begin, X_ALL - begin, step, (cy, cz))
+        lax.fori_loop(begin, X_ALL - begin, step, (cy, cz), unroll=4)
 
     def joule(x, carry):
         at = x + LOW
-        ex, ey, ez = (both(lambda v: v * v, load(f, at)) for f in range(3))
-        ey_ahead, ez_ahead = (both(lambda v: v * v, load(f, at + 1)) for f in (1, 2))
+        ex, ey, ez = (both(lambda v: v * v, load(EM_SWEEPS, f, at)) for f in range(3))
+        ey_ahead, ez_ahead = (both(lambda v: v * v, load(EM_SWEEPS, f, at + 1)) for f in (1, 2))
         a = both(lambda v: v + up_y(v), ex)
         c = both(lambda p, q, r: p + (q + r), a, ey, ey_ahead)
         c = c[0] + up_z(*c)[0]
@@ -339,10 +349,10 @@
         s = c + (d + up_y(d))
         heat[x] = sigma[x] * (0.25 * s[0:16])
         for f in range(3):
-            out[f, x] = main[f, at, 0:16, :]
+            out[f, x] = other[f, at, 0:16, :]
         return carry
 
-    lax.fori_loop(0, 16, joule, 0)
+    lax.fori_loop(0, 16, joule, 0, unroll=4)
 
     count = send.shape[0]
     spread = (rows((count, 256)) == position[...]).astype(jnp.bfloat16)
@@ -491,9 +501,13 @@
     count = groups * (CAP + 1)
     cube = (16, 16, 128)
     face = (16, 128)
-    fwd, bwd, scaled = call(
-        pack_x, [(X_LAYERS, 16, 128), (X_LAYERS, 16, 128), (4, 16, 16, 128)], name="pack_x"
-    )(field, source, sigma, warmth)
+    fwd, bwd, scaled, field, sigma, warmth, storage = call(
+        pack_x,
+        [(X_LAYERS, 16, 128), (X_LAYERS, 16, 128), (4, *cube), (3, *cube), cube, cube, cube],
+        [(3, *cube), pltpu.SemaphoreType.DMA((5,))],
+        name="pack_x",
+        in_specs=[pl.BlockSpec(memory_space=pltpu.HBM)] * 5,
+    )(field, source, sigma, warmth, storage)
     xf, xb = exchange("gx", fwd, bwd)
     position, nodes = pl.pallas_call(
         place,
@@ -517,7 +531,14 @@
     out, send, partial = call(
         relax,
         [(3, *cube), (count, 128), cube],
-        [(3, X_ALL, 24, 128), (8, X_ALL, 24, 128), cube, (2, X_ALL, 16, 128)],
+        [
+            (3, X_ALL, 24, 128),
+            (8, X_ALL, 24, 128),
+            (3, X_ALL, 24, 128),
+            (3, X_ALL, 24, 128),
+            cube,
+            (2, X_ALL, 16, 128),
+        ],
         name="relax",
     )(whole, xf, xb, yf, yb, below_z, above_z, sigma, warmth, storage, position, nodes)
     got = lax.all_to_all(

time: 93.5 us -> 84.8 us (0.907)
  the two profiles are of different devices: /device:TPU:197 before, /device:TPU:194 now
where the time goes in v2:
time: 84.8 us; the launch traced here: 84.4 us
  blocking collectives  21.5 us (25%)
  waiting for transfers between devices  20.6 us (24%)
  Pallas kernels  16.8 us (20%)
  starting transfers between devices  16.6 us (20%)
  local copies, waits for them, and re-layouts  8.24 us (10%)
    all_to_all x1, blocking collectives, local(): lax.all_to_all(send.reshape(count, 1, 128), ('gy', 'gz'), split_axis=0, c...  21.5 us
    ppermute x4, waiting for transfers between devices, exchange(): lax.ppermute(fwd, names, forward)  13.9 us
    pallas_call x1, Pallas kernels, local(): call(relax, [(3, *cube), (count, 128), cube], [(3, X_ALL, 24, 128), (8, X...  10.1 us
    ppermute x4, starting transfers between devices, exchange(): lax.ppermute(fwd, names, forward)  9.71 us
    unnamed x22, local copies, waits for them, and re-layouts  8.24 us
    ppermute x2, starting transfers between devices, exchange_z(): lax.ppermute(down, 'gz', [(j, i) for i, j in ring])  5.74 us
    ppermute x4, waiting for transfers between devices, exchange(): lax.ppermute(bwd, names, backward)  5.38 us
    pallas_call x1, Pallas kernels, local(): call(pack_z, [(7, X_ALL, 24, 128), (X_PAIRS, 24, 128), (X_PAIRS, 24, 128)...  1.88 us
  transfers between devices with their start and end apart: 12, of which 6 were waited for; matrix products, arithmetic and copies ran while one was open for 0% of the time, Pallas kernels for 2%

profile of v2, /device:TPU:194, one launch (start us, length us, event | category | flops | bytes accessed | tf_op | source)
XLA Modules:
  0.0 84.4 jit_solution(3768937213253559276)
XLA Ops:
  0.6 0.0 copy-start.2
  0.6 1.0 %copy-done.2 = f32[3,16,16,128]{3,2,1,0:T(8,128)S(1)} copy-done((f32[3,16,16,128]{3,2,1,0:T(8,128)S(1)}, f32[3,16,16,128]{3,2,1,0:T(8,128)}, u32[]{:S(2)}) %copy-start.2) | copy-done | bytes 393240
  1.6 0.0 copy-start.3
  1.6 1.0 %copy-done.3 = f32[3,16,16,128]{3,2,1,0:T(8,128)S(1)} copy-done((f32[3,16,16,128]{3,2,1,0:T(8,128)S(1)}, f32[3,16,16,128]{3,2,1,0:T(8,128)}, u32[]{:S(2)}) %copy-start.3) | copy-done | bytes 393240
  2.6 0.0 copy-start.5
  2.6 0.9 %copy-done.5 = f32[16,16,128]{2,1,0:T(8,128)S(1)} copy-done((f32[16,16,128]{2,1,0:T(8,128)S(1)}, f32[16,16,128]{2,1,0:T(8,128)}, u32[]{:S(2)}) %copy-start.5) | copy-done | bytes 131096
  3.5 0.0 copy-start.6
  3.5 0.9 %copy-done.6 = f32[16,16,128]{2,1,0:T(8,128)S(1)} copy-done((f32[16,16,128]{2,1,0:T(8,128)S(1)}, f32[16,16,128]{2,1,0:T(8,128)}, u32[]{:S(2)}) %copy-start.6) | copy-done | bytes 131096
  4.4 0.0 copy-start.7
  4.4 0.9 %copy-done.7 = f32[16,16,128]{2,1,0:T(8,128)S(1)} copy-done((f32[16,16,128]{2,1,0:T(8,128)S(1)}, f32[16,16,128]{2,1,0:T(8,128)}, u32[]{:S(2)}) %copy-start.7) | copy-done | bytes 131096
  5.3 1.0 %pack_x.1 = (f32[30,16,128]{2,1,0:T(8,128)S(1)}, f32[30,16,128]{2,1,0:T(8,128)S(1)}, f32[4,16,16,128]{3,2,1,0:T(8,128)S(1)}, f32[3,16,16,128]{3,2,1,0:T(8,128)S(...) custom-call(f32[3,16,16,128]{3,2,1,0:T(8,128)S(1)} %copy-done.2, ...), custom_call_target="tpu_custom_call" | custom-call | tf_op jit(solution)/shard_map/pack_x/pallas_call | solution.py:504
  6.3 0.0 copy-start.8
  6.4 3.6 %collective-permute-start = (f32[30,16,128]{2,1,0:T(8,128)S(1)}, f32[30,16,128]{2,1,0:T(8,128)S(1)}, u32[]{:S(2)}, u32[]{:S(2)}) collective-permute-start(f32[30,16,128]{2,1,0:T(8,128)S(1)} %get-tuple-element.29), channel_id=1, source_target_pairs={{0,64},{1,0},{2,66},{3,2},{4,68},{5,4},{6,70},{7,6},{8,72},{9,8},{... | collective-permute-start | bytes 737288 | tf_op jit(solution)/shard_map/ppermute | solution.py:490
  10.0 0.0 collective-permute-start.1
  10.0 5.2 %collective-permute-done.got_fwd.xf = f32[30,16,128]{2,1,0:T(8,128)S(1)} collective-permute-done((f32[30,16,128]{2,1,0:T(8,128)S(1)}, f32[30,16,128]{2,1,0:T(8,128)S(1)}, u32[]{:S(2)}, u32[]{:S(2)}) %collective-permute-start) | collective-permute-done | bytes 245792 | tf_op jit(solution)/shard_map/ppermute | solution.py:490
  15.2 2.2 %collective-permute-done.1.got_bwd.xb = f32[30,16,128]{2,1,0:T(8,128)S(1)} collective-permute-done((f32[30,16,128]{2,1,0:T(8,128)S(1)}, f32[30,16,128]{2,1,0:T(8,128)S(1)}, u32[]{:S(2)}, u32[]{:S(2)}) %collective-permute-start.1) | collective-permute-done | bytes 245792 | tf_op jit(solution)/shard_map/ppermute | solution.py:490
  17.4 0.1 pack_y.1
  17.5 0.0 copy-done.8
  17.5 1.5 %collective-permute-start.2 = (f32[25,32,128]{2,1,0:T(8,128)S(1)}, f32[25,32,128]{2,1,0:T(8,128)S(1)}, u32[]{:S(2)}, u32[]{:S(2)}) collective-permute-start(f32[25,32,128]{2,1,0:T(8,128)S(1)} %get-tuple-element.31), channel_id=1, source_target_pairs={{0,16},{1,0},{2,18},{3,2},{4,20},{5,4},{6,22},{7,6},{8,24},{9,8},{... | collective-permute-start | bytes 1228808 | tf_op jit(solution)/shard_map/ppermute | solution.py:490
  19.0 0.5 collective-permute-start.3
  19.6 8.6 %collective-permute-done.2.yf = f32[25,32,128]{2,1,0:T(8,128)S(1)} collective-permute-done((f32[25,32,128]{2,1,0:T(8,128)S(1)}, f32[25,32,128]{2,1,0:T(8,128)S(1)}, u32[]{:S(2)}, u32[]{:S(2)}) %collective-permute-start.2) | collective-permute-done | bytes 409632 | tf_op jit(solution)/shard_map/ppermute | solution.py:490
  28.2 0.0 collective-permute-done.3.yb
  28.2 0.0 copy-start
  28.2 1.9 %pack_z.1 = (f32[7,25,24,128]{3,2,1,0:T(8,128)S(1)}, f32[13,24,128]{2,1,0:T(8,128)}, f32[13,24,128]{2,1,0:T(8,128)}) custom-call(f32[3,16,16,128]{3,2,1,0:T(8,128)S(1)} %get-tuple-element.26.field, f32[4,16,16,128]{3,2,1,0:T(8,128)S(1)} %get-tuple-element.27.scaled, f32[16,16,128]{2,1,0:T(8,128)S(1)} %get-tuple-element.28.warmth, ...), custom_call_target="tpu_custom_call" | custom-call | tf_op jit(solution)/shard_map/pack_z/pallas_call | solution.py:524
  30.1 0.0 copy-done
  30.1 0.0 collective-permute-start.4
  30.1 3.0 %collective-permute-start.5 = (f32[13,24,128]{2,1,0:T(8,128)}, f32[13,24,128]{2,1,0:T(8,128)}, u32[]{:S(2)}, u32[]{:S(2)}) collective-permute-start(f32[13,24,128]{2,1,0:T(8,128)} %get-tuple-element.35), channel_id=1, source_target_pairs={{1,0},{2,1},{3,2},{4,3},{5,4},{6,5},{7,6},{8,7},{9,8},{10,9},{11,1... | collective-permute-start | bytes 479240 | tf_op jit(solution)/shard_map/ppermute | solution.py:496
  33.1 1.8 %place.1 = (s32[1,256]{1,0:T(1,128)}, f32[576,128]{1,0:T(8,128)}) custom-call(s32[1,256]{1,0:T(1,128)} %bitcast.8, s32[1,256]{1,0:T(1,128)} %bitcast.9), custom_call_target="tpu_custom_call" | custom-call | tf_op jit(solution)/shard_map/place/pallas_call | solution.py:512
  34.9 1.3 %collective-permute-done.4.below_z = f32[13,24,128]{2,1,0:T(8,128)S(1)} collective-permute-done((f32[13,24,128]{2,1,0:T(8,128)}, f32[13,24,128]{2,1,0:T(8,128)S(1)}, u32[]{:S(2)}, u32[]{:S(2)}) %collective-permute-start.4) | collective-permute-done | bytes 159776 | tf_op jit(solution)/shard_map/ppermute | solution.py:496
  36.2 0.0 collective-permute-done.5.above_z
  36.2 0.0 copy-start.1
  36.2 1.0 %copy-done.1 = f32[25,32,128]{2,1,0:T(8,128)S(1)} copy-done((f32[25,32,128]{2,1,0:T(8,128)S(1)}, f32[25,32,128]{2,1,0:T(8,128)}, u32[]{:S(2)}) %copy-start.1) | copy-done | bytes 409624
  37.2 0.0 copy-start.4
  37.2 1.0 %copy-done.4 = f32[576,128]{1,0:T(8,128)S(1)} copy-done((f32[576,128]{1,0:T(8,128)S(1)}, f32[576,128]{1,0:T(8,128)}, u32[]{:S(2)}) %copy-start.4) | copy-done | bytes 294936
  38.2 0.0 copy-start.9
  38.2 0.9 %copy-done.9 = f32[16,16,128]{2,1,0:T(8,128)S(1)} copy-done((f32[16,16,128]{2,1,0:T(8,128)S(1)}, f32[16,16,128]{2,1,0:T(8,128)}, u32[]{:S(2)}) %copy-start.9) | copy-done | bytes 131096
  39.1 0.0 copy-start.10
  39.1 0.7 copy-done.10
  39.8 10.1 %relax.1 = (f32[3,16,16,128]{3,2,1,0:T(8,128)}, f32[576,128]{1,0:T(8,128)S(1)}, f32[16,16,128]{2,1,0:T(8,128)S(1)}) custom-call(f32[7,25,24,128]{3,2,1,0:T(8,128)S(1)} %get-tuple-element.33.whole, f32[30,16,128]{2,1,0:T(8,128)S(1)} %collective-permute-done.got_fwd.xf, f32[30,16,128]{2,1,0:T(8,128)S(1)} %collective-permute-done.1.got_bwd.xb, ...), custom_call_target="tpu_custom_call" | custom-call | tf_op jit(solution)/shard_map/relax/pallas_call | solution.py:531
  49.9 21.5 %all_to_all.5 = f32[576,1,128]{2,1,0:T(1,128)S(1)} all-to-all(f32[576,1,128]{2,1,0:T(1,128)S(1)} %bitcast.7), channel_id=1, replica_groups=mesh['gx'=8,'gy'=4,'gz'=16] {'gy','gz'}, dimensions={0} | all-to-all | bytes 589824 | tf_op jit(solution)/shard_map/all_to_all | solution.py:544
  71.4 1.0 %warm.1 = (f32[16,128]{1,0:T(8,128)S(1)}, f32[16,128]{1,0:T(8,128)S(1)}, f32[16,128]{1,0:T(8,128)S(1)}, f32[16,128]{1,0:T(8,128)S(1)}, f32[16,128]{1,0:T(8,128)S...) custom-call(f32[576,128]{1,0:T(8,128)S(1)} %bitcast.6, f32[16,16,128]{2,1,0:T(8,128)S(1)} %get-tuple-element.42.partial, ...), custom_call_target="tpu_custom_call" | custom-call | tf_op jit(solution)/shard_map/warm/pallas_call | solution.py:547
  72.4 0.2 collective-permute-start.10
  72.6 2.8 %collective-permute-start.11 = (f32[16,128]{1,0:T(8,128)S(1)}, f32[16,128]{1,0:T(8,128)S(1)}, u32[]{:S(2)}, u32[]{:S(2)}) collective-permute-start(f32[16,128]{1,0:T(8,128)S(1)} %get-tuple-element.49), channel_id=1, source_target_pairs={{1,0},{2,1},{3,2},{4,3},{5,4},{6,5},{7,6},{8,7},{9,8},{10,9},{11,1... | collective-permute-start | bytes 24584 | tf_op jit(solution)/shard_map/ppermute | solution.py:496
  75.4 3.0 %collective-permute-start.6 = (f32[16,128]{1,0:T(8,128)S(1)}, f32[16,128]{1,0:T(8,128)S(1)}, u32[]{:S(2)}, u32[]{:S(2)}) collective-permute-start(f32[16,128]{1,0:T(8,128)S(1)} %get-tuple-element.44), channel_id=1, source_target_pairs={{0,64},{1,0},{2,66},{3,2},{4,68},{5,4},{6,70},{7,6},{8,72},{9,8},{... | collective-permute-start | bytes 24584 | tf_op jit(solution)/shard_map/ppermute | solution.py:490
  78.4 0.0 collective-permute-start.7
  78.4 1.6 %collective-permute-start.8 = (f32[16,128]{1,0:T(8,128)S(1)}, f32[16,128]{1,0:T(8,128)S(1)}, u32[]{:S(2)}, u32[]{:S(2)}) collective-permute-start(f32[16,128]{1,0:T(8,128)S(1)} %get-tuple-element.46), channel_id=1, source_target_pairs={{0,16},{1,0},{2,18},{3,2},{4,20},{5,4},{6,22},{7,6},{8,24},{9,8},{... | collective-permute-start | bytes 24584 | tf_op jit(solution)/shard_map/ppermute | solution.py:490
  80.0 0.0 collective-permute-done.10.from_below
  80.0 0.4 collective-permute-start.9
  80.4 0.0 collective-permute-done.11.from_above
  80.4 0.0 collective-permute-done.6.xf
  80.4 2.8 %collective-permute-done.7.xb = f32[16,128]{1,0:T(8,128)S(1)} collective-permute-done((f32[16,128]{1,0:T(8,128)S(1)}, f32[16,128]{1,0:T(8,128)S(1)}, u32[]{:S(2)}, u32[]{:S(2)}) %collective-permute-start.7) | collective-permute-done | bytes 8224 | tf_op jit(solution)/shard_map/ppermute | solution.py:490
  83.2 0.0 collective-permute-done.8.yf
  83.2 0.4 collective-permute-done.9.yb
  83.6 0.8 finish.1
Async XLA Ops:
  0.6 1.0 %copy-start.2 = (f32[3,16,16,128]{3,2,1,0:T(8,128)S(1)}, f32[3,16,16,128]{3,2,1,0:T(8,128)}, u32[]{:S(2)}) copy-start(f32[3,16,16,128]{3,2,1,0:T(8,128)} %refs_0_.1) | copy-start | bytes 1179652
  1.6 1.0 %copy-start.3 = (f32[3,16,16,128]{3,2,1,0:T(8,128)S(1)}, f32[3,16,16,128]{3,2,1,0:T(8,128)}, u32[]{:S(2)}) copy-start(f32[3,16,16,128]{3,2,1,0:T(8,128)} %refs_1_.1) | copy-start | bytes 1179652
  2.6 0.9 %copy-start.5 = (f32[16,16,128]{2,1,0:T(8,128)S(1)}, f32[16,16,128]{2,1,0:T(8,128)}, u32[]{:S(2)}) copy-start(f32[16,16,128]{2,1,0:T(8,128)} %refs_2_.1) | copy-start | bytes 393220
  3.5 0.9 %copy-start.6 = (f32[16,16,128]{2,1,0:T(8,128)S(1)}, f32[16,16,128]{2,1,0:T(8,128)}, u32[]{:S(2)}) copy-start(f32[16,16,128]{2,1,0:T(8,128)} %refs_3_.1) | copy-start | bytes 393220
  4.4 0.9 %copy-start.7 = (f32[16,16,128]{2,1,0:T(8,128)S(1)}, f32[16,16,128]{2,1,0:T(8,128)}, u32[]{:S(2)}) copy-start(f32[16,16,128]{2,1,0:T(8,128)} %refs_4_.1) | copy-start | bytes 393220
  6.3 11.2 %copy-start.8 = (f32[16,16,128]{2,1,0:T(8,128)}, f32[16,16,128]{2,1,0:T(8,128)S(1)}, u32[]{:S(2)}) copy-start(f32[16,16,128]{2,1,0:T(8,128)S(1)} %get-tuple-element.36.sigma) | copy-start | bytes 393220
  6.4 8.8 %collective-permute-start = (f32[30,16,128]{2,1,0:T(8,128)S(1)}, f32[30,16,128]{2,1,0:T(8,128)S(1)}, u32[]{:S(2)}, u32[]{:S(2)}) collective-permute-start(f32[30,16,128]{2,1,0:T(8,128)S(1)} %get-tuple-element.29), channel_id=1, source_target_pairs={{0,64},{1,0},{2,66},{3,2},{4,68},{5,4},{6,70},{7,6},{8,72},{9,8},{... | collective-permute-start | bytes 737288 | tf_op jit(solution)/shard_map/ppermute | solution.py:490
  10.0 7.4 %collective-permute-start.1 = (f32[30,16,128]{2,1,0:T(8,128)S(1)}, f32[30,16,128]{2,1,0:T(8,128)S(1)}, u32[]{:S(2)}, u32[]{:S(2)}) collective-permute-start(f32[30,16,128]{2,1,0:T(8,128)S(1)} %get-tuple-element.30), channel_id=1, source_target_pairs={{64,0},{0,1},{66,2},{2,3},{68,4},{4,5},{70,6},{6,7},{72,8},{8,9},{... | collective-permute-start | bytes 737288 | tf_op jit(solution)/shard_map/ppermute | solution.py:490
  17.5 10.7 %collective-permute-start.2 = (f32[25,32,128]{2,1,0:T(8,128)S(1)}, f32[25,32,128]{2,1,0:T(8,128)S(1)}, u32[]{:S(2)}, u32[]{:S(2)}) collective-permute-start(f32[25,32,128]{2,1,0:T(8,128)S(1)} %get-tuple-element.31), channel_id=1, source_target_pairs={{0,16},{1,0},{2,18},{3,2},{4,20},{5,4},{6,22},{7,6},{8,24},{9,8},{... | collective-permute-start | bytes 1228808 | tf_op jit(solution)/shard_map/ppermute | solution.py:490
  19.0 9.2 %collective-permute-start.3 = (f32[25,32,128]{2,1,0:T(8,128)S(1)}, f32[25,32,128]{2,1,0:T(8,128)S(1)}, u32[]{:S(2)}, u32[]{:S(2)}) collective-permute-start(f32[25,32,128]{2,1,0:T(8,128)S(1)} %get-tuple-element.32), channel_id=1, source_target_pairs={{16,0},{0,1},{18,2},{2,3},{20,4},{4,5},{22,6},{6,7},{24,8},{8,9},{... | collective-permute-start | bytes 1228808 | tf_op jit(solution)/shard_map/ppermute | solution.py:490
  28.2 1.9 %copy-start = (f32[25,32,128]{2,1,0:T(8,128)}, f32[25,32,128]{2,1,0:T(8,128)S(1)}, u32[]{:S(2)}) copy-start(f32[25,32,128]{2,1,0:T(8,128)S(1)} %collective-permute-done.3.yb) | copy-start | bytes 1228804
  30.1 6.1 %collective-permute-start.4 = (f32[13,24,128]{2,1,0:T(8,128)}, f32[13,24,128]{2,1,0:T(8,128)S(1)}, u32[]{:S(2)}, u32[]{:S(2)}) collective-permute-start(f32[13,24,128]{2,1,0:T(8,128)} %get-tuple-element.34), channel_id=1, source_target_pairs={{0,1},{1,2},{2,3},{3,4},{4,5},{5,6},{6,7},{7,8},{8,9},{9,10},{10,1... | collective-permute-start | bytes 479240 | tf_op jit(solution)/shard_map/ppermute | solution.py:496
  30.1 6.1 %collective-permute-start.5 = (f32[13,24,128]{2,1,0:T(8,128)}, f32[13,24,128]{2,1,0:T(8,128)}, u32[]{:S(2)}, u32[]{:S(2)}) collective-permute-start(f32[13,24,128]{2,1,0:T(8,128)} %get-tuple-element.35), channel_id=1, source_target_pairs={{1,0},{2,1},{3,2},{4,3},{5,4},{6,5},{7,6},{8,7},{9,8},{10,9},{11,1... | collective-permute-start | bytes 479240 | tf_op jit(solution)/shard_map/ppermute | solution.py:496
  36.2 1.0 %copy-start.1 = (f32[25,32,128]{2,1,0:T(8,128)S(1)}, f32[25,32,128]{2,1,0:T(8,128)}, u32[]{:S(2)}) copy-start(f32[25,32,128]{2,1,0:T(8,128)} %copy-done) | copy-start | bytes 1228804
  37.2 1.0 %copy-start.4 = (f32[576,128]{1,0:T(8,128)S(1)}, f32[576,128]{1,0:T(8,128)}, u32[]{:S(2)}) copy-start(f32[576,128]{1,0:T(8,128)} %get-tuple-element.39.nodes) | copy-start | bytes 884740
  38.2 0.9 %copy-start.9 = (f32[16,16,128]{2,1,0:T(8,128)S(1)}, f32[16,16,128]{2,1,0:T(8,128)}, u32[]{:S(2)}) copy-start(f32[16,16,128]{2,1,0:T(8,128)} %copy-done.8) | copy-start | bytes 393220
  39.1 0.7 copy-start.10
  72.4 7.6 %collective-permute-start.10 = (f32[16,128]{1,0:T(8,128)S(1)}, f32[16,128]{1,0:T(8,128)S(1)}, u32[]{:S(2)}, u32[]{:S(2)}) collective-permute-start(f32[16,128]{1,0:T(8,128)S(1)} %get-tuple-element.48), channel_id=1, source_target_pairs={{0,1},{1,2},{2,3},{3,4},{4,5},{5,6},{6,7},{7,8},{8,9},{9,10},{10,1... | collective-permute-start | bytes 24584 | tf_op jit(solution)/shard_map/ppermute | solution.py:496
  72.6 7.8 %collective-permute-start.11 = (f32[16,128]{1,0:T(8,128)S(1)}, f32[16,128]{1,0:T(8,128)S(1)}, u32[]{:S(2)}, u32[]{:S(2)}) collective-permute-start(f32[16,128]{1,0:T(8,128)S(1)} %get-tuple-element.49), channel_id=1, source_target_pairs={{1,0},{2,1},{3,2},{4,3},{5,4},{6,5},{7,6},{8,7},{9,8},{10,9},{11,1... | collective-permute-start | bytes 24584 | tf_op jit(solution)/shard_map/ppermute | solution.py:496
  75.4 5.0 %collective-permute-start.6 = (f32[16,128]{1,0:T(8,128)S(1)}, f32[16,128]{1,0:T(8,128)S(1)}, u32[]{:S(2)}, u32[]{:S(2)}) collective-permute-start(f32[16,128]{1,0:T(8,128)S(1)} %get-tuple-element.44), channel_id=1, source_target_pairs={{0,64},{1,0},{2,66},{3,2},{4,68},{5,4},{6,70},{7,6},{8,72},{9,8},{... | collective-permute-start | bytes 24584 | tf_op jit(solution)/shard_map/ppermute | solution.py:490
  78.4 4.9 %collective-permute-start.7 = (f32[16,128]{1,0:T(8,128)S(1)}, f32[16,128]{1,0:T(8,128)S(1)}, u32[]{:S(2)}, u32[]{:S(2)}) collective-permute-start(f32[16,128]{1,0:T(8,128)S(1)} %get-tuple-element.45), channel_id=1, source_target_pairs={{64,0},{0,1},{66,2},{2,3},{68,4},{4,5},{70,6},{6,7},{72,8},{8,9},{... | collective-permute-start | bytes 24584 | tf_op jit(solution)/shard_map/ppermute | solution.py:490
  78.4 4.9 %collective-permute-start.8 = (f32[16,128]{1,0:T(8,128)S(1)}, f32[16,128]{1,0:T(8,128)S(1)}, u32[]{:S(2)}, u32[]{:S(2)}) collective-permute-start(f32[16,128]{1,0:T(8,128)S(1)} %get-tuple-element.46), channel_id=1, source_target_pairs={{0,16},{1,0},{2,18},{3,2},{4,20},{5,4},{6,22},{7,6},{8,24},{9,8},{... | collective-permute-start | bytes 24584 | tf_op jit(solution)/shard_map/ppermute | solution.py:490
  80.0 3.7 %collective-permute-start.9 = (f32[16,128]{1,0:T(8,128)S(1)}, f32[16,128]{1,0:T(8,128)S(1)}, u32[]{:S(2)}, u32[]{:S(2)}) collective-permute-start(f32[16,128]{1,0:T(8,128)S(1)} %get-tuple-element.47), channel_id=1, source_target_pairs={{16,0},{0,1},{18,2},{2,3},{20,4},{4,5},{22,6},{6,7},{24,8},{8,9},{... | collective-permute-start | bytes 24584 | tf_op jit(solution)/shard_map/ppermute | solution.py:490

commit v3 on v2

--- a/solution.py
+++ b/solution.py
@@ -1,3 +1,4 @@
+import functools
 import math
 
 import jax
@@ -12,6 +13,7 @@
 CAP = 8
 LOW, HIGH = 4, 5
 F32 = jnp.float32
+FIRST_LIMIT = 62 << 20
 
 em_lower = 0.02
 em_upper = 3.0
@@ -67,12 +69,12 @@
     return values if by == 0 else pltpu.roll(values, by, axis)
 
 
-def call(body, out_shapes, scratch=(), name=None, **options):
+def call(body, out_shapes, scratch=(), name=None, limit=8 << 20, **options):
     return pl.pallas_call(
         body,
         out_shape=[jax.ShapeDtypeStruct(s, F32) for s in out_shapes],
         scratch_shapes=[pltpu.VMEM(s, F32) if isinstance(s, tuple) else s for s in scratch],
-        compiler_params=pltpu.CompilerParams(vmem_limit_bytes=40 << 20),
+        compiler_params=pltpu.CompilerParams(vmem_limit_bytes=limit),
         name=name,
         **options,
     )
@@ -83,9 +85,25 @@
     bwd[at] = jnp.where(first, down, up)
 
 
-def pack_x(*refs):
-    far, (fwd, bwd, scaled, field, sigma, warmth, storage, source, arrived) = refs[:5], refs[5:]
-    near = (field, source, sigma, warmth, storage)
+def y_tiles(v, first, fwd, bwd, at):
+    row = rows((8, 128))
+    low_half = row < 4
+    tops = [a[8:16] for a in v]
+    ends = [a[0:8] for a in v]
+    for pair in range(4):
+        a, b = 2 * pair, 2 * pair + 1
+        up = jnp.where(low_half, roll(tops[b], 4, 0), tops[a])
+        down = jnp.where(low_half, ends[a], roll(ends[b], 4, 0))
+        if pair == 3:
+            down = jnp.where(row == 5, roll(ends[0], 1, 0), down)
+            down = jnp.where(row == 6, roll(ends[2], 2, 0), down)
+        part = pl.ds(8 * pair, 8)
+        fwd[at, part] = jnp.where(first, up, down)
+        bwd[at, part] = jnp.where(first, down, up)
+
+
+def pack_xy(*refs):
+    far, (xf, xb, yf, yb), near, (scaled, arrived) = refs[:4], refs[4:8], refs[8:12], refs[12:]
     copies = [
         pltpu.make_async_copy(a, b, arrived.at[n]) for n, (a, b) in enumerate(zip(far, near))
     ]
@@ -93,6 +111,7 @@
         copy.start()
     for copy in copies:
         copy.wait()
+    field, source, sigma, warmth = near
     first = on_first_core()
     inverse = 1.0 / (4.0 + sigma[...])
     scaled[3] = inverse
@@ -109,7 +128,20 @@
     for at in range(X_LAYERS):
         up = layer(*ups[min(at, len(ups) - 1)])
         down = layer(*downs[min(at, len(downs) - 1)])
-        swap_store(first, fwd, bwd, at, up, down)
+        swap_store(first, xf, xb, at, up, down)
+
+    def step(x, carry):
+        y_tiles([layer(f, x) for f in range(8)], first, yf, yb, x)
+        return carry
+
+    lax.fori_loop(0, 16, step, 0, unroll=4)
+
+
+def scale(source, sigma, scaled):
+    inverse = 1.0 / (4.0 + sigma[...])
+    scaled[3] = inverse
+    for c in range(3):
+        scaled[c] = source[c] * inverse
 
 
 class Slabs:
@@ -139,64 +171,49 @@
         value = jnp.where(self.first, bwd[at], fwd[at])
         return jnp.where(self.above, value, 0.0)
 
-    def every(self, emit, unroll=4):
+    def halo(self, emit):
         zero = jnp.zeros((16, 128), F32)
-        for x in list(range(-LOW, 0)) + list(range(16, 16 + HIGH)):
+        for number, x in enumerate(HALO_X):
             values = [self.beside(f, x) for f in range(7)]
-            emit(x + LOW, [zero if v is None else v for v in values] + [zero])
-
+            emit(number, x + LOW, [zero if v is None else v for v in values] + [zero])
+
+    def inner(self, emit):
         def step(x, carry):
-            emit(x + LOW, [self.own(f, x) for f in range(8)])
+            emit(x, x + LOW, [self.own(f, x) for f in range(8)])
             return carry
 
-        lax.fori_loop(0, 16, step, 0, unroll=unroll)
-
-
-def pack_y(field, scaled, warmth, got_fwd, got_bwd, fwd, bwd):
-    slabs = Slabs(field, scaled, warmth, got_fwd, got_bwd)
-    row = rows((8, 128))
-    low_half = row < 4
-
-    def emit(at, v):
-        tops = [a[8:16] for a in v]
-        ends = [a[0:8] for a in v]
-        for pair in range(4):
-            a, b = 2 * pair, 2 * pair + 1
-            up = jnp.where(low_half, roll(tops[b], 4, 0), tops[a])
-            down = jnp.where(low_half, ends[a], roll(ends[b], 4, 0))
-            if pair == 3:
-                down = jnp.where(row == 5, roll(ends[0], 1, 0), down)
-                down = jnp.where(row == 6, roll(ends[2], 2, 0), down)
-            part = pl.ds(8 * pair, 8)
-            fwd[at, part] = jnp.where(slabs.first, up, down)
-            bwd[at, part] = jnp.where(slabs.first, down, up)
-
-    slabs.every(emit)
-
-
-def y_halo(first, got_fwd, got_bwd, at, pair):
+        lax.fori_loop(0, 16, step, 0, unroll=4)
+
+
+def pack_corners(xf, xb, fwd, bwd):
+    slabs = Slabs(None, None, None, xf, xb)
+    slabs.halo(lambda number, at, v: y_tiles(v, slabs.first, fwd, bwd, number))
+
+
+def y_halo(first, got, at, pair):
     gy = lax.axis_index("gy")
     part = pl.ds(8 * pair, 8)
-    f, b = got_fwd[at, part], got_bwd[at, part]
+    f, b = got[0][at, part], got[1][at, part]
     lower = jnp.where(gy > 0, jnp.where(first, f, b), 0.0)
     upper = jnp.where(gy < lax.axis_size("gy") - 1, jnp.where(first, b, f), 0.0)
     return lower, upper
 
 
+HALO_X = tuple(range(-LOW, 0)) + tuple(range(16, 16 + HIGH))
 X_ALL = LOW + 16 + HIGH
 X_PAIRS = (X_ALL + 1) // 2
 
 
-def pack_z(field, scaled, warmth, xf, xb, yf, yb, whole, up, down, packed):
+def pack_z(field, scaled, warmth, xf, xb, yf, yb, cf, cb, whole, up, down, packed):
     slabs = Slabs(field, scaled, warmth, xf, xb)
     first = slabs.first
     low_half = rows((8, 128)) < 4
     window = lanes((24, 128)) // 16
 
-    def emit(at, v):
+    def emit(got, number, at, v):
         acc = None
         for pair in range(4):
-            lower, upper = y_halo(first, yf, yb, at, pair)
+            lower, upper = y_halo(first, got, number, pair)
             last = []
             last.append(jnp.where(low_half, upper, lower))
             if pair < 3:
@@ -211,7 +228,8 @@
                 acc = moved if acc is None else jnp.where(window == f, moved, acc)
         packed[at] = acc
 
-    slabs.every(emit)
+    slabs.halo(functools.partial(emit, (cf, cb)))
+    slabs.inner(functools.partial(emit, (yf, yb)))
     packed[X_ALL] = jnp.zeros((24, 128), F32)
     half = (lanes((24, 128)) // 8) % 2 == 0
 
@@ -241,8 +259,8 @@
 
 
 def relax(
-    whole, xf, xb, yf, yb, below_z, above_z, sigma, warmth, storage, position, nodes,
-    out, send, partial, main, tail, other, far, heat, extra,
+    whole, xf, xb, yf, yb, cf, cb, below_z, above_z, sigma, warmth, storage, position, nodes,
+    out, send, partial, main, tail, other, far, heat, extra, sent,
 ):
     first = on_first_core()
     gx, gz = lax.axis_index("gx"), lax.axis_index("gz")
@@ -252,28 +270,33 @@
     edge = (lane < 8) | (lane >= 120)
     has_below, has_above = gz > 0, gz < lax.axis_size("gz") - 1
 
-    def unpack_one(at, packed):
+    def unpack_one(at, got, number, packed):
         for f in range(7):
             tail[f, at] = jnp.where(edge, roll(packed, -(16 * f + 8), 1), 0.0)
         tail[7, at] = roll(packed, 8, 1)
-        _, upper = y_halo(first, yf, yb, at, 3)
+        _, upper = y_halo(first, got, number, 3)
         for n, place in enumerate((5, 6)):
             extra[n, at, 0:8] = jnp.broadcast_to(upper[place : place + 1], (8, 128))
             extra[n, at, 8:16] = jnp.broadcast_to(tail[7, at, 16 + n : 17 + n, :], (8, 128))
 
-    def unpack(k, carry):
+    def unpack(k, odd):
         lower = jnp.where(has_below, below_z[k], 0.0)
         upper = jnp.where(has_above, above_z[k], 0.0)
-        unpack_one(2 * k, jnp.where(half, lower, roll(upper, 8, 1)))
-        second = jnp.where(half, roll(lower, -8, 1), upper)
-
-        unpack_one(2 * k + 1, second)
+        if odd:
+            return jnp.where(half, roll(lower, -8, 1), upper)
+        return jnp.where(half, lower, roll(upper, 8, 1))
+
+    for number, x in enumerate(HALO_X):
+        at = x + LOW
+        unpack_one(at, (cf, cb), number, unpack(at // 2, at % 2))
+
+    def unpack_pair(k, carry):
+        for odd in range(2):
+            at = 2 * k + LOW + odd
+            unpack_one(at, (yf, yb), 2 * k + odd, unpack(k + LOW // 2, odd))
         return carry
 
-    lax.fori_loop(0, X_ALL // 2, unpack, 0, unroll=4)
-    lower = jnp.where(has_below, below_z[X_PAIRS - 1], 0.0)
-    upper = jnp.where(has_above, above_z[X_PAIRS - 1], 0.0)
-    unpack_one(X_ALL - 1, jnp.where(half, lower, roll(upper, 8, 1)))
+    lax.fori_loop(0, 8, unpack_pair, 0, unroll=4)
 
     def up_y(v):
         return roll(v, -1, 0)
@@ -338,6 +361,9 @@
         _, (_, cy, cz) = curls_at(begin - 1)
         lax.fori_loop(begin, X_ALL - begin, step, (cy, cz), unroll=4)
 
+    result = pltpu.make_async_copy(other.at[:, pl.ds(LOW, 16), pl.ds(0, 16), :], out, sent)
+    result.start()
+
     def joule(x, carry):
         at = x + LOW
         ex, ey, ez = (both(lambda v: v * v, load(EM_SWEEPS, f, at)) for f in range(3))
@@ -348,8 +374,6 @@
         d = ez[0] + ez_ahead[0]
         s = c + (d + up_y(d))
         heat[x] = sigma[x] * (0.25 * s[0:16])
-        for f in range(3):
-            out[f, x] = other[f, at, 0:16, :]
         return carry
 
     lax.fori_loop(0, 16, joule, 0, unroll=4)
@@ -373,12 +397,13 @@
     for x in range(16):
         t = warmth[x]
         ends = tail[7, x + LOW, 0:16, :]
-        lower, upper = y_halo(first, yf, yb, x + LOW, 3)
+        lower, upper = y_halo(first, (yf, yb), x, 3)
         total = (warmth[x - 1] if x else under) + (warmth[x + 1] if x < 15 else over)
         total = total + jnp.where(row16 == 0, lower[3:4], roll(t, 1, 0))
         total = total + jnp.where(row16 == 15, upper[4:5], roll(t, -1, 0))
         total = total + up_z(t, ends)[0] + down_z(t, ends)[0]
         partial[x] = t + HEAT_WEIGHTS[0] * (total - 6.0 * t) / (6.0 + storage[x])
+    result.wait()
 
 
 def place(owners, columns, position, nodes):
@@ -501,32 +526,35 @@
     count = groups * (CAP + 1)
     cube = (16, 16, 128)
     face = (16, 128)
-    fwd, bwd, scaled, field, sigma, warmth, storage = call(
-        pack_x,
-        [(X_LAYERS, 16, 128), (X_LAYERS, 16, 128), (4, *cube), (3, *cube), cube, cube, cube],
-        [(3, *cube), pltpu.SemaphoreType.DMA((5,))],
-        name="pack_x",
-        in_specs=[pl.BlockSpec(memory_space=pltpu.HBM)] * 5,
-    )(field, source, sigma, warmth, storage)
-    xf, xb = exchange("gx", fwd, bwd)
+    x_message, y_message, corners = (X_LAYERS, 16, 128), (16, 32, 128), (len(HALO_X), 32, 128)
+    xf, xb, yf, yb = call(
+        pack_xy,
+        [x_message, x_message, y_message, y_message],
+        [(3, *cube), (3, *cube), cube, cube, (4, *cube), pltpu.SemaphoreType.DMA((4,))],
+        name="pack_xy",
+        limit=FIRST_LIMIT,
+        in_specs=[pl.BlockSpec(memory_space=pltpu.HBM)] * 4,
+    )(field, source, sigma, warmth)
+    xf, xb = exchange("gx", xf, xb)
+    yf, yb = exchange("gy", yf, yb)
+    (scaled,) = call(scale, [(4, *cube)], name="scale")(source, sigma)
     position, nodes = pl.pallas_call(
         place,
         out_shape=[
             jax.ShapeDtypeStruct((1, 256), jnp.int32),
             jax.ShapeDtypeStruct((count, 128), F32),
         ],
+        compiler_params=pltpu.CompilerParams(vmem_limit_bytes=8 << 20),
         name="place",
     )(partition.reshape(1, 256), column.reshape(1, 256))
-    fwd, bwd = call(pack_y, [(X_ALL, 32, 128), (X_ALL, 32, 128)], name="pack_y")(
-        field, scaled, warmth, xf, xb
-    )
-    yf, yb = exchange("gy", fwd, bwd)
+    cf, cb = call(pack_corners, [corners, corners], name="pack_corners")(xf, xb)
+    cf, cb = exchange("gy", cf, cb)
     whole, up, down = call(
         pack_z,
         [(7, X_ALL, 24, 128), (X_PAIRS, 24, 128), (X_PAIRS, 24, 128)],
         [(X_ALL + 1, 24, 128)],
         name="pack_z",
-    )(field, scaled, warmth, xf, xb, yf, yb)
+    )(field, scaled, warmth, xf, xb, yf, yb, cf, cb)
     below_z, above_z = exchange_z(up, down)
     out, send, partial = call(
         relax,
@@ -538,9 +566,12 @@
             (3, X_ALL, 24, 128),
             cube,
             (2, X_ALL, 16, 128),
+            pltpu.SemaphoreType.DMA,
         ],
         name="relax",
-    )(whole, xf, xb, yf, yb, below_z, above_z, sigma, warmth, storage, position, nodes)
+        limit=16 << 20,
+        out_specs=[pl.BlockSpec(memory_space=pltpu.HBM)] + [pl.BlockSpec(memory_space=pltpu.VMEM)] * 2,
+    )(whole, xf, xb, yf, yb, cf, cb, below_z, above_z, sigma, warmth, storage, position, nodes)
     got = lax.all_to_all(
         send.reshape(count, 1, 128), ("gy", "gz"), split_axis=0, concat_axis=0, tiled=True
     ).reshape(count, 128)

time: 84.8 us -> 70.4 us (0.83)
  the two profiles are of different devices: /device:TPU:194 before, /device:TPU:130 now
where the time goes in v3:
time: 70.4 us; the launch traced here: 69.9 us
  blocking collectives  22.6 us (32%)
  starting transfers between devices  17.6 us (25%)
  Pallas kernels  14.4 us (20%)
  waiting for transfers between devices  12.5 us (18%)
  local copies, waits for them, and re-layouts  1.93 us (3%)
  between operations  0.77 us (1%)
    all_to_all x1, blocking collectives, local(): lax.all_to_all(send.reshape(count, 1, 128), ('gy', 'gz'), split_axis=0, c...  22.6 us
    ppermute x5, starting transfers between devices, exchange(): lax.ppermute(fwd, names, forward)  10.2 us
    pallas_call x1, Pallas kernels, local(): call(relax, [(3, *cube), (count, 128), cube], [(3, X_ALL, 24, 128), (8, X...  8.62 us
    ppermute x2, starting transfers between devices, exchange_z(): lax.ppermute(down, 'gz', [(j, i) for i, j in ring])  5.9 us
    ppermute x5, waiting for transfers between devices, exchange(): lax.ppermute(fwd, names, forward)  4.69 us
    ppermute x5, waiting for transfers between devices, exchange(): lax.ppermute(bwd, names, backward)  4.15 us
    ppermute x2, waiting for transfers between devices, exchange_z(): lax.ppermute(up, 'gz', ring)  3.59 us
    pallas_call x1, Pallas kernels, local(): call(pack_xy, [x_message, x_message, y_message, y_message], [(3, *cube),...  2.36 us
  transfers between devices with their start and end apart: 14, of which 7 were waited for; matrix products, arithmetic and copies ran while one was open for 0% of the time, Pallas kernels for 1%

profile of v3, /device:TPU:130, one launch (start us, length us, event | category | flops | bytes accessed | tf_op | source)
XLA Modules:
  0.0 69.9 jit_solution(6733302207051522605)
XLA Ops:
  0.6 0.0 copy-start
  0.6 0.0 copy-start.1
  0.6 2.4 %pack_xy.1 = (f32[30,16,128]{2,1,0:T(8,128)}, f32[30,16,128]{2,1,0:T(8,128)}, f32[16,32,128]{2,1,0:T(8,128)}, f32[16,32,128]{2,1,0:T(8,128)}) custom-call(f32[3,16,16,128]{3,2,1,0:T(8,128)} %field.1, f32[3,16,16,128]{3,2,1,0:T(8,128)} %refs_1_.1, f32[16,16,128]{2,1,0:T(8,128)} %sigma.3, f32[16,16,128]{2,1,0:T(8,128)} %warmth.5), custom_call_target="tpu_custom_call" | custom-call | tf_op jit(solution)/shard_map/pack_xy/pallas_call | solution.py:530
  3.0 0.0 copy-start.6
  3.0 0.0 copy-start.7
  3.0 0.0 copy-start.3
  3.1 0.0 copy-start.5
  3.1 2.4 %collective-permute-start = (f32[30,16,128]{2,1,0:T(8,128)}, f32[30,16,128]{2,1,0:T(8,128)S(1)}, u32[]{:S(2)}, u32[]{:S(2)}) collective-permute-start(f32[30,16,128]{2,1,0:T(8,128)} %get-tuple-element.23), channel_id=1, source_target_pairs={{0,64},{1,0},{2,66},{3,2},{4,68},{5,4},{6,70},{7,6},{8,72},{9,8},{... | collective-permute-start | bytes 737288 | tf_op jit(solution)/shard_map/ppermute | solution.py:515
  5.5 0.0 collective-permute-start.1
  5.5 1.5 %collective-permute-start.2 = (f32[16,32,128]{2,1,0:T(8,128)}, f32[16,32,128]{2,1,0:T(8,128)S(1)}, u32[]{:S(2)}, u32[]{:S(2)}) collective-permute-start(f32[16,32,128]{2,1,0:T(8,128)} %get-tuple-element.25), channel_id=1, source_target_pairs={{0,16},{1,0},{2,18},{3,2},{4,20},{5,4},{6,22},{7,6},{8,24},{9,8},{... | collective-permute-start | bytes 786440 | tf_op jit(solution)/shard_map/ppermute | solution.py:515
  7.0 0.5 collective-permute-start.3
  7.5 3.5 %collective-permute-done.xf = f32[30,16,128]{2,1,0:T(8,128)S(1)} collective-permute-done((f32[30,16,128]{2,1,0:T(8,128)}, f32[30,16,128]{2,1,0:T(8,128)S(1)}, u32[]{:S(2)}, u32[]{:S(2)}) %collective-permute-start) | collective-permute-done | bytes 245792 | tf_op jit(solution)/shard_map/ppermute | solution.py:515
  11.0 2.4 %collective-permute-done.1.xb = f32[30,16,128]{2,1,0:T(8,128)S(1)} collective-permute-done((f32[30,16,128]{2,1,0:T(8,128)}, f32[30,16,128]{2,1,0:T(8,128)S(1)}, u32[]{:S(2)}, u32[]{:S(2)}) %collective-permute-start.1) | collective-permute-done | bytes 245792 | tf_op jit(solution)/shard_map/ppermute | solution.py:515
  13.4 0.1 pack_corners.1
  13.5 1.5 %collective-permute-start.4 = (f32[9,32,128]{2,1,0:T(8,128)S(1)}, f32[9,32,128]{2,1,0:T(8,128)S(1)}, u32[]{:S(2)}, u32[]{:S(2)}) collective-permute-start(f32[9,32,128]{2,1,0:T(8,128)S(1)} %get-tuple-element.27), channel_id=1, source_target_pairs={{0,16},{1,0},{2,18},{3,2},{4,20},{5,4},{6,22},{7,6},{8,24},{9,8},{... | collective-permute-start | bytes 442376 | tf_op jit(solution)/shard_map/ppermute | solution.py:515
  15.0 0.5 collective-permute-start.5
  15.5 0.0 copy-start.2
  15.5 1.0 %copy-done.2 = f32[3,16,16,128]{3,2,1,0:T(8,128)S(1)} copy-done((f32[3,16,16,128]{3,2,1,0:T(8,128)S(1)}, f32[3,16,16,128]{3,2,1,0:T(8,128)}, u32[]{:S(2)}) %copy-start.2) | copy-done | bytes 393240
  16.5 0.0 copy-start.4
  16.5 0.9 %copy-done.4 = f32[16,16,128]{2,1,0:T(8,128)S(1)} copy-done((f32[16,16,128]{2,1,0:T(8,128)S(1)}, f32[16,16,128]{2,1,0:T(8,128)}, u32[]{:S(2)}) %copy-start.4) | copy-done | bytes 131096
  17.5 0.0 collective-permute-done.2.yf
  17.5 0.0 collective-permute-done.3.yb
  17.5 1.1 %collective-permute-done.4.cf = f32[9,32,128]{2,1,0:T(8,128)S(1)} collective-permute-done((f32[9,32,128]{2,1,0:T(8,128)S(1)}, f32[9,32,128]{2,1,0:T(8,128)S(1)}, u32[]{:S(2)}, u32[]{:S(2)}) %collective-permute-start.4) | collective-permute-done | bytes 147488 | tf_op jit(solution)/shard_map/ppermute | solution.py:515
  18.7 1.5 %collective-permute-done.5.cb = f32[9,32,128]{2,1,0:T(8,128)S(1)} collective-permute-done((f32[9,32,128]{2,1,0:T(8,128)S(1)}, f32[9,32,128]{2,1,0:T(8,128)S(1)}, u32[]{:S(2)}, u32[]{:S(2)}) %collective-permute-start.5) | collective-permute-done | bytes 147488 | tf_op jit(solution)/shard_map/ppermute | solution.py:515
  20.1 0.0 copy-done
  20.1 0.0 copy-done.1
  20.2 1.1 %pack_z.1 = (f32[7,25,24,128]{3,2,1,0:T(8,128)S(1)}, f32[13,24,128]{2,1,0:T(8,128)S(1)}, f32[13,24,128]{2,1,0:T(8,128)S(1)}) custom-call(f32[3,16,16,128]{3,2,1,0:T(8,128)S(1)} %copy-done.1, f32[4,16,16,128]{3,2,1,0:T(8,128)S(1)} %scale.1.scaled, f32[16,16,128]{2,1,0:T(8,128)S(1)} %copy-done, f32[30,16,128]{2,1,0:T(8,128)S(1)} %collective-permute-done.xf, ...), custom_call_target="tpu_custom_call" | custom-call | tf_op jit(solution)/shard_map/pack_z/pallas_call | solution.py:552
  21.3 0.0 collective-permute-start.6
  21.3 2.9 %collective-permute-start.7 = (f32[13,24,128]{2,1,0:T(8,128)S(1)}, f32[13,24,128]{2,1,0:T(8,128)S(1)}, u32[]{:S(2)}, u32[]{:S(2)}) collective-permute-start(f32[13,24,128]{2,1,0:T(8,128)S(1)} %get-tuple-element.31), channel_id=1, source_target_pairs={{1,0},{2,1},{3,2},{4,3},{5,4},{6,5},{7,6},{8,7},{9,8},{10,9},{11,1... | collective-permute-start | bytes 479240 | tf_op jit(solution)/shard_map/ppermute | solution.py:521
  24.3 0.0 copy-done.6
  24.3 0.0 copy-done.7
  24.3 0.4 place.1
  24.7 2.5 %collective-permute-done.6.below_z = f32[13,24,128]{2,1,0:T(8,128)S(1)} collective-permute-done((f32[13,24,128]{2,1,0:T(8,128)S(1)}, f32[13,24,128]{2,1,0:T(8,128)S(1)}, u32[]{:S(2)}, u32[]{:S(2)}) %collective-permute-start.6) | collective-permute-done | bytes 159776 | tf_op jit(solution)/shard_map/ppermute | solution.py:521
  27.2 0.0 collective-permute-done.7.above_z
  27.2 0.0 copy-done.3
  27.2 0.0 copy-done.5
  27.2 8.6 %relax.1 = (f32[3,16,16,128]{3,2,1,0:T(8,128)}, f32[576,128]{1,0:T(8,128)S(1)}, f32[16,16,128]{2,1,0:T(8,128)S(1)}) custom-call(f32[7,25,24,128]{3,2,1,0:T(8,128)S(1)} %get-tuple-element.29.whole, f32[30,16,128]{2,1,0:T(8,128)S(1)} %collective-permute-done.xf, f32[30,16,128]{2,1,0:T(8,128)S(1)} %collective-permute-done.1.xb, ...), custom_call_target="tpu_custom_call" | custom-call | tf_op jit(solution)/shard_map/relax/pallas_call | solution.py:559
  35.8 22.6 %all_to_all.5 = f32[576,1,128]{2,1,0:T(1,128)S(1)} all-to-all(f32[576,1,128]{2,1,0:T(1,128)S(1)} %bitcast.7), channel_id=1, replica_groups=mesh['gx'=8,'gy'=4,'gz'=16] {'gy','gz'}, dimensions={0} | all-to-all | bytes 589824 | tf_op jit(solution)/shard_map/all_to_all | solution.py:575
  58.5 1.0 %warm.1 = (f32[16,128]{1,0:T(8,128)S(1)}, f32[16,128]{1,0:T(8,128)S(1)}, f32[16,128]{1,0:T(8,128)S(1)}, f32[16,128]{1,0:T(8,128)S(1)}, f32[16,128]{1,0:T(8,128)S...) custom-call(f32[576,128]{1,0:T(8,128)S(1)} %bitcast.6, f32[16,16,128]{2,1,0:T(8,128)S(1)} %get-tuple-element.36.partial, ...), custom_call_target="tpu_custom_call" | custom-call | tf_op jit(solution)/shard_map/warm/pallas_call | solution.py:578
  59.5 3.2 %collective-permute-start.8 = (f32[16,128]{1,0:T(8,128)S(1)}, f32[16,128]{1,0:T(8,128)S(1)}, u32[]{:S(2)}, u32[]{:S(2)}) collective-permute-start(f32[16,128]{1,0:T(8,128)S(1)} %get-tuple-element.38), channel_id=1, source_target_pairs={{0,64},{1,0},{2,66},{3,2},{4,68},{5,4},{6,70},{7,6},{8,72},{9,8},{... | collective-permute-start | bytes 24584 | tf_op jit(solution)/shard_map/ppermute | solution.py:515
  62.7 0.0 collective-permute-start.9
  62.7 1.6 %collective-permute-start.10 = (f32[16,128]{1,0:T(8,128)S(1)}, f32[16,128]{1,0:T(8,128)S(1)}, u32[]{:S(2)}, u32[]{:S(2)}) collective-permute-start(f32[16,128]{1,0:T(8,128)S(1)} %get-tuple-element.40), channel_id=1, source_target_pairs={{0,16},{1,0},{2,18},{3,2},{4,20},{5,4},{6,22},{7,6},{8,24},{9,8},{... | collective-permute-start | bytes 24584 | tf_op jit(solution)/shard_map/ppermute | solution.py:515
  64.3 0.4 collective-permute-start.11
  64.7 0.0 collective-permute-start.12
  64.7 0.0 collective-permute-done.8.xf
  64.8 3.0 %collective-permute-start.13 = (f32[16,128]{1,0:T(8,128)S(1)}, f32[16,128]{1,0:T(8,128)S(1)}, u32[]{:S(2)}, u32[]{:S(2)}) collective-permute-start(f32[16,128]{1,0:T(8,128)S(1)} %get-tuple-element.43), channel_id=1, source_target_pairs={{1,0},{2,1},{3,2},{4,3},{5,4},{6,5},{7,6},{8,7},{9,8},{10,9},{11,1... | collective-permute-start | bytes 24584 | tf_op jit(solution)/shard_map/ppermute | solution.py:521
  67.7 0.0 collective-permute-done.9.xb
  67.7 0.0 collective-permute-done.10.yf
  67.7 0.3 collective-permute-done.11.yb
  68.0 1.1 %collective-permute-done.12.from_below = f32[16,128]{1,0:T(8,128)S(1)} collective-permute-done((f32[16,128]{1,0:T(8,128)S(1)}, f32[16,128]{1,0:T(8,128)S(1)}, u32[]{:S(2)}, u32[]{:S(2)}) %collective-permute-start.12) | collective-permute-done | bytes 8224 | tf_op jit(solution)/shard_map/ppermute | solution.py:521
  69.0 0.0 collective-permute-done.13.from_above
  69.1 0.8 %finish.1 = f32[16,16,128]{2,1,0:T(8,128)} custom-call(f32[16,16,128]{2,1,0:T(8,128)S(1)} %get-tuple-element.37.rest, f32[16,16,128]{2,1,0:T(8,128)S(1)} %copy-done.3, f32[16,128]{1,0:T(8,128)S(1)} %collective-permute-done.8.xf, f32[16,128]{1,0:T(8,128)S(1)} %collective-permute-done.9.xb, f32[16,128]{1,0:T(8,128)S(1)} %collective-permute-done.10.yf, ...), custom_call_target="tpu_custom_call" | custom-call | tf_op jit(solution)/shard_map/finish/pallas_call | solution.py:584
  (1 shorter events, 0.0 us)
Async XLA Ops:
  0.6 19.5 %copy-start = (f32[16,16,128]{2,1,0:T(8,128)S(1)}, f32[16,16,128]{2,1,0:T(8,128)}, u32[]{:S(2)}) copy-start(f32[16,16,128]{2,1,0:T(8,128)} %warmth.5) | copy-start | bytes 393220
  0.6 19.5 %copy-start.1 = (f32[3,16,16,128]{3,2,1,0:T(8,128)S(1)}, f32[3,16,16,128]{3,2,1,0:T(8,128)}, u32[]{:S(2)}) copy-start(f32[3,16,16,128]{3,2,1,0:T(8,128)} %field.1) | copy-start | bytes 1179652
  3.0 21.2 %copy-start.6 = (s32[1,1,1,256,1]{3,4,2,1,0:T(1,128)S(1)}, s32[1,1,1,256,1]{3,4,2,1,0:T(1,128)}, u32[]{:S(2)}) copy-start(s32[1,1,1,256,1]{3,4,2,1,0:T(1,128)} %param.12) | copy-start | bytes 3076
  3.0 21.2 %copy-start.7 = (s32[1,1,1,256]{3,2,1,0:T(1,128)S(1)}, s32[1,1,1,256]{3,2,1,0:T(1,128)}, u32[]{:S(2)}) copy-start(s32[1,1,1,256]{3,2,1,0:T(1,128)} %param.13) | copy-start | bytes 3076
  3.0 24.2 %copy-start.3 = (f32[16,16,128]{2,1,0:T(8,128)S(1)}, f32[16,16,128]{2,1,0:T(8,128)}, u32[]{:S(2)}) copy-start(f32[16,16,128]{2,1,0:T(8,128)} %storage.5) | copy-start | bytes 393220
  3.1 24.2 %copy-start.5 = (f32[16,16,128]{2,1,0:T(8,128)S(1)}, f32[16,16,128]{2,1,0:T(8,128)}, u32[]{:S(2)}) copy-start(f32[16,16,128]{2,1,0:T(8,128)} %sigma.3) | copy-start | bytes 393220
  3.1 8.0 %collective-permute-start = (f32[30,16,128]{2,1,0:T(8,128)}, f32[30,16,128]{2,1,0:T(8,128)S(1)}, u32[]{:S(2)}, u32[]{:S(2)}) collective-permute-start(f32[30,16,128]{2,1,0:T(8,128)} %get-tuple-element.23), channel_id=1, source_target_pairs={{0,64},{1,0},{2,66},{3,2},{4,68},{5,4},{6,70},{7,6},{8,72},{9,8},{... | collective-permute-start | bytes 737288 | tf_op jit(solution)/shard_map/ppermute | solution.py:515
  5.5 8.0 %collective-permute-start.1 = (f32[30,16,128]{2,1,0:T(8,128)}, f32[30,16,128]{2,1,0:T(8,128)S(1)}, u32[]{:S(2)}, u32[]{:S(2)}) collective-permute-start(f32[30,16,128]{2,1,0:T(8,128)} %get-tuple-element.24), channel_id=1, source_target_pairs={{64,0},{0,1},{66,2},{2,3},{68,4},{4,5},{70,6},{6,7},{72,8},{8,9},{... | collective-permute-start | bytes 737288 | tf_op jit(solution)/shard_map/ppermute | solution.py:515
  5.5 12.0 %collective-permute-start.2 = (f32[16,32,128]{2,1,0:T(8,128)}, f32[16,32,128]{2,1,0:T(8,128)S(1)}, u32[]{:S(2)}, u32[]{:S(2)}) collective-permute-start(f32[16,32,128]{2,1,0:T(8,128)} %get-tuple-element.25), channel_id=1, source_target_pairs={{0,16},{1,0},{2,18},{3,2},{4,20},{5,4},{6,22},{7,6},{8,24},{9,8},{... | collective-permute-start | bytes 786440 | tf_op jit(solution)/shard_map/ppermute | solution.py:515
  7.0 10.5 %collective-permute-start.3 = (f32[16,32,128]{2,1,0:T(8,128)}, f32[16,32,128]{2,1,0:T(8,128)S(1)}, u32[]{:S(2)}, u32[]{:S(2)}) collective-permute-start(f32[16,32,128]{2,1,0:T(8,128)} %get-tuple-element.26), channel_id=1, source_target_pairs={{16,0},{0,1},{18,2},{2,3},{20,4},{4,5},{22,6},{6,7},{24,8},{8,9},{... | collective-permute-start | bytes 786440 | tf_op jit(solution)/shard_map/ppermute | solution.py:515
  13.5 5.2 %collective-permute-start.4 = (f32[9,32,128]{2,1,0:T(8,128)S(1)}, f32[9,32,128]{2,1,0:T(8,128)S(1)}, u32[]{:S(2)}, u32[]{:S(2)}) collective-permute-start(f32[9,32,128]{2,1,0:T(8,128)S(1)} %get-tuple-element.27), channel_id=1, source_target_pairs={{0,16},{1,0},{2,18},{3,2},{4,20},{5,4},{6,22},{7,6},{8,24},{9,8},{... | collective-permute-start | bytes 442376 | tf_op jit(solution)/shard_map/ppermute | solution.py:515
  15.0 5.1 %collective-permute-start.5 = (f32[9,32,128]{2,1,0:T(8,128)S(1)}, f32[9,32,128]{2,1,0:T(8,128)S(1)}, u32[]{:S(2)}, u32[]{:S(2)}) collective-permute-start(f32[9,32,128]{2,1,0:T(8,128)S(1)} %get-tuple-element.28), channel_id=1, source_target_pairs={{16,0},{0,1},{18,2},{2,3},{20,4},{4,5},{22,6},{6,7},{24,8},{8,9},{... | collective-permute-start | bytes 442376 | tf_op jit(solution)/shard_map/ppermute | solution.py:515
  15.5 1.0 %copy-start.2 = (f32[3,16,16,128]{3,2,1,0:T(8,128)S(1)}, f32[3,16,16,128]{3,2,1,0:T(8,128)}, u32[]{:S(2)}) copy-start(f32[3,16,16,128]{3,2,1,0:T(8,128)} %refs_1_.1) | copy-start | bytes 1179652
  16.5 0.9 %copy-start.4 = (f32[16,16,128]{2,1,0:T(8,128)S(1)}, f32[16,16,128]{2,1,0:T(8,128)}, u32[]{:S(2)}) copy-start(f32[16,16,128]{2,1,0:T(8,128)} %sigma.3) | copy-start | bytes 393220
  21.3 5.9 %collective-permute-start.6 = (f32[13,24,128]{2,1,0:T(8,128)S(1)}, f32[13,24,128]{2,1,0:T(8,128)S(1)}, u32[]{:S(2)}, u32[]{:S(2)}) collective-permute-start(f32[13,24,128]{2,1,0:T(8,128)S(1)} %get-tuple-element.30), channel_id=1, source_target_pairs={{0,1},{1,2},{2,3},{3,4},{4,5},{5,6},{6,7},{7,8},{8,9},{9,10},{10,1... | collective-permute-start | bytes 479240 | tf_op jit(solution)/shard_map/ppermute | solution.py:521
  21.3 5.9 %collective-permute-start.7 = (f32[13,24,128]{2,1,0:T(8,128)S(1)}, f32[13,24,128]{2,1,0:T(8,128)S(1)}, u32[]{:S(2)}, u32[]{:S(2)}) collective-permute-start(f32[13,24,128]{2,1,0:T(8,128)S(1)} %get-tuple-element.31), channel_id=1, source_target_pairs={{1,0},{2,1},{3,2},{4,3},{5,4},{6,5},{7,6},{8,7},{9,8},{10,9},{11,1... | collective-permute-start | bytes 479240 | tf_op jit(solution)/shard_map/ppermute | solution.py:521
  59.5 5.3 %collective-permute-start.8 = (f32[16,128]{1,0:T(8,128)S(1)}, f32[16,128]{1,0:T(8,128)S(1)}, u32[]{:S(2)}, u32[]{:S(2)}) collective-permute-start(f32[16,128]{1,0:T(8,128)S(1)} %get-tuple-element.38), channel_id=1, source_target_pairs={{0,64},{1,0},{2,66},{3,2},{4,68},{5,4},{6,70},{7,6},{8,72},{9,8},{... | collective-permute-start | bytes 24584 | tf_op jit(solution)/shard_map/ppermute | solution.py:515
  62.7 5.0 %collective-permute-start.9 = (f32[16,128]{1,0:T(8,128)S(1)}, f32[16,128]{1,0:T(8,128)S(1)}, u32[]{:S(2)}, u32[]{:S(2)}) collective-permute-start(f32[16,128]{1,0:T(8,128)S(1)} %get-tuple-element.39), channel_id=1, source_target_pairs={{64,0},{0,1},{66,2},{2,3},{68,4},{4,5},{70,6},{6,7},{72,8},{8,9},{... | collective-permute-start | bytes 24584 | tf_op jit(solution)/shard_map/ppermute | solution.py:515
  62.7 5.0 %collective-permute-start.10 = (f32[16,128]{1,0:T(8,128)S(1)}, f32[16,128]{1,0:T(8,128)S(1)}, u32[]{:S(2)}, u32[]{:S(2)}) collective-permute-start(f32[16,128]{1,0:T(8,128)S(1)} %get-tuple-element.40), channel_id=1, source_target_pairs={{0,16},{1,0},{2,18},{3,2},{4,20},{5,4},{6,22},{7,6},{8,24},{9,8},{... | collective-permute-start | bytes 24584 | tf_op jit(solution)/shard_map/ppermute | solution.py:515
  64.3 3.7 %collective-permute-start.11 = (f32[16,128]{1,0:T(8,128)S(1)}, f32[16,128]{1,0:T(8,128)S(1)}, u32[]{:S(2)}, u32[]{:S(2)}) collective-permute-start(f32[16,128]{1,0:T(8,128)S(1)} %get-tuple-element.41), channel_id=1, source_target_pairs={{16,0},{0,1},{18,2},{2,3},{20,4},{4,5},{22,6},{6,7},{24,8},{8,9},{... | collective-permute-start | bytes 24584 | tf_op jit(solution)/shard_map/ppermute | solution.py:515
  64.7 4.3 %collective-permute-start.12 = (f32[16,128]{1,0:T(8,128)S(1)}, f32[16,128]{1,0:T(8,128)S(1)}, u32[]{:S(2)}, u32[]{:S(2)}) collective-permute-start(f32[16,128]{1,0:T(8,128)S(1)} %get-tuple-element.42), channel_id=1, source_target_pairs={{0,1},{1,2},{2,3},{3,4},{4,5},{5,6},{6,7},{7,8},{8,9},{9,10},{10,1... | collective-permute-start | bytes 24584 | tf_op jit(solution)/shard_map/ppermute | solution.py:521
  64.8 4.3 %collective-permute-start.13 = (f32[16,128]{1,0:T(8,128)S(1)}, f32[16,128]{1,0:T(8,128)S(1)}, u32[]{:S(2)}, u32[]{:S(2)}) collective-permute-start(f32[16,128]{1,0:T(8,128)S(1)} %get-tuple-element.43), channel_id=1, source_target_pairs={{1,0},{2,1},{3,2},{4,3},{5,4},{6,5},{7,6},{8,7},{9,8},{10,9},{11,1... | collective-permute-start | bytes 24584 | tf_op jit(solution)/shard_map/ppermute | solution.py:521

commit v4 on v3

--- a/solution.py
+++ b/solution.py
@@ -201,10 +201,13 @@
 
 HALO_X = tuple(range(-LOW, 0)) + tuple(range(16, 16 + HIGH))
 X_ALL = LOW + 16 + HIGH
+GROUP_ALL = LOW + 4 + HIGH
+SWEEP_UNROLL = 4
 X_PAIRS = (X_ALL + 1) // 2
 
 
-def pack_z(field, scaled, warmth, xf, xb, yf, yb, cf, cb, whole, up, down, packed):
+def pack_z(field, scaled, warmth, xf, xb, yf, yb, cf, cb, position, whole, packed, up, down):
+    del position
     slabs = Slabs(field, scaled, warmth, xf, xb)
     first = slabs.first
     low_half = rows((8, 128)) < 4
@@ -222,8 +225,7 @@
                 last.append(roll(upper, 3, 0))
             for f, tile in zip((2 * pair, 2 * pair + 1), last):
                 slab = jnp.concatenate([v[f], tile], axis=0)
-                if f < 7:
-                    whole[f, at] = slab
+                whole[f, at] = slab
                 moved = roll(slab, 16 * f + 8, 1)
                 acc = moved if acc is None else jnp.where(window == f, moved, acc)
         packed[at] = acc
@@ -242,141 +244,142 @@
     lax.fori_loop(0, X_PAIRS, pair_up, 0, unroll=True)
 
 
-def up_z(main, tail):
-    last = lanes(main.shape) == 127
-    a, b = roll(main, -1, 1), roll(tail, -1, 1)
-    return jnp.where(last, b, a), jnp.where(last, a, b)
-
-
-def down_z(main, tail):
-    start = lanes(main.shape) == 0
-    a, b = roll(main, 1, 1), roll(tail, 1, 1)
-    return jnp.where(start, b, a), jnp.where(start, a, b)
-
-
-def both(function, *pairs):
-    return tuple(function(*parts) for parts in zip(*pairs))
-
-
-def relax(
-    whole, xf, xb, yf, yb, cf, cb, below_z, above_z, sigma, warmth, storage, position, nodes,
-    out, send, partial, main, tail, other, far, heat, extra, sent,
+def up_y(v):
+    return roll(v, -1, 0)
+
+
+def down_y(v):
+    return roll(v, 1, 0)
+
+
+def up_z(v):
+    return roll(v, -1, 1)
+
+
+def down_z(v):
+    return roll(v, 1, 1)
+
+
+def twist(a, b, c, d):
+    return (a - b) - (c - d)
+
+
+def relax(fields, first, second, layers):
+    row = rows((24, 128))
+    buffers = (fields, first, second, first, second)
+
+    def curls(source, at, outer):
+        ex, ey, ez = (source[f, at] for f in range(3))
+        ex_up, ez_up = up_y(ex), up_y(ez)
+        if outer:
+            ex_up = jnp.where(row == 19, fields[7, at, 16:17, :], ex_up)
+            ez_up = jnp.where(row == 19, fields[7, at, 17:18, :], ez_up)
+        cx = twist(ez_up, ez, up_z(ey), ey)
+        cy = twist(up_z(ex), ex, source[2, at + 1], ez)
+        cz = twist(source[1, at + 1], ey, ex_up, ex)
+        return (ex, ey, ez), (cx, cy, cz)
+
+    for number, weight in enumerate(EM_WEIGHTS):
+        source, target, outer = buffers[number], buffers[number + 1], number == 0
+
+        def step(at, carry, source=source, target=target, outer=outer, weight=weight):
+            cy_before, cz_before = carry
+            e, (cx, cy, cz) = curls(source, at, outer)
+            kx = twist(cz, down_y(cz), cy, down_z(cy))
+            ky = twist(cx, down_z(cx), cz, cz_before)
+            kz = twist(cy, cy_before, cx, down_y(cx))
+            g = fields[6, at] * weight
+            keep = (1.0 - weight) + 4.0 * g
+            for f, k in enumerate((kx, ky, kz)):
+                target[f, at] = keep * e[f] + weight * fields[3 + f, at] - g * k
+            return cy, cz
+
+        begin = 1 + number
+        _, (_, cy, cz) = curls(source, begin - 1, outer)
+        lax.fori_loop(begin, layers - begin, step, (cy, cz), unroll=SWEEP_UNROLL)
+
+
+def squares(field, at):
+    ex, ey, ez = (field[f, at] * field[f, at] for f in range(3))
+    ey_ahead, ez_ahead = (field[f, at + 1] * field[f, at + 1] for f in (1, 2))
+    upright = ez + ez_ahead
+    return (ex + up_y(ex)) + (ey + ey_ahead), upright + up_y(upright)
+
+
+def bulk(whole, final, flat, upright, spare):
+    relax(whole, spare, final, X_ALL)
+
+    def step(x, carry):
+        c, d = squares(final, x + LOW)
+        flat[x], upright[x] = c[0:16], d[0:16]
+        return carry
+
+    lax.fori_loop(0, 16, step, 0, unroll=4)
+
+
+def near_z(edge, group, inner):
+    lane = lanes(inner.shape)
+    high = roll(edge, 120 - 32 * group, 1)
+    low = roll(edge, -(32 * group + 24), 1)
+    return jnp.where(lane < 4, low, jnp.where(lane >= 124, high, inner)), high
+
+
+def edge(
+    packed, below_z, above_z, flat, upright, xf, xb, yf, yb, sigma, warmth, storage, position, nodes,
+    final, send, partial, beside, faces, fields, spare, heat,
 ):
     first = on_first_core()
     gx, gz = lax.axis_index("gx"), lax.axis_index("gz")
     lane = lanes((24, 128))
-    row = rows((24, 128))
     half = (lane // 8) % 2 == 0
-    edge = (lane < 8) | (lane >= 120)
+    window = lane // 16
     has_below, has_above = gz > 0, gz < lax.axis_size("gz") - 1
-
-    def unpack_one(at, got, number, packed):
-        for f in range(7):
-            tail[f, at] = jnp.where(edge, roll(packed, -(16 * f + 8), 1), 0.0)
-        tail[7, at] = roll(packed, 8, 1)
-        _, upper = y_halo(first, got, number, 3)
-        for n, place in enumerate((5, 6)):
-            extra[n, at, 0:8] = jnp.broadcast_to(upper[place : place + 1], (8, 128))
-            extra[n, at, 8:16] = jnp.broadcast_to(tail[7, at, 16 + n : 17 + n, :], (8, 128))
 
     def unpack(k, odd):
         lower = jnp.where(has_below, below_z[k], 0.0)
         upper = jnp.where(has_above, above_z[k], 0.0)
+        at = 2 * k + odd
         if odd:
-            return jnp.where(half, roll(lower, -8, 1), upper)
-        return jnp.where(half, lower, roll(upper, 8, 1))
-
-    for number, x in enumerate(HALO_X):
-        at = x + LOW
-        unpack_one(at, (cf, cb), number, unpack(at // 2, at % 2))
+            came = jnp.where(half, roll(lower, -8, 1), upper)
+        else:
+            came = jnp.where(half, lower, roll(upper, 8, 1))
+        beside[at] = came
+        faces[0, at] = jnp.where(half, packed[at], came)
+        faces[1, at] = jnp.where(half, came, packed[at])
 
     def unpack_pair(k, carry):
-        for odd in range(2):
-            at = 2 * k + LOW + odd
-            unpack_one(at, (yf, yb), 2 * k + odd, unpack(k + LOW // 2, odd))
+        unpack(k, 0)
+        unpack(k, 1)
         return carry
 
-    lax.fori_loop(0, 8, unpack_pair, 0, unroll=4)
-
-    def up_y(v):
-        return roll(v, -1, 0)
-
-    def down_y(v):
-        return roll(v, 1, 0)
-
-    buffers = [(whole, tail), (main, far), (other, tail), (main, far), (other, tail)]
-
-    def load(number, f, at):
-        return buffers[number][0][f, at], buffers[number][1][f, at]
-
-    def up_y_edge(v, n, at):
-        moved = both(up_y, v)
-        edges = (extra[n, at, 0:8], extra[n, at, 8:16])
-        return tuple(
-            jnp.where(row == 19, jnp.concatenate([e, e, e], axis=0), m)
-            for m, e in zip(moved, edges)
-        )
-
-    def curls(at, ahead, e, outer):
-        ex, ey, ez = e
-        ey_ahead, ez_ahead = ahead
-        if outer:
-            ex_up, ez_up = up_y_edge(ex, 0, at), up_y_edge(ez, 1, at)
-        else:
-            ex_up, ez_up = both(up_y, ex), both(up_y, ez)
-        cx = both(lambda a, b, c, d: (a - b) - (c - d), ez_up, ez, up_z(*ey), ey)
-        cy = both(lambda a, b, c, d: (a - b) - (c - d), up_z(*ex), ex, ez_ahead, ez)
-        cz = both(lambda a, b, c, d: (a - b) - (c - d), ey_ahead, ey, ex_up, ex)
-        return cx, cy, cz
-
-    for number, weight in enumerate(EM_WEIGHTS):
-        begin = 1 + number
-        outer = number == 0
-
-        def curls_at(at, number=number, outer=outer):
-            e = [load(number, f, at) for f in range(3)]
-            ahead = (load(number, 1, at + 1), load(number, 2, at + 1))
-            return e, curls(at, ahead, e, outer)
-
-        def step(at, carry, number=number, weight=weight, curls_at=curls_at):
-            cy_before, cz_before = carry
-            e, (cx, cy, cz) = curls_at(at)
-            kx = both(
-                lambda a, b, c, d: (a - b) - (c - d), cz, both(down_y, cz), cy, down_z(*cy)
-            )
-            ky = both(lambda a, b, c, d: (a - b) - (c - d), cx, down_z(*cx), cz, cz_before)
-            kz = both(
-                lambda a, b, c, d: (a - b) - (c - d), cy, cy_before, cx, both(down_y, cx)
-            )
-            g = (whole[6, at] * weight, tail[6, at] * weight)
-            keep = both(lambda v: (1.0 - weight) + 4.0 * v, g)
-            for f, k in enumerate((kx, ky, kz)):
-                h = (whole[3 + f, at], tail[3 + f, at])
-                new = both(
-                    lambda p, v, s, w, d: p * v + weight * s - w * d, keep, e[f], h, g, k
-                )
-                buffers[number + 1][0][f, at], buffers[number + 1][1][f, at] = new
-            return cy, cz
-
-        _, (_, cy, cz) = curls_at(begin - 1)
-        lax.fori_loop(begin, X_ALL - begin, step, (cy, cz), unroll=4)
-
-    result = pltpu.make_async_copy(other.at[:, pl.ds(LOW, 16), pl.ds(0, 16), :], out, sent)
-    result.start()
-
-    def joule(x, carry):
-        at = x + LOW
-        ex, ey, ez = (both(lambda v: v * v, load(EM_SWEEPS, f, at)) for f in range(3))
-        ey_ahead, ez_ahead = (both(lambda v: v * v, load(EM_SWEEPS, f, at + 1)) for f in (1, 2))
-        a = both(lambda v: v + up_y(v), ex)
-        c = both(lambda p, q, r: p + (q + r), a, ey, ey_ahead)
-        c = c[0] + up_z(*c)[0]
-        d = ez[0] + ez_ahead[0]
-        s = c + (d + up_y(d))
-        heat[x] = sigma[x] * (0.25 * s[0:16])
+    lax.fori_loop(0, X_ALL // 2, unpack_pair, 0, unroll=4)
+    unpack(X_ALL // 2, 0)
+
+    def regroup(i, carry):
+        v = [faces[j % 2, i + 4 * (j // 2)] for j in range(8)]
+        for d in (1, 2, 4):
+            plain = (window // d) % 2 == 0
+            for a in range(8):
+                if a & d == 0:
+                    p, q = v[a], v[a + d]
+                    v[a] = jnp.where(plain, p, roll(q, 16 * d, 1))
+                    v[a + d] = jnp.where(plain, roll(p, -16 * d, 1), q)
+        for f in range(8):
+            fields[f, i] = v[f]
         return carry
 
-    lax.fori_loop(0, 16, joule, 0, unroll=4)
+    lax.fori_loop(0, GROUP_ALL, regroup, 0, unroll=2)
+    relax(fields, spare, final, GROUP_ALL)
+    lane = lanes((16, 128))
+    for i in range(4):
+        c, d = squares(final, i + LOW)
+        c, d = c[0:16], d[0:16]
+        for group in range(4):
+            x = 4 * group + i
+            c_all, c_high = near_z(c, group, flat[x])
+            d_all, _ = near_z(d, group, upright[x])
+            c_up = jnp.where(lane == 127, roll(c_high, -1, 1), roll(c_all, -1, 1))
+            heat[x] = sigma[x] * (0.25 * ((c_all + c_up) + d_all))
 
     count = send.shape[0]
     spread = (rows((count, 256)) == position[...]).astype(jnp.bfloat16)
@@ -388,7 +391,7 @@
         total = total + jnp.dot(spread, piece, preferred_element_type=F32)
     send[...] = total
 
-    row16 = rows((16, 128))
+    row = rows((16, 128))
     low_at, high_at = UP_AT[7, -1], DOWN_AT[7, 16]
     under = jnp.where(gx > 0, jnp.where(first, xf[low_at], xb[low_at]), 0.0)
     over = jnp.where(
@@ -396,14 +399,23 @@
     )
     for x in range(16):
         t = warmth[x]
-        ends = tail[7, x + LOW, 0:16, :]
+        ends = roll(beside[x + LOW, 0:16, :], 8, 1)
         lower, upper = y_halo(first, (yf, yb), x, 3)
         total = (warmth[x - 1] if x else under) + (warmth[x + 1] if x < 15 else over)
-        total = total + jnp.where(row16 == 0, lower[3:4], roll(t, 1, 0))
-        total = total + jnp.where(row16 == 15, upper[4:5], roll(t, -1, 0))
-        total = total + up_z(t, ends)[0] + down_z(t, ends)[0]
+        total = total + jnp.where(row == 0, lower[3:4], down_y(t))
+        total = total + jnp.where(row == 15, upper[4:5], up_y(t))
+        total = total + jnp.where(lane == 0, down_z(ends), down_z(t))
+        total = total + jnp.where(lane == 127, up_z(ends), up_z(t))
         partial[x] = t + HEAT_WEIGHTS[0] * (total - 6.0 * t) / (6.0 + storage[x])
-    result.wait()
+
+
+def merge(final, near, out):
+    for f in range(3):
+        for i in range(4):
+            windows = near[f, i + LOW, 0:16, :]
+            for group in range(4):
+                x = 4 * group + i
+                out[f, x], _ = near_z(windows, group, final[f, x + LOW, 0:16, :])
 
 
 def place(owners, columns, position, nodes):
@@ -549,29 +561,35 @@
     )(partition.reshape(1, 256), column.reshape(1, 256))
     cf, cb = call(pack_corners, [corners, corners], name="pack_corners")(xf, xb)
     cf, cb = exchange("gy", cf, cb)
-    whole, up, down = call(
+    layer = (24, 128)
+    whole, packed, up, down = call(
         pack_z,
-        [(7, X_ALL, 24, 128), (X_PAIRS, 24, 128), (X_PAIRS, 24, 128)],
-        [(X_ALL + 1, 24, 128)],
+        [(8, X_ALL, *layer), (X_ALL + 1, *layer), (X_PAIRS, *layer), (X_PAIRS, *layer)],
         name="pack_z",
-    )(field, scaled, warmth, xf, xb, yf, yb, cf, cb)
+    )(field, scaled, warmth, xf, xb, yf, yb, cf, cb, position)
     below_z, above_z = exchange_z(up, down)
-    out, send, partial = call(
-        relax,
-        [(3, *cube), (count, 128), cube],
+    final, flat, upright = call(
+        bulk,
+        [(3, X_ALL, *layer), cube, cube],
+        [(3, X_ALL, *layer)],
+        name="bulk",
+        cost_estimate=pl.CostEstimate(flops=10**9, bytes_accessed=10**7, transcendentals=0),
+    )(whole)
+    near, send, partial = call(
+        edge,
+        [(3, GROUP_ALL, *layer), (count, 128), cube],
         [
-            (3, X_ALL, 24, 128),
-            (8, X_ALL, 24, 128),
-            (3, X_ALL, 24, 128),
-            (3, X_ALL, 24, 128),
+            (X_ALL, *layer),
+            (2, X_ALL, *layer),
+            (8, GROUP_ALL, *layer),
+            (3, GROUP_ALL, *layer),
             cube,
-            (2, X_ALL, 16, 128),
-            pltpu.SemaphoreType.DMA,
         ],
-        name="relax",
-        limit=16 << 20,
-        out_specs=[pl.BlockSpec(memory_space=pltpu.HBM)] + [pl.BlockSpec(memory_space=pltpu.VMEM)] * 2,
-    )(whole, xf, xb, yf, yb, cf, cb, below_z, above_z, sigma, warmth, storage, position, nodes)
+        name="edge",
+    )(
+        packed, below_z, above_z, flat, upright, xf, xb, yf, yb, sigma, warmth, storage,
+        position, nodes,
+    )
     got = lax.all_to_all(
         send.reshape(count, 1, 128), ("gy", "gz"), split_axis=0, concat_axis=0, tiled=True
     ).reshape(count, 128)
@@ -584,6 +602,12 @@
     (updated,) = call(finish, [cube], name="finish")(
         rest, storage, xf, xb, yf, yb, below_z, above_z
     )
+    (out,) = call(
+        merge,
+        [(3, *cube)],
+        name="merge",
+        cost_estimate=pl.CostEstimate(flops=10**9, bytes_accessed=10**6, transcendentals=0),
+    )(final, near)
     return out, updated
 
 

time: 70.4 us -> 69 us (0.980)
  the two profiles are of different devices: /device:TPU:130 before, /device:TPU:133 now
where the time goes in v4:
time: 69 us; the launch traced here: 68.8 us
  blocking collectives  24.2 us (35%)
  starting transfers between devices  17.6 us (26%)
  Pallas kernels  17.2 us (25%)
  waiting for transfers between devices  7 us (10%)
  local copies, waits for them, and re-layouts  1.92 us (3%)
  between operations  0.82 us (1%)
    all_to_all x1, blocking collectives, local(): lax.all_to_all(send.reshape(count, 1, 128), ('gy', 'gz'), split_axis=0, c...  24.2 us
    ppermute x5, starting transfers between devices, exchange(): lax.ppermute(bwd, names, backward)  8.84 us
    ppermute x2, starting transfers between devices, exchange_z(): lax.ppermute(up, 'gz', ring)  8.05 us
    pallas_call x1, Pallas kernels, local(): call(edge, [(3, GROUP_ALL, *layer), (count, 128), cube], [(X_ALL, *layer)...  5.62 us
    pallas_call x1, Pallas kernels, local(): call(bulk, [(3, X_ALL, *layer), cube, cube], [(3, X_ALL, *layer)], name='...  4.68 us
    ppermute x5, waiting for transfers between devices, exchange(): lax.ppermute(fwd, names, forward)  3.48 us
    pallas_call x1, Pallas kernels, local(): call(pack_xy, [x_message, x_message, y_message, y_message], [(3, *cube),...  2.4 us
    ppermute x2, waiting for transfers between devices, exchange_z(): lax.ppermute(down, 'gz', [(j, i) for i, j in ring])  2.33 us
  transfers between devices with their start and end apart: 14, of which 5 were waited for; matrix products, arithmetic and copies ran while one was open for 0% of the time, Pallas kernels for 9%

profile of v4, /device:TPU:133, one launch (start us, length us, event | category | flops | bytes accessed | tf_op | source)
XLA Modules:
  0.0 68.8 jit_solution(4736782964999582741)
XLA Ops:
  0.6 0.0 copy-start
  0.6 0.0 copy-start.2
  0.7 0.0 copy-start.7
  0.7 0.0 copy-start.6
  0.7 2.4 %pack_xy.1 = (f32[30,16,128]{2,1,0:T(8,128)}, f32[30,16,128]{2,1,0:T(8,128)}, f32[16,32,128]{2,1,0:T(8,128)}, f32[16,32,128]{2,1,0:T(8,128)}) custom-call(f32[3,16,16,128]{3,2,1,0:T(8,128)} %field.1, f32[3,16,16,128]{3,2,1,0:T(8,128)} %refs_1_.1, f32[16,16,128]{2,1,0:T(8,128)} %sigma.3, f32[16,16,128]{2,1,0:T(8,128)} %warmth.5), custom_call_target="tpu_custom_call" | custom-call | tf_op jit(solution)/shard_map/pack_xy/pallas_call | solution.py:542
  3.1 0.0 collective-permute-start
  3.1 2.1 %collective-permute-start.1 = (f32[30,16,128]{2,1,0:T(8,128)}, f32[30,16,128]{2,1,0:T(8,128)S(1)}, u32[]{:S(2)}, u32[]{:S(2)}) collective-permute-start(f32[30,16,128]{2,1,0:T(8,128)} %get-tuple-element.28), channel_id=1, source_target_pairs={{64,0},{0,1},{66,2},{2,3},{68,4},{4,5},{70,6},{6,7},{72,8},{8,9},{... | collective-permute-start | bytes 737288 | tf_op jit(solution)/shard_map/ppermute | solution.py:527
  5.2 0.3 collective-permute-start.2
  5.5 1.2 %collective-permute-start.3 = (f32[16,32,128]{2,1,0:T(8,128)}, f32[16,32,128]{2,1,0:T(8,128)S(1)}, u32[]{:S(2)}, u32[]{:S(2)}) collective-permute-start(f32[16,32,128]{2,1,0:T(8,128)} %get-tuple-element.30), channel_id=1, source_target_pairs={{16,0},{0,1},{18,2},{2,3},{20,4},{4,5},{22,6},{6,7},{24,8},{8,9},{... | collective-permute-start | bytes 786440 | tf_op jit(solution)/shard_map/ppermute | solution.py:527
  6.7 2.6 %collective-permute-done.xf = f32[30,16,128]{2,1,0:T(8,128)S(1)} collective-permute-done((f32[30,16,128]{2,1,0:T(8,128)}, f32[30,16,128]{2,1,0:T(8,128)S(1)}, u32[]{:S(2)}, u32[]{:S(2)}) %collective-permute-start) | collective-permute-done | bytes 245792 | tf_op jit(solution)/shard_map/ppermute | solution.py:527
  9.3 0.9 %collective-permute-done.1.xb = f32[30,16,128]{2,1,0:T(8,128)S(1)} collective-permute-done((f32[30,16,128]{2,1,0:T(8,128)}, f32[30,16,128]{2,1,0:T(8,128)S(1)}, u32[]{:S(2)}, u32[]{:S(2)}) %collective-permute-start.1) | collective-permute-done | bytes 245792 | tf_op jit(solution)/shard_map/ppermute | solution.py:527
  10.2 0.1 pack_corners.1
  10.3 0.3 collective-permute-start.4
  10.5 1.2 %collective-permute-start.5 = (f32[9,32,128]{2,1,0:T(8,128)S(1)}, f32[9,32,128]{2,1,0:T(8,128)S(1)}, u32[]{:S(2)}, u32[]{:S(2)}) collective-permute-start(f32[9,32,128]{2,1,0:T(8,128)S(1)} %get-tuple-element.32), channel_id=1, source_target_pairs={{16,0},{0,1},{18,2},{2,3},{20,4},{4,5},{22,6},{6,7},{24,8},{8,9},{... | collective-permute-start | bytes 442376 | tf_op jit(solution)/shard_map/ppermute | solution.py:527
  11.7 0.0 copy-start.1
  11.7 1.0 %copy-done.1 = f32[3,16,16,128]{3,2,1,0:T(8,128)S(1)} copy-done((f32[3,16,16,128]{3,2,1,0:T(8,128)S(1)}, f32[3,16,16,128]{3,2,1,0:T(8,128)}, u32[]{:S(2)}) %copy-start.1) | copy-done | bytes 393240
  12.7 0.0 copy-start.4
  12.7 0.9 %copy-done.4 = f32[16,16,128]{2,1,0:T(8,128)S(1)} copy-done((f32[16,16,128]{2,1,0:T(8,128)S(1)}, f32[16,16,128]{2,1,0:T(8,128)}, u32[]{:S(2)}) %copy-start.4) | copy-done | bytes 131096
  13.7 0.0 copy-done.7
  13.7 0.0 copy-done.6
  13.7 0.4 place.1
  14.1 0.0 collective-permute-done.2.yf
  14.1 0.0 collective-permute-done.3.yb
  14.2 0.9 %collective-permute-done.4.cf = f32[9,32,128]{2,1,0:T(8,128)S(1)} collective-permute-done((f32[9,32,128]{2,1,0:T(8,128)S(1)}, f32[9,32,128]{2,1,0:T(8,128)S(1)}, u32[]{:S(2)}, u32[]{:S(2)}) %collective-permute-start.4) | collective-permute-done | bytes 147488 | tf_op jit(solution)/shard_map/ppermute | solution.py:527
  15.0 0.3 collective-permute-done.5.cb
  15.3 0.0 copy-done
  15.3 0.0 copy-done.2
  15.3 0.0 copy-start.3
  15.3 0.0 copy-start.5
  15.3 1.2 %pack_z.1 = (f32[8,25,24,128]{3,2,1,0:T(8,128)S(1)}, f32[26,24,128]{2,1,0:T(8,128)S(1)}, f32[13,24,128]{2,1,0:T(8,128)S(1)}, f32[13,24,128]{2,1,0:T(8,128)S(1)}) custom-call(f32[3,16,16,128]{3,2,1,0:T(8,128)S(1)} %copy-done.2, f32[4,16,16,128]{3,2,1,0:T(8,128)S(1)} %scale.1.scaled, f32[16,16,128]{2,1,0:T(8,128)S(1)} %copy-done, ...), custom_call_target="tpu_custom_call" | custom-call | tf_op jit(solution)/shard_map/pack_z/pallas_call | solution.py:565
  16.5 6.4 %collective-permute-start.6 = (f32[13,24,128]{2,1,0:T(8,128)S(1)}, f32[13,24,128]{2,1,0:T(8,128)S(1)}, u32[]{:S(2)}, u32[]{:S(2)}) collective-permute-start(f32[13,24,128]{2,1,0:T(8,128)S(1)} %get-tuple-element.37), channel_id=1, source_target_pairs={{0,1},{1,2},{2,3},{3,4},{4,5},{5,6},{6,7},{7,8},{8,9},{9,10},{10,1... | collective-permute-start | bytes 479240 | tf_op jit(solution)/shard_map/ppermute | solution.py:533
  22.9 0.0 collective-permute-start.7
  22.9 4.7 %bulk.1 = (f32[3,25,24,128]{3,2,1,0:T(8,128)S(1)}, f32[16,16,128]{2,1,0:T(8,128)S(1)}, f32[16,16,128]{2,1,0:T(8,128)S(1)}) custom-call(f32[8,25,24,128]{3,2,1,0:T(8,128)S(1)} %get-tuple-element.34.whole), custom_call_target="tpu_custom_call" | custom-call | flops 1000000000 | bytes 10000000 | tf_op jit(solution)/shard_map/bulk/pallas_call | solution.py:571
  27.6 0.0 collective-permute-done.6.below_z
  27.6 0.0 collective-permute-done.7.above_z
  27.6 0.0 copy-done.3
  27.6 0.0 copy-done.5
  27.6 5.6 %edge.1 = (f32[3,13,24,128]{3,2,1,0:T(8,128)S(1)}, f32[576,128]{1,0:T(8,128)S(1)}, f32[16,16,128]{2,1,0:T(8,128)S(1)}) custom-call(f32[26,24,128]{2,1,0:T(8,128)S(1)} %get-tuple-element.36.packed, f32[13,24,128]{2,1,0:T(8,128)S(1)} %collective-permute-done.6.below_z, f32[13,24,128]{2,1,0:T(8,128)S(1)} %collective-permute-done.7.above_z, ...), custom_call_target="tpu_custom_call" | custom-call | tf_op jit(solution)/shard_map/edge/pallas_call | solution.py:578
  33.3 24.2 %all_to_all.5 = f32[576,1,128]{2,1,0:T(1,128)S(1)} all-to-all(f32[576,1,128]{2,1,0:T(1,128)S(1)} %bitcast.7), channel_id=1, replica_groups=mesh['gx'=8,'gy'=4,'gz'=16] {'gy','gz'}, dimensions={0} | all-to-all | bytes 589824 | tf_op jit(solution)/shard_map/all_to_all | solution.py:593
  57.4 1.0 %warm.1 = (f32[16,128]{1,0:T(8,128)S(1)}, f32[16,128]{1,0:T(8,128)S(1)}, f32[16,128]{1,0:T(8,128)S(1)}, f32[16,128]{1,0:T(8,128)S(1)}, f32[16,128]{1,0:T(8,128)S...) custom-call(f32[576,128]{1,0:T(8,128)S(1)} %bitcast.6, f32[16,16,128]{2,1,0:T(8,128)S(1)} %get-tuple-element.44.partial, ...), custom_call_target="tpu_custom_call" | custom-call | tf_op jit(solution)/shard_map/warm/pallas_call | solution.py:596
  58.5 0.0 collective-permute-start.8
  58.5 3.0 %collective-permute-start.9 = (f32[16,128]{1,0:T(8,128)S(1)}, f32[16,128]{1,0:T(8,128)S(1)}, u32[]{:S(2)}, u32[]{:S(2)}) collective-permute-start(f32[16,128]{1,0:T(8,128)S(1)} %get-tuple-element.47), channel_id=1, source_target_pairs={{64,0},{0,1},{66,2},{2,3},{68,4},{4,5},{70,6},{6,7},{72,8},{8,9},{... | collective-permute-start | bytes 24584 | tf_op jit(solution)/shard_map/ppermute | solution.py:527
  61.5 0.2 collective-permute-start.10
  61.6 1.3 %collective-permute-start.11 = (f32[16,128]{1,0:T(8,128)S(1)}, f32[16,128]{1,0:T(8,128)S(1)}, u32[]{:S(2)}, u32[]{:S(2)}) collective-permute-start(f32[16,128]{1,0:T(8,128)S(1)} %get-tuple-element.49), channel_id=1, source_target_pairs={{16,0},{0,1},{18,2},{2,3},{20,4},{4,5},{22,6},{6,7},{24,8},{8,9},{... | collective-permute-start | bytes 24584 | tf_op jit(solution)/shard_map/ppermute | solution.py:527
  63.0 1.6 %collective-permute-start.12 = (f32[16,128]{1,0:T(8,128)S(1)}, f32[16,128]{1,0:T(8,128)S(1)}, u32[]{:S(2)}, u32[]{:S(2)}) collective-permute-start(f32[16,128]{1,0:T(8,128)S(1)} %get-tuple-element.50), channel_id=1, source_target_pairs={{0,1},{1,2},{2,3},{3,4},{4,5},{5,6},{6,7},{7,8},{8,9},{9,10},{10,1... | collective-permute-start | bytes 24584 | tf_op jit(solution)/shard_map/ppermute | solution.py:533
  64.6 0.0 collective-permute-done.8.xf
  64.6 0.0 collective-permute-start.13
  64.6 1.0 %merge.1 = f32[3,16,16,128]{3,2,1,0:T(8,128)} custom-call(f32[3,25,24,128]{3,2,1,0:T(8,128)S(1)} %get-tuple-element.35.final, f32[3,13,24,128]{3,2,1,0:T(8,128)S(1)} %get-tuple-element.42.near), custom_call_target="tpu_custom_call" | custom-call | flops 1000000000 | bytes 1000000 | tf_op jit(solution)/shard_map/merge/pallas_call | solution.py:605
  65.6 0.0 collective-permute-done.9.xb
  65.6 0.0 collective-permute-done.10.yf
  65.6 0.0 collective-permute-done.11.yb
  65.6 0.0 collective-permute-done.12.from_below
  65.6 2.3 %collective-permute-done.13.from_above = f32[16,128]{1,0:T(8,128)S(1)} collective-permute-done((f32[16,128]{1,0:T(8,128)S(1)}, f32[16,128]{1,0:T(8,128)S(1)}, u32[]{:S(2)}, u32[]{:S(2)}) %collective-permute-start.13) | collective-permute-done | bytes 8224 | tf_op jit(solution)/shard_map/ppermute | solution.py:533
  68.0 0.8 %finish.1 = f32[16,16,128]{2,1,0:T(8,128)} custom-call(f32[16,16,128]{2,1,0:T(8,128)S(1)} %get-tuple-element.45.rest, f32[16,16,128]{2,1,0:T(8,128)S(1)} %copy-done.3, f32[16,128]{1,0:T(8,128)S(1)} %collective-permute-done.8.xf, f32[16,128]{1,0:T(8,128)S(1)} %collective-permute-done.9.xb, f32[16,128]{1,0:T(8,128)S(1)} %collective-permute-done.10.yf, ...), custom_call_target="tpu_custom_call" | custom-call | tf_op jit(solution)/shard_map/finish/pallas_call | solution.py:602
  (1 shorter events, 0.0 us)
Async XLA Ops:
  0.6 14.7 %copy-start = (f32[16,16,128]{2,1,0:T(8,128)S(1)}, f32[16,16,128]{2,1,0:T(8,128)}, u32[]{:S(2)}) copy-start(f32[16,16,128]{2,1,0:T(8,128)} %warmth.5) | copy-start | bytes 393220
  0.6 14.7 %copy-start.2 = (f32[3,16,16,128]{3,2,1,0:T(8,128)S(1)}, f32[3,16,16,128]{3,2,1,0:T(8,128)}, u32[]{:S(2)}) copy-start(f32[3,16,16,128]{3,2,1,0:T(8,128)} %field.1) | copy-start | bytes 1179652
  0.7 13.0 %copy-start.7 = (s32[1,1,1,256]{3,2,1,0:T(1,128)S(1)}, s32[1,1,1,256]{3,2,1,0:T(1,128)}, u32[]{:S(2)}) copy-start(s32[1,1,1,256]{3,2,1,0:T(1,128)} %param.13) | copy-start | bytes 3076
  0.7 13.0 %copy-start.6 = (s32[1,1,1,256,1]{3,4,2,1,0:T(1,128)S(1)}, s32[1,1,1,256,1]{3,4,2,1,0:T(1,128)}, u32[]{:S(2)}) copy-start(s32[1,1,1,256,1]{3,4,2,1,0:T(1,128)} %param.12) | copy-start | bytes 3076
  3.1 6.2 %collective-permute-start = (f32[30,16,128]{2,1,0:T(8,128)}, f32[30,16,128]{2,1,0:T(8,128)S(1)}, u32[]{:S(2)}, u32[]{:S(2)}) collective-permute-start(f32[30,16,128]{2,1,0:T(8,128)} %get-tuple-element.27), channel_id=1, source_target_pairs={{0,64},{1,0},{2,66},{3,2},{4,68},{5,4},{6,70},{7,6},{8,72},{9,8},{... | collective-permute-start | bytes 737288 | tf_op jit(solution)/shard_map/ppermute | solution.py:527
  3.1 7.1 %collective-permute-start.1 = (f32[30,16,128]{2,1,0:T(8,128)}, f32[30,16,128]{2,1,0:T(8,128)S(1)}, u32[]{:S(2)}, u32[]{:S(2)}) collective-permute-start(f32[30,16,128]{2,1,0:T(8,128)} %get-tuple-element.28), channel_id=1, source_target_pairs={{64,0},{0,1},{66,2},{2,3},{68,4},{4,5},{70,6},{6,7},{72,8},{8,9},{... | collective-permute-start | bytes 737288 | tf_op jit(solution)/shard_map/ppermute | solution.py:527
  5.2 8.9 %collective-permute-start.2 = (f32[16,32,128]{2,1,0:T(8,128)}, f32[16,32,128]{2,1,0:T(8,128)S(1)}, u32[]{:S(2)}, u32[]{:S(2)}) collective-permute-start(f32[16,32,128]{2,1,0:T(8,128)} %get-tuple-element.29), channel_id=1, source_target_pairs={{0,16},{1,0},{2,18},{3,2},{4,20},{5,4},{6,22},{7,6},{8,24},{9,8},{... | collective-permute-start | bytes 786440 | tf_op jit(solution)/shard_map/ppermute | solution.py:527
  5.5 8.7 %collective-permute-start.3 = (f32[16,32,128]{2,1,0:T(8,128)}, f32[16,32,128]{2,1,0:T(8,128)S(1)}, u32[]{:S(2)}, u32[]{:S(2)}) collective-permute-start(f32[16,32,128]{2,1,0:T(8,128)} %get-tuple-element.30), channel_id=1, source_target_pairs={{16,0},{0,1},{18,2},{2,3},{20,4},{4,5},{22,6},{6,7},{24,8},{8,9},{... | collective-permute-start | bytes 786440 | tf_op jit(solution)/shard_map/ppermute | solution.py:527
  10.3 4.8 %collective-permute-start.4 = (f32[9,32,128]{2,1,0:T(8,128)S(1)}, f32[9,32,128]{2,1,0:T(8,128)S(1)}, u32[]{:S(2)}, u32[]{:S(2)}) collective-permute-start(f32[9,32,128]{2,1,0:T(8,128)S(1)} %get-tuple-element.31), channel_id=1, source_target_pairs={{0,16},{1,0},{2,18},{3,2},{4,20},{5,4},{6,22},{7,6},{8,24},{9,8},{... | collective-permute-start | bytes 442376 | tf_op jit(solution)/shard_map/ppermute | solution.py:527
  10.5 4.8 %collective-permute-start.5 = (f32[9,32,128]{2,1,0:T(8,128)S(1)}, f32[9,32,128]{2,1,0:T(8,128)S(1)}, u32[]{:S(2)}, u32[]{:S(2)}) collective-permute-start(f32[9,32,128]{2,1,0:T(8,128)S(1)} %get-tuple-element.32), channel_id=1, source_target_pairs={{16,0},{0,1},{18,2},{2,3},{20,4},{4,5},{22,6},{6,7},{24,8},{8,9},{... | collective-permute-start | bytes 442376 | tf_op jit(solution)/shard_map/ppermute | solution.py:527
  11.7 1.0 %copy-start.1 = (f32[3,16,16,128]{3,2,1,0:T(8,128)S(1)}, f32[3,16,16,128]{3,2,1,0:T(8,128)}, u32[]{:S(2)}) copy-start(f32[3,16,16,128]{3,2,1,0:T(8,128)} %refs_1_.1) | copy-start | bytes 1179652
  12.7 0.9 %copy-start.4 = (f32[16,16,128]{2,1,0:T(8,128)S(1)}, f32[16,16,128]{2,1,0:T(8,128)}, u32[]{:S(2)}) copy-start(f32[16,16,128]{2,1,0:T(8,128)} %sigma.3) | copy-start | bytes 393220
  15.3 12.3 %copy-start.3 = (f32[16,16,128]{2,1,0:T(8,128)S(1)}, f32[16,16,128]{2,1,0:T(8,128)}, u32[]{:S(2)}) copy-start(f32[16,16,128]{2,1,0:T(8,128)} %storage.5) | copy-start | bytes 393220
  15.3 12.3 %copy-start.5 = (f32[16,16,128]{2,1,0:T(8,128)S(1)}, f32[16,16,128]{2,1,0:T(8,128)}, u32[]{:S(2)}) copy-start(f32[16,16,128]{2,1,0:T(8,128)} %sigma.3) | copy-start | bytes 393220
  16.5 11.1 %collective-permute-start.6 = (f32[13,24,128]{2,1,0:T(8,128)S(1)}, f32[13,24,128]{2,1,0:T(8,128)S(1)}, u32[]{:S(2)}, u32[]{:S(2)}) collective-permute-start(f32[13,24,128]{2,1,0:T(8,128)S(1)} %get-tuple-element.37), channel_id=1, source_target_pairs={{0,1},{1,2},{2,3},{3,4},{4,5},{5,6},{6,7},{7,8},{8,9},{9,10},{10,1... | collective-permute-start | bytes 479240 | tf_op jit(solution)/shard_map/ppermute | solution.py:533
  22.9 4.7 %collective-permute-start.7 = (f32[13,24,128]{2,1,0:T(8,128)S(1)}, f32[13,24,128]{2,1,0:T(8,128)S(1)}, u32[]{:S(2)}, u32[]{:S(2)}) collective-permute-start(f32[13,24,128]{2,1,0:T(8,128)S(1)} %get-tuple-element.38), channel_id=1, source_target_pairs={{1,0},{2,1},{3,2},{4,3},{5,4},{6,5},{7,6},{8,7},{9,8},{10,9},{11,1... | collective-permute-start | bytes 479240 | tf_op jit(solution)/shard_map/ppermute | solution.py:533
  58.5 6.1 %collective-permute-start.8 = (f32[16,128]{1,0:T(8,128)S(1)}, f32[16,128]{1,0:T(8,128)S(1)}, u32[]{:S(2)}, u32[]{:S(2)}) collective-permute-start(f32[16,128]{1,0:T(8,128)S(1)} %get-tuple-element.46), channel_id=1, source_target_pairs={{0,64},{1,0},{2,66},{3,2},{4,68},{5,4},{6,70},{7,6},{8,72},{9,8},{... | collective-permute-start | bytes 24584 | tf_op jit(solution)/shard_map/ppermute | solution.py:527
  58.5 7.1 %collective-permute-start.9 = (f32[16,128]{1,0:T(8,128)S(1)}, f32[16,128]{1,0:T(8,128)S(1)}, u32[]{:S(2)}, u32[]{:S(2)}) collective-permute-start(f32[16,128]{1,0:T(8,128)S(1)} %get-tuple-element.47), channel_id=1, source_target_pairs={{64,0},{0,1},{66,2},{2,3},{68,4},{4,5},{70,6},{6,7},{72,8},{8,9},{... | collective-permute-start | bytes 24584 | tf_op jit(solution)/shard_map/ppermute | solution.py:527
  61.5 4.1 %collective-permute-start.10 = (f32[16,128]{1,0:T(8,128)S(1)}, f32[16,128]{1,0:T(8,128)S(1)}, u32[]{:S(2)}, u32[]{:S(2)}) collective-permute-start(f32[16,128]{1,0:T(8,128)S(1)} %get-tuple-element.48), channel_id=1, source_target_pairs={{0,16},{1,0},{2,18},{3,2},{4,20},{5,4},{6,22},{7,6},{8,24},{9,8},{... | collective-permute-start | bytes 24584 | tf_op jit(solution)/shard_map/ppermute | solution.py:527
  61.6 4.0 %collective-permute-start.11 = (f32[16,128]{1,0:T(8,128)S(1)}, f32[16,128]{1,0:T(8,128)S(1)}, u32[]{:S(2)}, u32[]{:S(2)}) collective-permute-start(f32[16,128]{1,0:T(8,128)S(1)} %get-tuple-element.49), channel_id=1, source_target_pairs={{16,0},{0,1},{18,2},{2,3},{20,4},{4,5},{22,6},{6,7},{24,8},{8,9},{... | collective-permute-start | bytes 24584 | tf_op jit(solution)/shard_map/ppermute | solution.py:527
  63.0 2.7 %collective-permute-start.12 = (f32[16,128]{1,0:T(8,128)S(1)}, f32[16,128]{1,0:T(8,128)S(1)}, u32[]{:S(2)}, u32[]{:S(2)}) collective-permute-start(f32[16,128]{1,0:T(8,128)S(1)} %get-tuple-element.50), channel_id=1, source_target_pairs={{0,1},{1,2},{2,3},{3,4},{4,5},{5,6},{6,7},{7,8},{8,9},{9,10},{10,1... | collective-permute-start | bytes 24584 | tf_op jit(solution)/shard_map/ppermute | solution.py:533
  64.6 3.4 %collective-permute-start.13 = (f32[16,128]{1,0:T(8,128)S(1)}, f32[16,128]{1,0:T(8,128)S(1)}, u32[]{:S(2)}, u32[]{:S(2)}) collective-permute-start(f32[16,128]{1,0:T(8,128)S(1)} %get-tuple-element.51), channel_id=1, source_target_pairs={{1,0},{2,1},{3,2},{4,3},{5,4},{6,5},{7,6},{8,7},{9,8},{10,9},{11,1... | collective-permute-start | bytes 24584 | tf_op jit(solution)/shard_map/ppermute | solution.py:533

commit v5 on v4

--- a/solution.py
+++ b/solution.py
@@ -13,7 +13,6 @@
 CAP = 8
 LOW, HIGH = 4, 5
 F32 = jnp.float32
-FIRST_LIMIT = 62 << 20
 
 em_lower = 0.02
 em_upper = 3.0
@@ -69,10 +68,12 @@
     return values if by == 0 else pltpu.roll(values, by, axis)
 
 
-def call(body, out_shapes, scratch=(), name=None, limit=8 << 20, **options):
+def call(body, out_shapes, scratch=(), name=None, limit=8 << 20, near=False, **options):
     return pl.pallas_call(
         body,
-        out_shape=[jax.ShapeDtypeStruct(s, F32) for s in out_shapes],
+        out_shape=[
+            pltpu.VMEM(s, F32) if near else jax.ShapeDtypeStruct(s, F32) for s in out_shapes
+        ],
         scratch_shapes=[pltpu.VMEM(s, F32) if isinstance(s, tuple) else s for s in scratch],
         compiler_params=pltpu.CompilerParams(vmem_limit_bytes=limit),
         name=name,
@@ -103,7 +104,7 @@
 
 
 def pack_xy(*refs):
-    far, (xf, xb, yf, yb), near, (scaled, arrived) = refs[:4], refs[4:8], refs[8:12], refs[12:]
+    far, (xf, xb, yf, yb, scaled), near, arrived = refs[:4], refs[4:9], refs[9:13], refs[13]
     copies = [
         pltpu.make_async_copy(a, b, arrived.at[n]) for n, (a, b) in enumerate(zip(far, near))
     ]
@@ -137,13 +138,6 @@
     lax.fori_loop(0, 16, step, 0, unroll=4)
 
 
-def scale(source, sigma, scaled):
-    inverse = 1.0 / (4.0 + sigma[...])
-    scaled[3] = inverse
-    for c in range(3):
-        scaled[c] = source[c] * inverse
-
-
 class Slabs:
     def __init__(self, field, scaled, warmth, got_fwd, got_bwd):
         self.field, self.scaled, self.warmth = field, scaled, warmth
@@ -201,8 +195,8 @@
 
 HALO_X = tuple(range(-LOW, 0)) + tuple(range(16, 16 + HIGH))
 X_ALL = LOW + 16 + HIGH
-GROUP_ALL = LOW + 4 + HIGH
-SWEEP_UNROLL = 4
+BLOCKS = 5
+Y_LANES = LOW + 16 + HIGH
 X_PAIRS = (X_ALL + 1) // 2
 
 
@@ -244,142 +238,158 @@
     lax.fori_loop(0, X_PAIRS, pair_up, 0, unroll=True)
 
 
-def up_y(v):
-    return roll(v, -1, 0)
-
-
-def down_y(v):
-    return roll(v, 1, 0)
-
-
-def up_z(v):
-    return roll(v, -1, 1)
-
-
-def down_z(v):
-    return roll(v, 1, 1)
-
-
 def twist(a, b, c, d):
     return (a - b) - (c - d)
 
 
-def relax(fields, first, second, layers):
+def curls(e, e_up_y, e_up_z, e_up_x):
+    (ex, ey, ez), (ex_y, ez_y), (ex_z, ey_z), (ey_x, ez_x) = e, e_up_y, e_up_z, e_up_x
+    return twist(ez_y, ez, ey_z, ey), twist(ex_z, ex, ez_x, ez), twist(ey_x, ey, ex_y, ex)
+
+
+def relaxed(weight, e, h, g, c, c_down_x, c_down_y, c_down_z):
+    (cx, cy, cz), (cy_x, cz_x), (cx_y, cz_y), (cx_z, cy_z) = c, c_down_x, c_down_y, c_down_z
+    k = twist(cz, cz_y, cy, cy_z), twist(cx, cx_z, cz, cz_x), twist(cy, cy_x, cx, cx_y)
+    g = g * weight
+    keep = (1.0 - weight) + 4.0 * g
+    return [keep * e[f] + weight * h[f] - g * k[f] for f in range(3)]
+
+
+def bulk(whole, final, whole_sum, shifted, spare):
     row = rows((24, 128))
-    buffers = (fields, first, second, first, second)
-
-    def curls(source, at, outer):
-        ex, ey, ez = (source[f, at] for f in range(3))
-        ex_up, ez_up = up_y(ex), up_y(ez)
+    buffers = (whole, spare, final, spare, final)
+
+    def curls_at(source, at, outer):
+        e = [source[f, at] for f in range(3)]
+        up_y = [roll(e[0], -1, 0), roll(e[2], -1, 0)]
         if outer:
-            ex_up = jnp.where(row == 19, fields[7, at, 16:17, :], ex_up)
-            ez_up = jnp.where(row == 19, fields[7, at, 17:18, :], ez_up)
-        cx = twist(ez_up, ez, up_z(ey), ey)
-        cy = twist(up_z(ex), ex, source[2, at + 1], ez)
-        cz = twist(source[1, at + 1], ey, ex_up, ex)
-        return (ex, ey, ez), (cx, cy, cz)
+            up_y = [jnp.where(row == 19, whole[7, at, pl.ds(16 + n, 1), :], up_y[n]) for n in range(2)]
+        up_z = roll(e[0], -1, 1), roll(e[1], -1, 1)
+        return e, curls(e, up_y, up_z, (source[1, at + 1], source[2, at + 1]))
 
     for number, weight in enumerate(EM_WEIGHTS):
         source, target, outer = buffers[number], buffers[number + 1], number == 0
 
         def step(at, carry, source=source, target=target, outer=outer, weight=weight):
-            cy_before, cz_before = carry
-            e, (cx, cy, cz) = curls(source, at, outer)
-            kx = twist(cz, down_y(cz), cy, down_z(cy))
-            ky = twist(cx, down_z(cx), cz, cz_before)
-            kz = twist(cy, cy_before, cx, down_y(cx))
-            g = fields[6, at] * weight
-            keep = (1.0 - weight) + 4.0 * g
-            for f, k in enumerate((kx, ky, kz)):
-                target[f, at] = keep * e[f] + weight * fields[3 + f, at] - g * k
-            return cy, cz
+            e, c = curls_at(source, at, outer)
+            h, g = [whole[3 + f, at] for f in range(3)], whole[6, at]
+            down_y = roll(c[0], 1, 0), roll(c[2], 1, 0)
+            down_z = roll(c[0], 1, 1), roll(c[1], 1, 1)
+            new = relaxed(weight, e, h, g, c, carry, down_y, down_z)
+            for f in range(3):
+                target[f, at] = new[f]
+            return c[1], c[2]
 
         begin = 1 + number
-        _, (_, cy, cz) = curls(source, begin - 1, outer)
-        lax.fori_loop(begin, layers - begin, step, (cy, cz), unroll=SWEEP_UNROLL)
-
-
-def squares(field, at):
-    ex, ey, ez = (field[f, at] * field[f, at] for f in range(3))
-    ey_ahead, ez_ahead = (field[f, at + 1] * field[f, at + 1] for f in (1, 2))
-    upright = ez + ez_ahead
-    return (ex + up_y(ex)) + (ey + ey_ahead), upright + up_y(upright)
-
-
-def bulk(whole, final, flat, upright, spare):
-    relax(whole, spare, final, X_ALL)
+        _, c = curls_at(source, begin - 1, outer)
+        lax.fori_loop(begin, X_ALL - begin, step, (c[1], c[2]), unroll=4)
 
     def step(x, carry):
-        c, d = squares(final, x + LOW)
-        flat[x], upright[x] = c[0:16], d[0:16]
+        at = x + LOW
+        ex, ey, ez = (final[f, at] * final[f, at] for f in range(3))
+        ey_x, ez_x = (final[f, at + 1] * final[f, at + 1] for f in (1, 2))
+        flat, upright = (ex + roll(ex, -1, 0)) + (ey + ey_x), ez + ez_x
+        upright = upright + roll(upright, -1, 0)
+        whole_sum[x] = flat[0:16] + upright[0:16]
+        shifted[x] = roll(flat[0:16], -1, 1)
         return carry
 
     lax.fori_loop(0, 16, step, 0, unroll=4)
 
 
-def near_z(edge, group, inner):
-    lane = lanes(inner.shape)
-    high = roll(edge, 120 - 32 * group, 1)
-    low = roll(edge, -(32 * group + 24), 1)
-    return jnp.where(lane < 4, low, jnp.where(lane >= 124, high, inner)), high
+def of_layer(at):
+    return at % BLOCKS, Y_LANES * (at // BLOCKS)
 
 
 def edge(
-    packed, below_z, above_z, flat, upright, xf, xb, yf, yb, sigma, warmth, storage, position, nodes,
-    final, send, partial, beside, faces, fields, spare, heat,
+    packed, below_z, above_z, whole_sum, shifted, xf, xb, yf, yb, sigma, warmth, storage, position, nodes,
+    final, send, partial, beside, stack, fields, spare, last, heat,
 ):
     first = on_first_core()
     gx, gz = lax.axis_index("gx"), lax.axis_index("gz")
-    lane = lanes((24, 128))
-    half = (lane // 8) % 2 == 0
-    window = lane // 16
+    half = (lanes((24, 128)) // 8) % 2 == 0
     has_below, has_above = gz > 0, gz < lax.axis_size("gz") - 1
-
-    def unpack(k, odd):
+    nothing = jnp.zeros((1, 128), F32)
+    for block in range(BLOCKS):
+        for face in range(2):
+            for n in range(BLOCKS):
+                stack[block, face, Y_LANES * n + 24 : Y_LANES * n + 25, :] = nothing
+            stack[block, face, 125:128, :] = jnp.zeros((3, 128), F32)
+    for k in range(X_PAIRS):
         lower = jnp.where(has_below, below_z[k], 0.0)
         upper = jnp.where(has_above, above_z[k], 0.0)
-        at = 2 * k + odd
-        if odd:
-            came = jnp.where(half, roll(lower, -8, 1), upper)
-        else:
-            came = jnp.where(half, lower, roll(upper, 8, 1))
-        beside[at] = came
-        faces[0, at] = jnp.where(half, packed[at], came)
-        faces[1, at] = jnp.where(half, came, packed[at])
-
-    def unpack_pair(k, carry):
-        unpack(k, 0)
-        unpack(k, 1)
-        return carry
-
-    lax.fori_loop(0, X_ALL // 2, unpack_pair, 0, unroll=4)
-    unpack(X_ALL // 2, 0)
-
-    def regroup(i, carry):
-        v = [faces[j % 2, i + 4 * (j // 2)] for j in range(8)]
-        for d in (1, 2, 4):
-            plain = (window // d) % 2 == 0
-            for a in range(8):
-                if a & d == 0:
-                    p, q = v[a], v[a + d]
-                    v[a] = jnp.where(plain, p, roll(q, 16 * d, 1))
-                    v[a + d] = jnp.where(plain, roll(p, -16 * d, 1), q)
-        for f in range(8):
-            fields[f, i] = v[f]
-        return carry
-
-    lax.fori_loop(0, GROUP_ALL, regroup, 0, unroll=2)
-    relax(fields, spare, final, GROUP_ALL)
+        for at in range(2 * k, min(2 * k + 2, X_ALL)):
+            if at % 2:
+                came = jnp.where(half, roll(lower, -8, 1), upper)
+            else:
+                came = jnp.where(half, lower, roll(upper, 8, 1))
+            beside[at] = came
+            block, lane_at = of_layer(at)
+            own = packed[at]
+            for face in range(2):
+                window = jnp.where(half, came, own) if face else jnp.where(half, own, came)
+                stack[block, face, lane_at : lane_at + 24, :] = roll(window, 4, 0)
+    for block in range(BLOCKS):
+        for face in range(2):
+            turned = stack[block, face].T
+            for f in range(8):
+                fields[block, f, 16 * face : 16 * face + 16, :] = turned[16 * f : 16 * f + 16]
+    top = lanes((32, 128)) % Y_LANES == 24
+    for block in range(BLOCKS):
+        extra = fields[block, 7]
+        for f, by in ((0, 4), (2, 3)):
+            fields[block, f] = jnp.where(top, roll(extra, by, 1), fields[block, f])
+
+    buffers = (fields, spare, final, spare, final)
+
+    def ahead(source, block, f):
+        if block < BLOCKS - 1:
+            return source[block + 1, f]
+        return roll(source[0, f], -Y_LANES, 1)
+
+    def curls_at(source, block):
+        e = [source[block, f] for f in range(3)]
+        up_y = roll(e[0], -1, 1), roll(e[2], -1, 1)
+        up_z = roll(e[0], -1, 0), roll(e[1], -1, 0)
+        return e, curls(e, up_y, up_z, (ahead(source, block, 1), ahead(source, block, 2)))
+
+    for number, weight in enumerate(EM_WEIGHTS):
+        source, target = buffers[number], buffers[number + 1]
+        _, c = curls_at(source, BLOCKS - 1)
+        for f in range(3):
+            last[f] = c[f]
+        before = roll(c[1], Y_LANES, 1), roll(c[2], Y_LANES, 1)
+        for block in range(BLOCKS):
+            if block < BLOCKS - 1:
+                e, c = curls_at(source, block)
+            else:
+                e, c = [source[block, f] for f in range(3)], [last[f] for f in range(3)]
+            h, g = [fields[block, 3 + f] for f in range(3)], fields[block, 6]
+            down_y = roll(c[0], 1, 1), roll(c[2], 1, 1)
+            down_z = roll(c[0], 1, 0), roll(c[1], 1, 0)
+            new = relaxed(weight, e, h, g, c, before, down_y, down_z)
+            for f in range(3):
+                target[block, f] = new[f]
+            before = c[1], c[2]
+
+    for block in range(BLOCKS):
+        ex, ey, ez = (final[block, f] * final[block, f] for f in range(3))
+        ey_x, ez_x = (ahead(final, block, f) for f in (1, 2))
+        flat, upright = (ex + roll(ex, -1, 1)) + (ey + ey_x * ey_x), ez + ez_x * ez_x
+        both = flat + (upright + roll(upright, -1, 1))
+        stack[block, 0, 0:8, :] = both[24:32]
+        stack[block, 0, 120:128, :] = both[0:8]
+        stack[block, 0, 59:64, :] = flat[4:9]
+        stack[block, 0, 64:67, :] = flat[25:28]
+    for block in range(BLOCKS):
+        stack[block, 1] = stack[block, 0].T
     lane = lanes((16, 128))
-    for i in range(4):
-        c, d = squares(final, i + LOW)
-        c, d = c[0:16], d[0:16]
-        for group in range(4):
-            x = 4 * group + i
-            c_all, c_high = near_z(c, group, flat[x])
-            d_all, _ = near_z(d, group, upright[x])
-            c_up = jnp.where(lane == 127, roll(c_high, -1, 1), roll(c_all, -1, 1))
-            heat[x] = sigma[x] * (0.25 * ((c_all + c_up) + d_all))
+    for x in range(16):
+        block, lane_at = of_layer(x + LOW)
+        near = stack[block, 1, lane_at + LOW : lane_at + LOW + 16, :]
+        here = jnp.where((lane < 4) | (lane >= 124), near, whole_sum[x])
+        above = jnp.where((lane < 3) | (lane >= 123), roll(near, 64, 1), shifted[x])
+        heat[x] = sigma[x] * (0.25 * (here + above))
 
     count = send.shape[0]
     spread = (rows((count, 256)) == position[...]).astype(jnp.bfloat16)
@@ -402,20 +412,29 @@
         ends = roll(beside[x + LOW, 0:16, :], 8, 1)
         lower, upper = y_halo(first, (yf, yb), x, 3)
         total = (warmth[x - 1] if x else under) + (warmth[x + 1] if x < 15 else over)
-        total = total + jnp.where(row == 0, lower[3:4], down_y(t))
-        total = total + jnp.where(row == 15, upper[4:5], up_y(t))
-        total = total + jnp.where(lane == 0, down_z(ends), down_z(t))
-        total = total + jnp.where(lane == 127, up_z(ends), up_z(t))
+        total = total + jnp.where(row == 0, lower[3:4], roll(t, 1, 0))
+        total = total + jnp.where(row == 15, upper[4:5], roll(t, -1, 0))
+        total = total + roll(jnp.where(lane == 127, ends, t), 1, 1)
+        total = total + roll(jnp.where(lane == 0, ends, t), -1, 1)
         partial[x] = t + HEAT_WEIGHTS[0] * (total - 6.0 * t) / (6.0 + storage[x])
 
 
-def merge(final, near, out):
-    for f in range(3):
-        for i in range(4):
-            windows = near[f, i + LOW, 0:16, :]
-            for group in range(4):
-                x = 4 * group + i
-                out[f, x], _ = near_z(windows, group, final[f, x + LOW, 0:16, :])
+def merge(final, near, out, stack):
+    for block in range(BLOCKS):
+        for f in range(3):
+            stack[block, 32 * f : 32 * f + 8, :] = near[block, f, 24:32, :]
+            at = (32 * f - 8) % 128
+            stack[block, at : at + 8, :] = near[block, f, 0:8, :]
+    for block in range(BLOCKS):
+        stack[block] = stack[block].T
+    lane = lanes((16, 128))
+    outer = (lane < 4) | (lane >= 124)
+    for x in range(16):
+        block, lane_at = of_layer(x + LOW)
+        windows = stack[block, lane_at + LOW : lane_at + LOW + 16, :]
+        for f in range(3):
+            inner = final[f, x + LOW, 0:16, :]
+            out[f, x] = jnp.where(outer, roll(windows, -32 * f, 1), inner)
 
 
 def place(owners, columns, position, nodes):
@@ -539,17 +558,17 @@
     cube = (16, 16, 128)
     face = (16, 128)
     x_message, y_message, corners = (X_LAYERS, 16, 128), (16, 32, 128), (len(HALO_X), 32, 128)
-    xf, xb, yf, yb = call(
+    here = [pltpu.with_memory_space_constraint(v, pltpu.HBM) for v in (field, source, sigma, warmth)]
+    xf, xb, yf, yb, scaled = call(
         pack_xy,
-        [x_message, x_message, y_message, y_message],
-        [(3, *cube), (3, *cube), cube, cube, (4, *cube), pltpu.SemaphoreType.DMA((4,))],
+        [x_message, x_message, y_message, y_message, (4, *cube)],
+        [(3, *cube), (3, *cube), cube, cube, pltpu.SemaphoreType.DMA((4,))],
         name="pack_xy",
-        limit=FIRST_LIMIT,
+        near=True,
         in_specs=[pl.BlockSpec(memory_space=pltpu.HBM)] * 4,
-    )(field, source, sigma, warmth)
+    )(*here)
     xf, xb = exchange("gx", xf, xb)
     yf, yb = exchange("gy", yf, yb)
-    (scaled,) = call(scale, [(4, *cube)], name="scale")(source, sigma)
     position, nodes = pl.pallas_call(
         place,
         out_shape=[
@@ -568,7 +587,7 @@
         name="pack_z",
     )(field, scaled, warmth, xf, xb, yf, yb, cf, cb, position)
     below_z, above_z = exchange_z(up, down)
-    final, flat, upright = call(
+    final, whole_sum, shifted = call(
         bulk,
         [(3, X_ALL, *layer), cube, cube],
         [(3, X_ALL, *layer)],
@@ -577,17 +596,18 @@
     )(whole)
     near, send, partial = call(
         edge,
-        [(3, GROUP_ALL, *layer), (count, 128), cube],
+        [(BLOCKS, 3, 32, 128), (count, 128), cube],
         [
             (X_ALL, *layer),
-            (2, X_ALL, *layer),
-            (8, GROUP_ALL, *layer),
-            (3, GROUP_ALL, *layer),
+            (BLOCKS, 2, 128, 128),
+            (BLOCKS, 8, 32, 128),
+            (BLOCKS, 3, 32, 128),
+            (3, 32, 128),
             cube,
         ],
         name="edge",
     )(
-        packed, below_z, above_z, flat, upright, xf, xb, yf, yb, sigma, warmth, storage,
+        packed, below_z, above_z, whole_sum, shifted, xf, xb, yf, yb, sigma, warmth, storage,
         position, nodes,
     )
     got = lax.all_to_all(
@@ -605,6 +625,7 @@
     (out,) = call(
         merge,
         [(3, *cube)],
+        [(BLOCKS, 128, 128)],
         name="merge",
         cost_estimate=pl.CostEstimate(flops=10**9, bytes_accessed=10**6, transcendentals=0),
     )(final, near)

time: 69 us -> 66.2 us (0.959)
  Pallas kernels: 17.2 us -> 12.8 us
  local copies, waits for them, and re-layouts: 1.92 us -> 3.27 us
    pallas_call x4 -> x3, Pallas kernels: 9.08 us -> 4.45 us  [the longest x1 2.02 us: local(): call(edge, [(BLOCKS, 3, 32, 128), (count, 128), cube], [(X_ALL, *layer),...]
    unnamed x16 -> x14, local copies, waits for them, and re-layouts: 1.92 us -> 3.27 us
  transfers between devices with their start and end apart: 14 -> 14, of which waited for: 5 -> 5; matrix products, arithmetic and copies ran while one was open for 0% -> 0% of each run, Pallas kernels for 9% -> 10%
where the time goes in v5:
time: 66.2 us; the launch traced here: 66 us
  blocking collectives  24.2 us (37%)
  starting transfers between devices  17.6 us (27%)
  Pallas kernels  12.8 us (19%)
  waiting for transfers between devices  7.35 us (11%)
  local copies, waits for them, and re-layouts  3.27 us (5%)
  between operations  0.76 us (1%)
    all_to_all x1, blocking collectives, local(): lax.all_to_all(send.reshape(count, 1, 128), ('gy', 'gz'), split_axis=0, c...  24.2 us
    ppermute x5, starting transfers between devices, exchange(): lax.ppermute(bwd, names, backward)  8.8 us
    ppermute x2, starting transfers between devices, exchange_z(): lax.ppermute(up, 'gz', ring)  8.09 us
    pallas_call x1, Pallas kernels, local(): call(bulk, [(3, X_ALL, *layer), cube, cube], [(3, X_ALL, *layer)], name='...  4.91 us
    ppermute x5, waiting for transfers between devices, exchange(): lax.ppermute(fwd, names, forward)  3.89 us
    unnamed x14, local copies, waits for them, and re-layouts  3.27 us
    ppermute x2, waiting for transfers between devices, exchange_z(): lax.ppermute(down, 'gz', [(j, i) for i, j in ring])  2.28 us
    pallas_call x1, Pallas kernels, local(): call(edge, [(BLOCKS, 3, 32, 128), (count, 128), cube], [(X_ALL, *layer),...  2.02 us
  transfers between devices with their start and end apart: 14, of which 5 were waited for; matrix products, arithmetic and copies ran while one was open for 0% of the time, Pallas kernels for 10%

profile of v5, /device:TPU:133, one launch (start us, length us, event | category | flops | bytes accessed | tf_op | source)
XLA Modules:
  0.0 66.0 jit_solution(8025477411964042445)
XLA Ops:
  0.6 1.4 %pack_xy.1 = (f32[30,16,128]{2,1,0:T(8,128)S(1)}, f32[30,16,128]{2,1,0:T(8,128)S(1)}, f32[16,32,128]{2,1,0:T(8,128)S(1)}, f32[16,32,128]{2,1,0:T(8,128)S(1)}, f32[4,16,16,128]{3,2,1,0:T(8,128)S(1)}) custom-call(f32[3,16,16,128]{3,2,1,0:T(8,128)} %field.1, f32[3,16,16,128]{3,2,1,0:T(8,128)} %refs_1_.1, f32[16,16,128]{2,1,0:T(8,128)} %sigma.1, ...), custom_call_target="tpu_custom_call" | custom-call | tf_op jit(solution)/shard_map/pack_xy/pallas_call | solution.py:562
  2.0 0.0 collective-permute-start
  2.0 2.1 %collective-permute-start.1 = (f32[30,16,128]{2,1,0:T(8,128)S(1)}, f32[30,16,128]{2,1,0:T(8,128)S(1)}, u32[]{:S(2)}, u32[]{:S(2)}) collective-permute-start(f32[30,16,128]{2,1,0:T(8,128)S(1)} %get-tuple-element.30), channel_id=1, source_target_pairs={{64,0},{0,1},{66,2},{2,3},{68,4},{4,5},{70,6},{6,7},{72,8},{8,9},{... | collective-permute-start | bytes 737288 | tf_op jit(solution)/shard_map/ppermute | solution.py:546
  4.1 0.3 collective-permute-start.2
  4.4 1.2 %collective-permute-start.3 = (f32[16,32,128]{2,1,0:T(8,128)S(1)}, f32[16,32,128]{2,1,0:T(8,128)S(1)}, u32[]{:S(2)}, u32[]{:S(2)}) collective-permute-start(f32[16,32,128]{2,1,0:T(8,128)S(1)} %get-tuple-element.32), channel_id=1, source_target_pairs={{16,0},{0,1},{18,2},{2,3},{20,4},{4,5},{22,6},{6,7},{24,8},{8,9},{... | collective-permute-start | bytes 786440 | tf_op jit(solution)/shard_map/ppermute | solution.py:546
  5.6 2.4 %collective-permute-done.xf = f32[30,16,128]{2,1,0:T(8,128)S(1)} collective-permute-done((f32[30,16,128]{2,1,0:T(8,128)S(1)}, f32[30,16,128]{2,1,0:T(8,128)S(1)}, u32[]{:S(2)}, u32[]{:S(2)}) %collective-permute-start) | collective-permute-done | bytes 245792 | tf_op jit(solution)/shard_map/ppermute | solution.py:546
  8.0 0.9 %collective-permute-done.1.xb = f32[30,16,128]{2,1,0:T(8,128)S(1)} collective-permute-done((f32[30,16,128]{2,1,0:T(8,128)S(1)}, f32[30,16,128]{2,1,0:T(8,128)S(1)}, u32[]{:S(2)}, u32[]{:S(2)}) %collective-permute-start.1) | collective-permute-done | bytes 245792 | tf_op jit(solution)/shard_map/ppermute | solution.py:546
  8.9 0.1 pack_corners.1
  9.0 0.3 collective-permute-start.4
  9.3 1.2 %collective-permute-start.5 = (f32[9,32,128]{2,1,0:T(8,128)S(1)}, f32[9,32,128]{2,1,0:T(8,128)S(1)}, u32[]{:S(2)}, u32[]{:S(2)}) collective-permute-start(f32[9,32,128]{2,1,0:T(8,128)S(1)} %get-tuple-element.34), channel_id=1, source_target_pairs={{16,0},{0,1},{18,2},{2,3},{20,4},{4,5},{22,6},{6,7},{24,8},{8,9},{... | collective-permute-start | bytes 442376 | tf_op jit(solution)/shard_map/ppermute | solution.py:546
  10.5 0.0 copy-start.5
  10.5 0.7 %copy-done.5 = s32[1,1,1,256,1]{3,4,2,1,0:T(1,128)S(1)} copy-done((s32[1,1,1,256,1]{3,4,2,1,0:T(1,128)S(1)}, s32[1,1,1,256,1]{3,4,2,1,0:T(1,128)}, u32[]{:S(2)}) %copy-start.5) | copy-done | bytes 1048
  11.1 0.0 copy-start.6
  11.1 0.7 %copy-done.6 = s32[1,1,1,256]{3,2,1,0:T(1,128)S(1)} copy-done((s32[1,1,1,256]{3,2,1,0:T(1,128)S(1)}, s32[1,1,1,256]{3,2,1,0:T(1,128)}, u32[]{:S(2)}) %copy-start.6) | copy-done | bytes 1048
  11.8 0.4 place.1
  12.2 0.0 collective-permute-done.2.yf
  12.3 0.0 collective-permute-done.3.yb
  12.3 1.5 %collective-permute-done.4.cf = f32[9,32,128]{2,1,0:T(8,128)S(1)} collective-permute-done((f32[9,32,128]{2,1,0:T(8,128)S(1)}, f32[9,32,128]{2,1,0:T(8,128)S(1)}, u32[]{:S(2)}, u32[]{:S(2)}) %collective-permute-start.4) | collective-permute-done | bytes 147488 | tf_op jit(solution)/shard_map/ppermute | solution.py:546
  13.8 0.3 collective-permute-done.5.cb
  14.0 0.0 copy-start
  14.0 0.9 %copy-done = f32[16,16,128]{2,1,0:T(8,128)S(1)} copy-done((f32[16,16,128]{2,1,0:T(8,128)S(1)}, f32[16,16,128]{2,1,0:T(8,128)}, u32[]{:S(2)}) %copy-start) | copy-done | bytes 131096
  14.9 0.0 copy-start.2
  14.9 1.0 %copy-done.2 = f32[3,16,16,128]{3,2,1,0:T(8,128)S(1)} copy-done((f32[3,16,16,128]{3,2,1,0:T(8,128)S(1)}, f32[3,16,16,128]{3,2,1,0:T(8,128)}, u32[]{:S(2)}) %copy-start.2) | copy-done | bytes 393240
  15.9 0.0 copy-start.1
  15.9 0.0 copy-start.3
  15.9 0.0 copy-start.4
  15.9 1.2 %pack_z.1 = (f32[8,25,24,128]{3,2,1,0:T(8,128)S(1)}, f32[26,24,128]{2,1,0:T(8,128)S(1)}, f32[13,24,128]{2,1,0:T(8,128)S(1)}, f32[13,24,128]{2,1,0:T(8,128)S(1)}) custom-call(f32[3,16,16,128]{3,2,1,0:T(8,128)S(1)} %copy-done.2, f32[4,16,16,128]{3,2,1,0:T(8,128)S(1)} %get-tuple-element.28.scaled, f32[16,16,128]{2,1,0:T(8,128)S(1)} %copy-done, ...), custom_call_target="tpu_custom_call" | custom-call | tf_op jit(solution)/shard_map/pack_z/pallas_call | solution.py:584
  17.1 6.4 %collective-permute-start.6 = (f32[13,24,128]{2,1,0:T(8,128)S(1)}, f32[13,24,128]{2,1,0:T(8,128)S(1)}, u32[]{:S(2)}, u32[]{:S(2)}) collective-permute-start(f32[13,24,128]{2,1,0:T(8,128)S(1)} %get-tuple-element.39), channel_id=1, source_target_pairs={{0,1},{1,2},{2,3},{3,4},{4,5},{5,6},{6,7},{7,8},{8,9},{9,10},{10,1... | collective-permute-start | bytes 479240 | tf_op jit(solution)/shard_map/ppermute | solution.py:552
  23.5 0.0 collective-permute-start.7
  23.5 4.9 %bulk.1 = (f32[3,25,24,128]{3,2,1,0:T(8,128)S(1)}, f32[16,16,128]{2,1,0:T(8,128)S(1)}, f32[16,16,128]{2,1,0:T(8,128)S(1)}) custom-call(f32[8,25,24,128]{3,2,1,0:T(8,128)S(1)} %get-tuple-element.36.whole), custom_call_target="tpu_custom_call" | custom-call | flops 1000000000 | bytes 10000000 | tf_op jit(solution)/shard_map/bulk/pallas_call | solution.py:590
  28.4 0.0 collective-permute-done.6.below_z
  28.4 0.0 collective-permute-done.7.above_z
  28.5 0.0 copy-done.1
  28.5 0.0 copy-done.3
  28.5 0.0 copy-done.4
  28.5 2.0 %edge.1 = (f32[5,3,32,128]{3,2,1,0:T(8,128)S(1)}, f32[576,128]{1,0:T(8,128)S(1)}, f32[16,16,128]{2,1,0:T(8,128)S(1)}) custom-call(f32[26,24,128]{2,1,0:T(8,128)S(1)} %get-tuple-element.38.packed, f32[13,24,128]{2,1,0:T(8,128)S(1)} %collective-permute-done.6.below_z, f32[13,24,128]{2,1,0:T(8,128)S(1)} %collective-permute-done.7.above_z, ...), custom_call_target="tpu_custom_call" | custom-call | tf_op jit(solution)/shard_map/edge/pallas_call | solution.py:597
  30.5 24.2 %all_to_all.5 = f32[576,1,128]{2,1,0:T(1,128)S(1)} all-to-all(f32[576,1,128]{2,1,0:T(1,128)S(1)} %bitcast.7), channel_id=1, replica_groups=mesh['gx'=8,'gy'=4,'gz'=16] {'gy','gz'}, dimensions={0} | all-to-all | bytes 589824 | tf_op jit(solution)/shard_map/all_to_all | solution.py:613
  54.7 1.0 %warm.1 = (f32[16,128]{1,0:T(8,128)S(1)}, f32[16,128]{1,0:T(8,128)S(1)}, f32[16,128]{1,0:T(8,128)S(1)}, f32[16,128]{1,0:T(8,128)S(1)}, f32[16,128]{1,0:T(8,128)S...) custom-call(f32[576,128]{1,0:T(8,128)S(1)} %bitcast.6, f32[16,16,128]{2,1,0:T(8,128)S(1)} %get-tuple-element.46.partial, ...), custom_call_target="tpu_custom_call" | custom-call | tf_op jit(solution)/shard_map/warm/pallas_call | solution.py:616
  55.7 0.0 collective-permute-start.8
  55.7 3.0 %collective-permute-start.9 = (f32[16,128]{1,0:T(8,128)S(1)}, f32[16,128]{1,0:T(8,128)S(1)}, u32[]{:S(2)}, u32[]{:S(2)}) collective-permute-start(f32[16,128]{1,0:T(8,128)S(1)} %get-tuple-element.49), channel_id=1, source_target_pairs={{64,0},{0,1},{66,2},{2,3},{68,4},{4,5},{70,6},{6,7},{72,8},{8,9},{... | collective-permute-start | bytes 24584 | tf_op jit(solution)/shard_map/ppermute | solution.py:546
  58.7 0.2 collective-permute-start.10
  58.9 1.3 %collective-permute-start.11 = (f32[16,128]{1,0:T(8,128)S(1)}, f32[16,128]{1,0:T(8,128)S(1)}, u32[]{:S(2)}, u32[]{:S(2)}) collective-permute-start(f32[16,128]{1,0:T(8,128)S(1)} %get-tuple-element.51), channel_id=1, source_target_pairs={{16,0},{0,1},{18,2},{2,3},{20,4},{4,5},{22,6},{6,7},{24,8},{8,9},{... | collective-permute-start | bytes 24584 | tf_op jit(solution)/shard_map/ppermute | solution.py:546
  60.2 1.7 %collective-permute-start.12 = (f32[16,128]{1,0:T(8,128)S(1)}, f32[16,128]{1,0:T(8,128)S(1)}, u32[]{:S(2)}, u32[]{:S(2)}) collective-permute-start(f32[16,128]{1,0:T(8,128)S(1)} %get-tuple-element.52), channel_id=1, source_target_pairs={{0,1},{1,2},{2,3},{3,4},{4,5},{5,6},{6,7},{7,8},{8,9},{9,10},{10,1... | collective-permute-start | bytes 24584 | tf_op jit(solution)/shard_map/ppermute | solution.py:552
  61.8 0.0 collective-permute-done.8.xf
  61.8 0.0 collective-permute-start.13
  61.8 1.1 %merge.1 = f32[3,16,16,128]{3,2,1,0:T(8,128)} custom-call(f32[3,25,24,128]{3,2,1,0:T(8,128)S(1)} %get-tuple-element.37.final, f32[5,3,32,128]{3,2,1,0:T(8,128)S(1)} %get-tuple-element.44.near), custom_call_target="tpu_custom_call" | custom-call | flops 1000000000 | bytes 1000000 | tf_op jit(solution)/shard_map/merge/pallas_call | solution.py:625
  62.9 0.0 collective-permute-done.9.xb
  62.9 0.0 collective-permute-done.10.yf
  62.9 0.0 collective-permute-done.11.yb
  62.9 0.0 collective-permute-done.12.from_below
  62.9 2.3 %collective-permute-done.13.from_above = f32[16,128]{1,0:T(8,128)S(1)} collective-permute-done((f32[16,128]{1,0:T(8,128)S(1)}, f32[16,128]{1,0:T(8,128)S(1)}, u32[]{:S(2)}, u32[]{:S(2)}) %collective-permute-start.13) | collective-permute-done | bytes 8224 | tf_op jit(solution)/shard_map/ppermute | solution.py:552
  65.2 0.8 %finish.1 = f32[16,16,128]{2,1,0:T(8,128)} custom-call(f32[16,16,128]{2,1,0:T(8,128)S(1)} %get-tuple-element.47.rest, f32[16,16,128]{2,1,0:T(8,128)S(1)} %copy-done.3, f32[16,128]{1,0:T(8,128)S(1)} %collective-permute-done.8.xf, f32[16,128]{1,0:T(8,128)S(1)} %collective-permute-done.9.xb, f32[16,128]{1,0:T(8,128)S(1)} %collective-permute-done.10.yf, ...), custom_call_target="tpu_custom_call" | custom-call | tf_op jit(solution)/shard_map/finish/pallas_call | solution.py:622
Async XLA Ops:
  2.0 6.0 %collective-permute-start = (f32[30,16,128]{2,1,0:T(8,128)S(1)}, f32[30,16,128]{2,1,0:T(8,128)S(1)}, u32[]{:S(2)}, u32[]{:S(2)}) collective-permute-start(f32[30,16,128]{2,1,0:T(8,128)S(1)} %get-tuple-element.29), channel_id=1, source_target_pairs={{0,64},{1,0},{2,66},{3,2},{4,68},{5,4},{6,70},{7,6},{8,72},{9,8},{... | collective-permute-start | bytes 737288 | tf_op jit(solution)/shard_map/ppermute | solution.py:546
  2.0 6.9 %collective-permute-start.1 = (f32[30,16,128]{2,1,0:T(8,128)S(1)}, f32[30,16,128]{2,1,0:T(8,128)S(1)}, u32[]{:S(2)}, u32[]{:S(2)}) collective-permute-start(f32[30,16,128]{2,1,0:T(8,128)S(1)} %get-tuple-element.30), channel_id=1, source_target_pairs={{64,0},{0,1},{66,2},{2,3},{68,4},{4,5},{70,6},{6,7},{72,8},{8,9},{... | collective-permute-start | bytes 737288 | tf_op jit(solution)/shard_map/ppermute | solution.py:546
  4.1 8.1 %collective-permute-start.2 = (f32[16,32,128]{2,1,0:T(8,128)S(1)}, f32[16,32,128]{2,1,0:T(8,128)S(1)}, u32[]{:S(2)}, u32[]{:S(2)}) collective-permute-start(f32[16,32,128]{2,1,0:T(8,128)S(1)} %get-tuple-element.31), channel_id=1, source_target_pairs={{0,16},{1,0},{2,18},{3,2},{4,20},{5,4},{6,22},{7,6},{8,24},{9,8},{... | collective-permute-start | bytes 786440 | tf_op jit(solution)/shard_map/ppermute | solution.py:546
  4.4 7.9 %collective-permute-start.3 = (f32[16,32,128]{2,1,0:T(8,128)S(1)}, f32[16,32,128]{2,1,0:T(8,128)S(1)}, u32[]{:S(2)}, u32[]{:S(2)}) collective-permute-start(f32[16,32,128]{2,1,0:T(8,128)S(1)} %get-tuple-element.32), channel_id=1, source_target_pairs={{16,0},{0,1},{18,2},{2,3},{20,4},{4,5},{22,6},{6,7},{24,8},{8,9},{... | collective-permute-start | bytes 786440 | tf_op jit(solution)/shard_map/ppermute | solution.py:546
  9.0 4.8 %collective-permute-start.4 = (f32[9,32,128]{2,1,0:T(8,128)S(1)}, f32[9,32,128]{2,1,0:T(8,128)S(1)}, u32[]{:S(2)}, u32[]{:S(2)}) collective-permute-start(f32[9,32,128]{2,1,0:T(8,128)S(1)} %get-tuple-element.33), channel_id=1, source_target_pairs={{0,16},{1,0},{2,18},{3,2},{4,20},{5,4},{6,22},{7,6},{8,24},{9,8},{... | collective-permute-start | bytes 442376 | tf_op jit(solution)/shard_map/ppermute | solution.py:546
  9.3 4.8 %collective-permute-start.5 = (f32[9,32,128]{2,1,0:T(8,128)S(1)}, f32[9,32,128]{2,1,0:T(8,128)S(1)}, u32[]{:S(2)}, u32[]{:S(2)}) collective-permute-start(f32[9,32,128]{2,1,0:T(8,128)S(1)} %get-tuple-element.34), channel_id=1, source_target_pairs={{16,0},{0,1},{18,2},{2,3},{20,4},{4,5},{22,6},{6,7},{24,8},{8,9},{... | collective-permute-start | bytes 442376 | tf_op jit(solution)/shard_map/ppermute | solution.py:546
  10.5 0.7 %copy-start.5 = (s32[1,1,1,256,1]{3,4,2,1,0:T(1,128)S(1)}, s32[1,1,1,256,1]{3,4,2,1,0:T(1,128)}, u32[]{:S(2)}) copy-start(s32[1,1,1,256,1]{3,4,2,1,0:T(1,128)} %param.12) | copy-start | bytes 3076
  11.1 0.7 %copy-start.6 = (s32[1,1,1,256]{3,2,1,0:T(1,128)S(1)}, s32[1,1,1,256]{3,2,1,0:T(1,128)}, u32[]{:S(2)}) copy-start(s32[1,1,1,256]{3,2,1,0:T(1,128)} %param.13) | copy-start | bytes 3076
  14.0 0.9 %copy-start = (f32[16,16,128]{2,1,0:T(8,128)S(1)}, f32[16,16,128]{2,1,0:T(8,128)}, u32[]{:S(2)}) copy-start(f32[16,16,128]{2,1,0:T(8,128)} %warmth.5) | copy-start | bytes 393220
  14.9 1.0 %copy-start.2 = (f32[3,16,16,128]{3,2,1,0:T(8,128)S(1)}, f32[3,16,16,128]{3,2,1,0:T(8,128)}, u32[]{:S(2)}) copy-start(f32[3,16,16,128]{3,2,1,0:T(8,128)} %field.1) | copy-start | bytes 1179652
  15.9 12.5 %copy-start.1 = (f32[16,16,128]{2,1,0:T(8,128)S(1)}, f32[16,16,128]{2,1,0:T(8,128)}, u32[]{:S(2)}) copy-start(f32[16,16,128]{2,1,0:T(8,128)} %warmth.5) | copy-start | bytes 393220
  15.9 12.5 %copy-start.3 = (f32[16,16,128]{2,1,0:T(8,128)S(1)}, f32[16,16,128]{2,1,0:T(8,128)}, u32[]{:S(2)}) copy-start(f32[16,16,128]{2,1,0:T(8,128)} %storage.5) | copy-start | bytes 393220
  15.9 12.6 %copy-start.4 = (f32[16,16,128]{2,1,0:T(8,128)S(1)}, f32[16,16,128]{2,1,0:T(8,128)}, u32[]{:S(2)}) copy-start(f32[16,16,128]{2,1,0:T(8,128)} %sigma.1) | copy-start | bytes 393220
  17.1 11.4 %collective-permute-start.6 = (f32[13,24,128]{2,1,0:T(8,128)S(1)}, f32[13,24,128]{2,1,0:T(8,128)S(1)}, u32[]{:S(2)}, u32[]{:S(2)}) collective-permute-start(f32[13,24,128]{2,1,0:T(8,128)S(1)} %get-tuple-element.39), channel_id=1, source_target_pairs={{0,1},{1,2},{2,3},{3,4},{4,5},{5,6},{6,7},{7,8},{8,9},{9,10},{10,1... | collective-permute-start | bytes 479240 | tf_op jit(solution)/shard_map/ppermute | solution.py:552
  23.5 4.9 %collective-permute-start.7 = (f32[13,24,128]{2,1,0:T(8,128)S(1)}, f32[13,24,128]{2,1,0:T(8,128)S(1)}, u32[]{:S(2)}, u32[]{:S(2)}) collective-permute-start(f32[13,24,128]{2,1,0:T(8,128)S(1)} %get-tuple-element.40), channel_id=1, source_target_pairs={{1,0},{2,1},{3,2},{4,3},{5,4},{6,5},{7,6},{8,7},{9,8},{10,9},{11,1... | collective-permute-start | bytes 479240 | tf_op jit(solution)/shard_map/ppermute | solution.py:552
  55.7 6.1 %collective-permute-start.8 = (f32[16,128]{1,0:T(8,128)S(1)}, f32[16,128]{1,0:T(8,128)S(1)}, u32[]{:S(2)}, u32[]{:S(2)}) collective-permute-start(f32[16,128]{1,0:T(8,128)S(1)} %get-tuple-element.48), channel_id=1, source_target_pairs={{0,64},{1,0},{2,66},{3,2},{4,68},{5,4},{6,70},{7,6},{8,72},{9,8},{... | collective-permute-start | bytes 24584 | tf_op jit(solution)/shard_map/ppermute | solution.py:546
  55.7 7.2 %collective-permute-start.9 = (f32[16,128]{1,0:T(8,128)S(1)}, f32[16,128]{1,0:T(8,128)S(1)}, u32[]{:S(2)}, u32[]{:S(2)}) collective-permute-start(f32[16,128]{1,0:T(8,128)S(1)} %get-tuple-element.49), channel_id=1, source_target_pairs={{64,0},{0,1},{66,2},{2,3},{68,4},{4,5},{70,6},{6,7},{72,8},{8,9},{... | collective-permute-start | bytes 24584 | tf_op jit(solution)/shard_map/ppermute | solution.py:546
  58.7 4.2 %collective-permute-start.10 = (f32[16,128]{1,0:T(8,128)S(1)}, f32[16,128]{1,0:T(8,128)S(1)}, u32[]{:S(2)}, u32[]{:S(2)}) collective-permute-start(f32[16,128]{1,0:T(8,128)S(1)} %get-tuple-element.50), channel_id=1, source_target_pairs={{0,16},{1,0},{2,18},{3,2},{4,20},{5,4},{6,22},{7,6},{8,24},{9,8},{... | collective-permute-start | bytes 24584 | tf_op jit(solution)/shard_map/ppermute | solution.py:546
  58.9 4.0 %collective-permute-start.11 = (f32[16,128]{1,0:T(8,128)S(1)}, f32[16,128]{1,0:T(8,128)S(1)}, u32[]{:S(2)}, u32[]{:S(2)}) collective-permute-start(f32[16,128]{1,0:T(8,128)S(1)} %get-tuple-element.51), channel_id=1, source_target_pairs={{16,0},{0,1},{18,2},{2,3},{20,4},{4,5},{22,6},{6,7},{24,8},{8,9},{... | collective-permute-start | bytes 24584 | tf_op jit(solution)/shard_map/ppermute | solution.py:546
  60.2 2.7 %collective-permute-start.12 = (f32[16,128]{1,0:T(8,128)S(1)}, f32[16,128]{1,0:T(8,128)S(1)}, u32[]{:S(2)}, u32[]{:S(2)}) collective-permute-start(f32[16,128]{1,0:T(8,128)S(1)} %get-tuple-element.52), channel_id=1, source_target_pairs={{0,1},{1,2},{2,3},{3,4},{4,5},{5,6},{6,7},{7,8},{8,9},{9,10},{10,1... | collective-permute-start | bytes 24584 | tf_op jit(solution)/shard_map/ppermute | solution.py:552
  61.8 3.4 %collective-permute-start.13 = (f32[16,128]{1,0:T(8,128)S(1)}, f32[16,128]{1,0:T(8,128)S(1)}, u32[]{:S(2)}, u32[]{:S(2)}) collective-permute-start(f32[16,128]{1,0:T(8,128)S(1)} %get-tuple-element.53), channel_id=1, source_target_pairs={{1,0},{2,1},{3,2},{4,3},{5,4},{6,5},{7,6},{8,7},{9,8},{10,9},{11,1... | collective-permute-start | bytes 24584 | tf_op jit(solution)/shard_map/ppermute | solution.py:552

commit v6 on v5

--- a/solution.py
+++ b/solution.py
@@ -104,7 +104,7 @@
 
 
 def pack_xy(*refs):
-    far, (xf, xb, yf, yb, scaled), near, arrived = refs[:4], refs[4:9], refs[9:13], refs[13]
+    far, (xf, xb, yf, yb, scaled), near, arrived = refs[:5], refs[5:10], refs[10:15], refs[15]
     copies = [
         pltpu.make_async_copy(a, b, arrived.at[n]) for n, (a, b) in enumerate(zip(far, near))
     ]
@@ -112,7 +112,7 @@
         copy.start()
     for copy in copies:
         copy.wait()
-    field, source, sigma, warmth = near
+    field, sigma, warmth, _, source = near
     first = on_first_core()
     inverse = 1.0 / (4.0 + sigma[...])
     scaled[3] = inverse
@@ -138,50 +138,29 @@
     lax.fori_loop(0, 16, step, 0, unroll=4)
 
 
-class Slabs:
-    def __init__(self, field, scaled, warmth, got_fwd, got_bwd):
-        self.field, self.scaled, self.warmth = field, scaled, warmth
+class Halo:
+    def __init__(self, got_fwd, got_bwd):
         self.got_fwd, self.got_bwd = got_fwd, got_bwd
         self.first = on_first_core()
         gx = lax.axis_index("gx")
         self.below, self.above = gx > 0, gx < lax.axis_size("gx") - 1
 
-    def own(self, f, x):
-        if f < 3:
-            return self.field[f, x]
-        return self.warmth[x] if f == 7 else self.scaled[f - 3, x]
-
-    def beside(self, f, x):
-        fwd, bwd = self.got_fwd, self.got_bwd
+    def layer(self, f, x):
         if x < 0:
-            at = UP_AT.get((f, x))
-            if at is None:
-                return None
-            value = jnp.where(self.first, fwd[at], bwd[at])
-            return jnp.where(self.below, value, 0.0)
-        at = DOWN_AT.get((f, x))
+            at, near, far, inside = UP_AT.get((f, x)), self.got_fwd, self.got_bwd, self.below
+        else:
+            at, near, far, inside = DOWN_AT.get((f, x)), self.got_bwd, self.got_fwd, self.above
         if at is None:
             return None
-        value = jnp.where(self.first, bwd[at], fwd[at])
-        return jnp.where(self.above, value, 0.0)
-
-    def halo(self, emit):
-        zero = jnp.zeros((16, 128), F32)
-        for number, x in enumerate(HALO_X):
-            values = [self.beside(f, x) for f in range(7)]
-            emit(number, x + LOW, [zero if v is None else v for v in values] + [zero])
-
-    def inner(self, emit):
-        def step(x, carry):
-            emit(x, x + LOW, [self.own(f, x) for f in range(8)])
-            return carry
-
-        lax.fori_loop(0, 16, step, 0, unroll=4)
+        return jnp.where(inside, jnp.where(self.first, near[at], far[at]), 0.0)
 
 
 def pack_corners(xf, xb, fwd, bwd):
-    slabs = Slabs(None, None, None, xf, xb)
-    slabs.halo(lambda number, at, v: y_tiles(v, slabs.first, fwd, bwd, number))
+    halo = Halo(xf, xb)
+    zero = jnp.zeros((16, 128), F32)
+    for number, x in enumerate(HALO_X):
+        v = [halo.layer(f, x) for f in range(7)]
+        y_tiles([zero if a is None else a for a in v] + [zero], halo.first, fwd, bwd, number)
 
 
 def y_halo(first, got, at, pair):
@@ -200,42 +179,67 @@
 X_PAIRS = (X_ALL + 1) // 2
 
 
-def pack_z(field, scaled, warmth, xf, xb, yf, yb, cf, cb, position, whole, packed, up, down):
-    del position
-    slabs = Slabs(field, scaled, warmth, xf, xb)
-    first = slabs.first
+def y_slabs(first, got, at, v):
     low_half = rows((8, 128)) < 4
     window = lanes((24, 128)) // 16
-
-    def emit(got, number, at, v):
-        acc = None
-        for pair in range(4):
-            lower, upper = y_halo(first, got, number, pair)
-            last = []
-            last.append(jnp.where(low_half, upper, lower))
-            if pair < 3:
-                last.append(roll(jnp.where(low_half, lower, upper), 4, 0))
-            else:
-                last.append(roll(upper, 3, 0))
-            for f, tile in zip((2 * pair, 2 * pair + 1), last):
-                slab = jnp.concatenate([v[f], tile], axis=0)
-                whole[f, at] = slab
-                moved = roll(slab, 16 * f + 8, 1)
-                acc = moved if acc is None else jnp.where(window == f, moved, acc)
-        packed[at] = acc
-
-    slabs.halo(functools.partial(emit, (cf, cb)))
-    slabs.inner(functools.partial(emit, (yf, yb)))
-    packed[X_ALL] = jnp.zeros((24, 128), F32)
+    slabs, acc = [], None
+    for pair in range(4):
+        lower, upper = y_halo(first, got, at, pair)
+        ends = [jnp.where(low_half, upper, lower)]
+        if pair < 3:
+            ends.append(roll(jnp.where(low_half, lower, upper), 4, 0))
+        else:
+            ends.append(roll(upper, 3, 0))
+        for f, tile in zip((2 * pair, 2 * pair + 1), ends):
+            slabs.append(jnp.concatenate([v[f], tile], axis=0))
+            moved = roll(slabs[f], 16 * f + 8, 1)
+            acc = moved if acc is None else jnp.where(window == f, moved, acc)
+    return slabs, acc
+
+
+def z_tiles(a, b):
     half = (lanes((24, 128)) // 8) % 2 == 0
-
-    def pair_up(k, carry):
-        a, b = packed[2 * k], packed[2 * k + 1]
-        up[k] = jnp.where(half, a, roll(b, 8, 1))
-        down[k] = jnp.where(half, roll(a, -8, 1), b)
+    return jnp.where(half, a, roll(b, 8, 1)), jnp.where(half, roll(a, -8, 1), b)
+
+
+def pack_inner(field, scaled, warmth, yf, yb, position, whole, packed, up, down):
+    del position
+    first = on_first_core()
+
+    def step(k, carry):
+        windows = []
+        for x in (2 * k, 2 * k + 1):
+            v = [field[f, x] for f in range(3)] + [scaled[f, x] for f in range(4)] + [warmth[x]]
+            slabs, acc = y_slabs(first, (yf, yb), x, v)
+            for f in range(8):
+                whole[f, x] = slabs[f]
+            packed[x] = acc
+            windows.append(acc)
+        up[k], down[k] = z_tiles(*windows)
         return carry
 
-    lax.fori_loop(0, X_PAIRS, pair_up, 0, unroll=True)
+    lax.fori_loop(0, 8, step, 0, unroll=2)
+
+
+def pack_outer(xf, xb, cf, cb, inner_up, inner_down, whole, packed, up, down):
+    halo = Halo(xf, xb)
+    zero = jnp.zeros((16, 128), F32)
+    windows = []
+    for number, x in enumerate(HALO_X):
+        v = [halo.layer(f, x) for f in range(7)]
+        slabs, acc = y_slabs(
+            halo.first, (cf, cb), number, [zero if a is None else a for a in v] + [zero]
+        )
+        for f in range(8):
+            whole[f, number] = slabs[f]
+        packed[number] = acc
+        windows.append(acc)
+    windows.append(jnp.zeros((24, 128), F32))
+    for pair in range(len(windows) // 2):
+        k = pair if pair < LOW // 2 else pair + 8
+        up[k], down[k] = z_tiles(windows[2 * pair], windows[2 * pair + 1])
+    up[LOW // 2 : LOW // 2 + 8] = inner_up[...]
+    down[LOW // 2 : LOW // 2 + 8] = inner_down[...]
 
 
 def twist(a, b, c, d):
@@ -255,46 +259,81 @@
     return [keep * e[f] + weight * h[f] - g * k[f] for f in range(3)]
 
 
-def bulk(whole, final, whole_sum, shifted, spare):
+def lane_curls(get, source, at):
     row = rows((24, 128))
-    buffers = (whole, spare, final, spare, final)
-
-    def curls_at(source, at, outer):
-        e = [source[f, at] for f in range(3)]
-        up_y = [roll(e[0], -1, 0), roll(e[2], -1, 0)]
-        if outer:
-            up_y = [jnp.where(row == 19, whole[7, at, pl.ds(16 + n, 1), :], up_y[n]) for n in range(2)]
-        up_z = roll(e[0], -1, 1), roll(e[1], -1, 1)
-        return e, curls(e, up_y, up_z, (source[1, at + 1], source[2, at + 1]))
-
-    for number, weight in enumerate(EM_WEIGHTS):
-        source, target, outer = buffers[number], buffers[number + 1], number == 0
-
-        def step(at, carry, source=source, target=target, outer=outer, weight=weight):
-            e, c = curls_at(source, at, outer)
-            h, g = [whole[3 + f, at] for f in range(3)], whole[6, at]
-            down_y = roll(c[0], 1, 0), roll(c[2], 1, 0)
-            down_z = roll(c[0], 1, 1), roll(c[1], 1, 1)
-            new = relaxed(weight, e, h, g, c, carry, down_y, down_z)
+    e = [get(source, f, at) for f in range(3)]
+    up_y = roll(e[0], -1, 0), roll(e[2], -1, 0)
+    if source == 0:
+        up_y = [jnp.where(row == 19, get(0, 7, at)[16 + n : 17 + n], up_y[n]) for n in range(2)]
+    up_z = roll(e[0], -1, 1), roll(e[1], -1, 1)
+    return e, curls(e, up_y, up_z, (get(source, 1, at + 1), get(source, 2, at + 1)))
+
+
+def lane_sweep(get, source, at, carry):
+    e, c = lane_curls(get, source, at)
+    h, g = [get(0, 3 + f, at) for f in range(3)], get(0, 6, at)
+    down_y = roll(c[0], 1, 0), roll(c[2], 1, 0)
+    down_z = roll(c[0], 1, 1), roll(c[1], 1, 1)
+    new = relaxed(EM_WEIGHTS[source], e, h, g, c, carry, down_y, down_z)
+    return new, (c[1], c[2])
+
+
+def bulk(whole, swept):
+    def get(number, f, x):
+        return whole[f, x] if number == 0 else swept[number - 1, f, x]
+
+    for number in range(EM_SWEEPS):
+
+        def step(x, carry, number=number):
+            new, carry = lane_sweep(get, number, x, carry)
             for f in range(3):
-                target[f, at] = new[f]
-            return c[1], c[2]
-
-        begin = 1 + number
-        _, c = curls_at(source, begin - 1, outer)
-        lax.fori_loop(begin, X_ALL - begin, step, (c[1], c[2]), unroll=4)
-
-    def step(x, carry):
-        at = x + LOW
-        ex, ey, ez = (final[f, at] * final[f, at] for f in range(3))
-        ey_x, ez_x = (final[f, at + 1] * final[f, at + 1] for f in (1, 2))
-        flat, upright = (ex + roll(ex, -1, 0)) + (ey + ey_x), ez + ez_x
+                swept[number, f, x] = new[f]
+            return carry
+
+        _, c = lane_curls(get, number, number)
+        lax.fori_loop(number + 1, 15 - number, step, (c[1], c[2]), unroll=4)
+
+
+def swept_low(number):
+    return range(number - LOW, number)
+
+
+def swept_high(number):
+    return range(16 - number, 21 - number)
+
+
+def rest_of_bulk(inner, outer, swept, final, whole_sum, shifted, others):
+    def target(number):
+        return final if number == EM_SWEEPS else others.at[number - 1]
+
+    def get(number, f, x):
+        if number == 0:
+            return inner[f, x] if 0 <= x < 16 else outer[f, HALO_X.index(x)]
+        if number <= x <= 15 - number:
+            return swept[number - 1, f, x]
+        low, high = swept_low(number), swept_high(number)
+        return target(number)[f, low.index(x) if x < number else len(low) + high.index(x)]
+
+    for number in range(EM_SWEEPS):
+        to = target(number + 1)
+        at = 0
+        for layers in (swept_low(number + 1), swept_high(number + 1)):
+            _, c = lane_curls(get, number, layers[0] - 1)
+            carry = c[1], c[2]
+            for x in layers:
+                new, carry = lane_sweep(get, number, x, carry)
+                for f in range(3):
+                    to[f, at] = new[f]
+                at += 1
+
+    for x in range(16):
+        ex, ey, ez = (get(EM_SWEEPS, f, x) for f in range(3))
+        ey_x, ez_x = (get(EM_SWEEPS, f, x + 1) for f in (1, 2))
+        ex, upright = ex * ex, ez * ez + ez_x * ez_x
+        flat = (ex + roll(ex, -1, 0)) + (ey * ey + ey_x * ey_x)
         upright = upright + roll(upright, -1, 0)
         whole_sum[x] = flat[0:16] + upright[0:16]
         shifted[x] = roll(flat[0:16], -1, 1)
-        return carry
-
-    lax.fori_loop(0, 16, step, 0, unroll=4)
 
 
 def of_layer(at):
@@ -302,7 +341,7 @@
 
 
 def edge(
-    packed, below_z, above_z, whole_sum, shifted, xf, xb, yf, yb, sigma, warmth, storage, position, nodes,
+    inner, outer, below_z, above_z, whole_sum, shifted, xf, xb, yf, yb, sigma, warmth, storage, position, nodes,
     final, send, partial, beside, stack, fields, spare, last, heat,
 ):
     first = on_first_core()
@@ -325,7 +364,8 @@
                 came = jnp.where(half, lower, roll(upper, 8, 1))
             beside[at] = came
             block, lane_at = of_layer(at)
-            own = packed[at]
+            x = at - LOW
+            own = inner[x] if 0 <= x < 16 else outer[HALO_X.index(x)]
             for face in range(2):
                 window = jnp.where(half, came, own) if face else jnp.where(half, own, came)
                 stack[block, face, lane_at : lane_at + 24, :] = roll(window, 4, 0)
@@ -419,7 +459,7 @@
         partial[x] = t + HEAT_WEIGHTS[0] * (total - 6.0 * t) / (6.0 + storage[x])
 
 
-def merge(final, near, out, stack):
+def merge(swept, final, near, out, stack):
     for block in range(BLOCKS):
         for f in range(3):
             stack[block, 32 * f : 32 * f + 8, :] = near[block, f, 24:32, :]
@@ -433,7 +473,12 @@
         block, lane_at = of_layer(x + LOW)
         windows = stack[block, lane_at + LOW : lane_at + LOW + 16, :]
         for f in range(3):
-            inner = final[f, x + LOW, 0:16, :]
+            if EM_SWEEPS <= x <= 15 - EM_SWEEPS:
+                inner = swept[EM_SWEEPS - 1, f, x, 0:16, :]
+            else:
+                low, high = swept_low(EM_SWEEPS), swept_high(EM_SWEEPS)
+                at = low.index(x) if x in low else len(low) + high.index(x)
+                inner = final[f, at, 0:16, :]
             out[f, x] = jnp.where(outer, roll(windows, -32 * f, 1), inner)
 
 
@@ -558,15 +603,15 @@
     cube = (16, 16, 128)
     face = (16, 128)
     x_message, y_message, corners = (X_LAYERS, 16, 128), (16, 32, 128), (len(HALO_X), 32, 128)
-    here = [pltpu.with_memory_space_constraint(v, pltpu.HBM) for v in (field, source, sigma, warmth)]
-    xf, xb, yf, yb, scaled = call(
+    here = (field, sigma, warmth, storage, source)
+    xf, xb, yf, yb, scaled, field, sigma, warmth, storage = call(
         pack_xy,
-        [x_message, x_message, y_message, y_message, (4, *cube)],
-        [(3, *cube), (3, *cube), cube, cube, pltpu.SemaphoreType.DMA((4,))],
+        [x_message, x_message, y_message, y_message, (4, *cube), (3, *cube), cube, cube, cube],
+        [(3, *cube), pltpu.SemaphoreType.DMA((5,))],
         name="pack_xy",
         near=True,
-        in_specs=[pl.BlockSpec(memory_space=pltpu.HBM)] * 4,
-    )(*here)
+        in_specs=[pl.BlockSpec(memory_space=pltpu.HBM)] * 5,
+    )(*(pltpu.with_memory_space_constraint(v, pltpu.HBM) for v in here))
     xf, xb = exchange("gx", xf, xb)
     yf, yb = exchange("gy", yf, yb)
     position, nodes = pl.pallas_call(
@@ -580,20 +625,35 @@
     )(partition.reshape(1, 256), column.reshape(1, 256))
     cf, cb = call(pack_corners, [corners, corners], name="pack_corners")(xf, xb)
     cf, cb = exchange("gy", cf, cb)
-    layer = (24, 128)
-    whole, packed, up, down = call(
-        pack_z,
-        [(8, X_ALL, *layer), (X_ALL + 1, *layer), (X_PAIRS, *layer), (X_PAIRS, *layer)],
-        name="pack_z",
-    )(field, scaled, warmth, xf, xb, yf, yb, cf, cb, position)
+    layer, halo = (24, 128), len(HALO_X)
+    inner, inner_packed, inner_up, inner_down = call(
+        pack_inner,
+        [(8, 16, *layer), (16, *layer), (8, *layer), (8, *layer)],
+        name="pack_inner",
+        near=True,
+    )(field, scaled, warmth, yf, yb, position)
+    (swept,) = call(
+        bulk,
+        [(EM_SWEEPS, 3, 16, *layer)],
+        name="bulk",
+        near=True,
+        cost_estimate=pl.CostEstimate(flops=10**9, bytes_accessed=10**7, transcendentals=0),
+    )(inner)
+    outer, outer_packed, up, down = call(
+        pack_outer,
+        [(8, halo, *layer), (halo, *layer), (X_PAIRS, *layer), (X_PAIRS, *layer)],
+        name="pack_outer",
+        near=True,
+    )(xf, xb, cf, cb, inner_up, inner_down)
     below_z, above_z = exchange_z(up, down)
     final, whole_sum, shifted = call(
-        bulk,
-        [(3, X_ALL, *layer), cube, cube],
-        [(3, X_ALL, *layer)],
-        name="bulk",
+        rest_of_bulk,
+        [(3, halo, *layer), cube, cube],
+        [(EM_SWEEPS - 1, 3, halo, *layer)],
+        name="rest_of_bulk",
+        near=True,
         cost_estimate=pl.CostEstimate(flops=10**9, bytes_accessed=10**7, transcendentals=0),
-    )(whole)
+    )(inner, outer, swept)
     near, send, partial = call(
         edge,
         [(BLOCKS, 3, 32, 128), (count, 128), cube],
@@ -607,8 +667,8 @@
         ],
         name="edge",
     )(
-        packed, below_z, above_z, whole_sum, shifted, xf, xb, yf, yb, sigma, warmth, storage,
-        position, nodes,
+        inner_packed, outer_packed, below_z, above_z, whole_sum, shifted, xf, xb, yf, yb, sigma,
+        warmth, storage, position, nodes,
     )
     got = lax.all_to_all(
         send.reshape(count, 1, 128), ("gy", "gz"), split_axis=0, concat_axis=0, tiled=True
@@ -628,7 +688,7 @@
         [(BLOCKS, 128, 128)],
         name="merge",
         cost_estimate=pl.CostEstimate(flops=10**9, bytes_accessed=10**6, transcendentals=0),
-    )(final, near)
+    )(swept, final, near)
     return out, updated
 
 

time: 66.2 us -> 63.1 us (0.953)
  local copies, waits for them, and re-layouts: 3.27 us -> 1.36 us
  waiting for transfers between devices: 7.35 us -> 6.54 us
    unnamed x14 -> x4, local copies, waits for them, and re-layouts: 3.27 us -> 1.36 us
    ppermute x5, waiting for transfers between devices: 3.89 us -> 2.85 us  [exchange(): lax.ppermute(fwd, names, forward)]
    pallas_call x3 -> x5, Pallas kernels: 7.44 us -> 7.3 us  [the longest x1 2.64 us: local(): call(bulk, [(EM_SWEEPS, 3, 16, *layer)], name='bulk', near=True, cost_est...]
  transfers between devices with their start and end apart: 14 -> 14, of which waited for: 5 -> 6; matrix products, arithmetic and copies ran while one was open for 0% -> 0% of each run, Pallas kernels for 10% -> 11%
where the time goes in v6:
time: 63.1 us; the launch traced here: 62.9 us
  blocking collectives  24 us (38%)
  starting transfers between devices  17.6 us (28%)
  Pallas kernels  12.6 us (20%)
  waiting for transfers between devices  6.54 us (10%)
  local copies, waits for them, and re-layouts  1.36 us (2%)
  between operations  0.75 us (1%)
    all_to_all x1, blocking collectives, local(): lax.all_to_all(send.reshape(count, 1, 128), ('gy', 'gz'), split_axis=0, c...  24 us
    ppermute x5, starting transfers between devices, exchange(): lax.ppermute(bwd, names, backward)  8.78 us
    ppermute x2, starting transfers between devices, exchange_z(): lax.ppermute(up, 'gz', ring)  8.11 us
    ppermute x5, waiting for transfers between devices, exchange(): lax.ppermute(fwd, names, forward)  2.85 us
    pallas_call x1, Pallas kernels, local(): call(bulk, [(EM_SWEEPS, 3, 16, *layer)], name='bulk', near=True, cost_est...  2.64 us
    ppermute x2, waiting for transfers between devices, exchange_z(): lax.ppermute(down, 'gz', [(j, i) for i, j in ring])  2.51 us
    pallas_call x1, Pallas kernels, local(): call(edge, [(BLOCKS, 3, 32, 128), (count, 128), cube], [(X_ALL, *layer),...  2 us
    pallas_call x1, Pallas kernels, local(): call(rest_of_bulk, [(3, halo, *layer), cube, cube], [(EM_SWEEPS - 1, 3, h...  1.82 us
  transfers between devices with their start and end apart: 14, of which 6 were waited for; matrix products, arithmetic and copies ran while one was open for 0% of the time, Pallas kernels for 11%

profile of v6, /device:TPU:133, one launch (start us, length us, event | category | flops | bytes accessed | tf_op | source)
XLA Modules:
  0.0 62.9 jit_solution(10629531331869285)
XLA Ops:
  0.6 1.5 %pack_xy.1 = (f32[30,16,128]{2,1,0:T(8,128)S(1)}, f32[30,16,128]{2,1,0:T(8,128)S(1)}, f32[16,32,128]{2,1,0:T(8,128)S(1)}, f32[16,32,128]{2,1,0:T(8,128)S(1)}, f3...) custom-call(f32[3,16,16,128]{3,2,1,0:T(8,128)} %refs_0_.1, ...), custom_call_target="tpu_custom_call" | custom-call | tf_op jit(solution)/shard_map/pack_xy/pallas_call | solution.py:607
  2.1 0.0 collective-permute-start.2
  2.1 2.1 %collective-permute-start.3 = (f32[30,16,128]{2,1,0:T(8,128)S(1)}, f32[30,16,128]{2,1,0:T(8,128)S(1)}, u32[]{:S(2)}, u32[]{:S(2)}) collective-permute-start(f32[30,16,128]{2,1,0:T(8,128)S(1)} %get-tuple-element.44), channel_id=1, source_target_pairs={{64,0},{0,1},{66,2},{2,3},{68,4},{4,5},{70,6},{6,7},{72,8},{8,9},{... | collective-permute-start | bytes 737288 | tf_op jit(solution)/shard_map/ppermute | solution.py:591
  4.2 0.3 collective-permute-start
  4.5 1.2 %collective-permute-start.1 = (f32[16,32,128]{2,1,0:T(8,128)S(1)}, f32[16,32,128]{2,1,0:T(8,128)S(1)}, u32[]{:S(2)}, u32[]{:S(2)}) collective-permute-start(f32[16,32,128]{2,1,0:T(8,128)S(1)} %get-tuple-element.40), channel_id=1, source_target_pairs={{16,0},{0,1},{18,2},{2,3},{20,4},{4,5},{22,6},{6,7},{24,8},{8,9},{... | collective-permute-start | bytes 786440 | tf_op jit(solution)/shard_map/ppermute | solution.py:591
  5.7 2.4 %collective-permute-done.2.xf = f32[30,16,128]{2,1,0:T(8,128)S(1)} collective-permute-done((f32[30,16,128]{2,1,0:T(8,128)S(1)}, f32[30,16,128]{2,1,0:T(8,128)S(1)}, u32[]{:S(2)}, u32[]{:S(2)}) %collective-permute-start.2) | collective-permute-done | bytes 245792 | tf_op jit(solution)/shard_map/ppermute | solution.py:591
  8.1 0.9 %collective-permute-done.3.xb = f32[30,16,128]{2,1,0:T(8,128)S(1)} collective-permute-done((f32[30,16,128]{2,1,0:T(8,128)S(1)}, f32[30,16,128]{2,1,0:T(8,128)S(1)}, u32[]{:S(2)}, u32[]{:S(2)}) %collective-permute-start.3) | collective-permute-done | bytes 245792 | tf_op jit(solution)/shard_map/ppermute | solution.py:591
  9.0 0.1 pack_corners.1
  9.1 0.3 collective-permute-start.4
  9.3 1.2 %collective-permute-start.5 = (f32[9,32,128]{2,1,0:T(8,128)S(1)}, f32[9,32,128]{2,1,0:T(8,128)S(1)}, u32[]{:S(2)}, u32[]{:S(2)}) collective-permute-start(f32[9,32,128]{2,1,0:T(8,128)S(1)} %get-tuple-element.46), channel_id=1, source_target_pairs={{16,0},{0,1},{18,2},{2,3},{20,4},{4,5},{22,6},{6,7},{24,8},{8,9},{... | collective-permute-start | bytes 442376 | tf_op jit(solution)/shard_map/ppermute | solution.py:591
  10.6 0.0 copy-start
  10.6 0.7 %copy-done = s32[1,1,1,256,1]{3,4,2,1,0:T(1,128)S(1)} copy-done((s32[1,1,1,256,1]{3,4,2,1,0:T(1,128)S(1)}, s32[1,1,1,256,1]{3,4,2,1,0:T(1,128)}, u32[]{:S(2)}) %copy-start) | copy-done | bytes 1048
  11.2 0.0 copy-start.1
  11.2 0.7 %copy-done.1 = s32[1,1,1,256]{3,2,1,0:T(1,128)S(1)} copy-done((s32[1,1,1,256]{3,2,1,0:T(1,128)S(1)}, s32[1,1,1,256]{3,2,1,0:T(1,128)}, u32[]{:S(2)}) %copy-start.1) | copy-done | bytes 1048
  11.9 0.4 place.1
  12.3 0.0 collective-permute-done.yf
  12.3 0.0 collective-permute-done.1.yb
  12.4 1.0 %pack_inner.1 = (f32[8,16,24,128]{3,2,1,0:T(8,128)S(1)}, f32[16,24,128]{2,1,0:T(8,128)S(1)}, f32[8,24,128]{2,1,0:T(8,128)S(1)}, f32[8,24,128]{2,1,0:T(8,128)S(1)}) custom-call(f32[3,16,16,128]{3,2,1,0:T(8,128)S(1)} %get-tuple-element.36.field, f32[4,16,16,128]{3,2,1,0:T(8,128)S(1)} %get-tuple-element.37.scaled, f32[16,16,128]{2,1,0:T(8,128)S(1)} %get-tuple-element.38.warmth, ...), custom_call_target="tpu_custom_call" | custom-call | tf_op jit(solution)/shard_map/pack_inner/pallas_call | solution.py:629
  13.4 0.5 collective-permute-done.4.cf
  13.9 0.3 collective-permute-done.5.cb
  14.1 0.4 pack_outer.1
  14.5 6.4 %collective-permute-start.6 = (f32[13,24,128]{2,1,0:T(8,128)S(1)}, f32[13,24,128]{2,1,0:T(8,128)S(1)}, u32[]{:S(2)}, u32[]{:S(2)}) collective-permute-start(f32[13,24,128]{2,1,0:T(8,128)S(1)} %get-tuple-element.53), channel_id=1, source_target_pairs={{0,1},{1,2},{2,3},{3,4},{4,5},{5,6},{6,7},{7,8},{8,9},{9,10},{10,1... | collective-permute-start | bytes 479240 | tf_op jit(solution)/shard_map/ppermute | solution.py:597
  20.9 0.0 collective-permute-start.7
  20.9 2.6 %bulk.1.swept = f32[4,3,16,24,128]{4,3,2,1,0:T(8,128)S(1)} custom-call(f32[8,16,24,128]{3,2,1,0:T(8,128)S(1)} %get-tuple-element.42.whole.inner), custom_call_target="tpu_custom_call" | custom-call | flops 1000000000 | bytes 10000000 | tf_op jit(solution)/shard_map/bulk/pallas_call | solution.py:635
  23.6 1.8 %rest_of_bulk.1 = (f32[3,9,24,128]{3,2,1,0:T(8,128)S(1)}, f32[16,16,128]{2,1,0:T(8,128)S(1)}, f32[16,16,128]{2,1,0:T(8,128)S(1)}) custom-call(f32[8,16,24,128]{3,2,1,0:T(8,128)S(1)} %get-tuple-element.42.whole.inner, f32[8,9,24,128]{3,2,1,0:T(8,128)S(1)} %get-tuple-element.49.outer, f32[4,3,16,24,128]{4,3,2,1,0:T(8,128)S(1)} %bulk.1.swept), custom_call_target="tpu_custom_call" | custom-call | flops 1000000000 | bytes 10000000 | tf_op jit(solution)/shard_map/rest_of_bulk/pallas_call | solution.py:649
  25.4 0.0 collective-permute-done.6.below_z
  25.4 0.2 collective-permute-done.7.above_z
  25.6 2.0 %edge.1 = (f32[5,3,32,128]{3,2,1,0:T(8,128)S(1)}, f32[576,128]{1,0:T(8,128)S(1)}, f32[16,16,128]{2,1,0:T(8,128)S(1)}) custom-call(f32[16,24,128]{2,1,0:T(8,128)S(1)} %get-tuple-element.51.inner, f32[9,24,128]{2,1,0:T(8,128)S(1)} %get-tuple-element.52.outer, f32[13,24,128]{2,1,0:T(8,128)S(1)} %collective-permute-done.6.below_z, ...), custom_call_target="tpu_custom_call" | custom-call | tf_op jit(solution)/shard_map/edge/pallas_call | solution.py:657
  27.6 24.0 %all_to_all.5 = f32[576,1,128]{2,1,0:T(1,128)S(1)} all-to-all(f32[576,1,128]{2,1,0:T(1,128)S(1)} %bitcast.7), channel_id=1, replica_groups=mesh['gx'=8,'gy'=4,'gz'=16] {'gy','gz'}, dimensions={0} | all-to-all | bytes 589824 | tf_op jit(solution)/shard_map/all_to_all | solution.py:673
  51.6 1.0 %warm.1 = (f32[16,128]{1,0:T(8,128)S(1)}, f32[16,128]{1,0:T(8,128)S(1)}, f32[16,128]{1,0:T(8,128)S(1)}, f32[16,128]{1,0:T(8,128)S(1)}, f32[16,128]{1,0:T(8,128)S...) custom-call(f32[576,128]{1,0:T(8,128)S(1)} %bitcast.6, f32[16,16,128]{2,1,0:T(8,128)S(1)} %get-tuple-element.62.partial, ...), custom_call_target="tpu_custom_call" | custom-call | tf_op jit(solution)/shard_map/warm/pallas_call | solution.py:676
  52.6 0.0 collective-permute-start.8
  52.6 3.0 %collective-permute-start.9 = (f32[16,128]{1,0:T(8,128)S(1)}, f32[16,128]{1,0:T(8,128)S(1)}, u32[]{:S(2)}, u32[]{:S(2)}) collective-permute-start(f32[16,128]{1,0:T(8,128)S(1)} %get-tuple-element.65), channel_id=1, source_target_pairs={{64,0},{0,1},{66,2},{2,3},{68,4},{4,5},{70,6},{6,7},{72,8},{8,9},{... | collective-permute-start | bytes 24584 | tf_op jit(solution)/shard_map/ppermute | solution.py:591
  55.6 0.2 collective-permute-start.10
  55.8 1.3 %collective-permute-start.11 = (f32[16,128]{1,0:T(8,128)S(1)}, f32[16,128]{1,0:T(8,128)S(1)}, u32[]{:S(2)}, u32[]{:S(2)}) collective-permute-start(f32[16,128]{1,0:T(8,128)S(1)} %get-tuple-element.67), channel_id=1, source_target_pairs={{16,0},{0,1},{18,2},{2,3},{20,4},{4,5},{22,6},{6,7},{24,8},{8,9},{... | collective-permute-start | bytes 24584 | tf_op jit(solution)/shard_map/ppermute | solution.py:591
  57.0 1.7 %collective-permute-start.12 = (f32[16,128]{1,0:T(8,128)S(1)}, f32[16,128]{1,0:T(8,128)S(1)}, u32[]{:S(2)}, u32[]{:S(2)}) collective-permute-start(f32[16,128]{1,0:T(8,128)S(1)} %get-tuple-element.68), channel_id=1, source_target_pairs={{0,1},{1,2},{2,3},{3,4},{4,5},{5,6},{6,7},{7,8},{8,9},{9,10},{10,1... | collective-permute-start | bytes 24584 | tf_op jit(solution)/shard_map/ppermute | solution.py:597
  58.7 0.0 collective-permute-done.8.xf
  58.7 0.0 collective-permute-start.13
  58.7 1.1 %merge.1 = f32[3,16,16,128]{3,2,1,0:T(8,128)} custom-call(f32[4,3,16,24,128]{4,3,2,1,0:T(8,128)S(1)} %bulk.1.swept, f32[3,9,24,128]{3,2,1,0:T(8,128)S(1)} %get-tuple-element.50.final, f32[5,3,32,128]{3,2,1,0:T(8,128)S(1)} %get-tuple-element.60.near), custom_call_target="tpu_custom_call" | custom-call | flops 1000000000 | bytes 1000000 | tf_op jit(solution)/shard_map/merge/pallas_call | solution.py:685
  59.8 0.0 collective-permute-done.9.xb
  59.8 0.0 collective-permute-done.10.yf
  59.8 0.0 collective-permute-done.11.yb
  59.8 0.0 collective-permute-done.12.from_below
  59.8 2.3 %collective-permute-done.13.from_above = f32[16,128]{1,0:T(8,128)S(1)} collective-permute-done((f32[16,128]{1,0:T(8,128)S(1)}, f32[16,128]{1,0:T(8,128)S(1)}, u32[]{:S(2)}, u32[]{:S(2)}) %collective-permute-start.13) | collective-permute-done | bytes 8224 | tf_op jit(solution)/shard_map/ppermute | solution.py:597
  62.1 0.8 %finish.1 = f32[16,16,128]{2,1,0:T(8,128)} custom-call(f32[16,16,128]{2,1,0:T(8,128)S(1)} %get-tuple-element.63.rest, f32[16,16,128]{2,1,0:T(8,128)S(1)} %get-tuple-element.58.storage, f32[16,128]{1,0:T(8,128)S(1)} %collective-permute-done.8.xf, f32[16,128]{1,0:T(8,128)S(1)} %collective-permute-done.9.xb, f32[16,128]{1,0:T(8,128)S(1)} %collective-permute-done.10.yf, ...), custom_call_target="tpu_custom_call" | custom-call | tf_op jit(solution)/shard_map/finish/pallas_call | solution.py:682
Async XLA Ops:
  2.1 6.0 %collective-permute-start.2 = (f32[30,16,128]{2,1,0:T(8,128)S(1)}, f32[30,16,128]{2,1,0:T(8,128)S(1)}, u32[]{:S(2)}, u32[]{:S(2)}) collective-permute-start(f32[30,16,128]{2,1,0:T(8,128)S(1)} %get-tuple-element.43), channel_id=1, source_target_pairs={{0,64},{1,0},{2,66},{3,2},{4,68},{5,4},{6,70},{7,6},{8,72},{9,8},{... | collective-permute-start | bytes 737288 | tf_op jit(solution)/shard_map/ppermute | solution.py:591
  2.1 6.9 %collective-permute-start.3 = (f32[30,16,128]{2,1,0:T(8,128)S(1)}, f32[30,16,128]{2,1,0:T(8,128)S(1)}, u32[]{:S(2)}, u32[]{:S(2)}) collective-permute-start(f32[30,16,128]{2,1,0:T(8,128)S(1)} %get-tuple-element.44), channel_id=1, source_target_pairs={{64,0},{0,1},{66,2},{2,3},{68,4},{4,5},{70,6},{6,7},{72,8},{8,9},{... | collective-permute-start | bytes 737288 | tf_op jit(solution)/shard_map/ppermute | solution.py:591
  4.2 8.1 %collective-permute-start = (f32[16,32,128]{2,1,0:T(8,128)S(1)}, f32[16,32,128]{2,1,0:T(8,128)S(1)}, u32[]{:S(2)}, u32[]{:S(2)}) collective-permute-start(f32[16,32,128]{2,1,0:T(8,128)S(1)} %get-tuple-element.39), channel_id=1, source_target_pairs={{0,16},{1,0},{2,18},{3,2},{4,20},{5,4},{6,22},{7,6},{8,24},{9,8},{... | collective-permute-start | bytes 786440 | tf_op jit(solution)/shard_map/ppermute | solution.py:591
  4.5 7.9 %collective-permute-start.1 = (f32[16,32,128]{2,1,0:T(8,128)S(1)}, f32[16,32,128]{2,1,0:T(8,128)S(1)}, u32[]{:S(2)}, u32[]{:S(2)}) collective-permute-start(f32[16,32,128]{2,1,0:T(8,128)S(1)} %get-tuple-element.40), channel_id=1, source_target_pairs={{16,0},{0,1},{18,2},{2,3},{20,4},{4,5},{22,6},{6,7},{24,8},{8,9},{... | collective-permute-start | bytes 786440 | tf_op jit(solution)/shard_map/ppermute | solution.py:591
  9.1 4.8 %collective-permute-start.4 = (f32[9,32,128]{2,1,0:T(8,128)S(1)}, f32[9,32,128]{2,1,0:T(8,128)S(1)}, u32[]{:S(2)}, u32[]{:S(2)}) collective-permute-start(f32[9,32,128]{2,1,0:T(8,128)S(1)} %get-tuple-element.45), channel_id=1, source_target_pairs={{0,16},{1,0},{2,18},{3,2},{4,20},{5,4},{6,22},{7,6},{8,24},{9,8},{... | collective-permute-start | bytes 442376 | tf_op jit(solution)/shard_map/ppermute | solution.py:591
  9.3 4.8 %collective-permute-start.5 = (f32[9,32,128]{2,1,0:T(8,128)S(1)}, f32[9,32,128]{2,1,0:T(8,128)S(1)}, u32[]{:S(2)}, u32[]{:S(2)}) collective-permute-start(f32[9,32,128]{2,1,0:T(8,128)S(1)} %get-tuple-element.46), channel_id=1, source_target_pairs={{16,0},{0,1},{18,2},{2,3},{20,4},{4,5},{22,6},{6,7},{24,8},{8,9},{... | collective-permute-start | bytes 442376 | tf_op jit(solution)/shard_map/ppermute | solution.py:591
  10.6 0.7 %copy-start = (s32[1,1,1,256,1]{3,4,2,1,0:T(1,128)S(1)}, s32[1,1,1,256,1]{3,4,2,1,0:T(1,128)}, u32[]{:S(2)}) copy-start(s32[1,1,1,256,1]{3,4,2,1,0:T(1,128)} %param.12) | copy-start | bytes 3076
  11.2 0.7 %copy-start.1 = (s32[1,1,1,256]{3,2,1,0:T(1,128)S(1)}, s32[1,1,1,256]{3,2,1,0:T(1,128)}, u32[]{:S(2)}) copy-start(s32[1,1,1,256]{3,2,1,0:T(1,128)} %param.13) | copy-start | bytes 3076
  14.5 10.9 %collective-permute-start.6 = (f32[13,24,128]{2,1,0:T(8,128)S(1)}, f32[13,24,128]{2,1,0:T(8,128)S(1)}, u32[]{:S(2)}, u32[]{:S(2)}) collective-permute-start(f32[13,24,128]{2,1,0:T(8,128)S(1)} %get-tuple-element.53), channel_id=1, source_target_pairs={{0,1},{1,2},{2,3},{3,4},{4,5},{5,6},{6,7},{7,8},{8,9},{9,10},{10,1... | collective-permute-start | bytes 479240 | tf_op jit(solution)/shard_map/ppermute | solution.py:597
  20.9 4.7 %collective-permute-start.7 = (f32[13,24,128]{2,1,0:T(8,128)S(1)}, f32[13,24,128]{2,1,0:T(8,128)S(1)}, u32[]{:S(2)}, u32[]{:S(2)}) collective-permute-start(f32[13,24,128]{2,1,0:T(8,128)S(1)} %get-tuple-element.54), channel_id=1, source_target_pairs={{1,0},{2,1},{3,2},{4,3},{5,4},{6,5},{7,6},{8,7},{9,8},{10,9},{11,1... | collective-permute-start | bytes 479240 | tf_op jit(solution)/shard_map/ppermute | solution.py:597
  52.6 6.1 %collective-permute-start.8 = (f32[16,128]{1,0:T(8,128)S(1)}, f32[16,128]{1,0:T(8,128)S(1)}, u32[]{:S(2)}, u32[]{:S(2)}) collective-permute-start(f32[16,128]{1,0:T(8,128)S(1)} %get-tuple-element.64), channel_id=1, source_target_pairs={{0,64},{1,0},{2,66},{3,2},{4,68},{5,4},{6,70},{7,6},{8,72},{9,8},{... | collective-permute-start | bytes 24584 | tf_op jit(solution)/shard_map/ppermute | solution.py:591
  52.6 7.2 %collective-permute-start.9 = (f32[16,128]{1,0:T(8,128)S(1)}, f32[16,128]{1,0:T(8,128)S(1)}, u32[]{:S(2)}, u32[]{:S(2)}) collective-permute-start(f32[16,128]{1,0:T(8,128)S(1)} %get-tuple-element.65), channel_id=1, source_target_pairs={{64,0},{0,1},{66,2},{2,3},{68,4},{4,5},{70,6},{6,7},{72,8},{8,9},{... | collective-permute-start | bytes 24584 | tf_op jit(solution)/shard_map/ppermute | solution.py:591
  55.6 4.2 %collective-permute-start.10 = (f32[16,128]{1,0:T(8,128)S(1)}, f32[16,128]{1,0:T(8,128)S(1)}, u32[]{:S(2)}, u32[]{:S(2)}) collective-permute-start(f32[16,128]{1,0:T(8,128)S(1)} %get-tuple-element.66), channel_id=1, source_target_pairs={{0,16},{1,0},{2,18},{3,2},{4,20},{5,4},{6,22},{7,6},{8,24},{9,8},{... | collective-permute-start | bytes 24584 | tf_op jit(solution)/shard_map/ppermute | solution.py:591
  55.8 4.0 %collective-permute-start.11 = (f32[16,128]{1,0:T(8,128)S(1)}, f32[16,128]{1,0:T(8,128)S(1)}, u32[]{:S(2)}, u32[]{:S(2)}) collective-permute-start(f32[16,128]{1,0:T(8,128)S(1)} %get-tuple-element.67), channel_id=1, source_target_pairs={{16,0},{0,1},{18,2},{2,3},{20,4},{4,5},{22,6},{6,7},{24,8},{8,9},{... | collective-permute-start | bytes 24584 | tf_op jit(solution)/shard_map/ppermute | solution.py:591
  57.0 2.8 %collective-permute-start.12 = (f32[16,128]{1,0:T(8,128)S(1)}, f32[16,128]{1,0:T(8,128)S(1)}, u32[]{:S(2)}, u32[]{:S(2)}) collective-permute-start(f32[16,128]{1,0:T(8,128)S(1)} %get-tuple-element.68), channel_id=1, source_target_pairs={{0,1},{1,2},{2,3},{3,4},{4,5},{5,6},{6,7},{7,8},{8,9},{9,10},{10,1... | collective-permute-start | bytes 24584 | tf_op jit(solution)/shard_map/ppermute | solution.py:597
  58.7 3.4 %collective-permute-start.13 = (f32[16,128]{1,0:T(8,128)S(1)}, f32[16,128]{1,0:T(8,128)S(1)}, u32[]{:S(2)}, u32[]{:S(2)}) collective-permute-start(f32[16,128]{1,0:T(8,128)S(1)} %get-tuple-element.69), channel_id=1, source_target_pairs={{1,0},{2,1},{3,2},{4,3},{5,4},{6,5},{7,6},{8,7},{9,8},{10,9},{11,1... | collective-permute-start | bytes 24584 | tf_op jit(solution)/shard_map/ppermute | solution.py:597

commit v7 on v6

--- a/solution.py
+++ b/solution.py
@@ -155,7 +155,8 @@
         return jnp.where(inside, jnp.where(self.first, near[at], far[at]), 0.0)
 
 
-def pack_corners(xf, xb, fwd, bwd):
+def pack_corners(xf, xb, position, fwd, bwd):
+    del position
     halo = Halo(xf, xb)
     zero = jnp.zeros((16, 128), F32)
     for number, x in enumerate(HALO_X):
@@ -202,8 +203,7 @@
     return jnp.where(half, a, roll(b, 8, 1)), jnp.where(half, roll(a, -8, 1), b)
 
 
-def pack_inner(field, scaled, warmth, yf, yb, position, whole, packed, up, down):
-    del position
+def pack_inner(field, scaled, warmth, yf, yb, whole, packed, up, down):
     first = on_first_core()
 
     def step(k, carry):
@@ -221,7 +221,8 @@
     lax.fori_loop(0, 8, step, 0, unroll=2)
 
 
-def pack_outer(xf, xb, cf, cb, inner_up, inner_down, whole, packed, up, down):
+def pack_outer(xf, xb, cf, cb, inner_up, inner_down, swept, whole, packed, up, down):
+    del swept
     halo = Halo(xf, xb)
     zero = jnp.zeros((16, 128), F32)
     windows = []
@@ -302,7 +303,9 @@
     return range(16 - number, 21 - number)
 
 
-def rest_of_bulk(inner, outer, swept, final, whole_sum, shifted, others):
+def rest_of_bulk(
+    inner, outer, swept, xf, xb, yf, yb, warmth, storage, final, whole_sum, shifted, began, others
+):
     def target(number):
         return final if number == EM_SWEEPS else others.at[number - 1]
 
@@ -335,17 +338,33 @@
         whole_sum[x] = flat[0:16] + upright[0:16]
         shifted[x] = roll(flat[0:16], -1, 1)
 
+    first, gx = on_first_core(), lax.axis_index("gx")
+    row, lane = rows((16, 128)), lanes((16, 128))
+    low_at, high_at = UP_AT[7, -1], DOWN_AT[7, 16]
+    under = jnp.where(gx > 0, jnp.where(first, xf[low_at], xb[low_at]), 0.0)
+    over = jnp.where(
+        gx < lax.axis_size("gx") - 1, jnp.where(first, xb[high_at], xf[high_at]), 0.0
+    )
+    for x in range(16):
+        t = warmth[x]
+        lower, upper = y_halo(first, (yf, yb), x, 3)
+        total = (warmth[x - 1] if x else under) + (warmth[x + 1] if x < 15 else over)
+        total = total + jnp.where(row == 0, lower[3:4], roll(t, 1, 0))
+        total = total + jnp.where(row == 15, upper[4:5], roll(t, -1, 0))
+        total = total + jnp.where(lane == 0, 0.0, roll(t, 1, 1))
+        total = total + jnp.where(lane == 127, 0.0, roll(t, -1, 1))
+        began[x] = t + HEAT_WEIGHTS[0] * (total - 6.0 * t) / (6.0 + storage[x])
+
 
 def of_layer(at):
     return at % BLOCKS, Y_LANES * (at // BLOCKS)
 
 
 def edge(
-    inner, outer, below_z, above_z, whole_sum, shifted, xf, xb, yf, yb, sigma, warmth, storage, position, nodes,
+    inner, outer, below_z, above_z, whole_sum, shifted, sigma, began, storage, position, nodes,
     final, send, partial, beside, stack, fields, spare, last, heat,
 ):
-    first = on_first_core()
-    gx, gz = lax.axis_index("gx"), lax.axis_index("gz")
+    gz = lax.axis_index("gz")
     half = (lanes((24, 128)) // 8) % 2 == 0
     has_below, has_above = gz > 0, gz < lax.axis_size("gz") - 1
     nothing = jnp.zeros((1, 128), F32)
@@ -441,22 +460,10 @@
         total = total + jnp.dot(spread, piece, preferred_element_type=F32)
     send[...] = total
 
-    row = rows((16, 128))
-    low_at, high_at = UP_AT[7, -1], DOWN_AT[7, 16]
-    under = jnp.where(gx > 0, jnp.where(first, xf[low_at], xb[low_at]), 0.0)
-    over = jnp.where(
-        gx < lax.axis_size("gx") - 1, jnp.where(first, xb[high_at], xf[high_at]), 0.0
-    )
     for x in range(16):
-        t = warmth[x]
-        ends = roll(beside[x + LOW, 0:16, :], 8, 1)
-        lower, upper = y_halo(first, (yf, yb), x, 3)
-        total = (warmth[x - 1] if x else under) + (warmth[x + 1] if x < 15 else over)
-        total = total + jnp.where(row == 0, lower[3:4], roll(t, 1, 0))
-        total = total + jnp.where(row == 15, upper[4:5], roll(t, -1, 0))
-        total = total + roll(jnp.where(lane == 127, ends, t), 1, 1)
-        total = total + roll(jnp.where(lane == 0, ends, t), -1, 1)
-        partial[x] = t + HEAT_WEIGHTS[0] * (total - 6.0 * t) / (6.0 + storage[x])
+        ends = beside[x + LOW, 0:16, :]
+        halo = jnp.where(lane == 0, roll(ends, 9, 1), jnp.where(lane == 127, roll(ends, 7, 1), 0.0))
+        partial[x] = began[x] + HEAT_WEIGHTS[0] * halo / (6.0 + storage[x])
 
 
 def merge(swept, final, near, out, stack):
@@ -501,18 +508,20 @@
 def warm(got, partial, warmth, storage, xf, xb, yf, yb, up, down, rest, heat, mid):
     first = on_first_core()
     groups = got.shape[0] // (CAP + 1)
-    ids = got[pl.ds(CAP, groups, stride=CAP + 1), :]
-    lane = lanes((groups, 256))
+    ids = got[pl.ds(CAP, groups, stride=CAP + 1), :].T
+    node = rows((256, 1)) + 1
+    per = max(1, 128 // groups)
     total = None
-    for r in range(CAP):
-        hit = (ids[:, r : r + 1] == (lane + 1).astype(F32)).astype(jnp.bfloat16)
-        left = got[pl.ds(r, groups, stride=CAP + 1), :]
+    for r in range(0, CAP, per):
+        number = jnp.concatenate([ids[r + n : r + n + 1, :] for n in range(per)], axis=1)
+        hit = (number == node.astype(F32)).astype(jnp.bfloat16)
+        left = jnp.concatenate(
+            [got[pl.ds(r + n, groups, stride=CAP + 1), :] for n in range(per)], axis=0
+        )
         for _ in range(3):
             piece = left.astype(jnp.bfloat16)
             left = left - piece.astype(F32)
-            term = lax.dot_general(
-                hit, piece, (((0,), (0,)), ((), ())), preferred_element_type=F32
-            )
+            term = jnp.dot(hit, piece, preferred_element_type=F32)
             total = term if total is None else total + term
     heat[...] = total.reshape(16, 16, 128)
     lane = lanes((16, 128))
@@ -623,7 +632,9 @@
         compiler_params=pltpu.CompilerParams(vmem_limit_bytes=8 << 20),
         name="place",
     )(partition.reshape(1, 256), column.reshape(1, 256))
-    cf, cb = call(pack_corners, [corners, corners], name="pack_corners")(xf, xb)
+    cf, cb = call(pack_corners, [corners, corners], name="pack_corners")(
+        xf, xb, position
+    )
     cf, cb = exchange("gy", cf, cb)
     layer, halo = (24, 128), len(HALO_X)
     inner, inner_packed, inner_up, inner_down = call(
@@ -631,7 +642,7 @@
         [(8, 16, *layer), (16, *layer), (8, *layer), (8, *layer)],
         name="pack_inner",
         near=True,
-    )(field, scaled, warmth, yf, yb, position)
+    )(field, scaled, warmth, yf, yb)
     (swept,) = call(
         bulk,
         [(EM_SWEEPS, 3, 16, *layer)],
@@ -644,16 +655,16 @@
         [(8, halo, *layer), (halo, *layer), (X_PAIRS, *layer), (X_PAIRS, *layer)],
         name="pack_outer",
         near=True,
-    )(xf, xb, cf, cb, inner_up, inner_down)
+    )(xf, xb, cf, cb, inner_up, inner_down, swept)
     below_z, above_z = exchange_z(up, down)
-    final, whole_sum, shifted = call(
+    final, whole_sum, shifted, began = call(
         rest_of_bulk,
-        [(3, halo, *layer), cube, cube],
+        [(3, halo, *layer), cube, cube, cube],
         [(EM_SWEEPS - 1, 3, halo, *layer)],
         name="rest_of_bulk",
         near=True,
         cost_estimate=pl.CostEstimate(flops=10**9, bytes_accessed=10**7, transcendentals=0),
-    )(inner, outer, swept)
+    )(inner, outer, swept, xf, xb, yf, yb, warmth, storage)
     near, send, partial = call(
         edge,
         [(BLOCKS, 3, 32, 128), (count, 128), cube],
@@ -667,8 +678,8 @@
         ],
         name="edge",
     )(
-        inner_packed, outer_packed, below_z, above_z, whole_sum, shifted, xf, xb, yf, yb, sigma,
-        warmth, storage, position, nodes,
+        inner_packed, outer_packed, below_z, above_z, whole_sum, shifted, sigma, began, storage,
+        position, nodes,
     )
     got = lax.all_to_all(
         send.reshape(count, 1, 128), ("gy", "gz"), split_axis=0, concat_axis=0, tiled=True

time: 63.1 us -> 61.5 us (0.975)
  the two profiles are of different devices: /device:TPU:133 before, /device:TPU:130 now
where the time goes in v7:
time: 61.5 us; the launch traced here: 61 us
  blocking collectives  22.7 us (37%)
  starting transfers between devices  17.7 us (29%)
  Pallas kernels  12.5 us (20%)
  waiting for transfers between devices  6.08 us (10%)
  local copies, waits for them, and re-layouts  1.36 us (2%)
  between operations  0.73 us (1%)
    all_to_all x1, blocking collectives, local(): lax.all_to_all(send.reshape(count, 1, 128), ('gy', 'gz'), split_axis=0, c...  22.7 us
    ppermute x5, starting transfers between devices, exchange(): lax.ppermute(fwd, names, forward)  10.2 us
    ppermute x2, starting transfers between devices, exchange_z(): lax.ppermute(down, 'gz', [(j, i) for i, j in ring])  5.9 us
    ppermute x5, waiting for transfers between devices, exchange(): lax.ppermute(bwd, names, backward)  3.34 us
    pallas_call x1, Pallas kernels, local(): call(bulk, [(EM_SWEEPS, 3, 16, *layer)], name='bulk', near=True, cost_est...  2.64 us
    pallas_call x1, Pallas kernels, local(): call(rest_of_bulk, [(3, halo, *layer), cube, cube, cube], [(EM_SWEEPS - 1...  2.05 us
    pallas_call x1, Pallas kernels, local(): call(edge, [(BLOCKS, 3, 32, 128), (count, 128), cube], [(X_ALL, *layer),...  1.95 us
    ppermute x5, waiting for transfers between devices, exchange(): lax.ppermute(fwd, names, forward)  1.55 us
  transfers between devices with their start and end apart: 14, of which 5 were waited for; matrix products, arithmetic and copies ran while one was open for 0% of the time, Pallas kernels for 12%

profile of v7, /device:TPU:130, one launch (start us, length us, event | category | flops | bytes accessed | tf_op | source)
XLA Modules:
  0.0 61.0 jit_solution(11966725953521407840)
XLA Ops:
  0.6 1.5 %pack_xy.1 = (f32[30,16,128]{2,1,0:T(8,128)S(1)}, f32[30,16,128]{2,1,0:T(8,128)S(1)}, f32[16,32,128]{2,1,0:T(8,128)S(1)}, f32[16,32,128]{2,1,0:T(8,128)S(1)}, f3...) custom-call(f32[3,16,16,128]{3,2,1,0:T(8,128)} %refs_0_.1, ...), custom_call_target="tpu_custom_call" | custom-call | tf_op jit(solution)/shard_map/pack_xy/pallas_call | solution.py:616
  2.1 2.4 %collective-permute-start.2 = (f32[30,16,128]{2,1,0:T(8,128)S(1)}, f32[30,16,128]{2,1,0:T(8,128)S(1)}, u32[]{:S(2)}, u32[]{:S(2)}) collective-permute-start(f32[30,16,128]{2,1,0:T(8,128)S(1)} %get-tuple-element.43), channel_id=1, source_target_pairs={{0,64},{1,0},{2,66},{3,2},{4,68},{5,4},{6,70},{7,6},{8,72},{9,8},{... | collective-permute-start | bytes 737288 | tf_op jit(solution)/shard_map/ppermute | solution.py:600
  4.5 0.0 collective-permute-start.3
  4.5 1.5 %collective-permute-start = (f32[16,32,128]{2,1,0:T(8,128)S(1)}, f32[16,32,128]{2,1,0:T(8,128)S(1)}, u32[]{:S(2)}, u32[]{:S(2)}) collective-permute-start(f32[16,32,128]{2,1,0:T(8,128)S(1)} %get-tuple-element.40), channel_id=1, source_target_pairs={{0,16},{1,0},{2,18},{3,2},{4,20},{5,4},{6,22},{7,6},{8,24},{9,8},{... | collective-permute-start | bytes 786440 | tf_op jit(solution)/shard_map/ppermute | solution.py:600
  6.0 0.5 collective-permute-start.1
  6.5 0.0 copy-start
  6.5 0.7 %copy-done = s32[1,1,1,256,1]{3,4,2,1,0:T(1,128)S(1)} copy-done((s32[1,1,1,256,1]{3,4,2,1,0:T(1,128)S(1)}, s32[1,1,1,256,1]{3,4,2,1,0:T(1,128)}, u32[]{:S(2)}) %copy-start) | copy-done | bytes 1048
  7.2 0.0 copy-start.1
  7.2 0.7 %copy-done.1 = s32[1,1,1,256]{3,2,1,0:T(1,128)S(1)} copy-done((s32[1,1,1,256]{3,2,1,0:T(1,128)S(1)}, s32[1,1,1,256]{3,2,1,0:T(1,128)}, u32[]{:S(2)}) %copy-start.1) | copy-done | bytes 1048
  7.9 0.4 place.1
  8.3 1.5 %collective-permute-done.2.xf = f32[30,16,128]{2,1,0:T(8,128)S(1)} collective-permute-done((f32[30,16,128]{2,1,0:T(8,128)S(1)}, f32[30,16,128]{2,1,0:T(8,128)S(1)}, u32[]{:S(2)}, u32[]{:S(2)}) %collective-permute-start.2) | collective-permute-done | bytes 245792 | tf_op jit(solution)/shard_map/ppermute | solution.py:600
  9.8 2.4 %collective-permute-done.3.xb = f32[30,16,128]{2,1,0:T(8,128)S(1)} collective-permute-done((f32[30,16,128]{2,1,0:T(8,128)S(1)}, f32[30,16,128]{2,1,0:T(8,128)S(1)}, u32[]{:S(2)}, u32[]{:S(2)}) %collective-permute-start.3) | collective-permute-done | bytes 245792 | tf_op jit(solution)/shard_map/ppermute | solution.py:600
  12.2 0.1 pack_corners.1
  12.3 1.5 %collective-permute-start.4 = (f32[9,32,128]{2,1,0:T(8,128)S(1)}, f32[9,32,128]{2,1,0:T(8,128)S(1)}, u32[]{:S(2)}, u32[]{:S(2)}) collective-permute-start(f32[9,32,128]{2,1,0:T(8,128)S(1)} %get-tuple-element.46), channel_id=1, source_target_pairs={{0,16},{1,0},{2,18},{3,2},{4,20},{5,4},{6,22},{7,6},{8,24},{9,8},{... | collective-permute-start | bytes 442376 | tf_op jit(solution)/shard_map/ppermute | solution.py:600
  13.8 0.5 collective-permute-start.5
  14.4 0.0 collective-permute-done.yf
  14.4 0.0 collective-permute-done.1.yb
  14.4 1.0 %pack_inner.1 = (f32[8,16,24,128]{3,2,1,0:T(8,128)S(1)}, f32[16,24,128]{2,1,0:T(8,128)S(1)}, f32[8,24,128]{2,1,0:T(8,128)S(1)}, f32[8,24,128]{2,1,0:T(8,128)S(1)}) custom-call(f32[3,16,16,128]{3,2,1,0:T(8,128)S(1)} %get-tuple-element.37.field, f32[4,16,16,128]{3,2,1,0:T(8,128)S(1)} %get-tuple-element.38.scaled, f32[16,16,128]{2,1,0:T(8,128)S(1)} %get-tuple-element.39.warmth, ...), custom_call_target="tpu_custom_call" | custom-call | tf_op jit(solution)/shard_map/pack_inner/pallas_call | solution.py:640
  15.4 2.6 %bulk.1.swept = f32[4,3,16,24,128]{4,3,2,1,0:T(8,128)S(1)} custom-call(f32[8,16,24,128]{3,2,1,0:T(8,128)S(1)} %get-tuple-element.42.whole.inner), custom_call_target="tpu_custom_call" | custom-call | flops 1000000000 | bytes 10000000 | tf_op jit(solution)/shard_map/bulk/pallas_call | solution.py:646
  18.0 0.0 collective-permute-done.4.cf
  18.0 0.9 %collective-permute-done.5.cb = f32[9,32,128]{2,1,0:T(8,128)S(1)} collective-permute-done((f32[9,32,128]{2,1,0:T(8,128)S(1)}, f32[9,32,128]{2,1,0:T(8,128)S(1)}, u32[]{:S(2)}, u32[]{:S(2)}) %collective-permute-start.5) | collective-permute-done | bytes 147488 | tf_op jit(solution)/shard_map/ppermute | solution.py:600
  19.0 0.4 pack_outer.1
  19.3 0.0 collective-permute-start.6
  19.4 2.9 %collective-permute-start.7 = (f32[13,24,128]{2,1,0:T(8,128)S(1)}, f32[13,24,128]{2,1,0:T(8,128)S(1)}, u32[]{:S(2)}, u32[]{:S(2)}) collective-permute-start(f32[13,24,128]{2,1,0:T(8,128)S(1)} %get-tuple-element.56), channel_id=1, source_target_pairs={{1,0},{2,1},{3,2},{4,3},{5,4},{6,5},{7,6},{8,7},{9,8},{10,9},{11,1... | collective-permute-start | bytes 479240 | tf_op jit(solution)/shard_map/ppermute | solution.py:606
  22.3 2.0 %rest_of_bulk.1 = (f32[3,9,24,128]{3,2,1,0:T(8,128)S(1)}, f32[16,16,128]{2,1,0:T(8,128)S(1)}, f32[16,16,128]{2,1,0:T(8,128)S(1)}, f32[16,16,128]{2,1,0:T(8,128)S(1)}) custom-call(f32[8,16,24,128]{3,2,1,0:T(8,128)S(1)} %get-tuple-element.42.whole.inner, f32[8,9,24,128]{3,2,1,0:T(8,128)S(1)} %get-tuple-element.50.outer, f32[4,3,16,24,128]{4,3,2,1,0:T(8,128)S(1)} %bulk.1.swept, ...), custom_call_target="tpu_custom_call" | custom-call | flops 1000000000 | bytes 10000000 | tf_op jit(solution)/shard_map/rest_of_bulk/pallas_call | solution.py:660
  24.4 0.9 %collective-permute-done.6.below_z = f32[13,24,128]{2,1,0:T(8,128)S(1)} collective-permute-done((f32[13,24,128]{2,1,0:T(8,128)S(1)}, f32[13,24,128]{2,1,0:T(8,128)S(1)}, u32[]{:S(2)}, u32[]{:S(2)}) %collective-permute-start.6) | collective-permute-done | bytes 159776 | tf_op jit(solution)/shard_map/ppermute | solution.py:606
  25.3 0.0 collective-permute-done.7.above_z
  25.3 1.9 %edge.1 = (f32[5,3,32,128]{3,2,1,0:T(8,128)S(1)}, f32[576,128]{1,0:T(8,128)S(1)}, f32[16,16,128]{2,1,0:T(8,128)S(1)}) custom-call(f32[16,24,128]{2,1,0:T(8,128)S(1)} %get-tuple-element.53.inner, f32[9,24,128]{2,1,0:T(8,128)S(1)} %get-tuple-element.54.outer, f32[13,24,128]{2,1,0:T(8,128)S(1)} %collective-permute-done.6.below_z, ...), custom_call_target="tpu_custom_call" | custom-call | tf_op jit(solution)/shard_map/edge/pallas_call | solution.py:668
  27.2 22.7 %all_to_all.5 = f32[576,1,128]{2,1,0:T(1,128)S(1)} all-to-all(f32[576,1,128]{2,1,0:T(1,128)S(1)} %bitcast.7), channel_id=1, replica_groups=mesh['gx'=8,'gy'=4,'gz'=16] {'gy','gz'}, dimensions={0} | all-to-all | bytes 589824 | tf_op jit(solution)/shard_map/all_to_all | solution.py:684
  49.9 0.7 %warm.1 = (f32[16,128]{1,0:T(8,128)S(1)}, f32[16,128]{1,0:T(8,128)S(1)}, f32[16,128]{1,0:T(8,128)S(1)}, f32[16,128]{1,0:T(8,128)S(1)}, f32[16,128]{1,0:T(8,128)S...) custom-call(f32[576,128]{1,0:T(8,128)S(1)} %bitcast.6, f32[16,16,128]{2,1,0:T(8,128)S(1)} %get-tuple-element.64.partial, ...), custom_call_target="tpu_custom_call" | custom-call | tf_op jit(solution)/shard_map/warm/pallas_call | solution.py:687
  50.5 3.2 %collective-permute-start.8 = (f32[16,128]{1,0:T(8,128)S(1)}, f32[16,128]{1,0:T(8,128)S(1)}, u32[]{:S(2)}, u32[]{:S(2)}) collective-permute-start(f32[16,128]{1,0:T(8,128)S(1)} %get-tuple-element.66), channel_id=1, source_target_pairs={{0,64},{1,0},{2,66},{3,2},{4,68},{5,4},{6,70},{7,6},{8,72},{9,8},{... | collective-permute-start | bytes 24584 | tf_op jit(solution)/shard_map/ppermute | solution.py:600
  53.8 0.0 collective-permute-start.9
  53.8 1.6 %collective-permute-start.10 = (f32[16,128]{1,0:T(8,128)S(1)}, f32[16,128]{1,0:T(8,128)S(1)}, u32[]{:S(2)}, u32[]{:S(2)}) collective-permute-start(f32[16,128]{1,0:T(8,128)S(1)} %get-tuple-element.68), channel_id=1, source_target_pairs={{0,16},{1,0},{2,18},{3,2},{4,20},{5,4},{6,22},{7,6},{8,24},{9,8},{... | collective-permute-start | bytes 24584 | tf_op jit(solution)/shard_map/ppermute | solution.py:600
  55.4 0.4 collective-permute-start.11
  55.8 0.0 collective-permute-start.12
  55.8 0.0 collective-permute-done.8.xf
  55.8 3.0 %collective-permute-start.13 = (f32[16,128]{1,0:T(8,128)S(1)}, f32[16,128]{1,0:T(8,128)S(1)}, u32[]{:S(2)}, u32[]{:S(2)}) collective-permute-start(f32[16,128]{1,0:T(8,128)S(1)} %get-tuple-element.71), channel_id=1, source_target_pairs={{1,0},{2,1},{3,2},{4,3},{5,4},{6,5},{7,6},{8,7},{9,8},{10,9},{11,1... | collective-permute-start | bytes 24584 | tf_op jit(solution)/shard_map/ppermute | solution.py:606
  58.8 1.1 %merge.1 = f32[3,16,16,128]{3,2,1,0:T(8,128)} custom-call(f32[4,3,16,24,128]{4,3,2,1,0:T(8,128)S(1)} %bulk.1.swept, f32[3,9,24,128]{3,2,1,0:T(8,128)S(1)} %get-tuple-element.52.final, f32[5,3,32,128]{3,2,1,0:T(8,128)S(1)} %get-tuple-element.62.near), custom_call_target="tpu_custom_call" | custom-call | flops 1000000000 | bytes 1000000 | tf_op jit(solution)/shard_map/merge/pallas_call | solution.py:696
  59.9 0.0 collective-permute-done.9.xb
  59.9 0.0 collective-permute-done.10.yf
  59.9 0.0 collective-permute-done.11.yb
  59.9 0.2 collective-permute-done.12.from_below
  60.1 0.0 collective-permute-done.13.from_above
  60.2 0.8 %finish.1 = f32[16,16,128]{2,1,0:T(8,128)} custom-call(f32[16,16,128]{2,1,0:T(8,128)S(1)} %get-tuple-element.65.rest, f32[16,16,128]{2,1,0:T(8,128)S(1)} %get-tuple-element.51.storage, f32[16,128]{1,0:T(8,128)S(1)} %collective-permute-done.8.xf, f32[16,128]{1,0:T(8,128)S(1)} %collective-permute-done.9.xb, f32[16,128]{1,0:T(8,128)S(1)} %collective-permute-done.10.yf, ...), custom_call_target="tpu_custom_call" | custom-call | tf_op jit(solution)/shard_map/finish/pallas_call | solution.py:693
Async XLA Ops:
  2.1 7.7 %collective-permute-start.2 = (f32[30,16,128]{2,1,0:T(8,128)S(1)}, f32[30,16,128]{2,1,0:T(8,128)S(1)}, u32[]{:S(2)}, u32[]{:S(2)}) collective-permute-start(f32[30,16,128]{2,1,0:T(8,128)S(1)} %get-tuple-element.43), channel_id=1, source_target_pairs={{0,64},{1,0},{2,66},{3,2},{4,68},{5,4},{6,70},{7,6},{8,72},{9,8},{... | collective-permute-start | bytes 737288 | tf_op jit(solution)/shard_map/ppermute | solution.py:600
  4.5 7.8 %collective-permute-start.3 = (f32[30,16,128]{2,1,0:T(8,128)S(1)}, f32[30,16,128]{2,1,0:T(8,128)S(1)}, u32[]{:S(2)}, u32[]{:S(2)}) collective-permute-start(f32[30,16,128]{2,1,0:T(8,128)S(1)} %get-tuple-element.44), channel_id=1, source_target_pairs={{64,0},{0,1},{66,2},{2,3},{68,4},{4,5},{70,6},{6,7},{72,8},{8,9},{... | collective-permute-start | bytes 737288 | tf_op jit(solution)/shard_map/ppermute | solution.py:600
  4.5 9.9 %collective-permute-start = (f32[16,32,128]{2,1,0:T(8,128)S(1)}, f32[16,32,128]{2,1,0:T(8,128)S(1)}, u32[]{:S(2)}, u32[]{:S(2)}) collective-permute-start(f32[16,32,128]{2,1,0:T(8,128)S(1)} %get-tuple-element.40), channel_id=1, source_target_pairs={{0,16},{1,0},{2,18},{3,2},{4,20},{5,4},{6,22},{7,6},{8,24},{9,8},{... | collective-permute-start | bytes 786440 | tf_op jit(solution)/shard_map/ppermute | solution.py:600
  6.0 8.4 %collective-permute-start.1 = (f32[16,32,128]{2,1,0:T(8,128)S(1)}, f32[16,32,128]{2,1,0:T(8,128)S(1)}, u32[]{:S(2)}, u32[]{:S(2)}) collective-permute-start(f32[16,32,128]{2,1,0:T(8,128)S(1)} %get-tuple-element.41), channel_id=1, source_target_pairs={{16,0},{0,1},{18,2},{2,3},{20,4},{4,5},{22,6},{6,7},{24,8},{8,9},{... | collective-permute-start | bytes 786440 | tf_op jit(solution)/shard_map/ppermute | solution.py:600
  6.5 0.7 %copy-start = (s32[1,1,1,256,1]{3,4,2,1,0:T(1,128)S(1)}, s32[1,1,1,256,1]{3,4,2,1,0:T(1,128)}, u32[]{:S(2)}) copy-start(s32[1,1,1,256,1]{3,4,2,1,0:T(1,128)} %param.12) | copy-start | bytes 3076
  7.2 0.7 %copy-start.1 = (s32[1,1,1,256]{3,2,1,0:T(1,128)S(1)}, s32[1,1,1,256]{3,2,1,0:T(1,128)}, u32[]{:S(2)}) copy-start(s32[1,1,1,256]{3,2,1,0:T(1,128)} %param.13) | copy-start | bytes 3076
  12.3 5.7 %collective-permute-start.4 = (f32[9,32,128]{2,1,0:T(8,128)S(1)}, f32[9,32,128]{2,1,0:T(8,128)S(1)}, u32[]{:S(2)}, u32[]{:S(2)}) collective-permute-start(f32[9,32,128]{2,1,0:T(8,128)S(1)} %get-tuple-element.46), channel_id=1, source_target_pairs={{0,16},{1,0},{2,18},{3,2},{4,20},{5,4},{6,22},{7,6},{8,24},{9,8},{... | collective-permute-start | bytes 442376 | tf_op jit(solution)/shard_map/ppermute | solution.py:600
  13.8 5.1 %collective-permute-start.5 = (f32[9,32,128]{2,1,0:T(8,128)S(1)}, f32[9,32,128]{2,1,0:T(8,128)S(1)}, u32[]{:S(2)}, u32[]{:S(2)}) collective-permute-start(f32[9,32,128]{2,1,0:T(8,128)S(1)} %get-tuple-element.47), channel_id=1, source_target_pairs={{16,0},{0,1},{18,2},{2,3},{20,4},{4,5},{22,6},{6,7},{24,8},{8,9},{... | collective-permute-start | bytes 442376 | tf_op jit(solution)/shard_map/ppermute | solution.py:600
  19.3 5.9 %collective-permute-start.6 = (f32[13,24,128]{2,1,0:T(8,128)S(1)}, f32[13,24,128]{2,1,0:T(8,128)S(1)}, u32[]{:S(2)}, u32[]{:S(2)}) collective-permute-start(f32[13,24,128]{2,1,0:T(8,128)S(1)} %get-tuple-element.55), channel_id=1, source_target_pairs={{0,1},{1,2},{2,3},{3,4},{4,5},{5,6},{6,7},{7,8},{8,9},{9,10},{10,1... | collective-permute-start | bytes 479240 | tf_op jit(solution)/shard_map/ppermute | solution.py:606
  19.4 5.9 %collective-permute-start.7 = (f32[13,24,128]{2,1,0:T(8,128)S(1)}, f32[13,24,128]{2,1,0:T(8,128)S(1)}, u32[]{:S(2)}, u32[]{:S(2)}) collective-permute-start(f32[13,24,128]{2,1,0:T(8,128)S(1)} %get-tuple-element.56), channel_id=1, source_target_pairs={{1,0},{2,1},{3,2},{4,3},{5,4},{6,5},{7,6},{8,7},{9,8},{10,9},{11,1... | collective-permute-start | bytes 479240 | tf_op jit(solution)/shard_map/ppermute | solution.py:606
  50.5 5.3 %collective-permute-start.8 = (f32[16,128]{1,0:T(8,128)S(1)}, f32[16,128]{1,0:T(8,128)S(1)}, u32[]{:S(2)}, u32[]{:S(2)}) collective-permute-start(f32[16,128]{1,0:T(8,128)S(1)} %get-tuple-element.66), channel_id=1, source_target_pairs={{0,64},{1,0},{2,66},{3,2},{4,68},{5,4},{6,70},{7,6},{8,72},{9,8},{... | collective-permute-start | bytes 24584 | tf_op jit(solution)/shard_map/ppermute | solution.py:600
  53.8 6.1 %collective-permute-start.9 = (f32[16,128]{1,0:T(8,128)S(1)}, f32[16,128]{1,0:T(8,128)S(1)}, u32[]{:S(2)}, u32[]{:S(2)}) collective-permute-start(f32[16,128]{1,0:T(8,128)S(1)} %get-tuple-element.67), channel_id=1, source_target_pairs={{64,0},{0,1},{66,2},{2,3},{68,4},{4,5},{70,6},{6,7},{72,8},{8,9},{... | collective-permute-start | bytes 24584 | tf_op jit(solution)/shard_map/ppermute | solution.py:600
  53.8 6.1 %collective-permute-start.10 = (f32[16,128]{1,0:T(8,128)S(1)}, f32[16,128]{1,0:T(8,128)S(1)}, u32[]{:S(2)}, u32[]{:S(2)}) collective-permute-start(f32[16,128]{1,0:T(8,128)S(1)} %get-tuple-element.68), channel_id=1, source_target_pairs={{0,16},{1,0},{2,18},{3,2},{4,20},{5,4},{6,22},{7,6},{8,24},{9,8},{... | collective-permute-start | bytes 24584 | tf_op jit(solution)/shard_map/ppermute | solution.py:600
  55.4 4.5 %collective-permute-start.11 = (f32[16,128]{1,0:T(8,128)S(1)}, f32[16,128]{1,0:T(8,128)S(1)}, u32[]{:S(2)}, u32[]{:S(2)}) collective-permute-start(f32[16,128]{1,0:T(8,128)S(1)} %get-tuple-element.69), channel_id=1, source_target_pairs={{16,0},{0,1},{18,2},{2,3},{20,4},{4,5},{22,6},{6,7},{24,8},{8,9},{... | collective-permute-start | bytes 24584 | tf_op jit(solution)/shard_map/ppermute | solution.py:600
  55.8 4.3 %collective-permute-start.12 = (f32[16,128]{1,0:T(8,128)S(1)}, f32[16,128]{1,0:T(8,128)S(1)}, u32[]{:S(2)}, u32[]{:S(2)}) collective-permute-start(f32[16,128]{1,0:T(8,128)S(1)} %get-tuple-element.70), channel_id=1, source_target_pairs={{0,1},{1,2},{2,3},{3,4},{4,5},{5,6},{6,7},{7,8},{8,9},{9,10},{10,1... | collective-permute-start | bytes 24584 | tf_op jit(solution)/shard_map/ppermute | solution.py:606
  55.8 4.3 %collective-permute-start.13 = (f32[16,128]{1,0:T(8,128)S(1)}, f32[16,128]{1,0:T(8,128)S(1)}, u32[]{:S(2)}, u32[]{:S(2)}) collective-permute-start(f32[16,128]{1,0:T(8,128)S(1)} %get-tuple-element.71), channel_id=1, source_target_pairs={{1,0},{2,1},{3,2},{4,3},{5,4},{6,5},{7,6},{8,7},{9,8},{10,9},{11,1... | collective-permute-start | bytes 24584 | tf_op jit(solution)/shard_map/ppermute | solution.py:606

commit v8 on v7

--- a/solution.py
+++ b/solution.py
@@ -203,13 +203,36 @@
     return jnp.where(half, a, roll(b, 8, 1)), jnp.where(half, roll(a, -8, 1), b)
 
 
-def pack_inner(field, scaled, warmth, yf, yb, whole, packed, up, down):
-    first = on_first_core()
+def pack_inner(
+    field, scaled, warmth, storage, xf, xb, yf, yb, whole, packed, up, down, began, padded
+):
+    first, gx = on_first_core(), lax.axis_index("gx")
+    low_at, high_at = UP_AT[7, -1], DOWN_AT[7, 16]
+    padded[0] = jnp.where(gx > 0, jnp.where(first, xf[low_at], xb[low_at]), 0.0)
+    padded[17] = jnp.where(
+        gx < lax.axis_size("gx") - 1, jnp.where(first, xb[high_at], xf[high_at]), 0.0
+    )
+    padded[1:17] = warmth[...]
+    row, lane = rows((16, 128)), lanes((16, 128))
 
     def step(k, carry):
         windows = []
         for x in (2 * k, 2 * k + 1):
-            v = [field[f, x] for f in range(3)] + [scaled[f, x] for f in range(4)] + [warmth[x]]
+            t = warmth[x]
+            lower, upper = y_halo(first, (yf, yb), x, 3)
+            total = padded[x] + padded[x + 2]
+            total = total + jnp.where(row == 0, lower[3:4], roll(t, 1, 0))
+            total = total + jnp.where(row == 15, upper[4:5], roll(t, -1, 0))
+            total = total + jnp.where(lane == 0, 0.0, roll(t, 1, 1))
+            total = total + jnp.where(lane == 127, 0.0, roll(t, -1, 1))
+            weight = HEAT_WEIGHTS[0] / (6.0 + storage[x])
+            start = t + weight * (total - 6.0 * t)
+            began[x] = start
+            t = jnp.where(lane == 126, roll(start, -1, 1), t)
+            t = jnp.where(lane == 125, roll(weight, -2, 1), t)
+            t = jnp.where(lane == 1, roll(start, 1, 1), t)
+            t = jnp.where(lane == 2, roll(weight, 2, 1), t)
+            v = [field[f, x] for f in range(3)] + [scaled[f, x] for f in range(4)] + [t]
             slabs, acc = y_slabs(first, (yf, yb), x, v)
             for f in range(8):
                 whole[f, x] = slabs[f]
@@ -303,9 +326,7 @@
     return range(16 - number, 21 - number)
 
 
-def rest_of_bulk(
-    inner, outer, swept, xf, xb, yf, yb, warmth, storage, final, whole_sum, shifted, began, others
-):
+def rest_of_bulk(inner, outer, swept, final, whole_sum, shifted, others):
     def target(number):
         return final if number == EM_SWEEPS else others.at[number - 1]
 
@@ -338,30 +359,13 @@
         whole_sum[x] = flat[0:16] + upright[0:16]
         shifted[x] = roll(flat[0:16], -1, 1)
 
-    first, gx = on_first_core(), lax.axis_index("gx")
-    row, lane = rows((16, 128)), lanes((16, 128))
-    low_at, high_at = UP_AT[7, -1], DOWN_AT[7, 16]
-    under = jnp.where(gx > 0, jnp.where(first, xf[low_at], xb[low_at]), 0.0)
-    over = jnp.where(
-        gx < lax.axis_size("gx") - 1, jnp.where(first, xb[high_at], xf[high_at]), 0.0
-    )
-    for x in range(16):
-        t = warmth[x]
-        lower, upper = y_halo(first, (yf, yb), x, 3)
-        total = (warmth[x - 1] if x else under) + (warmth[x + 1] if x < 15 else over)
-        total = total + jnp.where(row == 0, lower[3:4], roll(t, 1, 0))
-        total = total + jnp.where(row == 15, upper[4:5], roll(t, -1, 0))
-        total = total + jnp.where(lane == 0, 0.0, roll(t, 1, 1))
-        total = total + jnp.where(lane == 127, 0.0, roll(t, -1, 1))
-        began[x] = t + HEAT_WEIGHTS[0] * (total - 6.0 * t) / (6.0 + storage[x])
-
 
 def of_layer(at):
     return at % BLOCKS, Y_LANES * (at // BLOCKS)
 
 
 def edge(
-    inner, outer, below_z, above_z, whole_sum, shifted, sigma, began, storage, position, nodes,
+    inner, outer, below_z, above_z, whole_sum, shifted, sigma, began, storage, position, into, nodes,
     final, send, partial, beside, stack, fields, spare, last, heat,
 ):
     gz = lax.axis_index("gz")
@@ -381,9 +385,10 @@
                 came = jnp.where(half, roll(lower, -8, 1), upper)
             else:
                 came = jnp.where(half, lower, roll(upper, 8, 1))
-            beside[at] = came
             block, lane_at = of_layer(at)
             x = at - LOW
+            if 0 <= x < 16:
+                beside[x] = came[0:16]
             own = inner[x] if 0 <= x < 16 else outer[HALO_X.index(x)]
             for face in range(2):
                 window = jnp.where(half, came, own) if face else jnp.where(half, own, came)
@@ -451,17 +456,18 @@
         heat[x] = sigma[x] * (0.25 * (here + above))
 
     count = send.shape[0]
-    spread = (rows((count, 256)) == position[...]).astype(jnp.bfloat16)
-    left = heat[...].reshape(256, 128)
+    columns = heat[...].reshape(256, 128)
     total = nodes[...]
-    for _ in range(3):
-        piece = left.astype(jnp.bfloat16)
-        left = left - piece.astype(F32)
-        total = total + jnp.dot(spread, piece, preferred_element_type=F32)
+    for n, left in enumerate((columns, columns[:, 127:128] * into[0], columns[:, 0:1] * into[1])):
+        spread = (rows((count, 256)) == position[n : n + 1, :]).astype(jnp.bfloat16)
+        for _ in range(3):
+            piece = left.astype(jnp.bfloat16)
+            left = left - piece.astype(F32)
+            total = total + jnp.dot(spread, piece, preferred_element_type=F32)
     send[...] = total
 
     for x in range(16):
-        ends = beside[x + LOW, 0:16, :]
+        ends = beside[x]
         halo = jnp.where(lane == 0, roll(ends, 9, 1), jnp.where(lane == 127, roll(ends, 7, 1), 0.0))
         partial[x] = began[x] + HEAT_WEIGHTS[0] * halo / (6.0 + storage[x])
 
@@ -489,23 +495,42 @@
             out[f, x] = jnp.where(outer, roll(windows, -32 * f, 1), inner)
 
 
-def place(owners, columns, position, nodes):
-    groups = lax.axis_size("gy") * lax.axis_size("gz")
+BELOW, ABOVE = CAP, 3 * CAP
+
+
+def place(owners, columns, position, into, nodes):
+    planes = lax.axis_size("gz")
+    groups = lax.axis_size("gy") * planes
     owner, column = owners[...], columns[...]
     member = rows((groups, 256)) == owner
     earlier = (rows((256, 256)) < lanes((256, 256))).astype(jnp.bfloat16)
     before = jnp.dot(member.astype(jnp.bfloat16), earlier, preferred_element_type=F32)
     rank = jnp.sum(jnp.where(member, before, 0.0), axis=0, keepdims=True).astype(jnp.int32)
-    position[...] = owner * (CAP + 1) + rank
     count = nodes.shape[0]
-    spread = (rows((count, 256)) == owner * (CAP + 1) + CAP).astype(jnp.bfloat16)
-    listed = jnp.where(rows((128, 256)) == rank, column + 1, 0).astype(F32).astype(jnp.bfloat16)
-    nodes[...] = lax.dot_general(
-        spread, listed, (((1,), (1,)), ((), ())), preferred_element_type=F32
-    )
-
-
-def warm(got, partial, warmth, storage, xf, xb, yf, yb, up, down, rest, heat, mid):
+    depth = lax.rem(owner, planes)
+    listing = owner * (CAP + 1) + CAP
+    to_above = jnp.where(depth < planes - 1, listing + (CAP + 1), -1)
+    to_below = jnp.where(depth > 0, listing - (CAP + 1), -1)
+    position[0:1, :] = owner * (CAP + 1) + rank
+    position[1:2, :] = to_above
+    position[2:3, :] = to_below
+    total = None
+    for target, start in ((listing, 0), (to_above, BELOW), (to_below, ABOVE)):
+        spread = (rows((count, 256)) == target).astype(jnp.bfloat16)
+        listed = jnp.where(rows((128, 256)) == rank + start, column + 1, 0).astype(F32)
+        term = lax.dot_general(
+            spread,
+            listed.astype(jnp.bfloat16),
+            (((1,), (1,)), ((), ())),
+            preferred_element_type=F32,
+        )
+        total = term if total is None else total + term
+    nodes[...] = total
+    for n, start in enumerate((BELOW + CAP, ABOVE + CAP)):
+        into[n] = (rows((128, 256)) == rank + start).astype(F32).T
+
+
+def warm(got, partial, warmth, storage, xf, xb, yf, yb, rest, heat, mid):
     first = on_first_core()
     groups = got.shape[0] // (CAP + 1)
     ids = got[pl.ds(CAP, groups, stride=CAP + 1), :].T
@@ -530,14 +555,11 @@
         mid[x] = partial[x] + HEAT_WEIGHTS[0] * heat[x] / (6.0 + storage[x])
     xf[...] = jnp.where(first, mid[15], mid[0])
     xb[...] = jnp.where(first, mid[0], mid[15])
-    ups = downs = jnp.zeros((16, 128), F32)
     for x in range(16):
         t = mid[x]
         top, end = t[15:16], t[0:1]
         yf[x : x + 1] = jnp.where(first, top, end)
         yb[x : x + 1] = jnp.where(first, end, top)
-        ups = jnp.where(lane == 8 * x, roll(t, 8 * x + 1, 1), ups)
-        downs = jnp.where(lane == 8 * x, roll(t, 8 * x, 1), downs)
         near = jnp.where(row == 0, 0.0, roll(t, 1, 0)) + jnp.where(row == 15, 0.0, roll(t, -1, 0))
         near = near + jnp.where(lane == 0, 0.0, roll(t, 1, 1))
         near = near + jnp.where(lane == 127, 0.0, roll(t, -1, 1))
@@ -548,30 +570,47 @@
         s = storage[x]
         push = s * warmth[x] + heat[x] - (6.0 + s) * t + near
         rest[x] = t + HEAT_WEIGHTS[1] * push / (6.0 + s)
-    up[...] = ups
-    down[...] = downs
-
-
-def finish(rest, storage, xf, xb, yf, yb, from_below, from_above, out):
+
+
+def beyond_z(got, beside, warmth, out):
+    groups = got.shape[0] // (CAP + 1)
+    listing = got[pl.ds(CAP, groups, stride=CAP + 1), :].T
+    node = (rows((256, 1)) + 1).astype(F32)
+    per = max(1, 128 // groups)
+
+    def beside_rows(at):
+        return jnp.concatenate([listing[at + n : at + n + 1, :] for n in range(per)], axis=1)
+
+    heat = []
+    for start in (BELOW, ABOVE):
+        total = None
+        for r in range(0, CAP, per):
+            hit = beside_rows(start + r) == node
+            term = jnp.where(hit, beside_rows(start + CAP + r), 0.0)
+            total = term if total is None else total + term
+        heat.append(jnp.sum(total, axis=1, keepdims=True))
+    lane = lanes((16, 128))
+    for x in range(16):
+        ends, t = beside[x], warmth[x]
+        part = slice(16 * x, 16 * x + 16)
+        low = ends[:, 118:119] + ends[:, 117:118] * (t[:, 0:1] + heat[0][part])
+        high = ends[:, 121:122] + ends[:, 122:123] * (t[:, 127:128] + heat[1][part])
+        out[x] = jnp.where(lane == 0, low, jnp.where(lane == 127, high, 0.0))
+
+
+def finish(rest, storage, xf, xb, yf, yb, beyond, out):
     first = on_first_core()
-    gx, gy, gz = (lax.axis_index(a) for a in ("gx", "gy", "gz"))
-    ends = [a > 0 for a in (gx, gy, gz)]
-    tops = [a < lax.axis_size(n) - 1 for a, n in ((gx, "gx"), (gy, "gy"), (gz, "gz"))]
+    gx, gy = lax.axis_index("gx"), lax.axis_index("gy")
     f, b = xf[...], xb[...]
-    x_low = jnp.where(ends[0], jnp.where(first, f, b), 0.0)
-    x_high = jnp.where(tops[0], jnp.where(first, b, f), 0.0)
+    x_low = jnp.where(gx > 0, jnp.where(first, f, b), 0.0)
+    x_high = jnp.where(gx < lax.axis_size("gx") - 1, jnp.where(first, b, f), 0.0)
     f, b = yf[...], yb[...]
-    y_low = jnp.where(ends[1], jnp.where(first, f, b), 0.0)
-    y_high = jnp.where(tops[1], jnp.where(first, b, f), 0.0)
-    z_low = jnp.where(ends[2], from_below[...], 0.0)
-    z_high = jnp.where(tops[2], from_above[...], 0.0)
-    lane = lanes((16, 128))
+    y_low = jnp.where(gy > 0, jnp.where(first, f, b), 0.0)
+    y_high = jnp.where(gy < lax.axis_size("gy") - 1, jnp.where(first, b, f), 0.0)
     row = rows((16, 128))
     for x in range(16):
-        near = jnp.where(row == 0, y_low[x : x + 1], 0.0)
+        near = beyond[x] + jnp.where(row == 0, y_low[x : x + 1], 0.0)
         near = near + jnp.where(row == 15, y_high[x : x + 1], 0.0)
-        near = near + jnp.where(lane == 0, roll(z_low, -8 * x, 1), 0.0)
-        near = near + jnp.where(lane == 127, roll(z_high, 127 - 8 * x, 1), 0.0)
         if x == 0:
             near = near + x_low
         if x == 15:
@@ -623,10 +662,11 @@
     )(*(pltpu.with_memory_space_constraint(v, pltpu.HBM) for v in here))
     xf, xb = exchange("gx", xf, xb)
     yf, yb = exchange("gy", yf, yb)
-    position, nodes = pl.pallas_call(
+    position, into, nodes = pl.pallas_call(
         place,
         out_shape=[
-            jax.ShapeDtypeStruct((1, 256), jnp.int32),
+            jax.ShapeDtypeStruct((3, 256), jnp.int32),
+            jax.ShapeDtypeStruct((2, 256, 128), F32),
             jax.ShapeDtypeStruct((count, 128), F32),
         ],
         compiler_params=pltpu.CompilerParams(vmem_limit_bytes=8 << 20),
@@ -637,12 +677,13 @@
     )
     cf, cb = exchange("gy", cf, cb)
     layer, halo = (24, 128), len(HALO_X)
-    inner, inner_packed, inner_up, inner_down = call(
+    inner, inner_packed, inner_up, inner_down, began = call(
         pack_inner,
-        [(8, 16, *layer), (16, *layer), (8, *layer), (8, *layer)],
+        [(8, 16, *layer), (16, *layer), (8, *layer), (8, *layer), cube],
+        [(18, 16, 128)],
         name="pack_inner",
         near=True,
-    )(field, scaled, warmth, yf, yb)
+    )(field, scaled, warmth, storage, xf, xb, yf, yb)
     (swept,) = call(
         bulk,
         [(EM_SWEEPS, 3, 16, *layer)],
@@ -657,19 +698,18 @@
         near=True,
     )(xf, xb, cf, cb, inner_up, inner_down, swept)
     below_z, above_z = exchange_z(up, down)
-    final, whole_sum, shifted, began = call(
+    final, whole_sum, shifted = call(
         rest_of_bulk,
-        [(3, halo, *layer), cube, cube, cube],
+        [(3, halo, *layer), cube, cube],
         [(EM_SWEEPS - 1, 3, halo, *layer)],
         name="rest_of_bulk",
         near=True,
         cost_estimate=pl.CostEstimate(flops=10**9, bytes_accessed=10**7, transcendentals=0),
-    )(inner, outer, swept, xf, xb, yf, yb, warmth, storage)
-    near, send, partial = call(
+    )(inner, outer, swept)
+    near, send, partial, beside = call(
         edge,
-        [(BLOCKS, 3, 32, 128), (count, 128), cube],
+        [(BLOCKS, 3, 32, 128), (count, 128), cube, cube],
         [
-            (X_ALL, *layer),
             (BLOCKS, 2, 128, 128),
             (BLOCKS, 8, 32, 128),
             (BLOCKS, 3, 32, 128),
@@ -679,20 +719,24 @@
         name="edge",
     )(
         inner_packed, outer_packed, below_z, above_z, whole_sum, shifted, sigma, began, storage,
-        position, nodes,
+        position, into, nodes,
     )
     got = lax.all_to_all(
         send.reshape(count, 1, 128), ("gy", "gz"), split_axis=0, concat_axis=0, tiled=True
     ).reshape(count, 128)
-    xf, xb, yf, yb, up, down, rest = call(
-        warm, [face, face, face, face, face, face, cube], [cube, cube], name="warm"
+    xf, xb, yf, yb, rest = call(
+        warm, [face, face, face, face, cube], [cube, cube], name="warm"
     )(got, partial, warmth, storage)
     xf, xb = exchange("gx", xf, xb)
     yf, yb = exchange("gy", yf, yb)
-    below_z, above_z = exchange_z(up, down)
-    (updated,) = call(finish, [cube], name="finish")(
-        rest, storage, xf, xb, yf, yb, below_z, above_z
-    )
+    (beyond,) = call(
+        beyond_z,
+        [cube],
+        name="beyond_z",
+        near=True,
+        cost_estimate=pl.CostEstimate(flops=10**9, bytes_accessed=10**6, transcendentals=0),
+    )(got, beside, warmth)
+    (updated,) = call(finish, [cube], name="finish")(rest, storage, xf, xb, yf, yb, beyond)
     (out,) = call(
         merge,
         [(3, *cube)],

time: 61.5 us -> 62.1 us (level)
  blocking collectives: 22.7 us -> 0 us
  waiting for transfers between devices: 6.08 us -> 18.4 us
  starting transfers between devices: 17.7 us -> 25.3 us
  Pallas kernels: 12.5 us -> 14.4 us
  local copies, waits for them, and re-layouts: 1.36 us -> 2.99 us
    all_to_all x1 -> x0, blocking collectives: 22.7 us -> none  [local(): lax.all_to_all(send.reshape(count, 1, 128), ('gy', 'gz'), split_axis=0, c...]
    all_to_all x0 -> x1, starting transfers between devices: none -> 10.6 us  [local(): lax.all_to_all(send.reshape(count, 1, 128), ('gy', 'gz'), split_axis=0, c...]
    all_to_all x0 -> x1, waiting for transfers between devices: none -> 10.2 us  [local(): lax.all_to_all(send.reshape(count, 1, 128), ('gy', 'gz'), split_axis=0, c...]
    ppermute x2 -> x1, starting transfers between devices: 5.9 us -> 2.94 us  [exchange_z(): lax.ppermute(down, 'gz', [(j, i) for i, j in ring])]
    ppermute x5, waiting for transfers between devices: 3.34 us -> 5.62 us  [exchange(): lax.ppermute(bwd, names, backward)]
    unnamed x4 -> x8, local copies, waits for them, and re-layouts: 1.36 us -> 2.99 us
    pallas_call x5 -> x6, Pallas kernels: 5.89 us -> 7.5 us  [the longest x1 3.2 us: local(): call(edge, [(BLOCKS, 3, 32, 128), (count, 128), cube, cube], [(BLOCKS, 2,...]
  transfers between devices with their start and end apart: 14 -> 13, of which waited for: 5 -> 7; matrix products, arithmetic and copies ran while one was open for 0% -> 0% of each run, Pallas kernels for 12% -> 13%
where the time goes in v8:
time: 62.1 us; the launch traced here: 61.8 us
  starting transfers between devices  25.3 us (41%)
  waiting for transfers between devices  18.4 us (30%)
  Pallas kernels  14.4 us (23%)
  local copies, waits for them, and re-layouts  2.99 us (5%)
  between operations  0.73 us (1%)
    all_to_all x1, starting transfers between devices, local(): lax.all_to_all(send.reshape(count, 1, 128), ('gy', 'gz'), split_axis=0, c...  10.6 us
    ppermute x5, starting transfers between devices, exchange(): lax.ppermute(fwd, names, forward)  10.2 us
    all_to_all x1, waiting for transfers between devices, local(): lax.all_to_all(send.reshape(count, 1, 128), ('gy', 'gz'), split_axis=0, c...  10.2 us
    ppermute x5, waiting for transfers between devices, exchange(): lax.ppermute(bwd, names, backward)  5.62 us
    pallas_call x1, Pallas kernels, local(): call(edge, [(BLOCKS, 3, 32, 128), (count, 128), cube, cube], [(BLOCKS, 2,...  3.2 us
    unnamed x8, local copies, waits for them, and re-layouts  2.99 us
    ppermute x1, starting transfers between devices, exchange_z(): lax.ppermute(down, 'gz', [(j, i) for i, j in ring])  2.94 us
    pallas_call x1, Pallas kernels, local(): call(bulk, [(EM_SWEEPS, 3, 16, *layer)], name='bulk', near=True, cost_est...  2.64 us
  transfers between devices with their start and end apart: 13, of which 7 were waited for; matrix products, arithmetic and copies ran while one was open for 0% of the time, Pallas kernels for 13%

profile of v8, /device:TPU:130, one launch (start us, length us, event | category | flops | bytes accessed | tf_op | source)
XLA Modules:
  0.0 61.8 jit_solution(2117948392025849001)
XLA Ops:
  0.6 1.5 %pack_xy.1 = (f32[30,16,128]{2,1,0:T(8,128)S(1)}, f32[30,16,128]{2,1,0:T(8,128)S(1)}, f32[16,32,128]{2,1,0:T(8,128)S(1)}, f32[16,32,128]{2,1,0:T(8,128)S(1)}, f3...) custom-call(f32[3,16,16,128]{3,2,1,0:T(8,128)} %refs_0_.1, ...), custom_call_target="tpu_custom_call" | custom-call | tf_op jit(solution)/shard_map/pack_xy/pallas_call | solution.py:655
  2.1 2.4 %collective-permute-start = (f32[30,16,128]{2,1,0:T(8,128)S(1)}, f32[30,16,128]{2,1,0:T(8,128)S(1)}, u32[]{:S(2)}, u32[]{:S(2)}) collective-permute-start(f32[30,16,128]{2,1,0:T(8,128)S(1)} %get-tuple-element.41), channel_id=1, source_target_pairs={{0,64},{1,0},{2,66},{3,2},{4,68},{5,4},{6,70},{7,6},{8,72},{9,8},{... | collective-permute-start | bytes 737288 | tf_op jit(solution)/shard_map/ppermute | solution.py:639
  4.5 0.0 collective-permute-start.1
  4.5 1.5 %collective-permute-start.2 = (f32[16,32,128]{2,1,0:T(8,128)S(1)}, f32[16,32,128]{2,1,0:T(8,128)S(1)}, u32[]{:S(2)}, u32[]{:S(2)}) collective-permute-start(f32[16,32,128]{2,1,0:T(8,128)S(1)} %get-tuple-element.43), channel_id=1, source_target_pairs={{0,16},{1,0},{2,18},{3,2},{4,20},{5,4},{6,22},{7,6},{8,24},{9,8},{... | collective-permute-start | bytes 786440 | tf_op jit(solution)/shard_map/ppermute | solution.py:639
  6.0 0.5 collective-permute-start.3
  6.5 0.0 copy-start
  6.5 0.7 %copy-done = s32[1,1,1,256,1]{3,4,2,1,0:T(1,128)S(1)} copy-done((s32[1,1,1,256,1]{3,4,2,1,0:T(1,128)S(1)}, s32[1,1,1,256,1]{3,4,2,1,0:T(1,128)}, u32[]{:S(2)}) %copy-start) | copy-done | bytes 1048
  7.2 0.0 copy-start.1
  7.2 0.7 %copy-done.1 = s32[1,1,1,256]{3,2,1,0:T(1,128)S(1)} copy-done((s32[1,1,1,256]{3,2,1,0:T(1,128)S(1)}, s32[1,1,1,256]{3,2,1,0:T(1,128)}, u32[]{:S(2)}) %copy-start.1) | copy-done | bytes 1048
  7.9 0.6 place.1
  8.5 1.4 %collective-permute-done.xf = f32[30,16,128]{2,1,0:T(8,128)S(1)} collective-permute-done((f32[30,16,128]{2,1,0:T(8,128)S(1)}, f32[30,16,128]{2,1,0:T(8,128)S(1)}, u32[]{:S(2)}, u32[]{:S(2)}) %collective-permute-start) | collective-permute-done | bytes 245792 | tf_op jit(solution)/shard_map/ppermute | solution.py:639
  9.8 2.4 %collective-permute-done.1.xb = f32[30,16,128]{2,1,0:T(8,128)S(1)} collective-permute-done((f32[30,16,128]{2,1,0:T(8,128)S(1)}, f32[30,16,128]{2,1,0:T(8,128)S(1)}, u32[]{:S(2)}, u32[]{:S(2)}) %collective-permute-start.1) | collective-permute-done | bytes 245792 | tf_op jit(solution)/shard_map/ppermute | solution.py:639
  12.3 0.1 pack_corners.1
  12.3 1.5 %collective-permute-start.4 = (f32[9,32,128]{2,1,0:T(8,128)S(1)}, f32[9,32,128]{2,1,0:T(8,128)S(1)}, u32[]{:S(2)}, u32[]{:S(2)}) collective-permute-start(f32[9,32,128]{2,1,0:T(8,128)S(1)} %get-tuple-element.47), channel_id=1, source_target_pairs={{0,16},{1,0},{2,18},{3,2},{4,20},{5,4},{6,22},{7,6},{8,24},{9,8},{... | collective-permute-start | bytes 442376 | tf_op jit(solution)/shard_map/ppermute | solution.py:639
  13.8 0.5 collective-permute-start.5
  14.4 0.0 collective-permute-done.2.yf
  14.4 0.0 collective-permute-done.3.yb
  14.4 1.3 %pack_inner.1 = (f32[8,16,24,128]{3,2,1,0:T(8,128)S(1)}, f32[16,24,128]{2,1,0:T(8,128)S(1)}, f32[8,24,128]{2,1,0:T(8,128)S(1)}, f32[8,24,128]{2,1,0:T(8,128)S(1)}, f32[16,16,128]{2,1,0:T(8,128)S(1)}) custom-call(f32[3,16,16,128]{3,2,1,0:T(8,128)S(1)} %get-tuple-element.37.field, f32[4,16,16,128]{3,2,1,0:T(8,128)S(1)} %get-tuple-element.38.scaled, ...), custom_call_target="tpu_custom_call" | custom-call | tf_op jit(solution)/shard_map/pack_inner/pallas_call | solution.py:680
  15.7 2.6 %bulk.1.swept = f32[4,3,16,24,128]{4,3,2,1,0:T(8,128)S(1)} custom-call(f32[8,16,24,128]{3,2,1,0:T(8,128)S(1)} %get-tuple-element.45.whole.inner), custom_call_target="tpu_custom_call" | custom-call | flops 1000000000 | bytes 10000000 | tf_op jit(solution)/shard_map/bulk/pallas_call | solution.py:687
  18.4 0.0 collective-permute-done.4.cf
  18.4 0.6 collective-permute-done.5.cb
  19.0 0.4 pack_outer.1
  19.3 0.0 collective-permute-start.6
  19.4 2.9 %collective-permute-start.7 = (f32[13,24,128]{2,1,0:T(8,128)S(1)}, f32[13,24,128]{2,1,0:T(8,128)S(1)}, u32[]{:S(2)}, u32[]{:S(2)}) collective-permute-start(f32[13,24,128]{2,1,0:T(8,128)S(1)} %get-tuple-element.56), channel_id=1, source_target_pairs={{1,0},{2,1},{3,2},{4,3},{5,4},{6,5},{7,6},{8,7},{9,8},{10,9},{11,1... | collective-permute-start | bytes 479240 | tf_op jit(solution)/shard_map/ppermute | solution.py:645
  22.3 1.8 %rest_of_bulk.1 = (f32[3,9,24,128]{3,2,1,0:T(8,128)S(1)}, f32[16,16,128]{2,1,0:T(8,128)S(1)}, f32[16,16,128]{2,1,0:T(8,128)S(1)}) custom-call(f32[8,16,24,128]{3,2,1,0:T(8,128)S(1)} %get-tuple-element.45.whole.inner, f32[8,9,24,128]{3,2,1,0:T(8,128)S(1)} %get-tuple-element.51.outer, f32[4,3,16,24,128]{4,3,2,1,0:T(8,128)S(1)} %bulk.1.swept), custom_call_target="tpu_custom_call" | custom-call | flops 1000000000 | bytes 10000000 | tf_op jit(solution)/shard_map/rest_of_bulk/pallas_call | solution.py:701
  24.1 1.2 %collective-permute-done.6.below_z = f32[13,24,128]{2,1,0:T(8,128)S(1)} collective-permute-done((f32[13,24,128]{2,1,0:T(8,128)S(1)}, f32[13,24,128]{2,1,0:T(8,128)S(1)}, u32[]{:S(2)}, u32[]{:S(2)}) %collective-permute-start.6) | collective-permute-done | bytes 159776 | tf_op jit(solution)/shard_map/ppermute | solution.py:645
  25.3 0.0 collective-permute-done.7.above_z
  25.3 3.2 %edge.1 = (f32[5,3,32,128]{3,2,1,0:T(8,128)S(1)}, f32[576,128]{1,0:T(8,128)}, f32[16,16,128]{2,1,0:T(8,128)S(1)}, f32[16,16,128]{2,1,0:T(8,128)S(1)}) custom-call(f32[16,24,128]{2,1,0:T(8,128)S(1)} %get-tuple-element.53.inner, f32[9,24,128]{2,1,0:T(8,128)S(1)} %get-tuple-element.54.outer, f32[13,24,128]{2,1,0:T(8,128)S(1)} %collective-permute-done.6.below_z, ...), custom_call_target="tpu_custom_call" | custom-call | tf_op jit(solution)/shard_map/edge/pallas_call | solution.py:709
  28.5 0.0 copy-start.2
  28.5 0.7 %copy-done.2 = f32[5,3,32,128]{3,2,1,0:T(8,128)} copy-done((f32[5,3,32,128]{3,2,1,0:T(8,128)}, f32[5,3,32,128]{3,2,1,0:T(8,128)S(1)}, u32[]{:S(2)}) %copy-start.2) | copy-done | bytes 245784
  29.2 10.6 %all-to-all-start = ((f32[576,1,128]{2,1,0:T(1,128)}), f32[576,1,128]{2,1,0:T(1,128)S(1)}, u32[]{:S(2)}, u32[]{:S(2)}) async-start(f32[576,1,128]{2,1,0:T(1,128)} %bitcast.3), calls=%async_computation | async-start | bytes 589824 | tf_op jit(solution)/shard_map/all_to_all | solution.py:724
  39.8 0.0 copy-start.3
  39.8 0.9 %copy-done.3 = f32[5,3,32,128]{3,2,1,0:T(8,128)S(1)} copy-done((f32[5,3,32,128]{3,2,1,0:T(8,128)S(1)}, f32[5,3,32,128]{3,2,1,0:T(8,128)}, u32[]{:S(2)}) %copy-start.3) | copy-done | bytes 245784
  40.8 1.1 %merge.1 = f32[3,16,16,128]{3,2,1,0:T(8,128)} custom-call(f32[4,3,16,24,128]{4,3,2,1,0:T(8,128)S(1)} %bulk.1.swept, f32[3,9,24,128]{3,2,1,0:T(8,128)S(1)} %get-tuple-element.52.final, f32[5,3,32,128]{3,2,1,0:T(8,128)S(1)} %copy-done.3), custom_call_target="tpu_custom_call" | custom-call | flops 1000000000 | bytes 1000000 | tf_op jit(solution)/shard_map/merge/pallas_call | solution.py:740
  41.8 10.2 %all-to-all-done = f32[576,1,128]{2,1,0:T(1,128)S(1)} async-done(((f32[576,1,128]{2,1,0:T(1,128)}), f32[576,1,128]{2,1,0:T(1,128)S(1)}, u32[]{:S(2)}, u32[]{:S(2)}) %all-to-all-start) | async-done | bytes 294944 | tf_op jit(solution)/shard_map/all_to_all | solution.py:724
  52.0 0.6 warm.1
  52.6 3.3 %collective-permute-start.8 = (f32[16,128]{1,0:T(8,128)S(1)}, f32[16,128]{1,0:T(8,128)S(1)}, u32[]{:S(2)}, u32[]{:S(2)}) collective-permute-start(f32[16,128]{1,0:T(8,128)S(1)} %get-tuple-element.67), channel_id=1, source_target_pairs={{0,64},{1,0},{2,66},{3,2},{4,68},{5,4},{6,70},{7,6},{8,72},{9,8},{... | collective-permute-start | bytes 24584 | tf_op jit(solution)/shard_map/ppermute | solution.py:639
  55.9 0.0 collective-permute-start.9
  55.9 1.6 %collective-permute-start.10 = (f32[16,128]{1,0:T(8,128)S(1)}, f32[16,128]{1,0:T(8,128)S(1)}, u32[]{:S(2)}, u32[]{:S(2)}) collective-permute-start(f32[16,128]{1,0:T(8,128)S(1)} %get-tuple-element.69), channel_id=1, source_target_pairs={{0,16},{1,0},{2,18},{3,2},{4,20},{5,4},{6,22},{7,6},{8,24},{9,8},{... | collective-permute-start | bytes 24584 | tf_op jit(solution)/shard_map/ppermute | solution.py:639
  57.5 0.4 collective-permute-start.11
  57.9 0.6 beyond_z.1.beyond
  58.5 0.0 collective-permute-done.8.xf
  58.5 1.0 %collective-permute-done.9.xb = f32[16,128]{1,0:T(8,128)S(1)} collective-permute-done((f32[16,128]{1,0:T(8,128)S(1)}, f32[16,128]{1,0:T(8,128)S(1)}, u32[]{:S(2)}, u32[]{:S(2)}) %collective-permute-start.9) | collective-permute-done | bytes 8224 | tf_op jit(solution)/shard_map/ppermute | solution.py:639
  59.6 0.0 collective-permute-done.10.yf
  59.6 1.6 %collective-permute-done.11.yb = f32[16,128]{1,0:T(8,128)S(1)} collective-permute-done((f32[16,128]{1,0:T(8,128)S(1)}, f32[16,128]{1,0:T(8,128)S(1)}, u32[]{:S(2)}, u32[]{:S(2)}) %collective-permute-start.11) | collective-permute-done | bytes 8224 | tf_op jit(solution)/shard_map/ppermute | solution.py:639
  61.1 0.7 %finish.1 = f32[16,16,128]{2,1,0:T(8,128)} custom-call(f32[16,16,128]{2,1,0:T(8,128)S(1)} %get-tuple-element.66.rest, f32[16,16,128]{2,1,0:T(8,128)S(1)} %get-tuple-element.40.storage, f32[16,128]{1,0:T(8,128)S(1)} %collective-permute-done.8.xf, f32[16,128]{1,0:T(8,128)S(1)} %collective-permute-done.9.xb, f32[16,128]{1,0:T(8,128)S(1)} %collective-permute-done.10.yf, ...), custom_call_target="tpu_custom_call" | custom-call | tf_op jit(solution)/shard_map/finish/pallas_call | solution.py:739
Async XLA Ops:
  2.1 7.7 %collective-permute-start = (f32[30,16,128]{2,1,0:T(8,128)S(1)}, f32[30,16,128]{2,1,0:T(8,128)S(1)}, u32[]{:S(2)}, u32[]{:S(2)}) collective-permute-start(f32[30,16,128]{2,1,0:T(8,128)S(1)} %get-tuple-element.41), channel_id=1, source_target_pairs={{0,64},{1,0},{2,66},{3,2},{4,68},{5,4},{6,70},{7,6},{8,72},{9,8},{... | collective-permute-start | bytes 737288 | tf_op jit(solution)/shard_map/ppermute | solution.py:639
  4.5 7.8 %collective-permute-start.1 = (f32[30,16,128]{2,1,0:T(8,128)S(1)}, f32[30,16,128]{2,1,0:T(8,128)S(1)}, u32[]{:S(2)}, u32[]{:S(2)}) collective-permute-start(f32[30,16,128]{2,1,0:T(8,128)S(1)} %get-tuple-element.42), channel_id=1, source_target_pairs={{64,0},{0,1},{66,2},{2,3},{68,4},{4,5},{70,6},{6,7},{72,8},{8,9},{... | collective-permute-start | bytes 737288 | tf_op jit(solution)/shard_map/ppermute | solution.py:639
  4.5 9.9 %collective-permute-start.2 = (f32[16,32,128]{2,1,0:T(8,128)S(1)}, f32[16,32,128]{2,1,0:T(8,128)S(1)}, u32[]{:S(2)}, u32[]{:S(2)}) collective-permute-start(f32[16,32,128]{2,1,0:T(8,128)S(1)} %get-tuple-element.43), channel_id=1, source_target_pairs={{0,16},{1,0},{2,18},{3,2},{4,20},{5,4},{6,22},{7,6},{8,24},{9,8},{... | collective-permute-start | bytes 786440 | tf_op jit(solution)/shard_map/ppermute | solution.py:639
  6.0 8.4 %collective-permute-start.3 = (f32[16,32,128]{2,1,0:T(8,128)S(1)}, f32[16,32,128]{2,1,0:T(8,128)S(1)}, u32[]{:S(2)}, u32[]{:S(2)}) collective-permute-start(f32[16,32,128]{2,1,0:T(8,128)S(1)} %get-tuple-element.44), channel_id=1, source_target_pairs={{16,0},{0,1},{18,2},{2,3},{20,4},{4,5},{22,6},{6,7},{24,8},{8,9},{... | collective-permute-start | bytes 786440 | tf_op jit(solution)/shard_map/ppermute | solution.py:639
  6.5 0.7 %copy-start = (s32[1,1,1,256,1]{3,4,2,1,0:T(1,128)S(1)}, s32[1,1,1,256,1]{3,4,2,1,0:T(1,128)}, u32[]{:S(2)}) copy-start(s32[1,1,1,256,1]{3,4,2,1,0:T(1,128)} %param.12) | copy-start | bytes 3076
  7.2 0.7 %copy-start.1 = (s32[1,1,1,256]{3,2,1,0:T(1,128)S(1)}, s32[1,1,1,256]{3,2,1,0:T(1,128)}, u32[]{:S(2)}) copy-start(s32[1,1,1,256]{3,2,1,0:T(1,128)} %param.13) | copy-start | bytes 3076
  12.3 6.0 %collective-permute-start.4 = (f32[9,32,128]{2,1,0:T(8,128)S(1)}, f32[9,32,128]{2,1,0:T(8,128)S(1)}, u32[]{:S(2)}, u32[]{:S(2)}) collective-permute-start(f32[9,32,128]{2,1,0:T(8,128)S(1)} %get-tuple-element.47), channel_id=1, source_target_pairs={{0,16},{1,0},{2,18},{3,2},{4,20},{5,4},{6,22},{7,6},{8,24},{9,8},{... | collective-permute-start | bytes 442376 | tf_op jit(solution)/shard_map/ppermute | solution.py:639
  13.8 5.1 %collective-permute-start.5 = (f32[9,32,128]{2,1,0:T(8,128)S(1)}, f32[9,32,128]{2,1,0:T(8,128)S(1)}, u32[]{:S(2)}, u32[]{:S(2)}) collective-permute-start(f32[9,32,128]{2,1,0:T(8,128)S(1)} %get-tuple-element.48), channel_id=1, source_target_pairs={{16,0},{0,1},{18,2},{2,3},{20,4},{4,5},{22,6},{6,7},{24,8},{8,9},{... | collective-permute-start | bytes 442376 | tf_op jit(solution)/shard_map/ppermute | solution.py:639
  19.3 5.9 %collective-permute-start.6 = (f32[13,24,128]{2,1,0:T(8,128)S(1)}, f32[13,24,128]{2,1,0:T(8,128)S(1)}, u32[]{:S(2)}, u32[]{:S(2)}) collective-permute-start(f32[13,24,128]{2,1,0:T(8,128)S(1)} %get-tuple-element.55), channel_id=1, source_target_pairs={{0,1},{1,2},{2,3},{3,4},{4,5},{5,6},{6,7},{7,8},{8,9},{9,10},{10,1... | collective-permute-start | bytes 479240 | tf_op jit(solution)/shard_map/ppermute | solution.py:645
  19.4 5.9 %collective-permute-start.7 = (f32[13,24,128]{2,1,0:T(8,128)S(1)}, f32[13,24,128]{2,1,0:T(8,128)S(1)}, u32[]{:S(2)}, u32[]{:S(2)}) collective-permute-start(f32[13,24,128]{2,1,0:T(8,128)S(1)} %get-tuple-element.56), channel_id=1, source_target_pairs={{1,0},{2,1},{3,2},{4,3},{5,4},{6,5},{7,6},{8,7},{9,8},{10,9},{11,1... | collective-permute-start | bytes 479240 | tf_op jit(solution)/shard_map/ppermute | solution.py:645
  28.5 0.7 %copy-start.2 = (f32[5,3,32,128]{3,2,1,0:T(8,128)}, f32[5,3,32,128]{3,2,1,0:T(8,128)S(1)}, u32[]{:S(2)}) copy-start(f32[5,3,32,128]{3,2,1,0:T(8,128)S(1)} %get-tuple-element.63.near) | copy-start | bytes 737284
  29.2 22.9 %all-to-all-start = ((f32[576,1,128]{2,1,0:T(1,128)}), f32[576,1,128]{2,1,0:T(1,128)S(1)}, u32[]{:S(2)}, u32[]{:S(2)}) async-start(f32[576,1,128]{2,1,0:T(1,128)} %bitcast.3), calls=%async_computation | async-start | bytes 589824 | tf_op jit(solution)/shard_map/all_to_all | solution.py:724
  39.8 0.9 %copy-start.3 = (f32[5,3,32,128]{3,2,1,0:T(8,128)S(1)}, f32[5,3,32,128]{3,2,1,0:T(8,128)}, u32[]{:S(2)}) copy-start(f32[5,3,32,128]{3,2,1,0:T(8,128)} %copy-done.2) | copy-start | bytes 737284
  52.6 5.9 %collective-permute-start.8 = (f32[16,128]{1,0:T(8,128)S(1)}, f32[16,128]{1,0:T(8,128)S(1)}, u32[]{:S(2)}, u32[]{:S(2)}) collective-permute-start(f32[16,128]{1,0:T(8,128)S(1)} %get-tuple-element.67), channel_id=1, source_target_pairs={{0,64},{1,0},{2,66},{3,2},{4,68},{5,4},{6,70},{7,6},{8,72},{9,8},{... | collective-permute-start | bytes 24584 | tf_op jit(solution)/shard_map/ppermute | solution.py:639
  55.9 3.7 %collective-permute-start.9 = (f32[16,128]{1,0:T(8,128)S(1)}, f32[16,128]{1,0:T(8,128)S(1)}, u32[]{:S(2)}, u32[]{:S(2)}) collective-permute-start(f32[16,128]{1,0:T(8,128)S(1)} %get-tuple-element.68), channel_id=1, source_target_pairs={{64,0},{0,1},{66,2},{2,3},{68,4},{4,5},{70,6},{6,7},{72,8},{8,9},{... | collective-permute-start | bytes 24584 | tf_op jit(solution)/shard_map/ppermute | solution.py:639
  55.9 3.7 %collective-permute-start.10 = (f32[16,128]{1,0:T(8,128)S(1)}, f32[16,128]{1,0:T(8,128)S(1)}, u32[]{:S(2)}, u32[]{:S(2)}) collective-permute-start(f32[16,128]{1,0:T(8,128)S(1)} %get-tuple-element.69), channel_id=1, source_target_pairs={{0,16},{1,0},{2,18},{3,2},{4,20},{5,4},{6,22},{7,6},{8,24},{9,8},{... | collective-permute-start | bytes 24584 | tf_op jit(solution)/shard_map/ppermute | solution.py:639
  57.5 3.7 %collective-permute-start.11 = (f32[16,128]{1,0:T(8,128)S(1)}, f32[16,128]{1,0:T(8,128)S(1)}, u32[]{:S(2)}, u32[]{:S(2)}) collective-permute-start(f32[16,128]{1,0:T(8,128)S(1)} %get-tuple-element.70), channel_id=1, source_target_pairs={{16,0},{0,1},{18,2},{2,3},{20,4},{4,5},{22,6},{6,7},{24,8},{8,9},{... | collective-permute-start | bytes 24584 | tf_op jit(solution)/shard_map/ppermute | solution.py:639

commit v9 on v8

--- a/solution.py
+++ b/solution.py
@@ -364,19 +364,36 @@
     return at % BLOCKS, Y_LANES * (at // BLOCKS)
 
 
+def clear_gaps(stack):
+    for block in range(BLOCKS):
+        for n in range(BLOCKS):
+            at = Y_LANES * n + 24
+            stack[block, at : at + 1, :] = jnp.zeros((1, 128), F32)
+        stack[block, 125:128, :] = jnp.zeros((3, 128), F32)
+
+
+def put_layer(stack, at, windows):
+    block, lane_at = of_layer(at)
+    stack[block, lane_at : lane_at + 24, :] = roll(windows, 4, 0)
+
+
+def turn(inner, outer, turned, stack):
+    clear_gaps(stack)
+    for at in range(X_ALL):
+        x = at - LOW
+        put_layer(stack, at, inner[x] if 0 <= x < 16 else outer[HALO_X.index(x)])
+    for block in range(BLOCKS):
+        turned[block] = stack[block].T
+
+
 def edge(
-    inner, outer, below_z, above_z, whole_sum, shifted, sigma, began, storage, position, into, nodes,
-    final, send, partial, beside, stack, fields, spare, last, heat,
+    own, below_z, above_z, whole_sum, shifted, sigma, position, into, nodes,
+    final, send, beside, stack, fields, spare, last, heat,
 ):
     gz = lax.axis_index("gz")
     half = (lanes((24, 128)) // 8) % 2 == 0
     has_below, has_above = gz > 0, gz < lax.axis_size("gz") - 1
-    nothing = jnp.zeros((1, 128), F32)
-    for block in range(BLOCKS):
-        for face in range(2):
-            for n in range(BLOCKS):
-                stack[block, face, Y_LANES * n + 24 : Y_LANES * n + 25, :] = nothing
-            stack[block, face, 125:128, :] = jnp.zeros((3, 128), F32)
+    clear_gaps(stack)
     for k in range(X_PAIRS):
         lower = jnp.where(has_below, below_z[k], 0.0)
         upper = jnp.where(has_above, above_z[k], 0.0)
@@ -385,19 +402,16 @@
                 came = jnp.where(half, roll(lower, -8, 1), upper)
             else:
                 came = jnp.where(half, lower, roll(upper, 8, 1))
-            block, lane_at = of_layer(at)
-            x = at - LOW
-            if 0 <= x < 16:
-                beside[x] = came[0:16]
-            own = inner[x] if 0 <= x < 16 else outer[HALO_X.index(x)]
-            for face in range(2):
-                window = jnp.where(half, came, own) if face else jnp.where(half, own, came)
-                stack[block, face, lane_at : lane_at + 24, :] = roll(window, 4, 0)
+            if 0 <= at - LOW < 16:
+                beside[at - LOW] = came[0:16]
+            put_layer(stack, at, came)
     for block in range(BLOCKS):
-        for face in range(2):
-            turned = stack[block, face].T
-            for f in range(8):
-                fields[block, f, 16 * face : 16 * face + 16, :] = turned[16 * f : 16 * f + 16]
+        came = stack[block].T
+        for f in range(8):
+            for n, part in enumerate((own, came, came, own)):
+                at = 16 * f + 8 * (n % 2)
+                values = part[block, at : at + 8, :] if part is own else part[at : at + 8]
+                fields[block, f, 8 * n : 8 * n + 8, :] = values
     top = lanes((32, 128)) % Y_LANES == 24
     for block in range(BLOCKS):
         extra = fields[block, 7]
@@ -441,31 +455,38 @@
         ey_x, ez_x = (ahead(final, block, f) for f in (1, 2))
         flat, upright = (ex + roll(ex, -1, 1)) + (ey + ey_x * ey_x), ez + ez_x * ez_x
         both = flat + (upright + roll(upright, -1, 1))
-        stack[block, 0, 0:8, :] = both[24:32]
-        stack[block, 0, 120:128, :] = both[0:8]
-        stack[block, 0, 59:64, :] = flat[4:9]
-        stack[block, 0, 64:67, :] = flat[25:28]
+        stack[block, 0:8, :] = both[24:32]
+        stack[block, 120:128, :] = both[0:8]
+        stack[block, 59:64, :] = flat[4:9]
+        stack[block, 64:67, :] = flat[25:28]
     for block in range(BLOCKS):
-        stack[block, 1] = stack[block, 0].T
+        stack[block] = stack[block].T
     lane = lanes((16, 128))
     for x in range(16):
         block, lane_at = of_layer(x + LOW)
-        near = stack[block, 1, lane_at + LOW : lane_at + LOW + 16, :]
+        near = stack[block, lane_at + LOW : lane_at + LOW + 16, :]
         here = jnp.where((lane < 4) | (lane >= 124), near, whole_sum[x])
         above = jnp.where((lane < 3) | (lane >= 123), roll(near, 64, 1), shifted[x])
         heat[x] = sigma[x] * (0.25 * (here + above))
 
-    count = send.shape[0]
+    def spread_out(target, columns, total):
+        hit = (rows((total.shape[0], columns.shape[0])) == target).astype(jnp.bfloat16)
+        for _ in range(3):
+            piece = columns.astype(jnp.bfloat16)
+            columns = columns - piece.astype(F32)
+            total = total + jnp.dot(hit, piece, preferred_element_type=F32)
+        return total
+
     columns = heat[...].reshape(256, 128)
-    total = nodes[...]
-    for n, left in enumerate((columns, columns[:, 127:128] * into[0], columns[:, 0:1] * into[1])):
-        spread = (rows((count, 256)) == position[n : n + 1, :]).astype(jnp.bfloat16)
-        for _ in range(3):
-            piece = left.astype(jnp.bfloat16)
-            left = left - piece.astype(F32)
-            total = total + jnp.dot(spread, piece, preferred_element_type=F32)
-    send[...] = total
-
+    send[...] = spread_out(position[0:1, :], columns, jnp.zeros(send.shape, F32))
+    ends = jnp.concatenate([columns[:, 127:128] * into[0], columns[:, 0:1] * into[1]], axis=0)
+    target = jnp.concatenate([position[1:2, :], position[2:3, :]], axis=1)
+    groups = nodes.shape[0]
+    send[pl.ds(CAP, groups, stride=CAP + 1), :] = spread_out(target, ends, nodes[...])
+
+
+def join_z(beside, began, storage, partial):
+    lane = lanes((16, 128))
     for x in range(16):
         ends = beside[x]
         halo = jnp.where(lane == 0, roll(ends, 9, 1), jnp.where(lane == 127, roll(ends, 7, 1), 0.0))
@@ -506,17 +527,15 @@
     earlier = (rows((256, 256)) < lanes((256, 256))).astype(jnp.bfloat16)
     before = jnp.dot(member.astype(jnp.bfloat16), earlier, preferred_element_type=F32)
     rank = jnp.sum(jnp.where(member, before, 0.0), axis=0, keepdims=True).astype(jnp.int32)
-    count = nodes.shape[0]
     depth = lax.rem(owner, planes)
-    listing = owner * (CAP + 1) + CAP
-    to_above = jnp.where(depth < planes - 1, listing + (CAP + 1), -1)
-    to_below = jnp.where(depth > 0, listing - (CAP + 1), -1)
+    to_above = jnp.where(depth < planes - 1, owner + 1, -1)
+    to_below = jnp.where(depth > 0, owner - 1, -1)
     position[0:1, :] = owner * (CAP + 1) + rank
     position[1:2, :] = to_above
     position[2:3, :] = to_below
     total = None
-    for target, start in ((listing, 0), (to_above, BELOW), (to_below, ABOVE)):
-        spread = (rows((count, 256)) == target).astype(jnp.bfloat16)
+    for target, start in ((owner, 0), (to_above, BELOW), (to_below, ABOVE)):
+        spread = (rows((groups, 256)) == target).astype(jnp.bfloat16)
         listed = jnp.where(rows((128, 256)) == rank + start, column + 1, 0).astype(F32)
         term = lax.dot_general(
             spread,
@@ -667,7 +686,7 @@
         out_shape=[
             jax.ShapeDtypeStruct((3, 256), jnp.int32),
             jax.ShapeDtypeStruct((2, 256, 128), F32),
-            jax.ShapeDtypeStruct((count, 128), F32),
+            jax.ShapeDtypeStruct((groups, 128), F32),
         ],
         compiler_params=pltpu.CompilerParams(vmem_limit_bytes=8 << 20),
         name="place",
@@ -706,21 +725,34 @@
         near=True,
         cost_estimate=pl.CostEstimate(flops=10**9, bytes_accessed=10**7, transcendentals=0),
     )(inner, outer, swept)
-    near, send, partial, beside = call(
+    (own,) = call(
+        turn,
+        [(BLOCKS, 128, 128)],
+        [(BLOCKS, 128, 128)],
+        name="turn",
+        near=True,
+        cost_estimate=pl.CostEstimate(flops=10**8, bytes_accessed=10**6, transcendentals=0),
+    )(inner_packed, outer_packed)
+    near, send, beside = call(
         edge,
-        [(BLOCKS, 3, 32, 128), (count, 128), cube, cube],
+        [(BLOCKS, 3, 32, 128), (count, 128), cube],
         [
-            (BLOCKS, 2, 128, 128),
+            (BLOCKS, 128, 128),
             (BLOCKS, 8, 32, 128),
             (BLOCKS, 3, 32, 128),
             (3, 32, 128),
             cube,
         ],
         name="edge",
-    )(
-        inner_packed, outer_packed, below_z, above_z, whole_sum, shifted, sigma, began, storage,
-        position, into, nodes,
-    )
+        near=True,
+    )(own, below_z, above_z, whole_sum, shifted, sigma, position, into, nodes)
+    (partial,) = call(
+        join_z,
+        [cube],
+        name="join_z",
+        near=True,
+        cost_estimate=pl.CostEstimate(flops=10**8, bytes_accessed=10**6, transcendentals=0),
+    )(beside, began, storage)
     got = lax.all_to_all(
         send.reshape(count, 1, 128), ("gy", "gz"), split_axis=0, concat_axis=0, tiled=True
     ).reshape(count, 128)

time: 62.1 us -> 60.8 us (0.979)
  local copies, waits for them, and re-layouts: 2.99 us -> 2.33 us
    unnamed x8, local copies, waits for them, and re-layouts: 2.99 us -> 2.33 us
    pallas_call x1 -> x3, Pallas kernels: 3.2 us -> 2.94 us  [the longest x1 2.64 us: local(): call(edge, [(BLOCKS, 3, 32, 128), (count, 128), cube], [(BLOCKS, 128, 128...]
where the time goes in v9:
time: 60.8 us; the launch traced here: 60.6 us
  starting transfers between devices  25.3 us (42%)
  waiting for transfers between devices  18.2 us (30%)
  Pallas kernels  14 us (23%)
  local copies, waits for them, and re-layouts  2.33 us (4%)
  between operations  0.75 us (1%)
    all_to_all x1, starting transfers between devices, local(): lax.all_to_all(send.reshape(count, 1, 128), ('gy', 'gz'), split_axis=0, c...  10.6 us
    ppermute x5, starting transfers between devices, exchange(): lax.ppermute(fwd, names, forward)  10.2 us
    all_to_all x1, waiting for transfers between devices, local(): lax.all_to_all(send.reshape(count, 1, 128), ('gy', 'gz'), split_axis=0, c...  10 us
    ppermute x5, waiting for transfers between devices, exchange(): lax.ppermute(bwd, names, backward)  5.63 us
    ppermute x1, starting transfers between devices, exchange_z(): lax.ppermute(down, 'gz', [(j, i) for i, j in ring])  2.94 us
    pallas_call x1, Pallas kernels, local(): call(edge, [(BLOCKS, 3, 32, 128), (count, 128), cube], [(BLOCKS, 128, 128...  2.64 us
    pallas_call x1, Pallas kernels, local(): call(bulk, [(EM_SWEEPS, 3, 16, *layer)], name='bulk', near=True, cost_est...  2.64 us
    unnamed x8, local copies, waits for them, and re-layouts  2.33 us
  transfers between devices with their start and end apart: 13, of which 7 were waited for; matrix products, arithmetic and copies ran while one was open for 0% of the time, Pallas kernels for 13%

profile of v9, /device:TPU:130, one launch (start us, length us, event | category | flops | bytes accessed | tf_op | source)
XLA Modules:
  0.0 60.6 jit_solution(3748410222554788913)
XLA Ops:
  0.6 1.5 %pack_xy.1 = (f32[30,16,128]{2,1,0:T(8,128)S(1)}, f32[30,16,128]{2,1,0:T(8,128)S(1)}, f32[16,32,128]{2,1,0:T(8,128)S(1)}, f32[16,32,128]{2,1,0:T(8,128)S(1)}, f3...) custom-call(f32[3,16,16,128]{3,2,1,0:T(8,128)} %refs_0_.1, ...), custom_call_target="tpu_custom_call" | custom-call | tf_op jit(solution)/shard_map/pack_xy/pallas_call | solution.py:674
  2.1 2.4 %collective-permute-start = (f32[30,16,128]{2,1,0:T(8,128)S(1)}, f32[30,16,128]{2,1,0:T(8,128)S(1)}, u32[]{:S(2)}, u32[]{:S(2)}) collective-permute-start(f32[30,16,128]{2,1,0:T(8,128)S(1)} %get-tuple-element.40), channel_id=1, source_target_pairs={{0,64},{1,0},{2,66},{3,2},{4,68},{5,4},{6,70},{7,6},{8,72},{9,8},{... | collective-permute-start | bytes 737288 | tf_op jit(solution)/shard_map/ppermute | solution.py:658
  4.5 0.0 collective-permute-start.1
  4.5 1.5 %collective-permute-start.2 = (f32[16,32,128]{2,1,0:T(8,128)S(1)}, f32[16,32,128]{2,1,0:T(8,128)S(1)}, u32[]{:S(2)}, u32[]{:S(2)}) collective-permute-start(f32[16,32,128]{2,1,0:T(8,128)S(1)} %get-tuple-element.42), channel_id=1, source_target_pairs={{0,16},{1,0},{2,18},{3,2},{4,20},{5,4},{6,22},{7,6},{8,24},{9,8},{... | collective-permute-start | bytes 786440 | tf_op jit(solution)/shard_map/ppermute | solution.py:658
  6.0 0.5 collective-permute-start.3
  6.5 0.0 copy-start
  6.5 0.7 %copy-done = s32[1,1,1,256,1]{3,4,2,1,0:T(1,128)S(1)} copy-done((s32[1,1,1,256,1]{3,4,2,1,0:T(1,128)S(1)}, s32[1,1,1,256,1]{3,4,2,1,0:T(1,128)}, u32[]{:S(2)}) %copy-start) | copy-done | bytes 1048
  7.2 0.0 copy-start.1
  7.2 0.7 %copy-done.1 = s32[1,1,1,256]{3,2,1,0:T(1,128)S(1)} copy-done((s32[1,1,1,256]{3,2,1,0:T(1,128)S(1)}, s32[1,1,1,256]{3,2,1,0:T(1,128)}, u32[]{:S(2)}) %copy-start.1) | copy-done | bytes 1048
  7.9 0.4 place.1
  8.3 1.6 %collective-permute-done.xf = f32[30,16,128]{2,1,0:T(8,128)S(1)} collective-permute-done((f32[30,16,128]{2,1,0:T(8,128)S(1)}, f32[30,16,128]{2,1,0:T(8,128)S(1)}, u32[]{:S(2)}, u32[]{:S(2)}) %collective-permute-start) | collective-permute-done | bytes 245792 | tf_op jit(solution)/shard_map/ppermute | solution.py:658
  9.8 2.4 %collective-permute-done.1.xb = f32[30,16,128]{2,1,0:T(8,128)S(1)} collective-permute-done((f32[30,16,128]{2,1,0:T(8,128)S(1)}, f32[30,16,128]{2,1,0:T(8,128)S(1)}, u32[]{:S(2)}, u32[]{:S(2)}) %collective-permute-start.1) | collective-permute-done | bytes 245792 | tf_op jit(solution)/shard_map/ppermute | solution.py:658
  12.3 0.1 pack_corners.1
  12.3 1.5 %collective-permute-start.4 = (f32[9,32,128]{2,1,0:T(8,128)S(1)}, f32[9,32,128]{2,1,0:T(8,128)S(1)}, u32[]{:S(2)}, u32[]{:S(2)}) collective-permute-start(f32[9,32,128]{2,1,0:T(8,128)S(1)} %get-tuple-element.46), channel_id=1, source_target_pairs={{0,16},{1,0},{2,18},{3,2},{4,20},{5,4},{6,22},{7,6},{8,24},{9,8},{... | collective-permute-start | bytes 442376 | tf_op jit(solution)/shard_map/ppermute | solution.py:658
  13.8 0.5 collective-permute-start.5
  14.4 0.0 collective-permute-done.2.yf
  14.4 0.0 collective-permute-done.3.yb
  14.4 1.3 %pack_inner.1 = (f32[8,16,24,128]{3,2,1,0:T(8,128)S(1)}, f32[16,24,128]{2,1,0:T(8,128)S(1)}, f32[8,24,128]{2,1,0:T(8,128)S(1)}, f32[8,24,128]{2,1,0:T(8,128)S(1)}, f32[16,16,128]{2,1,0:T(8,128)S(1)}) custom-call(f32[3,16,16,128]{3,2,1,0:T(8,128)S(1)} %get-tuple-element.36.field, f32[4,16,16,128]{3,2,1,0:T(8,128)S(1)} %get-tuple-element.37.scaled, ...), custom_call_target="tpu_custom_call" | custom-call | tf_op jit(solution)/shard_map/pack_inner/pallas_call | solution.py:699
  15.7 2.6 %bulk.1.swept = f32[4,3,16,24,128]{4,3,2,1,0:T(8,128)S(1)} custom-call(f32[8,16,24,128]{3,2,1,0:T(8,128)S(1)} %get-tuple-element.44.whole.inner), custom_call_target="tpu_custom_call" | custom-call | flops 1000000000 | bytes 10000000 | tf_op jit(solution)/shard_map/bulk/pallas_call | solution.py:706
  18.3 0.0 collective-permute-done.4.cf
  18.4 0.6 %collective-permute-done.5.cb = f32[9,32,128]{2,1,0:T(8,128)S(1)} collective-permute-done((f32[9,32,128]{2,1,0:T(8,128)S(1)}, f32[9,32,128]{2,1,0:T(8,128)S(1)}, u32[]{:S(2)}, u32[]{:S(2)}) %collective-permute-start.5) | collective-permute-done | bytes 147488 | tf_op jit(solution)/shard_map/ppermute | solution.py:658
  19.0 0.4 pack_outer.1
  19.3 0.0 collective-permute-start.6
  19.4 2.9 %collective-permute-start.7 = (f32[13,24,128]{2,1,0:T(8,128)S(1)}, f32[13,24,128]{2,1,0:T(8,128)S(1)}, u32[]{:S(2)}, u32[]{:S(2)}) collective-permute-start(f32[13,24,128]{2,1,0:T(8,128)S(1)} %get-tuple-element.55), channel_id=1, source_target_pairs={{1,0},{2,1},{3,2},{4,3},{5,4},{6,5},{7,6},{8,7},{9,8},{10,9},{11,1... | collective-permute-start | bytes 479240 | tf_op jit(solution)/shard_map/ppermute | solution.py:664
  22.3 0.2 turn.1.own
  22.5 1.8 %rest_of_bulk.1 = (f32[3,9,24,128]{3,2,1,0:T(8,128)S(1)}, f32[16,16,128]{2,1,0:T(8,128)S(1)}, f32[16,16,128]{2,1,0:T(8,128)S(1)}) custom-call(f32[8,16,24,128]{3,2,1,0:T(8,128)S(1)} %get-tuple-element.44.whole.inner, f32[8,9,24,128]{3,2,1,0:T(8,128)S(1)} %get-tuple-element.50.outer, f32[4,3,16,24,128]{4,3,2,1,0:T(8,128)S(1)} %bulk.1.swept), custom_call_target="tpu_custom_call" | custom-call | flops 1000000000 | bytes 10000000 | tf_op jit(solution)/shard_map/rest_of_bulk/pallas_call | solution.py:720
  24.3 0.0 copy-start.2
  24.3 1.0 %collective-permute-done.6.below_z = f32[13,24,128]{2,1,0:T(8,128)S(1)} collective-permute-done((f32[13,24,128]{2,1,0:T(8,128)S(1)}, f32[13,24,128]{2,1,0:T(8,128)S(1)}, u32[]{:S(2)}, u32[]{:S(2)}) %collective-permute-start.6) | collective-permute-done | bytes 159776 | tf_op jit(solution)/shard_map/ppermute | solution.py:664
  25.3 0.0 collective-permute-done.7.above_z
  25.3 2.6 %edge.1 = (f32[5,3,32,128]{3,2,1,0:T(8,128)S(1)}, f32[576,128]{1,0:T(8,128)}, f32[16,16,128]{2,1,0:T(8,128)S(1)}) custom-call(f32[5,128,128]{2,1,0:T(8,128)S(1)} %turn.1.own, f32[13,24,128]{2,1,0:T(8,128)S(1)} %collective-permute-done.6.below_z, f32[13,24,128]{2,1,0:T(8,128)S(1)} %collective-permute-done.7.above_z, ...), custom_call_target="tpu_custom_call" | custom-call | tf_op jit(solution)/shard_map/edge/pallas_call | solution.py:736
  27.9 0.0 copy-done.2
  27.9 10.6 %all-to-all-start = ((f32[576,1,128]{2,1,0:T(1,128)}), f32[576,1,128]{2,1,0:T(1,128)S(1)}, u32[]{:S(2)}, u32[]{:S(2)}) async-start(f32[576,1,128]{2,1,0:T(1,128)} %bitcast.3), calls=%async_computation | async-start | bytes 589824 | tf_op jit(solution)/shard_map/all_to_all | solution.py:756
  38.6 0.1 join_z.1.partial
  38.7 0.0 copy-start.3
  38.7 1.0 %copy-done.3 = f32[3,9,24,128]{3,2,1,0:T(8,128)S(1)} copy-done((f32[3,9,24,128]{3,2,1,0:T(8,128)S(1)}, f32[3,9,24,128]{3,2,1,0:T(8,128)}, u32[]{:S(2)}) %copy-start.3) | copy-done | bytes 331800
  39.7 1.1 %merge.1 = f32[3,16,16,128]{3,2,1,0:T(8,128)} custom-call(f32[4,3,16,24,128]{4,3,2,1,0:T(8,128)S(1)} %bulk.1.swept, f32[3,9,24,128]{3,2,1,0:T(8,128)S(1)} %copy-done.3, f32[5,3,32,128]{3,2,1,0:T(8,128)S(1)} %get-tuple-element.61.near), custom_call_target="tpu_custom_call" | custom-call | flops 1000000000 | bytes 1000000 | tf_op jit(solution)/shard_map/merge/pallas_call | solution.py:772
  40.8 10.0 %all-to-all-done = f32[576,1,128]{2,1,0:T(1,128)S(1)} async-done(((f32[576,1,128]{2,1,0:T(1,128)}), f32[576,1,128]{2,1,0:T(1,128)S(1)}, u32[]{:S(2)}, u32[]{:S(2)}) %all-to-all-start) | async-done | bytes 294944 | tf_op jit(solution)/shard_map/all_to_all | solution.py:756
  50.8 0.6 %warm.1 = (f32[16,128]{1,0:T(8,128)S(1)}, f32[16,128]{1,0:T(8,128)S(1)}, f32[16,128]{1,0:T(8,128)S(1)}, f32[16,128]{1,0:T(8,128)S(1)}, f32[16,16,128]{2,1,0:T(8,128)S(1)}) custom-call(f32[576,128]{1,0:T(8,128)S(1)} %bitcast.6, f32[16,16,128]{2,1,0:T(8,128)S(1)} %join_z.1.partial, f32[16,16,128]{2,1,0:T(8,128)S(1)} %get-tuple-element.38.warmth, ...), custom_call_target="tpu_custom_call" | custom-call | tf_op jit(solution)/shard_map/warm/pallas_call | solution.py:759
  51.4 3.2 %collective-permute-start.8 = (f32[16,128]{1,0:T(8,128)S(1)}, f32[16,128]{1,0:T(8,128)S(1)}, u32[]{:S(2)}, u32[]{:S(2)}) collective-permute-start(f32[16,128]{1,0:T(8,128)S(1)} %get-tuple-element.66), channel_id=1, source_target_pairs={{0,64},{1,0},{2,66},{3,2},{4,68},{5,4},{6,70},{7,6},{8,72},{9,8},{... | collective-permute-start | bytes 24584 | tf_op jit(solution)/shard_map/ppermute | solution.py:658
  54.6 0.0 collective-permute-start.9
  54.6 1.6 %collective-permute-start.10 = (f32[16,128]{1,0:T(8,128)S(1)}, f32[16,128]{1,0:T(8,128)S(1)}, u32[]{:S(2)}, u32[]{:S(2)}) collective-permute-start(f32[16,128]{1,0:T(8,128)S(1)} %get-tuple-element.68), channel_id=1, source_target_pairs={{0,16},{1,0},{2,18},{3,2},{4,20},{5,4},{6,22},{7,6},{8,24},{9,8},{... | collective-permute-start | bytes 24584 | tf_op jit(solution)/shard_map/ppermute | solution.py:658
  56.2 0.4 collective-permute-start.11
  56.7 0.6 beyond_z.1.beyond
  57.3 0.0 collective-permute-done.8.xf
  57.3 1.0 %collective-permute-done.9.xb = f32[16,128]{1,0:T(8,128)S(1)} collective-permute-done((f32[16,128]{1,0:T(8,128)S(1)}, f32[16,128]{1,0:T(8,128)S(1)}, u32[]{:S(2)}, u32[]{:S(2)}) %collective-permute-start.9) | collective-permute-done | bytes 8224 | tf_op jit(solution)/shard_map/ppermute | solution.py:658
  58.3 0.0 collective-permute-done.10.yf
  58.3 1.6 %collective-permute-done.11.yb = f32[16,128]{1,0:T(8,128)S(1)} collective-permute-done((f32[16,128]{1,0:T(8,128)S(1)}, f32[16,128]{1,0:T(8,128)S(1)}, u32[]{:S(2)}, u32[]{:S(2)}) %collective-permute-start.11) | collective-permute-done | bytes 8224 | tf_op jit(solution)/shard_map/ppermute | solution.py:658
  59.9 0.7 %finish.1 = f32[16,16,128]{2,1,0:T(8,128)} custom-call(f32[16,16,128]{2,1,0:T(8,128)S(1)} %get-tuple-element.65.rest, f32[16,16,128]{2,1,0:T(8,128)S(1)} %get-tuple-element.39.storage, f32[16,128]{1,0:T(8,128)S(1)} %collective-permute-done.8.xf, f32[16,128]{1,0:T(8,128)S(1)} %collective-permute-done.9.xb, f32[16,128]{1,0:T(8,128)S(1)} %collective-permute-done.10.yf, ...), custom_call_target="tpu_custom_call" | custom-call | tf_op jit(solution)/shard_map/finish/pallas_call | solution.py:771
Async XLA Ops:
  2.1 7.7 %collective-permute-start = (f32[30,16,128]{2,1,0:T(8,128)S(1)}, f32[30,16,128]{2,1,0:T(8,128)S(1)}, u32[]{:S(2)}, u32[]{:S(2)}) collective-permute-start(f32[30,16,128]{2,1,0:T(8,128)S(1)} %get-tuple-element.40), channel_id=1, source_target_pairs={{0,64},{1,0},{2,66},{3,2},{4,68},{5,4},{6,70},{7,6},{8,72},{9,8},{... | collective-permute-start | bytes 737288 | tf_op jit(solution)/shard_map/ppermute | solution.py:658
  4.5 7.8 %collective-permute-start.1 = (f32[30,16,128]{2,1,0:T(8,128)S(1)}, f32[30,16,128]{2,1,0:T(8,128)S(1)}, u32[]{:S(2)}, u32[]{:S(2)}) collective-permute-start(f32[30,16,128]{2,1,0:T(8,128)S(1)} %get-tuple-element.41), channel_id=1, source_target_pairs={{64,0},{0,1},{66,2},{2,3},{68,4},{4,5},{70,6},{6,7},{72,8},{8,9},{... | collective-permute-start | bytes 737288 | tf_op jit(solution)/shard_map/ppermute | solution.py:658
  4.5 9.9 %collective-permute-start.2 = (f32[16,32,128]{2,1,0:T(8,128)S(1)}, f32[16,32,128]{2,1,0:T(8,128)S(1)}, u32[]{:S(2)}, u32[]{:S(2)}) collective-permute-start(f32[16,32,128]{2,1,0:T(8,128)S(1)} %get-tuple-element.42), channel_id=1, source_target_pairs={{0,16},{1,0},{2,18},{3,2},{4,20},{5,4},{6,22},{7,6},{8,24},{9,8},{... | collective-permute-start | bytes 786440 | tf_op jit(solution)/shard_map/ppermute | solution.py:658
  6.0 8.4 %collective-permute-start.3 = (f32[16,32,128]{2,1,0:T(8,128)S(1)}, f32[16,32,128]{2,1,0:T(8,128)S(1)}, u32[]{:S(2)}, u32[]{:S(2)}) collective-permute-start(f32[16,32,128]{2,1,0:T(8,128)S(1)} %get-tuple-element.43), channel_id=1, source_target_pairs={{16,0},{0,1},{18,2},{2,3},{20,4},{4,5},{22,6},{6,7},{24,8},{8,9},{... | collective-permute-start | bytes 786440 | tf_op jit(solution)/shard_map/ppermute | solution.py:658
  6.5 0.7 %copy-start = (s32[1,1,1,256,1]{3,4,2,1,0:T(1,128)S(1)}, s32[1,1,1,256,1]{3,4,2,1,0:T(1,128)}, u32[]{:S(2)}) copy-start(s32[1,1,1,256,1]{3,4,2,1,0:T(1,128)} %param.12) | copy-start | bytes 3076
  7.2 0.7 %copy-start.1 = (s32[1,1,1,256]{3,2,1,0:T(1,128)S(1)}, s32[1,1,1,256]{3,2,1,0:T(1,128)}, u32[]{:S(2)}) copy-start(s32[1,1,1,256]{3,2,1,0:T(1,128)} %param.13) | copy-start | bytes 3076
  12.3 6.0 %collective-permute-start.4 = (f32[9,32,128]{2,1,0:T(8,128)S(1)}, f32[9,32,128]{2,1,0:T(8,128)S(1)}, u32[]{:S(2)}, u32[]{:S(2)}) collective-permute-start(f32[9,32,128]{2,1,0:T(8,128)S(1)} %get-tuple-element.46), channel_id=1, source_target_pairs={{0,16},{1,0},{2,18},{3,2},{4,20},{5,4},{6,22},{7,6},{8,24},{9,8},{... | collective-permute-start | bytes 442376 | tf_op jit(solution)/shard_map/ppermute | solution.py:658
  13.8 5.1 %collective-permute-start.5 = (f32[9,32,128]{2,1,0:T(8,128)S(1)}, f32[9,32,128]{2,1,0:T(8,128)S(1)}, u32[]{:S(2)}, u32[]{:S(2)}) collective-permute-start(f32[9,32,128]{2,1,0:T(8,128)S(1)} %get-tuple-element.47), channel_id=1, source_target_pairs={{16,0},{0,1},{18,2},{2,3},{20,4},{4,5},{22,6},{6,7},{24,8},{8,9},{... | collective-permute-start | bytes 442376 | tf_op jit(solution)/shard_map/ppermute | solution.py:658
  19.3 5.9 %collective-permute-start.6 = (f32[13,24,128]{2,1,0:T(8,128)S(1)}, f32[13,24,128]{2,1,0:T(8,128)S(1)}, u32[]{:S(2)}, u32[]{:S(2)}) collective-permute-start(f32[13,24,128]{2,1,0:T(8,128)S(1)} %get-tuple-element.54), channel_id=1, source_target_pairs={{0,1},{1,2},{2,3},{3,4},{4,5},{5,6},{6,7},{7,8},{8,9},{9,10},{10,1... | collective-permute-start | bytes 479240 | tf_op jit(solution)/shard_map/ppermute | solution.py:664
  19.4 5.9 %collective-permute-start.7 = (f32[13,24,128]{2,1,0:T(8,128)S(1)}, f32[13,24,128]{2,1,0:T(8,128)S(1)}, u32[]{:S(2)}, u32[]{:S(2)}) collective-permute-start(f32[13,24,128]{2,1,0:T(8,128)S(1)} %get-tuple-element.55), channel_id=1, source_target_pairs={{1,0},{2,1},{3,2},{4,3},{5,4},{6,5},{7,6},{8,7},{9,8},{10,9},{11,1... | collective-permute-start | bytes 479240 | tf_op jit(solution)/shard_map/ppermute | solution.py:664
  24.3 3.6 %copy-start.2 = (f32[3,9,24,128]{3,2,1,0:T(8,128)}, f32[3,9,24,128]{3,2,1,0:T(8,128)S(1)}, u32[]{:S(2)}) copy-start(f32[3,9,24,128]{3,2,1,0:T(8,128)S(1)} %get-tuple-element.51.final) | copy-start | bytes 995332
  27.9 22.9 %all-to-all-start = ((f32[576,1,128]{2,1,0:T(1,128)}), f32[576,1,128]{2,1,0:T(1,128)S(1)}, u32[]{:S(2)}, u32[]{:S(2)}) async-start(f32[576,1,128]{2,1,0:T(1,128)} %bitcast.3), calls=%async_computation | async-start | bytes 589824 | tf_op jit(solution)/shard_map/all_to_all | solution.py:756
  38.7 1.0 %copy-start.3 = (f32[3,9,24,128]{3,2,1,0:T(8,128)S(1)}, f32[3,9,24,128]{3,2,1,0:T(8,128)}, u32[]{:S(2)}) copy-start(f32[3,9,24,128]{3,2,1,0:T(8,128)} %copy-done.2) | copy-start | bytes 995332
  51.4 5.9 %collective-permute-start.8 = (f32[16,128]{1,0:T(8,128)S(1)}, f32[16,128]{1,0:T(8,128)S(1)}, u32[]{:S(2)}, u32[]{:S(2)}) collective-permute-start(f32[16,128]{1,0:T(8,128)S(1)} %get-tuple-element.66), channel_id=1, source_target_pairs={{0,64},{1,0},{2,66},{3,2},{4,68},{5,4},{6,70},{7,6},{8,72},{9,8},{... | collective-permute-start | bytes 24584 | tf_op jit(solution)/shard_map/ppermute | solution.py:658
  54.6 3.7 %collective-permute-start.9 = (f32[16,128]{1,0:T(8,128)S(1)}, f32[16,128]{1,0:T(8,128)S(1)}, u32[]{:S(2)}, u32[]{:S(2)}) collective-permute-start(f32[16,128]{1,0:T(8,128)S(1)} %get-tuple-element.67), channel_id=1, source_target_pairs={{64,0},{0,1},{66,2},{2,3},{68,4},{4,5},{70,6},{6,7},{72,8},{8,9},{... | collective-permute-start | bytes 24584 | tf_op jit(solution)/shard_map/ppermute | solution.py:658
  54.6 3.7 %collective-permute-start.10 = (f32[16,128]{1,0:T(8,128)S(1)}, f32[16,128]{1,0:T(8,128)S(1)}, u32[]{:S(2)}, u32[]{:S(2)}) collective-permute-start(f32[16,128]{1,0:T(8,128)S(1)} %get-tuple-element.68), channel_id=1, source_target_pairs={{0,16},{1,0},{2,18},{3,2},{4,20},{5,4},{6,22},{7,6},{8,24},{9,8},{... | collective-permute-start | bytes 24584 | tf_op jit(solution)/shard_map/ppermute | solution.py:658
  56.2 3.7 %collective-permute-start.11 = (f32[16,128]{1,0:T(8,128)S(1)}, f32[16,128]{1,0:T(8,128)S(1)}, u32[]{:S(2)}, u32[]{:S(2)}) collective-permute-start(f32[16,128]{1,0:T(8,128)S(1)} %get-tuple-element.69), channel_id=1, source_target_pairs={{16,0},{0,1},{18,2},{2,3},{20,4},{4,5},{22,6},{6,7},{24,8},{8,9},{... | collective-permute-start | bytes 24584 | tf_op jit(solution)/shard_map/ppermute | solution.py:658

commit v10 on v9

--- a/solution.py
+++ b/solution.py
@@ -103,17 +103,18 @@
         bwd[at, part] = jnp.where(first, down, up)
 
 
-def pack_xy(*refs):
-    far, (xf, xb, yf, yb, scaled), near, arrived = refs[:5], refs[5:10], refs[10:15], refs[15]
+def pack_x(*refs):
+    far, (xf, xb, scaled), near, arrived = refs[:5], refs[5:8], refs[8:13], refs[13]
     copies = [
         pltpu.make_async_copy(a, b, arrived.at[n]) for n, (a, b) in enumerate(zip(far, near))
     ]
     for copy in copies:
         copy.start()
-    for copy in copies:
-        copy.wait()
-    field, sigma, warmth, _, source = near
+    field, sigma, warmth, storage, source = near
+    del storage
     first = on_first_core()
+    for at in (0, 1, 2, 4):
+        copies[at].wait()
     inverse = 1.0 / (4.0 + sigma[...])
     scaled[3] = inverse
     for c in range(3):
@@ -130,9 +131,15 @@
         up = layer(*ups[min(at, len(ups) - 1)])
         down = layer(*downs[min(at, len(downs) - 1)])
         swap_store(first, xf, xb, at, up, down)
+    copies[3].wait()
+
+
+def pack_y(field, scaled, warmth, yf, yb):
+    first = on_first_core()
 
     def step(x, carry):
-        y_tiles([layer(f, x) for f in range(8)], first, yf, yb, x)
+        v = [field[f, x] for f in range(3)] + [scaled[f, x] for f in range(4)] + [warmth[x]]
+        y_tiles(v, first, yf, yb, x)
         return carry
 
     lax.fori_loop(0, 16, step, 0, unroll=4)
@@ -155,8 +162,8 @@
         return jnp.where(inside, jnp.where(self.first, near[at], far[at]), 0.0)
 
 
-def pack_corners(xf, xb, position, fwd, bwd):
-    del position
+def pack_corners(xf, xb, targets, fwd, bwd):
+    del targets
     halo = Halo(xf, xb)
     zero = jnp.zeros((16, 128), F32)
     for number, x in enumerate(HALO_X):
@@ -387,7 +394,7 @@
 
 
 def edge(
-    own, below_z, above_z, whole_sum, shifted, sigma, position, into, nodes,
+    own, below_z, above_z, whole_sum, shifted, sigma, targets, spread_rows, into, nodes,
     final, send, beside, stack, fields, spare, last, heat,
 ):
     gz = lax.axis_index("gz")
@@ -469,31 +476,25 @@
         above = jnp.where((lane < 3) | (lane >= 123), roll(near, 64, 1), shifted[x])
         heat[x] = sigma[x] * (0.25 * (here + above))
 
-    def spread_out(target, columns, total):
-        hit = (rows((total.shape[0], columns.shape[0])) == target).astype(jnp.bfloat16)
+    def spread_out(hit, columns, total):
         for _ in range(3):
             piece = columns.astype(jnp.bfloat16)
             columns = columns - piece.astype(F32)
-            total = total + jnp.dot(hit, piece, preferred_element_type=F32)
+            term = jnp.dot(hit, piece, preferred_element_type=F32)
+            total = term if total is None else total + term
         return total
 
     columns = heat[...].reshape(256, 128)
-    send[...] = spread_out(position[0:1, :], columns, jnp.zeros(send.shape, F32))
+    send[...] = spread_out(spread_rows[...], columns, None)
     ends = jnp.concatenate([columns[:, 127:128] * into[0], columns[:, 0:1] * into[1]], axis=0)
-    target = jnp.concatenate([position[1:2, :], position[2:3, :]], axis=1)
+    target = jnp.concatenate([targets[0:1, :], targets[1:2, :]], axis=1)
     groups = nodes.shape[0]
-    send[pl.ds(CAP, groups, stride=CAP + 1), :] = spread_out(target, ends, nodes[...])
-
-
-def join_z(beside, began, storage, partial):
-    lane = lanes((16, 128))
-    for x in range(16):
-        ends = beside[x]
-        halo = jnp.where(lane == 0, roll(ends, 9, 1), jnp.where(lane == 127, roll(ends, 7, 1), 0.0))
-        partial[x] = began[x] + HEAT_WEIGHTS[0] * halo / (6.0 + storage[x])
-
-
-def merge(swept, final, near, out, stack):
+    hit = (rows((groups, 512)) == target).astype(jnp.bfloat16)
+    send[pl.ds(CAP, groups, stride=CAP + 1), :] = spread_out(hit, ends, nodes[...])
+
+
+def merge(swept, final, near, got, beside, warmth, out, beyond, stack):
+    beyond_z(got, beside, warmth, beyond)
     for block in range(BLOCKS):
         for f in range(3):
             stack[block, 32 * f : 32 * f + 8, :] = near[block, f, 24:32, :]
@@ -519,7 +520,7 @@
 BELOW, ABOVE = CAP, 3 * CAP
 
 
-def place(owners, columns, position, into, nodes):
+def place(owners, columns, targets, spread_rows, into, nodes):
     planes = lax.axis_size("gz")
     groups = lax.axis_size("gy") * planes
     owner, column = owners[...], columns[...]
@@ -530,9 +531,10 @@
     depth = lax.rem(owner, planes)
     to_above = jnp.where(depth < planes - 1, owner + 1, -1)
     to_below = jnp.where(depth > 0, owner - 1, -1)
-    position[0:1, :] = owner * (CAP + 1) + rank
-    position[1:2, :] = to_above
-    position[2:3, :] = to_below
+    count = spread_rows.shape[0]
+    spread_rows[...] = (rows((count, 256)) == owner * (CAP + 1) + rank).astype(jnp.bfloat16)
+    targets[0:1, :] = to_above
+    targets[1:2, :] = to_below
     total = None
     for target, start in ((owner, 0), (to_above, BELOW), (to_below, ABOVE)):
         spread = (rows((groups, 256)) == target).astype(jnp.bfloat16)
@@ -549,7 +551,7 @@
         into[n] = (rows((128, 256)) == rank + start).astype(F32).T
 
 
-def warm(got, partial, warmth, storage, xf, xb, yf, yb, rest, heat, mid):
+def warm(got, beside, began, warmth, storage, xf, xb, yf, yb, rest, heat, mid):
     first = on_first_core()
     groups = got.shape[0] // (CAP + 1)
     ids = got[pl.ds(CAP, groups, stride=CAP + 1), :].T
@@ -571,7 +573,9 @@
     lane = lanes((16, 128))
     row = rows((16, 128))
     for x in range(16):
-        mid[x] = partial[x] + HEAT_WEIGHTS[0] * heat[x] / (6.0 + storage[x])
+        ends = beside[x]
+        halo = jnp.where(lane == 0, roll(ends, 9, 1), jnp.where(lane == 127, roll(ends, 7, 1), 0.0))
+        mid[x] = began[x] + HEAT_WEIGHTS[0] * (heat[x] + halo) / (6.0 + storage[x])
     xf[...] = jnp.where(first, mid[15], mid[0])
     xb[...] = jnp.where(first, mid[0], mid[15])
     for x in range(16):
@@ -671,20 +675,22 @@
     face = (16, 128)
     x_message, y_message, corners = (X_LAYERS, 16, 128), (16, 32, 128), (len(HALO_X), 32, 128)
     here = (field, sigma, warmth, storage, source)
-    xf, xb, yf, yb, scaled, field, sigma, warmth, storage = call(
-        pack_xy,
-        [x_message, x_message, y_message, y_message, (4, *cube), (3, *cube), cube, cube, cube],
+    xf, xb, scaled, field, sigma, warmth, storage = call(
+        pack_x,
+        [x_message, x_message, (4, *cube), (3, *cube), cube, cube, cube],
         [(3, *cube), pltpu.SemaphoreType.DMA((5,))],
-        name="pack_xy",
+        name="pack_x",
         near=True,
         in_specs=[pl.BlockSpec(memory_space=pltpu.HBM)] * 5,
     )(*(pltpu.with_memory_space_constraint(v, pltpu.HBM) for v in here))
     xf, xb = exchange("gx", xf, xb)
+    yf, yb = call(pack_y, [y_message, y_message], name="pack_y", near=True)(field, scaled, warmth)
     yf, yb = exchange("gy", yf, yb)
-    position, into, nodes = pl.pallas_call(
+    targets, spread_rows, into, nodes = pl.pallas_call(
         place,
         out_shape=[
-            jax.ShapeDtypeStruct((3, 256), jnp.int32),
+            jax.ShapeDtypeStruct((2, 256), jnp.int32),
+            jax.ShapeDtypeStruct((count, 256), jnp.bfloat16),
             jax.ShapeDtypeStruct((2, 256, 128), F32),
             jax.ShapeDtypeStruct((groups, 128), F32),
         ],
@@ -692,7 +698,7 @@
         name="place",
     )(partition.reshape(1, 256), column.reshape(1, 256))
     cf, cb = call(pack_corners, [corners, corners], name="pack_corners")(
-        xf, xb, position
+        xf, xb, targets
     )
     cf, cb = exchange("gy", cf, cb)
     layer, halo = (24, 128), len(HALO_X)
@@ -745,37 +751,25 @@
         ],
         name="edge",
         near=True,
-    )(own, below_z, above_z, whole_sum, shifted, sigma, position, into, nodes)
-    (partial,) = call(
-        join_z,
-        [cube],
-        name="join_z",
-        near=True,
-        cost_estimate=pl.CostEstimate(flops=10**8, bytes_accessed=10**6, transcendentals=0),
-    )(beside, began, storage)
+    )(
+        own, below_z, above_z, whole_sum, shifted, sigma, targets, spread_rows, into, nodes
+    )
     got = lax.all_to_all(
         send.reshape(count, 1, 128), ("gy", "gz"), split_axis=0, concat_axis=0, tiled=True
     ).reshape(count, 128)
     xf, xb, yf, yb, rest = call(
         warm, [face, face, face, face, cube], [cube, cube], name="warm"
-    )(got, partial, warmth, storage)
+    )(got, beside, began, warmth, storage)
     xf, xb = exchange("gx", xf, xb)
     yf, yb = exchange("gy", yf, yb)
-    (beyond,) = call(
-        beyond_z,
-        [cube],
-        name="beyond_z",
-        near=True,
-        cost_estimate=pl.CostEstimate(flops=10**9, bytes_accessed=10**6, transcendentals=0),
-    )(got, beside, warmth)
-    (updated,) = call(finish, [cube], name="finish")(rest, storage, xf, xb, yf, yb, beyond)
-    (out,) = call(
+    out, beyond = call(
         merge,
-        [(3, *cube)],
+        [(3, *cube), cube],
         [(BLOCKS, 128, 128)],
         name="merge",
         cost_estimate=pl.CostEstimate(flops=10**9, bytes_accessed=10**6, transcendentals=0),
-    )(swept, final, near)
+    )(swept, final, near, got, beside, warmth)
+    (updated,) = call(finish, [cube], name="finish")(rest, storage, xf, xb, yf, yb, beyond)
     return out, updated
 
 

time: 60.8 us -> 59.8 us (0.984)
  blocking collectives: 0 us -> 22.6 us
  waiting for transfers between devices: 18.2 us -> 6.66 us
  starting transfers between devices: 25.3 us -> 14.7 us
  local copies, waits for them, and re-layouts: 2.33 us -> 1.36 us
    all_to_all x0 -> x1, blocking collectives: none -> 22.6 us  [local(): lax.all_to_all(send.reshape(count, 1, 128), ('gy', 'gz'), split_axis=0, c...]
    all_to_all x1 -> x0, starting transfers between devices: 10.6 us -> none  [local(): lax.all_to_all(send.reshape(count, 1, 128), ('gy', 'gz'), split_axis=0, c...]
    all_to_all x1 -> x0, waiting for transfers between devices: 10 us -> none  [local(): lax.all_to_all(send.reshape(count, 1, 128), ('gy', 'gz'), split_axis=0, c...]
    ppermute x5, waiting for transfers between devices: 5.63 us -> 4.35 us  [exchange(): lax.ppermute(bwd, names, backward)]
    unnamed x8 -> x4, local copies, waits for them, and re-layouts: 2.33 us -> 1.36 us
    pallas_call x1, Pallas kernels: 2.64 us -> 1.94 us  [local(): call(edge, [(BLOCKS, 3, 32, 128), (count, 128), cube], [(BLOCKS, 128, 128...]
    pallas_call x6 -> x5, Pallas kernels: 3.69 us -> 3.9 us  [the longest x1 1.86 us: local(): call(merge, [(3, *cube), cube], [(BLOCKS, 128, 128)], name='merge', cost_...]
  transfers between devices with their start and end apart: 13 -> 12, of which waited for: 7 -> 5; matrix products, arithmetic and copies ran while one was open for 0% -> 0% of each run, Pallas kernels for 13% -> 14%
where the time goes in v10:
time: 59.8 us; the launch traced here: 59.6 us
  blocking collectives  22.6 us (38%)
  starting transfers between devices  14.7 us (25%)
  Pallas kernels  13.5 us (23%)
  waiting for transfers between devices  6.66 us (11%)
  local copies, waits for them, and re-layouts  1.36 us (2%)
  between operations  0.73 us (1%)
    all_to_all x1, blocking collectives, local(): lax.all_to_all(send.reshape(count, 1, 128), ('gy', 'gz'), split_axis=0, c...  22.6 us
    ppermute x5, starting transfers between devices, exchange(): lax.ppermute(fwd, names, forward)  10.2 us
    ppermute x5, waiting for transfers between devices, exchange(): lax.ppermute(bwd, names, backward)  4.35 us
    ppermute x1, starting transfers between devices, exchange_z(): lax.ppermute(down, 'gz', [(j, i) for i, j in ring])  2.94 us
    pallas_call x1, Pallas kernels, local(): call(bulk, [(EM_SWEEPS, 3, 16, *layer)], name='bulk', near=True, cost_est...  2.64 us
    pallas_call x1, Pallas kernels, local(): call(edge, [(BLOCKS, 3, 32, 128), (count, 128), cube], [(BLOCKS, 128, 128...  1.94 us
    pallas_call x1, Pallas kernels, local(): call(merge, [(3, *cube), cube], [(BLOCKS, 128, 128)], name='merge', cost_...  1.86 us
    pallas_call x1, Pallas kernels, local(): call(rest_of_bulk, [(3, halo, *layer), cube, cube], [(EM_SWEEPS - 1, 3, h...  1.82 us
  transfers between devices with their start and end apart: 12, of which 5 were waited for; matrix products, arithmetic and copies ran while one was open for 0% of the time, Pallas kernels for 14%

profile of v10, /device:TPU:130, one launch (start us, length us, event | category | flops | bytes accessed | tf_op | source)
XLA Modules:
  0.0 59.6 jit_solution(129345110102560335)
XLA Ops:
  0.6 1.4 %pack_x.1 = (f32[30,16,128]{2,1,0:T(8,128)S(1)}, f32[30,16,128]{2,1,0:T(8,128)S(1)}, f32[4,16,16,128]{3,2,1,0:T(8,128)S(1)}, f32[3,16,16,128]{3,2,1,0:T(8,128)S(...) custom-call(f32[3,16,16,128]{3,2,1,0:T(8,128)} %refs_0_.1, ...), custom_call_target="tpu_custom_call" | custom-call | tf_op jit(solution)/shard_map/pack_x/pallas_call | solution.py:678
  2.0 2.4 %collective-permute-start = (f32[30,16,128]{2,1,0:T(8,128)S(1)}, f32[30,16,128]{2,1,0:T(8,128)S(1)}, u32[]{:S(2)}, u32[]{:S(2)}) collective-permute-start(f32[30,16,128]{2,1,0:T(8,128)S(1)} %get-tuple-element.43), channel_id=1, source_target_pairs={{0,64},{1,0},{2,66},{3,2},{4,68},{5,4},{6,70},{7,6},{8,72},{9,8},{... | collective-permute-start | bytes 737288 | tf_op jit(solution)/shard_map/ppermute | solution.py:662
  4.4 0.0 collective-permute-start.1
  4.4 0.1 pack_y.1
  4.5 1.5 %collective-permute-start.2 = (f32[16,32,128]{2,1,0:T(8,128)S(1)}, f32[16,32,128]{2,1,0:T(8,128)S(1)}, u32[]{:S(2)}, u32[]{:S(2)}) collective-permute-start(f32[16,32,128]{2,1,0:T(8,128)S(1)} %get-tuple-element.45), channel_id=1, source_target_pairs={{0,16},{1,0},{2,18},{3,2},{4,20},{5,4},{6,22},{7,6},{8,24},{9,8},{... | collective-permute-start | bytes 786440 | tf_op jit(solution)/shard_map/ppermute | solution.py:662
  6.0 0.5 collective-permute-start.3
  6.5 0.0 copy-start
  6.5 0.7 %copy-done = s32[1,1,1,256,1]{3,4,2,1,0:T(1,128)S(1)} copy-done((s32[1,1,1,256,1]{3,4,2,1,0:T(1,128)S(1)}, s32[1,1,1,256,1]{3,4,2,1,0:T(1,128)}, u32[]{:S(2)}) %copy-start) | copy-done | bytes 1048
  7.2 0.0 copy-start.1
  7.2 0.7 %copy-done.1 = s32[1,1,1,256]{3,2,1,0:T(1,128)S(1)} copy-done((s32[1,1,1,256]{3,2,1,0:T(1,128)S(1)}, s32[1,1,1,256]{3,2,1,0:T(1,128)}, u32[]{:S(2)}) %copy-start.1) | copy-done | bytes 1048
  7.9 0.5 place.1
  8.4 1.3 %collective-permute-done.xf = f32[30,16,128]{2,1,0:T(8,128)S(1)} collective-permute-done((f32[30,16,128]{2,1,0:T(8,128)S(1)}, f32[30,16,128]{2,1,0:T(8,128)S(1)}, u32[]{:S(2)}, u32[]{:S(2)}) %collective-permute-start) | collective-permute-done | bytes 245792 | tf_op jit(solution)/shard_map/ppermute | solution.py:662
  9.8 2.4 %collective-permute-done.1.xb = f32[30,16,128]{2,1,0:T(8,128)S(1)} collective-permute-done((f32[30,16,128]{2,1,0:T(8,128)S(1)}, f32[30,16,128]{2,1,0:T(8,128)S(1)}, u32[]{:S(2)}, u32[]{:S(2)}) %collective-permute-start.1) | collective-permute-done | bytes 245792 | tf_op jit(solution)/shard_map/ppermute | solution.py:662
  12.2 0.1 pack_corners.1
  12.2 1.5 %collective-permute-start.4 = (f32[9,32,128]{2,1,0:T(8,128)S(1)}, f32[9,32,128]{2,1,0:T(8,128)S(1)}, u32[]{:S(2)}, u32[]{:S(2)}) collective-permute-start(f32[9,32,128]{2,1,0:T(8,128)S(1)} %get-tuple-element.49), channel_id=1, source_target_pairs={{0,16},{1,0},{2,18},{3,2},{4,20},{5,4},{6,22},{7,6},{8,24},{9,8},{... | collective-permute-start | bytes 442376 | tf_op jit(solution)/shard_map/ppermute | solution.py:662
  13.7 0.5 collective-permute-start.5
  14.3 0.0 collective-permute-done.2.yf
  14.3 0.0 collective-permute-done.3.yb
  14.3 1.3 %pack_inner.1 = (f32[8,16,24,128]{3,2,1,0:T(8,128)S(1)}, f32[16,24,128]{2,1,0:T(8,128)S(1)}, f32[8,24,128]{2,1,0:T(8,128)S(1)}, f32[8,24,128]{2,1,0:T(8,128)S(1)}, f32[16,16,128]{2,1,0:T(8,128)S(1)}) custom-call(f32[3,16,16,128]{3,2,1,0:T(8,128)S(1)} %get-tuple-element.39.field, f32[4,16,16,128]{3,2,1,0:T(8,128)S(1)} %get-tuple-element.40.scaled, ...), custom_call_target="tpu_custom_call" | custom-call | tf_op jit(solution)/shard_map/pack_inner/pallas_call | solution.py:705
  15.6 2.6 %bulk.1.swept = f32[4,3,16,24,128]{4,3,2,1,0:T(8,128)S(1)} custom-call(f32[8,16,24,128]{3,2,1,0:T(8,128)S(1)} %get-tuple-element.47.whole.inner), custom_call_target="tpu_custom_call" | custom-call | flops 1000000000 | bytes 10000000 | tf_op jit(solution)/shard_map/bulk/pallas_call | solution.py:712
  18.3 0.0 collective-permute-done.4.cf
  18.3 0.6 %collective-permute-done.5.cb = f32[9,32,128]{2,1,0:T(8,128)S(1)} collective-permute-done((f32[9,32,128]{2,1,0:T(8,128)S(1)}, f32[9,32,128]{2,1,0:T(8,128)S(1)}, u32[]{:S(2)}, u32[]{:S(2)}) %collective-permute-start.5) | collective-permute-done | bytes 147488 | tf_op jit(solution)/shard_map/ppermute | solution.py:662
  18.9 0.4 pack_outer.1
  19.3 0.0 collective-permute-start.6
  19.3 2.9 %collective-permute-start.7 = (f32[13,24,128]{2,1,0:T(8,128)S(1)}, f32[13,24,128]{2,1,0:T(8,128)S(1)}, u32[]{:S(2)}, u32[]{:S(2)}) collective-permute-start(f32[13,24,128]{2,1,0:T(8,128)S(1)} %get-tuple-element.58), channel_id=1, source_target_pairs={{1,0},{2,1},{3,2},{4,3},{5,4},{6,5},{7,6},{8,7},{9,8},{10,9},{11,1... | collective-permute-start | bytes 479240 | tf_op jit(solution)/shard_map/ppermute | solution.py:668
  22.2 0.2 turn.1.own
  22.4 1.8 %rest_of_bulk.1 = (f32[3,9,24,128]{3,2,1,0:T(8,128)S(1)}, f32[16,16,128]{2,1,0:T(8,128)S(1)}, f32[16,16,128]{2,1,0:T(8,128)S(1)}) custom-call(f32[8,16,24,128]{3,2,1,0:T(8,128)S(1)} %get-tuple-element.47.whole.inner, f32[8,9,24,128]{3,2,1,0:T(8,128)S(1)} %get-tuple-element.53.outer, f32[4,3,16,24,128]{4,3,2,1,0:T(8,128)S(1)} %bulk.1.swept), custom_call_target="tpu_custom_call" | custom-call | flops 1000000000 | bytes 10000000 | tf_op jit(solution)/shard_map/rest_of_bulk/pallas_call | solution.py:726
  24.2 1.0 %collective-permute-done.6.below_z = f32[13,24,128]{2,1,0:T(8,128)S(1)} collective-permute-done((f32[13,24,128]{2,1,0:T(8,128)S(1)}, f32[13,24,128]{2,1,0:T(8,128)S(1)}, u32[]{:S(2)}, u32[]{:S(2)}) %collective-permute-start.6) | collective-permute-done | bytes 159776 | tf_op jit(solution)/shard_map/ppermute | solution.py:668
  25.2 0.0 collective-permute-done.7.above_z
  25.2 1.9 %edge.1 = (f32[5,3,32,128]{3,2,1,0:T(8,128)S(1)}, f32[576,128]{1,0:T(8,128)S(1)}, f32[16,16,128]{2,1,0:T(8,128)S(1)}) custom-call(f32[5,128,128]{2,1,0:T(8,128)S(1)} %turn.1.own, f32[13,24,128]{2,1,0:T(8,128)S(1)} %collective-permute-done.6.below_z, f32[13,24,128]{2,1,0:T(8,128)S(1)} %collective-permute-done.7.above_z, ...), custom_call_target="tpu_custom_call" | custom-call | tf_op jit(solution)/shard_map/edge/pallas_call | solution.py:742
  27.1 22.6 %all_to_all.5 = f32[576,1,128]{2,1,0:T(1,128)S(1)} all-to-all(f32[576,1,128]{2,1,0:T(1,128)S(1)} %bitcast.8), channel_id=1, replica_groups=mesh['gx'=8,'gy'=4,'gz'=16] {'gy','gz'}, dimensions={0} | all-to-all | bytes 589824 | tf_op jit(solution)/shard_map/all_to_all | solution.py:757
  49.8 0.6 %warm.1 = (f32[16,128]{1,0:T(8,128)S(1)}, f32[16,128]{1,0:T(8,128)S(1)}, f32[16,128]{1,0:T(8,128)S(1)}, f32[16,128]{1,0:T(8,128)S(1)}, f32[16,16,128]{2,1,0:T(8,128)S(1)}) custom-call(f32[576,128]{1,0:T(8,128)S(1)} %bitcast.6, f32[16,16,128]{2,1,0:T(8,128)S(1)} %get-tuple-element.67.beside, f32[16,16,128]{2,1,0:T(8,128)S(1)} %get-tuple-element.69.began, ...), custom_call_target="tpu_custom_call" | custom-call | tf_op jit(solution)/shard_map/warm/pallas_call | solution.py:760
  50.4 3.3 %collective-permute-start.8 = (f32[16,128]{1,0:T(8,128)S(1)}, f32[16,128]{1,0:T(8,128)S(1)}, u32[]{:S(2)}, u32[]{:S(2)}) collective-permute-start(f32[16,128]{1,0:T(8,128)S(1)} %get-tuple-element.71), channel_id=1, source_target_pairs={{0,64},{1,0},{2,66},{3,2},{4,68},{5,4},{6,70},{7,6},{8,72},{9,8},{... | collective-permute-start | bytes 24584 | tf_op jit(solution)/shard_map/ppermute | solution.py:662
  53.6 0.0 collective-permute-start.9
  53.6 1.6 %collective-permute-start.10 = (f32[16,128]{1,0:T(8,128)S(1)}, f32[16,128]{1,0:T(8,128)S(1)}, u32[]{:S(2)}, u32[]{:S(2)}) collective-permute-start(f32[16,128]{1,0:T(8,128)S(1)} %get-tuple-element.73), channel_id=1, source_target_pairs={{0,16},{1,0},{2,18},{3,2},{4,20},{5,4},{6,22},{7,6},{8,24},{9,8},{... | collective-permute-start | bytes 24584 | tf_op jit(solution)/shard_map/ppermute | solution.py:662
  55.2 0.4 collective-permute-start.11
  55.7 1.9 %merge.1 = (f32[3,16,16,128]{3,2,1,0:T(8,128)}, f32[16,16,128]{2,1,0:T(8,128)S(1)}) custom-call(f32[4,3,16,24,128]{4,3,2,1,0:T(8,128)S(1)} %bulk.1.swept, f32[3,9,24,128]{3,2,1,0:T(8,128)S(1)} %get-tuple-element.54.final, f32[5,3,32,128]{3,2,1,0:T(8,128)S(1)} %get-tuple-element.65.near, f32[576,128]{1,0:T(8,128)S(1)} %bitcast.7, ...), custom_call_target="tpu_custom_call" | custom-call | flops 1000000000 | bytes 1000000 | tf_op jit(solution)/shard_map/merge/pallas_call | solution.py:765
  57.5 0.0 collective-permute-done.8.xf
  57.5 0.0 collective-permute-done.9.xb
  57.5 0.0 collective-permute-done.10.yf
  57.5 1.3 %collective-permute-done.11.yb = f32[16,128]{1,0:T(8,128)S(1)} collective-permute-done((f32[16,128]{1,0:T(8,128)S(1)}, f32[16,128]{1,0:T(8,128)S(1)}, u32[]{:S(2)}, u32[]{:S(2)}) %collective-permute-start.11) | collective-permute-done | bytes 8224 | tf_op jit(solution)/shard_map/ppermute | solution.py:662
  58.9 0.7 %finish.1 = f32[16,16,128]{2,1,0:T(8,128)} custom-call(f32[16,16,128]{2,1,0:T(8,128)S(1)} %get-tuple-element.70.rest, f32[16,16,128]{2,1,0:T(8,128)S(1)} %get-tuple-element.42.storage, f32[16,128]{1,0:T(8,128)S(1)} %collective-permute-done.8.xf, f32[16,128]{1,0:T(8,128)S(1)} %collective-permute-done.9.xb, f32[16,128]{1,0:T(8,128)S(1)} %collective-permute-done.10.yf, ...), custom_call_target="tpu_custom_call" | custom-call | tf_op jit(solution)/shard_map/finish/pallas_call | solution.py:772
Async XLA Ops:
  2.0 7.7 %collective-permute-start = (f32[30,16,128]{2,1,0:T(8,128)S(1)}, f32[30,16,128]{2,1,0:T(8,128)S(1)}, u32[]{:S(2)}, u32[]{:S(2)}) collective-permute-start(f32[30,16,128]{2,1,0:T(8,128)S(1)} %get-tuple-element.43), channel_id=1, source_target_pairs={{0,64},{1,0},{2,66},{3,2},{4,68},{5,4},{6,70},{7,6},{8,72},{9,8},{... | collective-permute-start | bytes 737288 | tf_op jit(solution)/shard_map/ppermute | solution.py:662
  4.4 7.8 %collective-permute-start.1 = (f32[30,16,128]{2,1,0:T(8,128)S(1)}, f32[30,16,128]{2,1,0:T(8,128)S(1)}, u32[]{:S(2)}, u32[]{:S(2)}) collective-permute-start(f32[30,16,128]{2,1,0:T(8,128)S(1)} %get-tuple-element.44), channel_id=1, source_target_pairs={{64,0},{0,1},{66,2},{2,3},{68,4},{4,5},{70,6},{6,7},{72,8},{8,9},{... | collective-permute-start | bytes 737288 | tf_op jit(solution)/shard_map/ppermute | solution.py:662
  4.5 9.8 %collective-permute-start.2 = (f32[16,32,128]{2,1,0:T(8,128)S(1)}, f32[16,32,128]{2,1,0:T(8,128)S(1)}, u32[]{:S(2)}, u32[]{:S(2)}) collective-permute-start(f32[16,32,128]{2,1,0:T(8,128)S(1)} %get-tuple-element.45), channel_id=1, source_target_pairs={{0,16},{1,0},{2,18},{3,2},{4,20},{5,4},{6,22},{7,6},{8,24},{9,8},{... | collective-permute-start | bytes 786440 | tf_op jit(solution)/shard_map/ppermute | solution.py:662
  6.0 8.3 %collective-permute-start.3 = (f32[16,32,128]{2,1,0:T(8,128)S(1)}, f32[16,32,128]{2,1,0:T(8,128)S(1)}, u32[]{:S(2)}, u32[]{:S(2)}) collective-permute-start(f32[16,32,128]{2,1,0:T(8,128)S(1)} %get-tuple-element.46), channel_id=1, source_target_pairs={{16,0},{0,1},{18,2},{2,3},{20,4},{4,5},{22,6},{6,7},{24,8},{8,9},{... | collective-permute-start | bytes 786440 | tf_op jit(solution)/shard_map/ppermute | solution.py:662
  6.5 0.7 %copy-start = (s32[1,1,1,256,1]{3,4,2,1,0:T(1,128)S(1)}, s32[1,1,1,256,1]{3,4,2,1,0:T(1,128)}, u32[]{:S(2)}) copy-start(s32[1,1,1,256,1]{3,4,2,1,0:T(1,128)} %param.12) | copy-start | bytes 3076
  7.2 0.7 %copy-start.1 = (s32[1,1,1,256]{3,2,1,0:T(1,128)S(1)}, s32[1,1,1,256]{3,2,1,0:T(1,128)}, u32[]{:S(2)}) copy-start(s32[1,1,1,256]{3,2,1,0:T(1,128)} %param.13) | copy-start | bytes 3076
  12.2 6.0 %collective-permute-start.4 = (f32[9,32,128]{2,1,0:T(8,128)S(1)}, f32[9,32,128]{2,1,0:T(8,128)S(1)}, u32[]{:S(2)}, u32[]{:S(2)}) collective-permute-start(f32[9,32,128]{2,1,0:T(8,128)S(1)} %get-tuple-element.49), channel_id=1, source_target_pairs={{0,16},{1,0},{2,18},{3,2},{4,20},{5,4},{6,22},{7,6},{8,24},{9,8},{... | collective-permute-start | bytes 442376 | tf_op jit(solution)/shard_map/ppermute | solution.py:662
  13.7 5.1 %collective-permute-start.5 = (f32[9,32,128]{2,1,0:T(8,128)S(1)}, f32[9,32,128]{2,1,0:T(8,128)S(1)}, u32[]{:S(2)}, u32[]{:S(2)}) collective-permute-start(f32[9,32,128]{2,1,0:T(8,128)S(1)} %get-tuple-element.50), channel_id=1, source_target_pairs={{16,0},{0,1},{18,2},{2,3},{20,4},{4,5},{22,6},{6,7},{24,8},{8,9},{... | collective-permute-start | bytes 442376 | tf_op jit(solution)/shard_map/ppermute | solution.py:662
  19.3 5.9 %collective-permute-start.6 = (f32[13,24,128]{2,1,0:T(8,128)S(1)}, f32[13,24,128]{2,1,0:T(8,128)S(1)}, u32[]{:S(2)}, u32[]{:S(2)}) collective-permute-start(f32[13,24,128]{2,1,0:T(8,128)S(1)} %get-tuple-element.57), channel_id=1, source_target_pairs={{0,1},{1,2},{2,3},{3,4},{4,5},{5,6},{6,7},{7,8},{8,9},{9,10},{10,1... | collective-permute-start | bytes 479240 | tf_op jit(solution)/shard_map/ppermute | solution.py:668
  19.3 5.9 %collective-permute-start.7 = (f32[13,24,128]{2,1,0:T(8,128)S(1)}, f32[13,24,128]{2,1,0:T(8,128)S(1)}, u32[]{:S(2)}, u32[]{:S(2)}) collective-permute-start(f32[13,24,128]{2,1,0:T(8,128)S(1)} %get-tuple-element.58), channel_id=1, source_target_pairs={{1,0},{2,1},{3,2},{4,3},{5,4},{6,5},{7,6},{8,7},{9,8},{10,9},{11,1... | collective-permute-start | bytes 479240 | tf_op jit(solution)/shard_map/ppermute | solution.py:668
  50.4 7.1 %collective-permute-start.8 = (f32[16,128]{1,0:T(8,128)S(1)}, f32[16,128]{1,0:T(8,128)S(1)}, u32[]{:S(2)}, u32[]{:S(2)}) collective-permute-start(f32[16,128]{1,0:T(8,128)S(1)} %get-tuple-element.71), channel_id=1, source_target_pairs={{0,64},{1,0},{2,66},{3,2},{4,68},{5,4},{6,70},{7,6},{8,72},{9,8},{... | collective-permute-start | bytes 24584 | tf_op jit(solution)/shard_map/ppermute | solution.py:662
  53.6 3.9 %collective-permute-start.9 = (f32[16,128]{1,0:T(8,128)S(1)}, f32[16,128]{1,0:T(8,128)S(1)}, u32[]{:S(2)}, u32[]{:S(2)}) collective-permute-start(f32[16,128]{1,0:T(8,128)S(1)} %get-tuple-element.72), channel_id=1, source_target_pairs={{64,0},{0,1},{66,2},{2,3},{68,4},{4,5},{70,6},{6,7},{72,8},{8,9},{... | collective-permute-start | bytes 24584 | tf_op jit(solution)/shard_map/ppermute | solution.py:662
  53.6 3.9 %collective-permute-start.10 = (f32[16,128]{1,0:T(8,128)S(1)}, f32[16,128]{1,0:T(8,128)S(1)}, u32[]{:S(2)}, u32[]{:S(2)}) collective-permute-start(f32[16,128]{1,0:T(8,128)S(1)} %get-tuple-element.73), channel_id=1, source_target_pairs={{0,16},{1,0},{2,18},{3,2},{4,20},{5,4},{6,22},{7,6},{8,24},{9,8},{... | collective-permute-start | bytes 24584 | tf_op jit(solution)/shard_map/ppermute | solution.py:662
  55.2 3.7 %collective-permute-start.11 = (f32[16,128]{1,0:T(8,128)S(1)}, f32[16,128]{1,0:T(8,128)S(1)}, u32[]{:S(2)}, u32[]{:S(2)}) collective-permute-start(f32[16,128]{1,0:T(8,128)S(1)} %get-tuple-element.74), channel_id=1, source_target_pairs={{16,0},{0,1},{18,2},{2,3},{20,4},{4,5},{22,6},{6,7},{24,8},{8,9},{... | collective-permute-start | bytes 24584 | tf_op jit(solution)/shard_map/ppermute | solution.py:662

commit v11 on v10

--- a/solution.py
+++ b/solution.py
@@ -86,18 +86,25 @@
     bwd[at] = jnp.where(first, down, up)
 
 
-def y_tiles(v, first, fwd, bwd, at):
+def y_tiles(v):
     row = rows((8, 128))
     low_half = row < 4
     tops = [a[8:16] for a in v]
     ends = [a[0:8] for a in v]
+    ups, downs = [], []
     for pair in range(4):
         a, b = 2 * pair, 2 * pair + 1
-        up = jnp.where(low_half, roll(tops[b], 4, 0), tops[a])
+        ups.append(jnp.where(low_half, roll(tops[b], 4, 0), tops[a]))
         down = jnp.where(low_half, ends[a], roll(ends[b], 4, 0))
         if pair == 3:
             down = jnp.where(row == 5, roll(ends[0], 1, 0), down)
             down = jnp.where(row == 6, roll(ends[2], 2, 0), down)
+        downs.append(down)
+    return ups, downs
+
+
+def put_y_tiles(tiles, first, fwd, bwd, at):
+    for pair, (up, down) in enumerate(zip(*tiles)):
         part = pl.ds(8 * pair, 8)
         fwd[at, part] = jnp.where(first, up, down)
         bwd[at, part] = jnp.where(first, down, up)
@@ -139,7 +146,7 @@
 
     def step(x, carry):
         v = [field[f, x] for f in range(3)] + [scaled[f, x] for f in range(4)] + [warmth[x]]
-        y_tiles(v, first, yf, yb, x)
+        put_y_tiles(y_tiles(v), first, yf, yb, x)
         return carry
 
     lax.fori_loop(0, 16, step, 0, unroll=4)
@@ -166,9 +173,18 @@
     del targets
     halo = Halo(xf, xb)
     zero = jnp.zeros((16, 128), F32)
-    for number, x in enumerate(HALO_X):
+    row = rows((8, 128)) % 4
+    tiles = {}
+    for x in HALO_X:
         v = [halo.layer(f, x) for f in range(7)]
-        y_tiles([zero if a is None else a for a in v] + [zero], halo.first, fwd, bwd, number)
+        tiles[x] = y_tiles([zero if a is None else a for a in v] + [zero])
+    for at, (x, sharer, shift) in enumerate(CORNERS):
+        ups, downs = tiles[x]
+        if sharer is not None:
+            other_ups, other_downs = tiles[sharer]
+            ups = [jnp.where(row >= 4 - shift, a, roll(b, -shift, 0)) for a, b in zip(ups, other_ups)]
+            downs = [jnp.where(row < shift, a, roll(b, shift, 0)) for a, b in zip(downs, other_downs)]
+        put_y_tiles((ups, downs), halo.first, fwd, bwd, at)
 
 
 def y_halo(first, got, at, pair):
@@ -180,6 +196,9 @@
     return lower, upper
 
 
+CORNERS = (
+    (-3, None, 0), (-2, None, 0), (-1, None, 0), (16, None, 0), (17, None, 0), (19, -4, 2), (18, 20, 3),
+)
 HALO_X = tuple(range(-LOW, 0)) + tuple(range(16, 16 + HIGH))
 X_ALL = LOW + 16 + HIGH
 BLOCKS = 5
@@ -187,12 +206,13 @@
 X_PAIRS = (X_ALL + 1) // 2
 
 
-def y_slabs(first, got, at, v):
+def y_slabs(first, got, at, v, shift=0):
     low_half = rows((8, 128)) < 4
     window = lanes((24, 128)) // 16
     slabs, acc = [], None
     for pair in range(4):
         lower, upper = y_halo(first, got, at, pair)
+        lower, upper = roll(lower, shift, 0), roll(upper, -shift, 0)
         ends = [jnp.where(low_half, upper, lower)]
         if pair < 3:
             ends.append(roll(jnp.where(low_half, lower, upper), 4, 0))
@@ -256,10 +276,14 @@
     halo = Halo(xf, xb)
     zero = jnp.zeros((16, 128), F32)
     windows = []
+    place_of = {}
+    for at, (x, sharer, shift) in enumerate(CORNERS):
+        place_of[x], place_of[sharer] = (at, 0), (at, shift)
     for number, x in enumerate(HALO_X):
         v = [halo.layer(f, x) for f in range(7)]
+        at, shift = place_of[x]
         slabs, acc = y_slabs(
-            halo.first, (cf, cb), number, [zero if a is None else a for a in v] + [zero]
+            halo.first, (cf, cb), at, [zero if a is None else a for a in v] + [zero], shift
         )
         for f in range(8):
             whole[f, number] = slabs[f]
@@ -313,7 +337,7 @@
     def get(number, f, x):
         return whole[f, x] if number == 0 else swept[number - 1, f, x]
 
-    for number in range(EM_SWEEPS):
+    for number in range(EM_SWEEPS - 1):
 
         def step(x, carry, number=number):
             new, carry = lane_sweep(get, number, x, carry)
@@ -334,27 +358,31 @@
 
 
 def rest_of_bulk(inner, outer, swept, final, whole_sum, shifted, others):
-    def target(number):
-        return final if number == EM_SWEEPS else others.at[number - 1]
-
     def get(number, f, x):
         if number == 0:
             return inner[f, x] if 0 <= x < 16 else outer[f, HALO_X.index(x)]
+        if number == EM_SWEEPS:
+            return final[f, x]
         if number <= x <= 15 - number:
             return swept[number - 1, f, x]
         low, high = swept_low(number), swept_high(number)
-        return target(number)[f, low.index(x) if x < number else len(low) + high.index(x)]
+        return others[number - 1, f, low.index(x) if x < number else len(low) + high.index(x)]
 
     for number in range(EM_SWEEPS):
-        to = target(number + 1)
         at = 0
-        for layers in (swept_low(number + 1), swept_high(number + 1)):
+        ranges = (swept_low(number + 1), swept_high(number + 1))
+        if number == EM_SWEEPS - 1:
+            ranges = (range(17),)
+        for layers in ranges:
             _, c = lane_curls(get, number, layers[0] - 1)
             carry = c[1], c[2]
             for x in layers:
                 new, carry = lane_sweep(get, number, x, carry)
                 for f in range(3):
-                    to[f, at] = new[f]
+                    if number == EM_SWEEPS - 1:
+                        final[f, x] = new[f]
+                    else:
+                        others[number, f, at] = new[f]
                 at += 1
 
     for x in range(16):
@@ -493,7 +521,7 @@
     send[pl.ds(CAP, groups, stride=CAP + 1), :] = spread_out(hit, ends, nodes[...])
 
 
-def merge(swept, final, near, got, beside, warmth, out, beyond, stack):
+def merge(final, near, got, beside, warmth, out, beyond, stack):
     beyond_z(got, beside, warmth, beyond)
     for block in range(BLOCKS):
         for f in range(3):
@@ -508,12 +536,7 @@
         block, lane_at = of_layer(x + LOW)
         windows = stack[block, lane_at + LOW : lane_at + LOW + 16, :]
         for f in range(3):
-            if EM_SWEEPS <= x <= 15 - EM_SWEEPS:
-                inner = swept[EM_SWEEPS - 1, f, x, 0:16, :]
-            else:
-                low, high = swept_low(EM_SWEEPS), swept_high(EM_SWEEPS)
-                at = low.index(x) if x in low else len(low) + high.index(x)
-                inner = final[f, at, 0:16, :]
+            inner = final[f, x, 0:16, :]
             out[f, x] = jnp.where(outer, roll(windows, -32 * f, 1), inner)
 
 
@@ -673,7 +696,7 @@
     count = groups * (CAP + 1)
     cube = (16, 16, 128)
     face = (16, 128)
-    x_message, y_message, corners = (X_LAYERS, 16, 128), (16, 32, 128), (len(HALO_X), 32, 128)
+    x_message, y_message, corners = (X_LAYERS, 16, 128), (16, 32, 128), (len(CORNERS), 32, 128)
     here = (field, sigma, warmth, storage, source)
     xf, xb, scaled, field, sigma, warmth, storage = call(
         pack_x,
@@ -711,7 +734,7 @@
     )(field, scaled, warmth, storage, xf, xb, yf, yb)
     (swept,) = call(
         bulk,
-        [(EM_SWEEPS, 3, 16, *layer)],
+        [(EM_SWEEPS - 1, 3, 16, *layer)],
         name="bulk",
         near=True,
         cost_estimate=pl.CostEstimate(flops=10**9, bytes_accessed=10**7, transcendentals=0),
@@ -725,7 +748,7 @@
     below_z, above_z = exchange_z(up, down)
     final, whole_sum, shifted = call(
         rest_of_bulk,
-        [(3, halo, *layer), cube, cube],
+        [(3, 17, *layer), cube, cube],
         [(EM_SWEEPS - 1, 3, halo, *layer)],
         name="rest_of_bulk",
         near=True,
@@ -768,7 +791,7 @@
         [(BLOCKS, 128, 128)],
         name="merge",
         cost_estimate=pl.CostEstimate(flops=10**9, bytes_accessed=10**6, transcendentals=0),
-    )(swept, final, near, got, beside, warmth)
+    )(final, near, got, beside, warmth)
     (updated,) = call(finish, [cube], name="finish")(rest, storage, xf, xb, yf, yb, beyond)
     return out, updated
 

time: 59.8 us -> 59.4 us (level)
  local copies, waits for them, and re-layouts: 1.36 us -> 0.01 us
  waiting for transfers between devices: 6.66 us -> 7.5 us
    ppermute x5, waiting for transfers between devices: 1.36 us -> 2.71 us  [exchange(): lax.ppermute(fwd, names, forward)]
    unnamed x4, local copies, waits for them, and re-layouts: 1.36 us -> 0.01 us
  transfers between devices with their start and end apart: 12 -> 12, of which waited for: 5 -> 5; matrix products, arithmetic and copies ran while one was open for 0% -> 0% of each run, Pallas kernels for 14% -> 15%
where the time goes in v11:
time: 59.4 us; the launch traced here: 59.3 us
  blocking collectives  22.6 us (38%)
  starting transfers between devices  14.7 us (25%)
  Pallas kernels  13.7 us (23%)
  waiting for transfers between devices  7.5 us (13%)
  between operations  0.74 us (1%)
    all_to_all x1, blocking collectives, local(): lax.all_to_all(send.reshape(count, 1, 128), ('gy', 'gz'), split_axis=0, c...  22.6 us
    ppermute x5, starting transfers between devices, exchange(): lax.ppermute(fwd, names, forward)  10.2 us
    ppermute x5, waiting for transfers between devices, exchange(): lax.ppermute(bwd, names, backward)  4.42 us
    ppermute x1, starting transfers between devices, exchange_z(): lax.ppermute(down, 'gz', [(j, i) for i, j in ring])  2.94 us
    ppermute x5, waiting for transfers between devices, exchange(): lax.ppermute(fwd, names, forward)  2.71 us
    pallas_call x1, Pallas kernels, local(): call(rest_of_bulk, [(3, 17, *layer), cube, cube], [(EM_SWEEPS - 1, 3, hal...  2.41 us
    pallas_call x1, Pallas kernels, local(): call(bulk, [(EM_SWEEPS - 1, 3, 16, *layer)], name='bulk', near=True, cost...  2.22 us
    pallas_call x1, Pallas kernels, local(): call(edge, [(BLOCKS, 3, 32, 128), (count, 128), cube], [(BLOCKS, 128, 128...  1.94 us
  transfers between devices with their start and end apart: 12, of which 5 were waited for; matrix products, arithmetic and copies ran while one was open for 0% of the time, Pallas kernels for 15%

profile of v11, /device:TPU:130, one launch (start us, length us, event | category | flops | bytes accessed | tf_op | source)
XLA Modules:
  0.0 59.3 jit_solution(1330067176952936097)
XLA Ops:
  0.6 0.0 copy-start.1
  0.6 0.0 copy-start
  0.7 1.4 %pack_x.1 = (f32[30,16,128]{2,1,0:T(8,128)S(1)}, f32[30,16,128]{2,1,0:T(8,128)S(1)}, f32[4,16,16,128]{3,2,1,0:T(8,128)S(1)}, f32[3,16,16,128]{3,2,1,0:T(8,128)S(...) custom-call(f32[3,16,16,128]{3,2,1,0:T(8,128)} %refs_0_.1, ...), custom_call_target="tpu_custom_call" | custom-call | tf_op jit(solution)/shard_map/pack_x/pallas_call | solution.py:701
  2.0 2.4 %collective-permute-start = (f32[30,16,128]{2,1,0:T(8,128)S(1)}, f32[30,16,128]{2,1,0:T(8,128)S(1)}, u32[]{:S(2)}, u32[]{:S(2)}) collective-permute-start(f32[30,16,128]{2,1,0:T(8,128)S(1)} %get-tuple-element.43), channel_id=1, source_target_pairs={{0,64},{1,0},{2,66},{3,2},{4,68},{5,4},{6,70},{7,6},{8,72},{9,8},{... | collective-permute-start | bytes 737288 | tf_op jit(solution)/shard_map/ppermute | solution.py:685
  4.4 0.0 collective-permute-start.1
  4.4 0.1 pack_y.1
  4.5 1.5 %collective-permute-start.2 = (f32[16,32,128]{2,1,0:T(8,128)S(1)}, f32[16,32,128]{2,1,0:T(8,128)S(1)}, u32[]{:S(2)}, u32[]{:S(2)}) collective-permute-start(f32[16,32,128]{2,1,0:T(8,128)S(1)} %get-tuple-element.45), channel_id=1, source_target_pairs={{0,16},{1,0},{2,18},{3,2},{4,20},{5,4},{6,22},{7,6},{8,24},{9,8},{... | collective-permute-start | bytes 786440 | tf_op jit(solution)/shard_map/ppermute | solution.py:685
  6.0 0.5 collective-permute-start.3
  6.6 0.0 copy-done.1
  6.6 0.0 copy-done
  6.6 0.5 place.1
  7.1 2.7 %collective-permute-done.xf = f32[30,16,128]{2,1,0:T(8,128)S(1)} collective-permute-done((f32[30,16,128]{2,1,0:T(8,128)S(1)}, f32[30,16,128]{2,1,0:T(8,128)S(1)}, u32[]{:S(2)}, u32[]{:S(2)}) %collective-permute-start) | collective-permute-done | bytes 245792 | tf_op jit(solution)/shard_map/ppermute | solution.py:685
  9.8 2.4 %collective-permute-done.1.xb = f32[30,16,128]{2,1,0:T(8,128)S(1)} collective-permute-done((f32[30,16,128]{2,1,0:T(8,128)S(1)}, f32[30,16,128]{2,1,0:T(8,128)S(1)}, u32[]{:S(2)}, u32[]{:S(2)}) %collective-permute-start.1) | collective-permute-done | bytes 245792 | tf_op jit(solution)/shard_map/ppermute | solution.py:685
  12.2 0.1 pack_corners.1
  12.3 1.5 %collective-permute-start.4 = (f32[7,32,128]{2,1,0:T(8,128)S(1)}, f32[7,32,128]{2,1,0:T(8,128)S(1)}, u32[]{:S(2)}, u32[]{:S(2)}) collective-permute-start(f32[7,32,128]{2,1,0:T(8,128)S(1)} %get-tuple-element.49), channel_id=1, source_target_pairs={{0,16},{1,0},{2,18},{3,2},{4,20},{5,4},{6,22},{7,6},{8,24},{9,8},{... | collective-permute-start | bytes 344072 | tf_op jit(solution)/shard_map/ppermute | solution.py:685
  13.8 0.5 collective-permute-start.5
  14.3 0.0 collective-permute-done.2.yf
  14.3 0.0 collective-permute-done.3.yb
  14.3 1.3 %pack_inner.1 = (f32[8,16,24,128]{3,2,1,0:T(8,128)S(1)}, f32[16,24,128]{2,1,0:T(8,128)S(1)}, f32[8,24,128]{2,1,0:T(8,128)S(1)}, f32[8,24,128]{2,1,0:T(8,128)S(1)}, f32[16,16,128]{2,1,0:T(8,128)S(1)}) custom-call(f32[3,16,16,128]{3,2,1,0:T(8,128)S(1)} %get-tuple-element.39.field, f32[4,16,16,128]{3,2,1,0:T(8,128)S(1)} %get-tuple-element.40.scaled, ...), custom_call_target="tpu_custom_call" | custom-call | tf_op jit(solution)/shard_map/pack_inner/pallas_call | solution.py:728
  15.7 2.2 %bulk.1.swept = f32[3,3,16,24,128]{4,3,2,1,0:T(8,128)S(1)} custom-call(f32[8,16,24,128]{3,2,1,0:T(8,128)S(1)} %get-tuple-element.47.whole.inner), custom_call_target="tpu_custom_call" | custom-call | flops 1000000000 | bytes 10000000 | tf_op jit(solution)/shard_map/bulk/pallas_call | solution.py:735
  17.9 0.0 collective-permute-done.4.cf
  17.9 0.7 %collective-permute-done.5.cb = f32[7,32,128]{2,1,0:T(8,128)S(1)} collective-permute-done((f32[7,32,128]{2,1,0:T(8,128)S(1)}, f32[7,32,128]{2,1,0:T(8,128)S(1)}, u32[]{:S(2)}, u32[]{:S(2)}) %collective-permute-start.5) | collective-permute-done | bytes 114720 | tf_op jit(solution)/shard_map/ppermute | solution.py:685
  18.6 0.4 pack_outer.1
  18.9 0.0 collective-permute-start.6
  19.0 2.9 %collective-permute-start.7 = (f32[13,24,128]{2,1,0:T(8,128)S(1)}, f32[13,24,128]{2,1,0:T(8,128)S(1)}, u32[]{:S(2)}, u32[]{:S(2)}) collective-permute-start(f32[13,24,128]{2,1,0:T(8,128)S(1)} %get-tuple-element.58), channel_id=1, source_target_pairs={{1,0},{2,1},{3,2},{4,3},{5,4},{6,5},{7,6},{8,7},{9,8},{10,9},{11,1... | collective-permute-start | bytes 479240 | tf_op jit(solution)/shard_map/ppermute | solution.py:691
  21.9 0.2 turn.1.own
  22.1 2.4 %rest_of_bulk.1 = (f32[3,17,24,128]{3,2,1,0:T(8,128)S(1)}, f32[16,16,128]{2,1,0:T(8,128)S(1)}, f32[16,16,128]{2,1,0:T(8,128)S(1)}) custom-call(f32[8,16,24,128]{3,2,1,0:T(8,128)S(1)} %get-tuple-element.47.whole.inner, f32[8,9,24,128]{3,2,1,0:T(8,128)S(1)} %get-tuple-element.53.outer, f32[3,3,16,24,128]{4,3,2,1,0:T(8,128)S(1)} %bulk.1.swept), custom_call_target="tpu_custom_call" | custom-call | flops 1000000000 | bytes 10000000 | tf_op jit(solution)/shard_map/rest_of_bulk/pallas_call | solution.py:749
  24.5 0.4 collective-permute-done.6.below_z
  24.9 0.0 collective-permute-done.7.above_z
  24.9 1.9 %edge.1 = (f32[5,3,32,128]{3,2,1,0:T(8,128)S(1)}, f32[576,128]{1,0:T(8,128)S(1)}, f32[16,16,128]{2,1,0:T(8,128)S(1)}) custom-call(f32[5,128,128]{2,1,0:T(8,128)S(1)} %turn.1.own, f32[13,24,128]{2,1,0:T(8,128)S(1)} %collective-permute-done.6.below_z, f32[13,24,128]{2,1,0:T(8,128)S(1)} %collective-permute-done.7.above_z, ...), custom_call_target="tpu_custom_call" | custom-call | tf_op jit(solution)/shard_map/edge/pallas_call | solution.py:765
  26.8 22.6 %all_to_all.5 = f32[576,1,128]{2,1,0:T(1,128)S(1)} all-to-all(f32[576,1,128]{2,1,0:T(1,128)S(1)} %bitcast.8), channel_id=1, replica_groups=mesh['gx'=8,'gy'=4,'gz'=16] {'gy','gz'}, dimensions={0} | all-to-all | bytes 589824 | tf_op jit(solution)/shard_map/all_to_all | solution.py:780
  49.4 0.6 %warm.1 = (f32[16,128]{1,0:T(8,128)S(1)}, f32[16,128]{1,0:T(8,128)S(1)}, f32[16,128]{1,0:T(8,128)S(1)}, f32[16,128]{1,0:T(8,128)S(1)}, f32[16,16,128]{2,1,0:T(8,128)S(1)}) custom-call(f32[576,128]{1,0:T(8,128)S(1)} %bitcast.6, f32[16,16,128]{2,1,0:T(8,128)S(1)} %get-tuple-element.67.beside, f32[16,16,128]{2,1,0:T(8,128)S(1)} %get-tuple-element.69.began, ...), custom_call_target="tpu_custom_call" | custom-call | tf_op jit(solution)/shard_map/warm/pallas_call | solution.py:783
  50.1 3.2 %collective-permute-start.8 = (f32[16,128]{1,0:T(8,128)S(1)}, f32[16,128]{1,0:T(8,128)S(1)}, u32[]{:S(2)}, u32[]{:S(2)}) collective-permute-start(f32[16,128]{1,0:T(8,128)S(1)} %get-tuple-element.71), channel_id=1, source_target_pairs={{0,64},{1,0},{2,66},{3,2},{4,68},{5,4},{6,70},{7,6},{8,72},{9,8},{... | collective-permute-start | bytes 24584 | tf_op jit(solution)/shard_map/ppermute | solution.py:685
  53.3 0.0 collective-permute-start.9
  53.3 1.6 %collective-permute-start.10 = (f32[16,128]{1,0:T(8,128)S(1)}, f32[16,128]{1,0:T(8,128)S(1)}, u32[]{:S(2)}, u32[]{:S(2)}) collective-permute-start(f32[16,128]{1,0:T(8,128)S(1)} %get-tuple-element.73), channel_id=1, source_target_pairs={{0,16},{1,0},{2,18},{3,2},{4,20},{5,4},{6,22},{7,6},{8,24},{9,8},{... | collective-permute-start | bytes 24584 | tf_op jit(solution)/shard_map/ppermute | solution.py:685
  54.9 0.4 collective-permute-start.11
  55.3 1.9 %merge.1 = (f32[3,16,16,128]{3,2,1,0:T(8,128)}, f32[16,16,128]{2,1,0:T(8,128)S(1)}) custom-call(f32[3,17,24,128]{3,2,1,0:T(8,128)S(1)} %get-tuple-element.54.final, f32[5,3,32,128]{3,2,1,0:T(8,128)S(1)} %get-tuple-element.65.near, f32[576,128]{1,0:T(8,128)S(1)} %bitcast.7, f32[16,16,128]{2,1,0:T(8,128)S(1)} %get-tuple-element.67.beside, ...), custom_call_target="tpu_custom_call" | custom-call | flops 1000000000 | bytes 1000000 | tf_op jit(solution)/shard_map/merge/pallas_call | solution.py:788
  57.2 0.0 collective-permute-done.8.xf
  57.2 0.0 collective-permute-done.9.xb
  57.2 0.0 collective-permute-done.10.yf
  57.2 1.3 %collective-permute-done.11.yb = f32[16,128]{1,0:T(8,128)S(1)} collective-permute-done((f32[16,128]{1,0:T(8,128)S(1)}, f32[16,128]{1,0:T(8,128)S(1)}, u32[]{:S(2)}, u32[]{:S(2)}) %collective-permute-start.11) | collective-permute-done | bytes 8224 | tf_op jit(solution)/shard_map/ppermute | solution.py:685
  58.6 0.7 %finish.1 = f32[16,16,128]{2,1,0:T(8,128)} custom-call(f32[16,16,128]{2,1,0:T(8,128)S(1)} %get-tuple-element.70.rest, f32[16,16,128]{2,1,0:T(8,128)S(1)} %get-tuple-element.42.storage, f32[16,128]{1,0:T(8,128)S(1)} %collective-permute-done.8.xf, f32[16,128]{1,0:T(8,128)S(1)} %collective-permute-done.9.xb, f32[16,128]{1,0:T(8,128)S(1)} %collective-permute-done.10.yf, ...), custom_call_target="tpu_custom_call" | custom-call | tf_op jit(solution)/shard_map/finish/pallas_call | solution.py:795
Async XLA Ops:
  0.6 5.9 %copy-start.1 = (s32[1,1,1,256]{3,2,1,0:T(1,128)S(1)}, s32[1,1,1,256]{3,2,1,0:T(1,128)}, u32[]{:S(2)}) copy-start(s32[1,1,1,256]{3,2,1,0:T(1,128)} %param.13) | copy-start | bytes 3076
  0.6 5.9 %copy-start = (s32[1,1,1,256,1]{3,4,2,1,0:T(1,128)S(1)}, s32[1,1,1,256,1]{3,4,2,1,0:T(1,128)}, u32[]{:S(2)}) copy-start(s32[1,1,1,256,1]{3,4,2,1,0:T(1,128)} %param.12) | copy-start | bytes 3076
  2.0 7.7 %collective-permute-start = (f32[30,16,128]{2,1,0:T(8,128)S(1)}, f32[30,16,128]{2,1,0:T(8,128)S(1)}, u32[]{:S(2)}, u32[]{:S(2)}) collective-permute-start(f32[30,16,128]{2,1,0:T(8,128)S(1)} %get-tuple-element.43), channel_id=1, source_target_pairs={{0,64},{1,0},{2,66},{3,2},{4,68},{5,4},{6,70},{7,6},{8,72},{9,8},{... | collective-permute-start | bytes 737288 | tf_op jit(solution)/shard_map/ppermute | solution.py:685
  4.4 7.8 %collective-permute-start.1 = (f32[30,16,128]{2,1,0:T(8,128)S(1)}, f32[30,16,128]{2,1,0:T(8,128)S(1)}, u32[]{:S(2)}, u32[]{:S(2)}) collective-permute-start(f32[30,16,128]{2,1,0:T(8,128)S(1)} %get-tuple-element.44), channel_id=1, source_target_pairs={{64,0},{0,1},{66,2},{2,3},{68,4},{4,5},{70,6},{6,7},{72,8},{8,9},{... | collective-permute-start | bytes 737288 | tf_op jit(solution)/shard_map/ppermute | solution.py:685
  4.5 9.8 %collective-permute-start.2 = (f32[16,32,128]{2,1,0:T(8,128)S(1)}, f32[16,32,128]{2,1,0:T(8,128)S(1)}, u32[]{:S(2)}, u32[]{:S(2)}) collective-permute-start(f32[16,32,128]{2,1,0:T(8,128)S(1)} %get-tuple-element.45), channel_id=1, source_target_pairs={{0,16},{1,0},{2,18},{3,2},{4,20},{5,4},{6,22},{7,6},{8,24},{9,8},{... | collective-permute-start | bytes 786440 | tf_op jit(solution)/shard_map/ppermute | solution.py:685
  6.0 8.3 %collective-permute-start.3 = (f32[16,32,128]{2,1,0:T(8,128)S(1)}, f32[16,32,128]{2,1,0:T(8,128)S(1)}, u32[]{:S(2)}, u32[]{:S(2)}) collective-permute-start(f32[16,32,128]{2,1,0:T(8,128)S(1)} %get-tuple-element.46), channel_id=1, source_target_pairs={{16,0},{0,1},{18,2},{2,3},{20,4},{4,5},{22,6},{6,7},{24,8},{8,9},{... | collective-permute-start | bytes 786440 | tf_op jit(solution)/shard_map/ppermute | solution.py:685
  12.3 5.6 %collective-permute-start.4 = (f32[7,32,128]{2,1,0:T(8,128)S(1)}, f32[7,32,128]{2,1,0:T(8,128)S(1)}, u32[]{:S(2)}, u32[]{:S(2)}) collective-permute-start(f32[7,32,128]{2,1,0:T(8,128)S(1)} %get-tuple-element.49), channel_id=1, source_target_pairs={{0,16},{1,0},{2,18},{3,2},{4,20},{5,4},{6,22},{7,6},{8,24},{9,8},{... | collective-permute-start | bytes 344072 | tf_op jit(solution)/shard_map/ppermute | solution.py:685
  13.8 4.8 %collective-permute-start.5 = (f32[7,32,128]{2,1,0:T(8,128)S(1)}, f32[7,32,128]{2,1,0:T(8,128)S(1)}, u32[]{:S(2)}, u32[]{:S(2)}) collective-permute-start(f32[7,32,128]{2,1,0:T(8,128)S(1)} %get-tuple-element.50), channel_id=1, source_target_pairs={{16,0},{0,1},{18,2},{2,3},{20,4},{4,5},{22,6},{6,7},{24,8},{8,9},{... | collective-permute-start | bytes 344072 | tf_op jit(solution)/shard_map/ppermute | solution.py:685
  18.9 5.9 %collective-permute-start.6 = (f32[13,24,128]{2,1,0:T(8,128)S(1)}, f32[13,24,128]{2,1,0:T(8,128)S(1)}, u32[]{:S(2)}, u32[]{:S(2)}) collective-permute-start(f32[13,24,128]{2,1,0:T(8,128)S(1)} %get-tuple-element.57), channel_id=1, source_target_pairs={{0,1},{1,2},{2,3},{3,4},{4,5},{5,6},{6,7},{7,8},{8,9},{9,10},{10,1... | collective-permute-start | bytes 479240 | tf_op jit(solution)/shard_map/ppermute | solution.py:691
  19.0 5.9 %collective-permute-start.7 = (f32[13,24,128]{2,1,0:T(8,128)S(1)}, f32[13,24,128]{2,1,0:T(8,128)S(1)}, u32[]{:S(2)}, u32[]{:S(2)}) collective-permute-start(f32[13,24,128]{2,1,0:T(8,128)S(1)} %get-tuple-element.58), channel_id=1, source_target_pairs={{1,0},{2,1},{3,2},{4,3},{5,4},{6,5},{7,6},{8,7},{9,8},{10,9},{11,1... | collective-permute-start | bytes 479240 | tf_op jit(solution)/shard_map/ppermute | solution.py:691
  50.1 7.1 %collective-permute-start.8 = (f32[16,128]{1,0:T(8,128)S(1)}, f32[16,128]{1,0:T(8,128)S(1)}, u32[]{:S(2)}, u32[]{:S(2)}) collective-permute-start(f32[16,128]{1,0:T(8,128)S(1)} %get-tuple-element.71), channel_id=1, source_target_pairs={{0,64},{1,0},{2,66},{3,2},{4,68},{5,4},{6,70},{7,6},{8,72},{9,8},{... | collective-permute-start | bytes 24584 | tf_op jit(solution)/shard_map/ppermute | solution.py:685
  53.3 3.9 %collective-permute-start.9 = (f32[16,128]{1,0:T(8,128)S(1)}, f32[16,128]{1,0:T(8,128)S(1)}, u32[]{:S(2)}, u32[]{:S(2)}) collective-permute-start(f32[16,128]{1,0:T(8,128)S(1)} %get-tuple-element.72), channel_id=1, source_target_pairs={{64,0},{0,1},{66,2},{2,3},{68,4},{4,5},{70,6},{6,7},{72,8},{8,9},{... | collective-permute-start | bytes 24584 | tf_op jit(solution)/shard_map/ppermute | solution.py:685
  53.3 3.9 %collective-permute-start.10 = (f32[16,128]{1,0:T(8,128)S(1)}, f32[16,128]{1,0:T(8,128)S(1)}, u32[]{:S(2)}, u32[]{:S(2)}) collective-permute-start(f32[16,128]{1,0:T(8,128)S(1)} %get-tuple-element.73), channel_id=1, source_target_pairs={{0,16},{1,0},{2,18},{3,2},{4,20},{5,4},{6,22},{7,6},{8,24},{9,8},{... | collective-permute-start | bytes 24584 | tf_op jit(solution)/shard_map/ppermute | solution.py:685
  54.9 3.7 %collective-permute-start.11 = (f32[16,128]{1,0:T(8,128)S(1)}, f32[16,128]{1,0:T(8,128)S(1)}, u32[]{:S(2)}, u32[]{:S(2)}) collective-permute-start(f32[16,128]{1,0:T(8,128)S(1)} %get-tuple-element.74), channel_id=1, source_target_pairs={{16,0},{0,1},{18,2},{2,3},{20,4},{4,5},{22,6},{6,7},{24,8},{8,9},{... | collective-permute-start | bytes 24584 | tf_op jit(solution)/shard_map/ppermute | solution.py:685

commit v12 on v11

--- a/solution.py
+++ b/solution.py
@@ -521,8 +521,9 @@
     send[pl.ds(CAP, groups, stride=CAP + 1), :] = spread_out(hit, ends, nodes[...])
 
 
-def merge(final, near, got, beside, warmth, out, beyond, stack):
+def merge(final, near, got, beside, warmth, storage, heat, mid, out, beyond, rest, stack):
     beyond_z(got, beside, warmth, beyond)
+    own_part(mid, heat, warmth, storage, rest)
     for block in range(BLOCKS):
         for f in range(3):
             stack[block, 32 * f : 32 * f + 8, :] = near[block, f, 24:32, :]
@@ -574,7 +575,7 @@
         into[n] = (rows((128, 256)) == rank + start).astype(F32).T
 
 
-def warm(got, beside, began, warmth, storage, xf, xb, yf, yb, rest, heat, mid):
+def warm(got, beside, began, storage, xf, xb, yf, yb, heat, mid):
     first = on_first_core()
     groups = got.shape[0] // (CAP + 1)
     ids = got[pl.ds(CAP, groups, stride=CAP + 1), :].T
@@ -594,7 +595,6 @@
             total = term if total is None else total + term
     heat[...] = total.reshape(16, 16, 128)
     lane = lanes((16, 128))
-    row = rows((16, 128))
     for x in range(16):
         ends = beside[x]
         halo = jnp.where(lane == 0, roll(ends, 9, 1), jnp.where(lane == 127, roll(ends, 7, 1), 0.0))
@@ -606,6 +606,12 @@
         top, end = t[15:16], t[0:1]
         yf[x : x + 1] = jnp.where(first, top, end)
         yb[x : x + 1] = jnp.where(first, end, top)
+
+
+def own_part(mid, heat, warmth, storage, rest):
+    lane, row = lanes((16, 128)), rows((16, 128))
+    for x in range(16):
+        t = mid[x]
         near = jnp.where(row == 0, 0.0, roll(t, 1, 0)) + jnp.where(row == 15, 0.0, roll(t, -1, 0))
         near = near + jnp.where(lane == 0, 0.0, roll(t, 1, 1))
         near = near + jnp.where(lane == 127, 0.0, roll(t, -1, 1))
@@ -780,18 +786,18 @@
     got = lax.all_to_all(
         send.reshape(count, 1, 128), ("gy", "gz"), split_axis=0, concat_axis=0, tiled=True
     ).reshape(count, 128)
-    xf, xb, yf, yb, rest = call(
-        warm, [face, face, face, face, cube], [cube, cube], name="warm"
-    )(got, beside, began, warmth, storage)
+    xf, xb, yf, yb, heat, mid = call(
+        warm, [face, face, face, face, cube, cube], name="warm", near=True
+    )(got, beside, began, storage)
     xf, xb = exchange("gx", xf, xb)
     yf, yb = exchange("gy", yf, yb)
-    out, beyond = call(
+    out, beyond, rest = call(
         merge,
-        [(3, *cube), cube],
+        [(3, *cube), cube, cube],
         [(BLOCKS, 128, 128)],
         name="merge",
         cost_estimate=pl.CostEstimate(flops=10**9, bytes_accessed=10**6, transcendentals=0),
-    )(final, near, got, beside, warmth)
+    )(final, near, got, beside, warmth, storage, heat, mid)
     (updated,) = call(finish, [cube], name="finish")(rest, storage, xf, xb, yf, yb, beyond)
     return out, updated
 

time: 59.4 us -> 59.3 us (level)
  no operation moved by 1% of the time
where the time goes in v12:
time: 59.3 us; the launch traced here: 59.1 us
  blocking collectives  22.6 us (38%)
  starting transfers between devices  14.7 us (25%)
  Pallas kernels  13.6 us (23%)
  waiting for transfers between devices  7.42 us (13%)
  between operations  0.74 us (1%)
    all_to_all x1, blocking collectives, local(): lax.all_to_all(send.reshape(count, 1, 128), ('gy', 'gz'), split_axis=0, c...  22.6 us
    ppermute x5, starting transfers between devices, exchange(): lax.ppermute(fwd, names, forward)  10.2 us
    ppermute x5, waiting for transfers between devices, exchange(): lax.ppermute(bwd, names, backward)  4.34 us
    ppermute x1, starting transfers between devices, exchange_z(): lax.ppermute(down, 'gz', [(j, i) for i, j in ring])  2.94 us
    ppermute x5, waiting for transfers between devices, exchange(): lax.ppermute(fwd, names, forward)  2.71 us
    pallas_call x1, Pallas kernels, local(): call(rest_of_bulk, [(3, 17, *layer), cube, cube], [(EM_SWEEPS - 1, 3, hal...  2.41 us
    pallas_call x1, Pallas kernels, local(): call(bulk, [(EM_SWEEPS - 1, 3, 16, *layer)], name='bulk', near=True, cost...  2.22 us
    pallas_call x1, Pallas kernels, local(): call(merge, [(3, *cube), cube, cube], [(BLOCKS, 128, 128)], name='merge',...  1.95 us
  transfers between devices with their start and end apart: 12, of which 5 were waited for; matrix products, arithmetic and copies ran while one was open for 0% of the time, Pallas kernels for 15%

profile of v12, /device:TPU:130, one launch (start us, length us, event | category | flops | bytes accessed | tf_op | source)
XLA Modules:
  0.0 59.1 jit_solution(4530362005818852114)
XLA Ops:
  0.6 0.0 copy-start.1
  0.6 0.0 copy-start
  0.7 1.4 %pack_x.1 = (f32[30,16,128]{2,1,0:T(8,128)S(1)}, f32[30,16,128]{2,1,0:T(8,128)S(1)}, f32[4,16,16,128]{3,2,1,0:T(8,128)S(1)}, f32[3,16,16,128]{3,2,1,0:T(8,128)S(...) custom-call(f32[3,16,16,128]{3,2,1,0:T(8,128)} %refs_0_.1, ...), custom_call_target="tpu_custom_call" | custom-call | tf_op jit(solution)/shard_map/pack_x/pallas_call | solution.py:707
  2.0 2.4 %collective-permute-start = (f32[30,16,128]{2,1,0:T(8,128)S(1)}, f32[30,16,128]{2,1,0:T(8,128)S(1)}, u32[]{:S(2)}, u32[]{:S(2)}) collective-permute-start(f32[30,16,128]{2,1,0:T(8,128)S(1)} %get-tuple-element.45), channel_id=1, source_target_pairs={{0,64},{1,0},{2,66},{3,2},{4,68},{5,4},{6,70},{7,6},{8,72},{9,8},{... | collective-permute-start | bytes 737288 | tf_op jit(solution)/shard_map/ppermute | solution.py:691
  4.4 0.0 collective-permute-start.1
  4.4 0.1 pack_y.1
  4.5 1.5 %collective-permute-start.2 = (f32[16,32,128]{2,1,0:T(8,128)S(1)}, f32[16,32,128]{2,1,0:T(8,128)S(1)}, u32[]{:S(2)}, u32[]{:S(2)}) collective-permute-start(f32[16,32,128]{2,1,0:T(8,128)S(1)} %get-tuple-element.47), channel_id=1, source_target_pairs={{0,16},{1,0},{2,18},{3,2},{4,20},{5,4},{6,22},{7,6},{8,24},{9,8},{... | collective-permute-start | bytes 786440 | tf_op jit(solution)/shard_map/ppermute | solution.py:691
  6.0 0.5 collective-permute-start.3
  6.6 0.0 copy-done.1
  6.6 0.0 copy-done
  6.6 0.5 place.1
  7.1 2.7 %collective-permute-done.xf = f32[30,16,128]{2,1,0:T(8,128)S(1)} collective-permute-done((f32[30,16,128]{2,1,0:T(8,128)S(1)}, f32[30,16,128]{2,1,0:T(8,128)S(1)}, u32[]{:S(2)}, u32[]{:S(2)}) %collective-permute-start) | collective-permute-done | bytes 245792 | tf_op jit(solution)/shard_map/ppermute | solution.py:691
  9.8 2.4 %collective-permute-done.1.xb = f32[30,16,128]{2,1,0:T(8,128)S(1)} collective-permute-done((f32[30,16,128]{2,1,0:T(8,128)S(1)}, f32[30,16,128]{2,1,0:T(8,128)S(1)}, u32[]{:S(2)}, u32[]{:S(2)}) %collective-permute-start.1) | collective-permute-done | bytes 245792 | tf_op jit(solution)/shard_map/ppermute | solution.py:691
  12.2 0.1 pack_corners.1
  12.3 1.5 %collective-permute-start.4 = (f32[7,32,128]{2,1,0:T(8,128)S(1)}, f32[7,32,128]{2,1,0:T(8,128)S(1)}, u32[]{:S(2)}, u32[]{:S(2)}) collective-permute-start(f32[7,32,128]{2,1,0:T(8,128)S(1)} %get-tuple-element.51), channel_id=1, source_target_pairs={{0,16},{1,0},{2,18},{3,2},{4,20},{5,4},{6,22},{7,6},{8,24},{9,8},{... | collective-permute-start | bytes 344072 | tf_op jit(solution)/shard_map/ppermute | solution.py:691
  13.8 0.5 collective-permute-start.5
  14.3 0.0 collective-permute-done.2.yf
  14.3 0.0 collective-permute-done.3.yb
  14.3 1.3 %pack_inner.1 = (f32[8,16,24,128]{3,2,1,0:T(8,128)S(1)}, f32[16,24,128]{2,1,0:T(8,128)S(1)}, f32[8,24,128]{2,1,0:T(8,128)S(1)}, f32[8,24,128]{2,1,0:T(8,128)S(1)}, f32[16,16,128]{2,1,0:T(8,128)S(1)}) custom-call(f32[3,16,16,128]{3,2,1,0:T(8,128)S(1)} %get-tuple-element.41.field, f32[4,16,16,128]{3,2,1,0:T(8,128)S(1)} %get-tuple-element.42.scaled, ...), custom_call_target="tpu_custom_call" | custom-call | tf_op jit(solution)/shard_map/pack_inner/pallas_call | solution.py:734
  15.7 2.2 %bulk.1.swept = f32[3,3,16,24,128]{4,3,2,1,0:T(8,128)S(1)} custom-call(f32[8,16,24,128]{3,2,1,0:T(8,128)S(1)} %get-tuple-element.49.whole.inner), custom_call_target="tpu_custom_call" | custom-call | flops 1000000000 | bytes 10000000 | tf_op jit(solution)/shard_map/bulk/pallas_call | solution.py:741
  17.9 0.0 collective-permute-done.4.cf
  17.9 0.7 %collective-permute-done.5.cb = f32[7,32,128]{2,1,0:T(8,128)S(1)} collective-permute-done((f32[7,32,128]{2,1,0:T(8,128)S(1)}, f32[7,32,128]{2,1,0:T(8,128)S(1)}, u32[]{:S(2)}, u32[]{:S(2)}) %collective-permute-start.5) | collective-permute-done | bytes 114720 | tf_op jit(solution)/shard_map/ppermute | solution.py:691
  18.6 0.4 pack_outer.1
  18.9 0.0 collective-permute-start.6
  19.0 2.9 %collective-permute-start.7 = (f32[13,24,128]{2,1,0:T(8,128)S(1)}, f32[13,24,128]{2,1,0:T(8,128)S(1)}, u32[]{:S(2)}, u32[]{:S(2)}) collective-permute-start(f32[13,24,128]{2,1,0:T(8,128)S(1)} %get-tuple-element.60), channel_id=1, source_target_pairs={{1,0},{2,1},{3,2},{4,3},{5,4},{6,5},{7,6},{8,7},{9,8},{10,9},{11,1... | collective-permute-start | bytes 479240 | tf_op jit(solution)/shard_map/ppermute | solution.py:697
  21.9 0.2 turn.1.own
  22.1 2.4 %rest_of_bulk.1 = (f32[3,17,24,128]{3,2,1,0:T(8,128)S(1)}, f32[16,16,128]{2,1,0:T(8,128)S(1)}, f32[16,16,128]{2,1,0:T(8,128)S(1)}) custom-call(f32[8,16,24,128]{3,2,1,0:T(8,128)S(1)} %get-tuple-element.49.whole.inner, f32[8,9,24,128]{3,2,1,0:T(8,128)S(1)} %get-tuple-element.55.outer, f32[3,3,16,24,128]{4,3,2,1,0:T(8,128)S(1)} %bulk.1.swept), custom_call_target="tpu_custom_call" | custom-call | flops 1000000000 | bytes 10000000 | tf_op jit(solution)/shard_map/rest_of_bulk/pallas_call | solution.py:755
  24.5 0.4 collective-permute-done.6.below_z
  24.9 0.0 collective-permute-done.7.above_z
  24.9 1.9 %edge.1 = (f32[5,3,32,128]{3,2,1,0:T(8,128)S(1)}, f32[576,128]{1,0:T(8,128)S(1)}, f32[16,16,128]{2,1,0:T(8,128)S(1)}) custom-call(f32[5,128,128]{2,1,0:T(8,128)S(1)} %turn.1.own, f32[13,24,128]{2,1,0:T(8,128)S(1)} %collective-permute-done.6.below_z, f32[13,24,128]{2,1,0:T(8,128)S(1)} %collective-permute-done.7.above_z, ...), custom_call_target="tpu_custom_call" | custom-call | tf_op jit(solution)/shard_map/edge/pallas_call | solution.py:771
  26.8 22.6 %all_to_all.5 = f32[576,1,128]{2,1,0:T(1,128)S(1)} all-to-all(f32[576,1,128]{2,1,0:T(1,128)S(1)} %bitcast.8), channel_id=1, replica_groups=mesh['gx'=8,'gy'=4,'gz'=16] {'gy','gz'}, dimensions={0} | all-to-all | bytes 589824 | tf_op jit(solution)/shard_map/all_to_all | solution.py:786
  49.4 0.5 warm.1
  49.9 3.3 %collective-permute-start.8 = (f32[16,128]{1,0:T(8,128)S(1)}, f32[16,128]{1,0:T(8,128)S(1)}, u32[]{:S(2)}, u32[]{:S(2)}) collective-permute-start(f32[16,128]{1,0:T(8,128)S(1)} %get-tuple-element.75), channel_id=1, source_target_pairs={{0,64},{1,0},{2,66},{3,2},{4,68},{5,4},{6,70},{7,6},{8,72},{9,8},{... | collective-permute-start | bytes 24584 | tf_op jit(solution)/shard_map/ppermute | solution.py:691
  53.2 0.0 collective-permute-start.9
  53.2 1.6 %collective-permute-start.10 = (f32[16,128]{1,0:T(8,128)S(1)}, f32[16,128]{1,0:T(8,128)S(1)}, u32[]{:S(2)}, u32[]{:S(2)}) collective-permute-start(f32[16,128]{1,0:T(8,128)S(1)} %get-tuple-element.77), channel_id=1, source_target_pairs={{0,16},{1,0},{2,18},{3,2},{4,20},{5,4},{6,22},{7,6},{8,24},{9,8},{... | collective-permute-start | bytes 24584 | tf_op jit(solution)/shard_map/ppermute | solution.py:691
  54.8 0.4 collective-permute-start.11
  55.2 1.9 %merge.1 = (f32[3,16,16,128]{3,2,1,0:T(8,128)}, f32[16,16,128]{2,1,0:T(8,128)S(1)}, f32[16,16,128]{2,1,0:T(8,128)S(1)}) custom-call(f32[3,17,24,128]{3,2,1,0:T(8,128)S(1)} %get-tuple-element.56.final, f32[5,3,32,128]{3,2,1,0:T(8,128)S(1)} %get-tuple-element.67.near, f32[576,128]{1,0:T(8,128)S(1)} %bitcast.7, f32[16,16,128]{2,1,0:T(8,128)S(1)} %get-tuple-element.69.beside, ...), custom_call_target="tpu_custom_call" | custom-call | flops 1000000000 | bytes 1000000 | tf_op jit(solution)/shard_map/merge/pallas_call | solution.py:794
  57.2 0.0 collective-permute-done.8.xf
  57.2 0.0 collective-permute-done.9.xb
  57.2 0.0 collective-permute-done.10.yf
  57.2 1.2 %collective-permute-done.11.yb = f32[16,128]{1,0:T(8,128)S(1)} collective-permute-done((f32[16,128]{1,0:T(8,128)S(1)}, f32[16,128]{1,0:T(8,128)S(1)}, u32[]{:S(2)}, u32[]{:S(2)}) %collective-permute-start.11) | collective-permute-done | bytes 8224 | tf_op jit(solution)/shard_map/ppermute | solution.py:691
  58.4 0.7 %finish.1 = f32[16,16,128]{2,1,0:T(8,128)} custom-call(f32[16,16,128]{2,1,0:T(8,128)S(1)} %get-tuple-element.74.rest, f32[16,16,128]{2,1,0:T(8,128)S(1)} %get-tuple-element.44.storage, f32[16,128]{1,0:T(8,128)S(1)} %collective-permute-done.8.xf, f32[16,128]{1,0:T(8,128)S(1)} %collective-permute-done.9.xb, f32[16,128]{1,0:T(8,128)S(1)} %collective-permute-done.10.yf, ...), custom_call_target="tpu_custom_call" | custom-call | tf_op jit(solution)/shard_map/finish/pallas_call | solution.py:801
Async XLA Ops:
  0.6 5.9 %copy-start.1 = (s32[1,1,1,256]{3,2,1,0:T(1,128)S(1)}, s32[1,1,1,256]{3,2,1,0:T(1,128)}, u32[]{:S(2)}) copy-start(s32[1,1,1,256]{3,2,1,0:T(1,128)} %param.13) | copy-start | bytes 3076
  0.6 5.9 %copy-start = (s32[1,1,1,256,1]{3,4,2,1,0:T(1,128)S(1)}, s32[1,1,1,256,1]{3,4,2,1,0:T(1,128)}, u32[]{:S(2)}) copy-start(s32[1,1,1,256,1]{3,4,2,1,0:T(1,128)} %param.12) | copy-start | bytes 3076
  2.0 7.7 %collective-permute-start = (f32[30,16,128]{2,1,0:T(8,128)S(1)}, f32[30,16,128]{2,1,0:T(8,128)S(1)}, u32[]{:S(2)}, u32[]{:S(2)}) collective-permute-start(f32[30,16,128]{2,1,0:T(8,128)S(1)} %get-tuple-element.45), channel_id=1, source_target_pairs={{0,64},{1,0},{2,66},{3,2},{4,68},{5,4},{6,70},{7,6},{8,72},{9,8},{... | collective-permute-start | bytes 737288 | tf_op jit(solution)/shard_map/ppermute | solution.py:691
  4.4 7.8 %collective-permute-start.1 = (f32[30,16,128]{2,1,0:T(8,128)S(1)}, f32[30,16,128]{2,1,0:T(8,128)S(1)}, u32[]{:S(2)}, u32[]{:S(2)}) collective-permute-start(f32[30,16,128]{2,1,0:T(8,128)S(1)} %get-tuple-element.46), channel_id=1, source_target_pairs={{64,0},{0,1},{66,2},{2,3},{68,4},{4,5},{70,6},{6,7},{72,8},{8,9},{... | collective-permute-start | bytes 737288 | tf_op jit(solution)/shard_map/ppermute | solution.py:691
  4.5 9.8 %collective-permute-start.2 = (f32[16,32,128]{2,1,0:T(8,128)S(1)}, f32[16,32,128]{2,1,0:T(8,128)S(1)}, u32[]{:S(2)}, u32[]{:S(2)}) collective-permute-start(f32[16,32,128]{2,1,0:T(8,128)S(1)} %get-tuple-element.47), channel_id=1, source_target_pairs={{0,16},{1,0},{2,18},{3,2},{4,20},{5,4},{6,22},{7,6},{8,24},{9,8},{... | collective-permute-start | bytes 786440 | tf_op jit(solution)/shard_map/ppermute | solution.py:691
  6.0 8.3 %collective-permute-start.3 = (f32[16,32,128]{2,1,0:T(8,128)S(1)}, f32[16,32,128]{2,1,0:T(8,128)S(1)}, u32[]{:S(2)}, u32[]{:S(2)}) collective-permute-start(f32[16,32,128]{2,1,0:T(8,128)S(1)} %get-tuple-element.48), channel_id=1, source_target_pairs={{16,0},{0,1},{18,2},{2,3},{20,4},{4,5},{22,6},{6,7},{24,8},{8,9},{... | collective-permute-start | bytes 786440 | tf_op jit(solution)/shard_map/ppermute | solution.py:691
  12.3 5.6 %collective-permute-start.4 = (f32[7,32,128]{2,1,0:T(8,128)S(1)}, f32[7,32,128]{2,1,0:T(8,128)S(1)}, u32[]{:S(2)}, u32[]{:S(2)}) collective-permute-start(f32[7,32,128]{2,1,0:T(8,128)S(1)} %get-tuple-element.51), channel_id=1, source_target_pairs={{0,16},{1,0},{2,18},{3,2},{4,20},{5,4},{6,22},{7,6},{8,24},{9,8},{... | collective-permute-start | bytes 344072 | tf_op jit(solution)/shard_map/ppermute | solution.py:691
  13.8 4.8 %collective-permute-start.5 = (f32[7,32,128]{2,1,0:T(8,128)S(1)}, f32[7,32,128]{2,1,0:T(8,128)S(1)}, u32[]{:S(2)}, u32[]{:S(2)}) collective-permute-start(f32[7,32,128]{2,1,0:T(8,128)S(1)} %get-tuple-element.52), channel_id=1, source_target_pairs={{16,0},{0,1},{18,2},{2,3},{20,4},{4,5},{22,6},{6,7},{24,8},{8,9},{... | collective-permute-start | bytes 344072 | tf_op jit(solution)/shard_map/ppermute | solution.py:691
  18.9 5.9 %collective-permute-start.6 = (f32[13,24,128]{2,1,0:T(8,128)S(1)}, f32[13,24,128]{2,1,0:T(8,128)S(1)}, u32[]{:S(2)}, u32[]{:S(2)}) collective-permute-start(f32[13,24,128]{2,1,0:T(8,128)S(1)} %get-tuple-element.59), channel_id=1, source_target_pairs={{0,1},{1,2},{2,3},{3,4},{4,5},{5,6},{6,7},{7,8},{8,9},{9,10},{10,1... | collective-permute-start | bytes 479240 | tf_op jit(solution)/shard_map/ppermute | solution.py:697
  19.0 5.9 %collective-permute-start.7 = (f32[13,24,128]{2,1,0:T(8,128)S(1)}, f32[13,24,128]{2,1,0:T(8,128)S(1)}, u32[]{:S(2)}, u32[]{:S(2)}) collective-permute-start(f32[13,24,128]{2,1,0:T(8,128)S(1)} %get-tuple-element.60), channel_id=1, source_target_pairs={{1,0},{2,1},{3,2},{4,3},{5,4},{6,5},{7,6},{8,7},{9,8},{10,9},{11,1... | collective-permute-start | bytes 479240 | tf_op jit(solution)/shard_map/ppermute | solution.py:697
  49.9 7.2 %collective-permute-start.8 = (f32[16,128]{1,0:T(8,128)S(1)}, f32[16,128]{1,0:T(8,128)S(1)}, u32[]{:S(2)}, u32[]{:S(2)}) collective-permute-start(f32[16,128]{1,0:T(8,128)S(1)} %get-tuple-element.75), channel_id=1, source_target_pairs={{0,64},{1,0},{2,66},{3,2},{4,68},{5,4},{6,70},{7,6},{8,72},{9,8},{... | collective-permute-start | bytes 24584 | tf_op jit(solution)/shard_map/ppermute | solution.py:691
  53.2 4.0 %collective-permute-start.9 = (f32[16,128]{1,0:T(8,128)S(1)}, f32[16,128]{1,0:T(8,128)S(1)}, u32[]{:S(2)}, u32[]{:S(2)}) collective-permute-start(f32[16,128]{1,0:T(8,128)S(1)} %get-tuple-element.76), channel_id=1, source_target_pairs={{64,0},{0,1},{66,2},{2,3},{68,4},{4,5},{70,6},{6,7},{72,8},{8,9},{... | collective-permute-start | bytes 24584 | tf_op jit(solution)/shard_map/ppermute | solution.py:691
  53.2 4.0 %collective-permute-start.10 = (f32[16,128]{1,0:T(8,128)S(1)}, f32[16,128]{1,0:T(8,128)S(1)}, u32[]{:S(2)}, u32[]{:S(2)}) collective-permute-start(f32[16,128]{1,0:T(8,128)S(1)} %get-tuple-element.77), channel_id=1, source_target_pairs={{0,16},{1,0},{2,18},{3,2},{4,20},{5,4},{6,22},{7,6},{8,24},{9,8},{... | collective-permute-start | bytes 24584 | tf_op jit(solution)/shard_map/ppermute | solution.py:691
  54.8 3.7 %collective-permute-start.11 = (f32[16,128]{1,0:T(8,128)S(1)}, f32[16,128]{1,0:T(8,128)S(1)}, u32[]{:S(2)}, u32[]{:S(2)}) collective-permute-start(f32[16,128]{1,0:T(8,128)S(1)} %get-tuple-element.78), channel_id=1, source_target_pairs={{16,0},{0,1},{18,2},{2,3},{20,4},{4,5},{22,6},{6,7},{24,8},{8,9},{... | collective-permute-start | bytes 24584 | tf_op jit(solution)/shard_map/ppermute | solution.py:691

commit v13 on v12

--- a/solution.py
+++ b/solution.py
@@ -268,7 +268,7 @@
         up[k], down[k] = z_tiles(*windows)
         return carry
 
-    lax.fori_loop(0, 8, step, 0, unroll=2)
+    lax.fori_loop(0, 8, step, 0, unroll=4)
 
 
 def pack_outer(xf, xb, cf, cb, inner_up, inner_down, swept, whole, packed, up, down):
@@ -346,7 +346,7 @@
             return carry
 
         _, c = lane_curls(get, number, number)
-        lax.fori_loop(number + 1, 15 - number, step, (c[1], c[2]), unroll=4)
+        lax.fori_loop(number + 1, 15 - number, step, (c[1], c[2]), unroll=6)
 
 
 def swept_low(number):

time: 59.3 us -> 59.3 us (level)
  no operation moved by 1% of the time
where the time goes in v13:
time: 59.3 us; the launch traced here: 59.1 us
  blocking collectives  22.6 us (38%)
  starting transfers between devices  14.7 us (25%)
  Pallas kernels  13.7 us (23%)
  waiting for transfers between devices  7.32 us (12%)
  between operations  0.74 us (1%)
    all_to_all x1, blocking collectives, local(): lax.all_to_all(send.reshape(count, 1, 128), ('gy', 'gz'), split_axis=0, c...  22.6 us
    ppermute x5, starting transfers between devices, exchange(): lax.ppermute(fwd, names, forward)  10.2 us
    ppermute x5, waiting for transfers between devices, exchange(): lax.ppermute(bwd, names, backward)  4.24 us
    ppermute x1, starting transfers between devices, exchange_z(): lax.ppermute(down, 'gz', [(j, i) for i, j in ring])  2.94 us
    ppermute x5, waiting for transfers between devices, exchange(): lax.ppermute(fwd, names, forward)  2.71 us
    pallas_call x1, Pallas kernels, local(): call(rest_of_bulk, [(3, 17, *layer), cube, cube], [(EM_SWEEPS - 1, 3, hal...  2.41 us
    pallas_call x1, Pallas kernels, local(): call(bulk, [(EM_SWEEPS - 1, 3, 16, *layer)], name='bulk', near=True, cost...  2.02 us
    pallas_call x1, Pallas kernels, local(): call(merge, [(3, *cube), cube, cube], [(BLOCKS, 128, 128)], name='merge',...  1.95 us
  transfers between devices with their start and end apart: 12, of which 5 were waited for; matrix products, arithmetic and copies ran while one was open for 0% of the time, Pallas kernels for 15%

profile of v13, /device:TPU:130, one launch (start us, length us, event | category | flops | bytes accessed | tf_op | source)
XLA Modules:
  0.0 59.1 jit_solution(2099214768689681390)
XLA Ops:
  0.6 0.0 copy-start.1
  0.6 0.0 copy-start
  0.7 1.4 %pack_x.1 = (f32[30,16,128]{2,1,0:T(8,128)S(1)}, f32[30,16,128]{2,1,0:T(8,128)S(1)}, f32[4,16,16,128]{3,2,1,0:T(8,128)S(1)}, f32[3,16,16,128]{3,2,1,0:T(8,128)S(...) custom-call(f32[3,16,16,128]{3,2,1,0:T(8,128)} %refs_0_.1, ...), custom_call_target="tpu_custom_call" | custom-call | tf_op jit(solution)/shard_map/pack_x/pallas_call | solution.py:707
  2.0 2.4 %collective-permute-start = (f32[30,16,128]{2,1,0:T(8,128)S(1)}, f32[30,16,128]{2,1,0:T(8,128)S(1)}, u32[]{:S(2)}, u32[]{:S(2)}) collective-permute-start(f32[30,16,128]{2,1,0:T(8,128)S(1)} %get-tuple-element.45), channel_id=1, source_target_pairs={{0,64},{1,0},{2,66},{3,2},{4,68},{5,4},{6,70},{7,6},{8,72},{9,8},{... | collective-permute-start | bytes 737288 | tf_op jit(solution)/shard_map/ppermute | solution.py:691
  4.4 0.0 collective-permute-start.1
  4.4 0.1 pack_y.1
  4.5 1.5 %collective-permute-start.2 = (f32[16,32,128]{2,1,0:T(8,128)S(1)}, f32[16,32,128]{2,1,0:T(8,128)S(1)}, u32[]{:S(2)}, u32[]{:S(2)}) collective-permute-start(f32[16,32,128]{2,1,0:T(8,128)S(1)} %get-tuple-element.47), channel_id=1, source_target_pairs={{0,16},{1,0},{2,18},{3,2},{4,20},{5,4},{6,22},{7,6},{8,24},{9,8},{... | collective-permute-start | bytes 786440 | tf_op jit(solution)/shard_map/ppermute | solution.py:691
  6.0 0.5 collective-permute-start.3
  6.6 0.0 copy-done.1
  6.6 0.0 copy-done
  6.6 0.5 place.1
  7.1 2.7 %collective-permute-done.xf = f32[30,16,128]{2,1,0:T(8,128)S(1)} collective-permute-done((f32[30,16,128]{2,1,0:T(8,128)S(1)}, f32[30,16,128]{2,1,0:T(8,128)S(1)}, u32[]{:S(2)}, u32[]{:S(2)}) %collective-permute-start) | collective-permute-done | bytes 245792 | tf_op jit(solution)/shard_map/ppermute | solution.py:691
  9.8 2.4 %collective-permute-done.1.xb = f32[30,16,128]{2,1,0:T(8,128)S(1)} collective-permute-done((f32[30,16,128]{2,1,0:T(8,128)S(1)}, f32[30,16,128]{2,1,0:T(8,128)S(1)}, u32[]{:S(2)}, u32[]{:S(2)}) %collective-permute-start.1) | collective-permute-done | bytes 245792 | tf_op jit(solution)/shard_map/ppermute | solution.py:691
  12.2 0.1 pack_corners.1
  12.3 1.5 %collective-permute-start.4 = (f32[7,32,128]{2,1,0:T(8,128)S(1)}, f32[7,32,128]{2,1,0:T(8,128)S(1)}, u32[]{:S(2)}, u32[]{:S(2)}) collective-permute-start(f32[7,32,128]{2,1,0:T(8,128)S(1)} %get-tuple-element.51), channel_id=1, source_target_pairs={{0,16},{1,0},{2,18},{3,2},{4,20},{5,4},{6,22},{7,6},{8,24},{9,8},{... | collective-permute-start | bytes 344072 | tf_op jit(solution)/shard_map/ppermute | solution.py:691
  13.8 0.5 collective-permute-start.5
  14.3 0.0 collective-permute-done.2.yf
  14.3 0.0 collective-permute-done.3.yb
  14.3 1.6 %pack_inner.1 = (f32[8,16,24,128]{3,2,1,0:T(8,128)S(1)}, f32[16,24,128]{2,1,0:T(8,128)S(1)}, f32[8,24,128]{2,1,0:T(8,128)S(1)}, f32[8,24,128]{2,1,0:T(8,128)S(1)}, f32[16,16,128]{2,1,0:T(8,128)S(1)}) custom-call(f32[3,16,16,128]{3,2,1,0:T(8,128)S(1)} %get-tuple-element.41.field, f32[4,16,16,128]{3,2,1,0:T(8,128)S(1)} %get-tuple-element.42.scaled, ...), custom_call_target="tpu_custom_call" | custom-call | tf_op jit(solution)/shard_map/pack_inner/pallas_call | solution.py:734
  16.0 2.0 %bulk.1.swept = f32[3,3,16,24,128]{4,3,2,1,0:T(8,128)S(1)} custom-call(f32[8,16,24,128]{3,2,1,0:T(8,128)S(1)} %get-tuple-element.49.whole.inner), custom_call_target="tpu_custom_call" | custom-call | flops 1000000000 | bytes 10000000 | tf_op jit(solution)/shard_map/bulk/pallas_call | solution.py:741
  18.0 0.0 collective-permute-done.4.cf
  18.0 0.6 collective-permute-done.5.cb
  18.6 0.4 pack_outer.1
  18.9 0.0 collective-permute-start.6
  19.0 2.9 %collective-permute-start.7 = (f32[13,24,128]{2,1,0:T(8,128)S(1)}, f32[13,24,128]{2,1,0:T(8,128)S(1)}, u32[]{:S(2)}, u32[]{:S(2)}) collective-permute-start(f32[13,24,128]{2,1,0:T(8,128)S(1)} %get-tuple-element.60), channel_id=1, source_target_pairs={{1,0},{2,1},{3,2},{4,3},{5,4},{6,5},{7,6},{8,7},{9,8},{10,9},{11,1... | collective-permute-start | bytes 479240 | tf_op jit(solution)/shard_map/ppermute | solution.py:697
  21.9 0.2 turn.1.own
  22.1 2.4 %rest_of_bulk.1 = (f32[3,17,24,128]{3,2,1,0:T(8,128)S(1)}, f32[16,16,128]{2,1,0:T(8,128)S(1)}, f32[16,16,128]{2,1,0:T(8,128)S(1)}) custom-call(f32[8,16,24,128]{3,2,1,0:T(8,128)S(1)} %get-tuple-element.49.whole.inner, f32[8,9,24,128]{3,2,1,0:T(8,128)S(1)} %get-tuple-element.55.outer, f32[3,3,16,24,128]{4,3,2,1,0:T(8,128)S(1)} %bulk.1.swept), custom_call_target="tpu_custom_call" | custom-call | flops 1000000000 | bytes 10000000 | tf_op jit(solution)/shard_map/rest_of_bulk/pallas_call | solution.py:755
  24.5 0.4 collective-permute-done.6.below_z
  24.9 0.0 collective-permute-done.7.above_z
  24.9 1.9 %edge.1 = (f32[5,3,32,128]{3,2,1,0:T(8,128)S(1)}, f32[576,128]{1,0:T(8,128)S(1)}, f32[16,16,128]{2,1,0:T(8,128)S(1)}) custom-call(f32[5,128,128]{2,1,0:T(8,128)S(1)} %turn.1.own, f32[13,24,128]{2,1,0:T(8,128)S(1)} %collective-permute-done.6.below_z, f32[13,24,128]{2,1,0:T(8,128)S(1)} %collective-permute-done.7.above_z, ...), custom_call_target="tpu_custom_call" | custom-call | tf_op jit(solution)/shard_map/edge/pallas_call | solution.py:771
  26.8 22.6 %all_to_all.5 = f32[576,1,128]{2,1,0:T(1,128)S(1)} all-to-all(f32[576,1,128]{2,1,0:T(1,128)S(1)} %bitcast.8), channel_id=1, replica_groups=mesh['gx'=8,'gy'=4,'gz'=16] {'gy','gz'}, dimensions={0} | all-to-all | bytes 589824 | tf_op jit(solution)/shard_map/all_to_all | solution.py:786
  49.4 0.5 warm.1
  49.9 3.3 %collective-permute-start.8 = (f32[16,128]{1,0:T(8,128)S(1)}, f32[16,128]{1,0:T(8,128)S(1)}, u32[]{:S(2)}, u32[]{:S(2)}) collective-permute-start(f32[16,128]{1,0:T(8,128)S(1)} %get-tuple-element.75), channel_id=1, source_target_pairs={{0,64},{1,0},{2,66},{3,2},{4,68},{5,4},{6,70},{7,6},{8,72},{9,8},{... | collective-permute-start | bytes 24584 | tf_op jit(solution)/shard_map/ppermute | solution.py:691
  53.2 0.0 collective-permute-start.9
  53.2 1.6 %collective-permute-start.10 = (f32[16,128]{1,0:T(8,128)S(1)}, f32[16,128]{1,0:T(8,128)S(1)}, u32[]{:S(2)}, u32[]{:S(2)}) collective-permute-start(f32[16,128]{1,0:T(8,128)S(1)} %get-tuple-element.77), channel_id=1, source_target_pairs={{0,16},{1,0},{2,18},{3,2},{4,20},{5,4},{6,22},{7,6},{8,24},{9,8},{... | collective-permute-start | bytes 24584 | tf_op jit(solution)/shard_map/ppermute | solution.py:691
  54.8 0.4 collective-permute-start.11
  55.2 1.9 %merge.1 = (f32[3,16,16,128]{3,2,1,0:T(8,128)}, f32[16,16,128]{2,1,0:T(8,128)S(1)}, f32[16,16,128]{2,1,0:T(8,128)S(1)}) custom-call(f32[3,17,24,128]{3,2,1,0:T(8,128)S(1)} %get-tuple-element.56.final, f32[5,3,32,128]{3,2,1,0:T(8,128)S(1)} %get-tuple-element.67.near, f32[576,128]{1,0:T(8,128)S(1)} %bitcast.7, f32[16,16,128]{2,1,0:T(8,128)S(1)} %get-tuple-element.69.beside, ...), custom_call_target="tpu_custom_call" | custom-call | flops 1000000000 | bytes 1000000 | tf_op jit(solution)/shard_map/merge/pallas_call | solution.py:794
  57.2 0.0 collective-permute-done.8.xf
  57.2 0.0 collective-permute-done.9.xb
  57.2 0.0 collective-permute-done.10.yf
  57.2 1.2 %collective-permute-done.11.yb = f32[16,128]{1,0:T(8,128)S(1)} collective-permute-done((f32[16,128]{1,0:T(8,128)S(1)}, f32[16,128]{1,0:T(8,128)S(1)}, u32[]{:S(2)}, u32[]{:S(2)}) %collective-permute-start.11) | collective-permute-done | bytes 8224 | tf_op jit(solution)/shard_map/ppermute | solution.py:691
  58.4 0.7 %finish.1 = f32[16,16,128]{2,1,0:T(8,128)} custom-call(f32[16,16,128]{2,1,0:T(8,128)S(1)} %get-tuple-element.74.rest, f32[16,16,128]{2,1,0:T(8,128)S(1)} %get-tuple-element.44.storage, f32[16,128]{1,0:T(8,128)S(1)} %collective-permute-done.8.xf, f32[16,128]{1,0:T(8,128)S(1)} %collective-permute-done.9.xb, f32[16,128]{1,0:T(8,128)S(1)} %collective-permute-done.10.yf, ...), custom_call_target="tpu_custom_call" | custom-call | tf_op jit(solution)/shard_map/finish/pallas_call | solution.py:801
Async XLA Ops:
  0.6 5.9 %copy-start.1 = (s32[1,1,1,256]{3,2,1,0:T(1,128)S(1)}, s32[1,1,1,256]{3,2,1,0:T(1,128)}, u32[]{:S(2)}) copy-start(s32[1,1,1,256]{3,2,1,0:T(1,128)} %param.13) | copy-start | bytes 3076
  0.6 5.9 %copy-start = (s32[1,1,1,256,1]{3,4,2,1,0:T(1,128)S(1)}, s32[1,1,1,256,1]{3,4,2,1,0:T(1,128)}, u32[]{:S(2)}) copy-start(s32[1,1,1,256,1]{3,4,2,1,0:T(1,128)} %param.12) | copy-start | bytes 3076
  2.0 7.7 %collective-permute-start = (f32[30,16,128]{2,1,0:T(8,128)S(1)}, f32[30,16,128]{2,1,0:T(8,128)S(1)}, u32[]{:S(2)}, u32[]{:S(2)}) collective-permute-start(f32[30,16,128]{2,1,0:T(8,128)S(1)} %get-tuple-element.45), channel_id=1, source_target_pairs={{0,64},{1,0},{2,66},{3,2},{4,68},{5,4},{6,70},{7,6},{8,72},{9,8},{... | collective-permute-start | bytes 737288 | tf_op jit(solution)/shard_map/ppermute | solution.py:691
  4.4 7.8 %collective-permute-start.1 = (f32[30,16,128]{2,1,0:T(8,128)S(1)}, f32[30,16,128]{2,1,0:T(8,128)S(1)}, u32[]{:S(2)}, u32[]{:S(2)}) collective-permute-start(f32[30,16,128]{2,1,0:T(8,128)S(1)} %get-tuple-element.46), channel_id=1, source_target_pairs={{64,0},{0,1},{66,2},{2,3},{68,4},{4,5},{70,6},{6,7},{72,8},{8,9},{... | collective-permute-start | bytes 737288 | tf_op jit(solution)/shard_map/ppermute | solution.py:691
  4.5 9.8 %collective-permute-start.2 = (f32[16,32,128]{2,1,0:T(8,128)S(1)}, f32[16,32,128]{2,1,0:T(8,128)S(1)}, u32[]{:S(2)}, u32[]{:S(2)}) collective-permute-start(f32[16,32,128]{2,1,0:T(8,128)S(1)} %get-tuple-element.47), channel_id=1, source_target_pairs={{0,16},{1,0},{2,18},{3,2},{4,20},{5,4},{6,22},{7,6},{8,24},{9,8},{... | collective-permute-start | bytes 786440 | tf_op jit(solution)/shard_map/ppermute | solution.py:691
  6.0 8.3 %collective-permute-start.3 = (f32[16,32,128]{2,1,0:T(8,128)S(1)}, f32[16,32,128]{2,1,0:T(8,128)S(1)}, u32[]{:S(2)}, u32[]{:S(2)}) collective-permute-start(f32[16,32,128]{2,1,0:T(8,128)S(1)} %get-tuple-element.48), channel_id=1, source_target_pairs={{16,0},{0,1},{18,2},{2,3},{20,4},{4,5},{22,6},{6,7},{24,8},{8,9},{... | collective-permute-start | bytes 786440 | tf_op jit(solution)/shard_map/ppermute | solution.py:691
  12.3 5.7 %collective-permute-start.4 = (f32[7,32,128]{2,1,0:T(8,128)S(1)}, f32[7,32,128]{2,1,0:T(8,128)S(1)}, u32[]{:S(2)}, u32[]{:S(2)}) collective-permute-start(f32[7,32,128]{2,1,0:T(8,128)S(1)} %get-tuple-element.51), channel_id=1, source_target_pairs={{0,16},{1,0},{2,18},{3,2},{4,20},{5,4},{6,22},{7,6},{8,24},{9,8},{... | collective-permute-start | bytes 344072 | tf_op jit(solution)/shard_map/ppermute | solution.py:691
  13.8 4.8 %collective-permute-start.5 = (f32[7,32,128]{2,1,0:T(8,128)S(1)}, f32[7,32,128]{2,1,0:T(8,128)S(1)}, u32[]{:S(2)}, u32[]{:S(2)}) collective-permute-start(f32[7,32,128]{2,1,0:T(8,128)S(1)} %get-tuple-element.52), channel_id=1, source_target_pairs={{16,0},{0,1},{18,2},{2,3},{20,4},{4,5},{22,6},{6,7},{24,8},{8,9},{... | collective-permute-start | bytes 344072 | tf_op jit(solution)/shard_map/ppermute | solution.py:691
  18.9 5.9 %collective-permute-start.6 = (f32[13,24,128]{2,1,0:T(8,128)S(1)}, f32[13,24,128]{2,1,0:T(8,128)S(1)}, u32[]{:S(2)}, u32[]{:S(2)}) collective-permute-start(f32[13,24,128]{2,1,0:T(8,128)S(1)} %get-tuple-element.59), channel_id=1, source_target_pairs={{0,1},{1,2},{2,3},{3,4},{4,5},{5,6},{6,7},{7,8},{8,9},{9,10},{10,1... | collective-permute-start | bytes 479240 | tf_op jit(solution)/shard_map/ppermute | solution.py:697
  19.0 5.9 %collective-permute-start.7 = (f32[13,24,128]{2,1,0:T(8,128)S(1)}, f32[13,24,128]{2,1,0:T(8,128)S(1)}, u32[]{:S(2)}, u32[]{:S(2)}) collective-permute-start(f32[13,24,128]{2,1,0:T(8,128)S(1)} %get-tuple-element.60), channel_id=1, source_target_pairs={{1,0},{2,1},{3,2},{4,3},{5,4},{6,5},{7,6},{8,7},{9,8},{10,9},{11,1... | collective-permute-start | bytes 479240 | tf_op jit(solution)/shard_map/ppermute | solution.py:697
  49.9 7.2 %collective-permute-start.8 = (f32[16,128]{1,0:T(8,128)S(1)}, f32[16,128]{1,0:T(8,128)S(1)}, u32[]{:S(2)}, u32[]{:S(2)}) collective-permute-start(f32[16,128]{1,0:T(8,128)S(1)} %get-tuple-element.75), channel_id=1, source_target_pairs={{0,64},{1,0},{2,66},{3,2},{4,68},{5,4},{6,70},{7,6},{8,72},{9,8},{... | collective-permute-start | bytes 24584 | tf_op jit(solution)/shard_map/ppermute | solution.py:691
  53.2 4.0 %collective-permute-start.9 = (f32[16,128]{1,0:T(8,128)S(1)}, f32[16,128]{1,0:T(8,128)S(1)}, u32[]{:S(2)}, u32[]{:S(2)}) collective-permute-start(f32[16,128]{1,0:T(8,128)S(1)} %get-tuple-element.76), channel_id=1, source_target_pairs={{64,0},{0,1},{66,2},{2,3},{68,4},{4,5},{70,6},{6,7},{72,8},{8,9},{... | collective-permute-start | bytes 24584 | tf_op jit(solution)/shard_map/ppermute | solution.py:691
  53.2 4.0 %collective-permute-start.10 = (f32[16,128]{1,0:T(8,128)S(1)}, f32[16,128]{1,0:T(8,128)S(1)}, u32[]{:S(2)}, u32[]{:S(2)}) collective-permute-start(f32[16,128]{1,0:T(8,128)S(1)} %get-tuple-element.77), channel_id=1, source_target_pairs={{0,16},{1,0},{2,18},{3,2},{4,20},{5,4},{6,22},{7,6},{8,24},{9,8},{... | collective-permute-start | bytes 24584 | tf_op jit(solution)/shard_map/ppermute | solution.py:691
  54.8 3.7 %collective-permute-start.11 = (f32[16,128]{1,0:T(8,128)S(1)}, f32[16,128]{1,0:T(8,128)S(1)}, u32[]{:S(2)}, u32[]{:S(2)}) collective-permute-start(f32[16,128]{1,0:T(8,128)S(1)} %get-tuple-element.78), channel_id=1, source_target_pairs={{16,0},{0,1},{18,2},{2,3},{20,4},{4,5},{22,6},{6,7},{24,8},{8,9},{... | collective-permute-start | bytes 24584 | tf_op jit(solution)/shard_map/ppermute | solution.py:691

commit v14 on v13

--- a/solution.py
+++ b/solution.py
@@ -141,7 +141,8 @@
     copies[3].wait()
 
 
-def pack_y(field, scaled, warmth, yf, yb):
+def pack_y(field, scaled, warmth, targets, yf, yb):
+    del targets
     first = on_first_core()
 
     def step(x, carry):
@@ -713,8 +714,6 @@
         in_specs=[pl.BlockSpec(memory_space=pltpu.HBM)] * 5,
     )(*(pltpu.with_memory_space_constraint(v, pltpu.HBM) for v in here))
     xf, xb = exchange("gx", xf, xb)
-    yf, yb = call(pack_y, [y_message, y_message], name="pack_y", near=True)(field, scaled, warmth)
-    yf, yb = exchange("gy", yf, yb)
     targets, spread_rows, into, nodes = pl.pallas_call(
         place,
         out_shape=[
@@ -726,6 +725,10 @@
         compiler_params=pltpu.CompilerParams(vmem_limit_bytes=8 << 20),
         name="place",
     )(partition.reshape(1, 256), column.reshape(1, 256))
+    yf, yb = call(pack_y, [y_message, y_message], name="pack_y", near=True)(
+        field, scaled, warmth, targets
+    )
+    yf, yb = exchange("gy", yf, yb)
     cf, cb = call(pack_corners, [corners, corners], name="pack_corners")(
         xf, xb, targets
     )

time: 59.3 us -> 61.1 us (1.030)
  the two profiles are of different devices: /device:TPU:130 before, /device:TPU:194 now
where the time goes in v14:
time: 61.1 us; the launch traced here: 61 us
  blocking collectives  23.1 us (38%)
  starting transfers between devices  15.5 us (25%)
  Pallas kernels  13.7 us (22%)
  waiting for transfers between devices  6.51 us (11%)
  local copies, waits for them, and re-layouts  1.36 us (2%)
  between operations  0.73 us (1%)
    all_to_all x1, blocking collectives, local(): lax.all_to_all(send.reshape(count, 1, 128), ('gy', 'gz'), split_axis=0, c...  23.1 us
    ppermute x5, starting transfers between devices, exchange(): lax.ppermute(fwd, names, forward)  11 us
    ppermute x5, waiting for transfers between devices, exchange(): lax.ppermute(bwd, names, backward)  3.81 us
    ppermute x1, starting transfers between devices, exchange_z(): lax.ppermute(down, 'gz', [(j, i) for i, j in ring])  2.94 us
    pallas_call x1, Pallas kernels, local(): call(rest_of_bulk, [(3, 17, *layer), cube, cube], [(EM_SWEEPS - 1, 3, hal...  2.41 us
    ppermute x5, waiting for transfers between devices, exchange(): lax.ppermute(fwd, names, forward)  2.33 us
    pallas_call x1, Pallas kernels, local(): call(bulk, [(EM_SWEEPS - 1, 3, 16, *layer)], name='bulk', near=True, cost...  2.02 us
    pallas_call x1, Pallas kernels, local(): call(merge, [(3, *cube), cube, cube], [(BLOCKS, 128, 128)], name='merge',...  1.95 us
  transfers between devices with their start and end apart: 12, of which 7 were waited for; matrix products, arithmetic and copies ran while one was open for 0% of the time, Pallas kernels for 14%

profile of v14, /device:TPU:194, one launch (start us, length us, event | category | flops | bytes accessed | tf_op | source)
XLA Modules:
  0.0 61.0 jit_solution(320965144195798357)
XLA Ops:
  0.6 1.4 %pack_x.1 = (f32[30,16,128]{2,1,0:T(8,128)S(1)}, f32[30,16,128]{2,1,0:T(8,128)S(1)}, f32[4,16,16,128]{3,2,1,0:T(8,128)S(1)}, f32[3,16,16,128]{3,2,1,0:T(8,128)S(...) custom-call(f32[3,16,16,128]{3,2,1,0:T(8,128)} %refs_0_.1, ...), custom_call_target="tpu_custom_call" | custom-call | tf_op jit(solution)/shard_map/pack_x/pallas_call | solution.py:708
  2.0 3.6 %collective-permute-start = (f32[30,16,128]{2,1,0:T(8,128)S(1)}, f32[30,16,128]{2,1,0:T(8,128)S(1)}, u32[]{:S(2)}, u32[]{:S(2)}) collective-permute-start(f32[30,16,128]{2,1,0:T(8,128)S(1)} %get-tuple-element.45), channel_id=1, source_target_pairs={{0,64},{1,0},{2,66},{3,2},{4,68},{5,4},{6,70},{7,6},{8,72},{9,8},{... | collective-permute-start | bytes 737288 | tf_op jit(solution)/shard_map/ppermute | solution.py:692
  5.6 0.0 collective-permute-start.1
  5.6 0.0 copy-start
  5.6 0.7 %copy-done = s32[1,1,1,256,1]{3,4,2,1,0:T(1,128)S(1)} copy-done((s32[1,1,1,256,1]{3,4,2,1,0:T(1,128)S(1)}, s32[1,1,1,256,1]{3,4,2,1,0:T(1,128)}, u32[]{:S(2)}) %copy-start) | copy-done | bytes 1048
  6.3 0.0 copy-start.1
  6.3 0.7 %copy-done.1 = s32[1,1,1,256]{3,2,1,0:T(1,128)S(1)} copy-done((s32[1,1,1,256]{3,2,1,0:T(1,128)S(1)}, s32[1,1,1,256]{3,2,1,0:T(1,128)}, u32[]{:S(2)}) %copy-start.1) | copy-done | bytes 1048
  7.0 0.5 place.1
  7.5 0.1 pack_y.1
  7.6 1.5 %collective-permute-start.2 = (f32[16,32,128]{2,1,0:T(8,128)S(1)}, f32[16,32,128]{2,1,0:T(8,128)S(1)}, u32[]{:S(2)}, u32[]{:S(2)}) collective-permute-start(f32[16,32,128]{2,1,0:T(8,128)S(1)} %get-tuple-element.48), channel_id=1, source_target_pairs={{0,16},{1,0},{2,18},{3,2},{4,20},{5,4},{6,22},{7,6},{8,24},{9,8},{... | collective-permute-start | bytes 786440 | tf_op jit(solution)/shard_map/ppermute | solution.py:692
  9.1 0.5 collective-permute-start.3
  9.6 1.2 %collective-permute-done.xf = f32[30,16,128]{2,1,0:T(8,128)S(1)} collective-permute-done((f32[30,16,128]{2,1,0:T(8,128)S(1)}, f32[30,16,128]{2,1,0:T(8,128)S(1)}, u32[]{:S(2)}, u32[]{:S(2)}) %collective-permute-start) | collective-permute-done | bytes 245792 | tf_op jit(solution)/shard_map/ppermute | solution.py:692
  10.9 2.2 %collective-permute-done.1.xb = f32[30,16,128]{2,1,0:T(8,128)S(1)} collective-permute-done((f32[30,16,128]{2,1,0:T(8,128)S(1)}, f32[30,16,128]{2,1,0:T(8,128)S(1)}, u32[]{:S(2)}, u32[]{:S(2)}) %collective-permute-start.1) | collective-permute-done | bytes 245792 | tf_op jit(solution)/shard_map/ppermute | solution.py:692
  13.0 0.1 pack_corners.1
  13.1 1.5 %collective-permute-start.4 = (f32[7,32,128]{2,1,0:T(8,128)S(1)}, f32[7,32,128]{2,1,0:T(8,128)S(1)}, u32[]{:S(2)}, u32[]{:S(2)}) collective-permute-start(f32[7,32,128]{2,1,0:T(8,128)S(1)} %get-tuple-element.51), channel_id=1, source_target_pairs={{0,16},{1,0},{2,18},{3,2},{4,20},{5,4},{6,22},{7,6},{8,24},{9,8},{... | collective-permute-start | bytes 344072 | tf_op jit(solution)/shard_map/ppermute | solution.py:692
  14.6 0.5 collective-permute-start.5
  15.1 1.1 %collective-permute-done.2.yf = f32[16,32,128]{2,1,0:T(8,128)S(1)} collective-permute-done((f32[16,32,128]{2,1,0:T(8,128)S(1)}, f32[16,32,128]{2,1,0:T(8,128)S(1)}, u32[]{:S(2)}, u32[]{:S(2)}) %collective-permute-start.2) | collective-permute-done | bytes 262176 | tf_op jit(solution)/shard_map/ppermute | solution.py:692
  16.2 0.4 collective-permute-done.3.yb
  16.6 1.6 %pack_inner.1 = (f32[8,16,24,128]{3,2,1,0:T(8,128)S(1)}, f32[16,24,128]{2,1,0:T(8,128)S(1)}, f32[8,24,128]{2,1,0:T(8,128)S(1)}, f32[8,24,128]{2,1,0:T(8,128)S(1)}, f32[16,16,128]{2,1,0:T(8,128)S(1)}) custom-call(f32[3,16,16,128]{3,2,1,0:T(8,128)S(1)} %get-tuple-element.41.field, f32[4,16,16,128]{3,2,1,0:T(8,128)S(1)} %get-tuple-element.42.scaled, ...), custom_call_target="tpu_custom_call" | custom-call | tf_op jit(solution)/shard_map/pack_inner/pallas_call | solution.py:737
  18.3 2.0 %bulk.1.swept = f32[3,3,16,24,128]{4,3,2,1,0:T(8,128)S(1)} custom-call(f32[8,16,24,128]{3,2,1,0:T(8,128)S(1)} %get-tuple-element.50.whole.inner), custom_call_target="tpu_custom_call" | custom-call | flops 1000000000 | bytes 10000000 | tf_op jit(solution)/shard_map/bulk/pallas_call | solution.py:744
  20.3 0.0 collective-permute-done.4.cf
  20.3 0.0 collective-permute-done.5.cb
  20.3 0.4 pack_outer.1
  20.7 0.0 collective-permute-start.6
  20.7 2.9 %collective-permute-start.7 = (f32[13,24,128]{2,1,0:T(8,128)S(1)}, f32[13,24,128]{2,1,0:T(8,128)S(1)}, u32[]{:S(2)}, u32[]{:S(2)}) collective-permute-start(f32[13,24,128]{2,1,0:T(8,128)S(1)} %get-tuple-element.60), channel_id=1, source_target_pairs={{1,0},{2,1},{3,2},{4,3},{5,4},{6,5},{7,6},{8,7},{9,8},{10,9},{11,1... | collective-permute-start | bytes 479240 | tf_op jit(solution)/shard_map/ppermute | solution.py:698
  23.6 0.2 turn.1.own
  23.8 2.4 %rest_of_bulk.1 = (f32[3,17,24,128]{3,2,1,0:T(8,128)S(1)}, f32[16,16,128]{2,1,0:T(8,128)S(1)}, f32[16,16,128]{2,1,0:T(8,128)S(1)}) custom-call(f32[8,16,24,128]{3,2,1,0:T(8,128)S(1)} %get-tuple-element.50.whole.inner, f32[8,9,24,128]{3,2,1,0:T(8,128)S(1)} %get-tuple-element.55.outer, f32[3,3,16,24,128]{4,3,2,1,0:T(8,128)S(1)} %bulk.1.swept), custom_call_target="tpu_custom_call" | custom-call | flops 1000000000 | bytes 10000000 | tf_op jit(solution)/shard_map/rest_of_bulk/pallas_call | solution.py:758
  26.2 0.4 collective-permute-done.6.below_z
  26.6 0.0 collective-permute-done.7.above_z
  26.6 1.9 %edge.1 = (f32[5,3,32,128]{3,2,1,0:T(8,128)S(1)}, f32[576,128]{1,0:T(8,128)S(1)}, f32[16,16,128]{2,1,0:T(8,128)S(1)}) custom-call(f32[5,128,128]{2,1,0:T(8,128)S(1)} %turn.1.own, f32[13,24,128]{2,1,0:T(8,128)S(1)} %collective-permute-done.6.below_z, f32[13,24,128]{2,1,0:T(8,128)S(1)} %collective-permute-done.7.above_z, ...), custom_call_target="tpu_custom_call" | custom-call | tf_op jit(solution)/shard_map/edge/pallas_call | solution.py:774
  28.5 23.1 %all_to_all.5 = f32[576,1,128]{2,1,0:T(1,128)S(1)} all-to-all(f32[576,1,128]{2,1,0:T(1,128)S(1)} %bitcast.8), channel_id=1, replica_groups=mesh['gx'=8,'gy'=4,'gz'=16] {'gy','gz'}, dimensions={0} | all-to-all | bytes 589824 | tf_op jit(solution)/shard_map/all_to_all | solution.py:789
  51.7 0.5 warm.1
  52.2 2.8 %collective-permute-start.8 = (f32[16,128]{1,0:T(8,128)S(1)}, f32[16,128]{1,0:T(8,128)S(1)}, u32[]{:S(2)}, u32[]{:S(2)}) collective-permute-start(f32[16,128]{1,0:T(8,128)S(1)} %get-tuple-element.75), channel_id=1, source_target_pairs={{0,64},{1,0},{2,66},{3,2},{4,68},{5,4},{6,70},{7,6},{8,72},{9,8},{... | collective-permute-start | bytes 24584 | tf_op jit(solution)/shard_map/ppermute | solution.py:692
  55.0 0.0 collective-permute-start.9
  55.0 1.6 %collective-permute-start.10 = (f32[16,128]{1,0:T(8,128)S(1)}, f32[16,128]{1,0:T(8,128)S(1)}, u32[]{:S(2)}, u32[]{:S(2)}) collective-permute-start(f32[16,128]{1,0:T(8,128)S(1)} %get-tuple-element.77), channel_id=1, source_target_pairs={{0,16},{1,0},{2,18},{3,2},{4,20},{5,4},{6,22},{7,6},{8,24},{9,8},{... | collective-permute-start | bytes 24584 | tf_op jit(solution)/shard_map/ppermute | solution.py:692
  56.6 0.4 collective-permute-start.11
  57.0 1.9 %merge.1 = (f32[3,16,16,128]{3,2,1,0:T(8,128)}, f32[16,16,128]{2,1,0:T(8,128)S(1)}, f32[16,16,128]{2,1,0:T(8,128)S(1)}) custom-call(f32[3,17,24,128]{3,2,1,0:T(8,128)S(1)} %get-tuple-element.56.final, f32[5,3,32,128]{3,2,1,0:T(8,128)S(1)} %get-tuple-element.67.near, f32[576,128]{1,0:T(8,128)S(1)} %bitcast.7, f32[16,16,128]{2,1,0:T(8,128)S(1)} %get-tuple-element.69.beside, ...), custom_call_target="tpu_custom_call" | custom-call | flops 1000000000 | bytes 1000000 | tf_op jit(solution)/shard_map/merge/pallas_call | solution.py:797
  59.0 0.0 collective-permute-done.8.xf
  59.0 0.9 %collective-permute-done.9.xb = f32[16,128]{1,0:T(8,128)S(1)} collective-permute-done((f32[16,128]{1,0:T(8,128)S(1)}, f32[16,128]{1,0:T(8,128)S(1)}, u32[]{:S(2)}, u32[]{:S(2)}) %collective-permute-start.9) | collective-permute-done | bytes 8224 | tf_op jit(solution)/shard_map/ppermute | solution.py:692
  59.9 0.0 collective-permute-done.10.yf
  59.9 0.4 collective-permute-done.11.yb
  60.2 0.7 %finish.1 = f32[16,16,128]{2,1,0:T(8,128)} custom-call(f32[16,16,128]{2,1,0:T(8,128)S(1)} %get-tuple-element.74.rest, f32[16,16,128]{2,1,0:T(8,128)S(1)} %get-tuple-element.44.storage, f32[16,128]{1,0:T(8,128)S(1)} %collective-permute-done.8.xf, f32[16,128]{1,0:T(8,128)S(1)} %collective-permute-done.9.xb, f32[16,128]{1,0:T(8,128)S(1)} %collective-permute-done.10.yf, ...), custom_call_target="tpu_custom_call" | custom-call | tf_op jit(solution)/shard_map/finish/pallas_call | solution.py:804
Async XLA Ops:
  2.0 8.8 %collective-permute-start = (f32[30,16,128]{2,1,0:T(8,128)S(1)}, f32[30,16,128]{2,1,0:T(8,128)S(1)}, u32[]{:S(2)}, u32[]{:S(2)}) collective-permute-start(f32[30,16,128]{2,1,0:T(8,128)S(1)} %get-tuple-element.45), channel_id=1, source_target_pairs={{0,64},{1,0},{2,66},{3,2},{4,68},{5,4},{6,70},{7,6},{8,72},{9,8},{... | collective-permute-start | bytes 737288 | tf_op jit(solution)/shard_map/ppermute | solution.py:692
  5.6 7.4 %collective-permute-start.1 = (f32[30,16,128]{2,1,0:T(8,128)S(1)}, f32[30,16,128]{2,1,0:T(8,128)S(1)}, u32[]{:S(2)}, u32[]{:S(2)}) collective-permute-start(f32[30,16,128]{2,1,0:T(8,128)S(1)} %get-tuple-element.46), channel_id=1, source_target_pairs={{64,0},{0,1},{66,2},{2,3},{68,4},{4,5},{70,6},{6,7},{72,8},{8,9},{... | collective-permute-start | bytes 737288 | tf_op jit(solution)/shard_map/ppermute | solution.py:692
  5.6 0.7 %copy-start = (s32[1,1,1,256,1]{3,4,2,1,0:T(1,128)S(1)}, s32[1,1,1,256,1]{3,4,2,1,0:T(1,128)}, u32[]{:S(2)}) copy-start(s32[1,1,1,256,1]{3,4,2,1,0:T(1,128)} %param.12) | copy-start | bytes 3076
  6.3 0.7 %copy-start.1 = (s32[1,1,1,256]{3,2,1,0:T(1,128)S(1)}, s32[1,1,1,256]{3,2,1,0:T(1,128)}, u32[]{:S(2)}) copy-start(s32[1,1,1,256]{3,2,1,0:T(1,128)} %param.13) | copy-start | bytes 3076
  7.6 8.6 %collective-permute-start.2 = (f32[16,32,128]{2,1,0:T(8,128)S(1)}, f32[16,32,128]{2,1,0:T(8,128)S(1)}, u32[]{:S(2)}, u32[]{:S(2)}) collective-permute-start(f32[16,32,128]{2,1,0:T(8,128)S(1)} %get-tuple-element.48), channel_id=1, source_target_pairs={{0,16},{1,0},{2,18},{3,2},{4,20},{5,4},{6,22},{7,6},{8,24},{9,8},{... | collective-permute-start | bytes 786440 | tf_op jit(solution)/shard_map/ppermute | solution.py:692
  9.1 7.5 %collective-permute-start.3 = (f32[16,32,128]{2,1,0:T(8,128)S(1)}, f32[16,32,128]{2,1,0:T(8,128)S(1)}, u32[]{:S(2)}, u32[]{:S(2)}) collective-permute-start(f32[16,32,128]{2,1,0:T(8,128)S(1)} %get-tuple-element.49), channel_id=1, source_target_pairs={{16,0},{0,1},{18,2},{2,3},{20,4},{4,5},{22,6},{6,7},{24,8},{8,9},{... | collective-permute-start | bytes 786440 | tf_op jit(solution)/shard_map/ppermute | solution.py:692
  13.1 7.2 %collective-permute-start.4 = (f32[7,32,128]{2,1,0:T(8,128)S(1)}, f32[7,32,128]{2,1,0:T(8,128)S(1)}, u32[]{:S(2)}, u32[]{:S(2)}) collective-permute-start(f32[7,32,128]{2,1,0:T(8,128)S(1)} %get-tuple-element.51), channel_id=1, source_target_pairs={{0,16},{1,0},{2,18},{3,2},{4,20},{5,4},{6,22},{7,6},{8,24},{9,8},{... | collective-permute-start | bytes 344072 | tf_op jit(solution)/shard_map/ppermute | solution.py:692
  14.6 5.7 %collective-permute-start.5 = (f32[7,32,128]{2,1,0:T(8,128)S(1)}, f32[7,32,128]{2,1,0:T(8,128)S(1)}, u32[]{:S(2)}, u32[]{:S(2)}) collective-permute-start(f32[7,32,128]{2,1,0:T(8,128)S(1)} %get-tuple-element.52), channel_id=1, source_target_pairs={{16,0},{0,1},{18,2},{2,3},{20,4},{4,5},{22,6},{6,7},{24,8},{8,9},{... | collective-permute-start | bytes 344072 | tf_op jit(solution)/shard_map/ppermute | solution.py:692
  20.7 5.9 %collective-permute-start.6 = (f32[13,24,128]{2,1,0:T(8,128)S(1)}, f32[13,24,128]{2,1,0:T(8,128)S(1)}, u32[]{:S(2)}, u32[]{:S(2)}) collective-permute-start(f32[13,24,128]{2,1,0:T(8,128)S(1)} %get-tuple-element.59), channel_id=1, source_target_pairs={{0,1},{1,2},{2,3},{3,4},{4,5},{5,6},{6,7},{7,8},{8,9},{9,10},{10,1... | collective-permute-start | bytes 479240 | tf_op jit(solution)/shard_map/ppermute | solution.py:698
  20.7 5.9 %collective-permute-start.7 = (f32[13,24,128]{2,1,0:T(8,128)S(1)}, f32[13,24,128]{2,1,0:T(8,128)S(1)}, u32[]{:S(2)}, u32[]{:S(2)}) collective-permute-start(f32[13,24,128]{2,1,0:T(8,128)S(1)} %get-tuple-element.60), channel_id=1, source_target_pairs={{1,0},{2,1},{3,2},{4,3},{5,4},{6,5},{7,6},{8,7},{9,8},{10,9},{11,1... | collective-permute-start | bytes 479240 | tf_op jit(solution)/shard_map/ppermute | solution.py:698
  52.2 6.8 %collective-permute-start.8 = (f32[16,128]{1,0:T(8,128)S(1)}, f32[16,128]{1,0:T(8,128)S(1)}, u32[]{:S(2)}, u32[]{:S(2)}) collective-permute-start(f32[16,128]{1,0:T(8,128)S(1)} %get-tuple-element.75), channel_id=1, source_target_pairs={{0,64},{1,0},{2,66},{3,2},{4,68},{5,4},{6,70},{7,6},{8,72},{9,8},{... | collective-permute-start | bytes 24584 | tf_op jit(solution)/shard_map/ppermute | solution.py:692
  55.0 4.9 %collective-permute-start.9 = (f32[16,128]{1,0:T(8,128)S(1)}, f32[16,128]{1,0:T(8,128)S(1)}, u32[]{:S(2)}, u32[]{:S(2)}) collective-permute-start(f32[16,128]{1,0:T(8,128)S(1)} %get-tuple-element.76), channel_id=1, source_target_pairs={{64,0},{0,1},{66,2},{2,3},{68,4},{4,5},{70,6},{6,7},{72,8},{8,9},{... | collective-permute-start | bytes 24584 | tf_op jit(solution)/shard_map/ppermute | solution.py:692
  55.0 4.9 %collective-permute-start.10 = (f32[16,128]{1,0:T(8,128)S(1)}, f32[16,128]{1,0:T(8,128)S(1)}, u32[]{:S(2)}, u32[]{:S(2)}) collective-permute-start(f32[16,128]{1,0:T(8,128)S(1)} %get-tuple-element.77), channel_id=1, source_target_pairs={{0,16},{1,0},{2,18},{3,2},{4,20},{5,4},{6,22},{7,6},{8,24},{9,8},{... | collective-permute-start | bytes 24584 | tf_op jit(solution)/shard_map/ppermute | solution.py:692
  56.6 3.7 %collective-permute-start.11 = (f32[16,128]{1,0:T(8,128)S(1)}, f32[16,128]{1,0:T(8,128)S(1)}, u32[]{:S(2)}, u32[]{:S(2)}) collective-permute-start(f32[16,128]{1,0:T(8,128)S(1)} %get-tuple-element.78), channel_id=1, source_target_pairs={{16,0},{0,1},{18,2},{2,3},{20,4},{4,5},{22,6},{6,7},{24,8},{8,9},{... | collective-permute-start | bytes 24584 | tf_op jit(solution)/shard_map/ppermute | solution.py:692

commit v15 on v13

--- a/solution.py
+++ b/solution.py
@@ -110,8 +110,8 @@
         bwd[at, part] = jnp.where(first, down, up)
 
 
-def pack_x(*refs):
-    far, (xf, xb, scaled), near, arrived = refs[:5], refs[5:8], refs[8:13], refs[13]
+def pack_first(*refs):
+    far, (yf, yb, scaled), near, arrived = refs[:5], refs[5:8], refs[8:13], refs[13]
     copies = [
         pltpu.make_async_copy(a, b, arrived.at[n]) for n, (a, b) in enumerate(zip(far, near))
     ]
@@ -127,6 +127,18 @@
     for c in range(3):
         scaled[c] = source[c] * inverse
 
+    def step(x, carry):
+        v = [field[f, x] for f in range(3)] + [scaled[f, x] for f in range(4)] + [warmth[x]]
+        put_y_tiles(y_tiles(v), first, yf, yb, x)
+        return carry
+
+    lax.fori_loop(0, 16, step, 0, unroll=4)
+    copies[3].wait()
+
+
+def pack_second(field, scaled, warmth, xf, xb):
+    first = on_first_core()
+
     def layer(f, x):
         if f < 3:
             return field[f, x]
@@ -138,18 +150,6 @@
         up = layer(*ups[min(at, len(ups) - 1)])
         down = layer(*downs[min(at, len(downs) - 1)])
         swap_store(first, xf, xb, at, up, down)
-    copies[3].wait()
-
-
-def pack_y(field, scaled, warmth, yf, yb):
-    first = on_first_core()
-
-    def step(x, carry):
-        v = [field[f, x] for f in range(3)] + [scaled[f, x] for f in range(4)] + [warmth[x]]
-        put_y_tiles(y_tiles(v), first, yf, yb, x)
-        return carry
-
-    lax.fori_loop(0, 16, step, 0, unroll=4)
 
 
 class Halo:
@@ -704,17 +704,19 @@
     face = (16, 128)
     x_message, y_message, corners = (X_LAYERS, 16, 128), (16, 32, 128), (len(CORNERS), 32, 128)
     here = (field, sigma, warmth, storage, source)
-    xf, xb, scaled, field, sigma, warmth, storage = call(
-        pack_x,
-        [x_message, x_message, (4, *cube), (3, *cube), cube, cube, cube],
+    yf, yb, scaled, field, sigma, warmth, storage = call(
+        pack_first,
+        [y_message, y_message, (4, *cube), (3, *cube), cube, cube, cube],
         [(3, *cube), pltpu.SemaphoreType.DMA((5,))],
-        name="pack_x",
+        name="pack_first",
         near=True,
         in_specs=[pl.BlockSpec(memory_space=pltpu.HBM)] * 5,
     )(*(pltpu.with_memory_space_constraint(v, pltpu.HBM) for v in here))
+    yf, yb = exchange("gy", yf, yb)
+    xf, xb = call(pack_second, [x_message, x_message], name="pack_second", near=True)(
+        field, scaled, warmth
+    )
     xf, xb = exchange("gx", xf, xb)
-    yf, yb = call(pack_y, [y_message, y_message], name="pack_y", near=True)(field, scaled, warmth)
-    yf, yb = exchange("gy", yf, yb)
     targets, spread_rows, into, nodes = pl.pallas_call(
         place,
         out_shape=[

time: 59.3 us -> 59.4 us (level)
  no operation moved by 1% of the time
where the time goes in v15:
time: 59.4 us; the launch traced here: 59.3 us
  blocking collectives  22.6 us (38%)
  starting transfers between devices  14.7 us (25%)
  Pallas kernels  13.7 us (23%)
  waiting for transfers between devices  7.43 us (13%)
  between operations  0.74 us (1%)
    all_to_all x1, blocking collectives, local(): lax.all_to_all(send.reshape(count, 1, 128), ('gy', 'gz'), split_axis=0, c...  22.6 us
    ppermute x5, starting transfers between devices, exchange(): lax.ppermute(fwd, names, forward)  10.2 us
    ppermute x5, waiting for transfers between devices, exchange(): lax.ppermute(bwd, names, backward)  4.25 us
    ppermute x1, starting transfers between devices, exchange_z(): lax.ppermute(down, 'gz', [(j, i) for i, j in ring])  2.94 us
    ppermute x5, waiting for transfers between devices, exchange(): lax.ppermute(fwd, names, forward)  2.81 us
    pallas_call x1, Pallas kernels, local(): call(rest_of_bulk, [(3, 17, *layer), cube, cube], [(EM_SWEEPS - 1, 3, hal...  2.41 us
    pallas_call x1, Pallas kernels, local(): call(bulk, [(EM_SWEEPS - 1, 3, 16, *layer)], name='bulk', near=True, cost...  2.02 us
    pallas_call x1, Pallas kernels, local(): call(merge, [(3, *cube), cube, cube], [(BLOCKS, 128, 128)], name='merge',...  1.95 us
  transfers between devices with their start and end apart: 12, of which 5 were waited for; matrix products, arithmetic and copies ran while one was open for 0% of the time, Pallas kernels for 15%

profile of v15, /device:TPU:130, one launch (start us, length us, event | category | flops | bytes accessed | tf_op | source)
XLA Modules:
  0.0 59.3 jit_solution(18273272549385812895)
XLA Ops:
  0.6 0.0 copy-start.1
  0.6 0.0 copy-start
  0.7 1.4 %pack_first.1 = (f32[16,32,128]{2,1,0:T(8,128)S(1)}, f32[16,32,128]{2,1,0:T(8,128)S(1)}, f32[4,16,16,128]{3,2,1,0:T(8,128)S(1)}, f32[3,16,16,128]{3,2,1,0:T(8,12...) custom-call(f32[3,16,16,128]{3,2,1,0:T(8,128)} %refs_0_.1, ...), custom_call_target="tpu_custom_call" | custom-call | tf_op jit(solution)/shard_map/pack_first/pallas_call | solution.py:707
  2.2 2.4 %collective-permute-start = (f32[30,16,128]{2,1,0:T(8,128)S(1)}, f32[30,16,128]{2,1,0:T(8,128)S(1)}, u32[]{:S(2)}, u32[]{:S(2)}) collective-permute-start(f32[30,16,128]{2,1,0:T(8,128)S(1)} %get-tuple-element.45), channel_id=1, source_target_pairs={{0,64},{1,0},{2,66},{3,2},{4,68},{5,4},{6,70},{7,6},{8,72},{9,8},{... | collective-permute-start | bytes 737288 | tf_op jit(solution)/shard_map/ppermute | solution.py:691
  4.5 0.0 collective-permute-start.1
  4.5 1.5 %collective-permute-start.2 = (f32[16,32,128]{2,1,0:T(8,128)S(1)}, f32[16,32,128]{2,1,0:T(8,128)S(1)}, u32[]{:S(2)}, u32[]{:S(2)}) collective-permute-start(f32[16,32,128]{2,1,0:T(8,128)S(1)} %get-tuple-element.47), channel_id=1, source_target_pairs={{0,16},{1,0},{2,18},{3,2},{4,20},{5,4},{6,22},{7,6},{8,24},{9,8},{... | collective-permute-start | bytes 786440 | tf_op jit(solution)/shard_map/ppermute | solution.py:691
  6.0 0.5 collective-permute-start.3
  6.6 0.0 copy-done.1
  6.6 0.0 copy-done
  6.6 0.5 place.1
  7.1 2.8 %collective-permute-done.xf = f32[30,16,128]{2,1,0:T(8,128)S(1)} collective-permute-done((f32[30,16,128]{2,1,0:T(8,128)S(1)}, f32[30,16,128]{2,1,0:T(8,128)S(1)}, u32[]{:S(2)}, u32[]{:S(2)}) %collective-permute-start) | collective-permute-done | bytes 245792 | tf_op jit(solution)/shard_map/ppermute | solution.py:691
  9.9 2.4 %collective-permute-done.1.xb = f32[30,16,128]{2,1,0:T(8,128)S(1)} collective-permute-done((f32[30,16,128]{2,1,0:T(8,128)S(1)}, f32[30,16,128]{2,1,0:T(8,128)S(1)}, u32[]{:S(2)}, u32[]{:S(2)}) %collective-permute-start.1) | collective-permute-done | bytes 245792 | tf_op jit(solution)/shard_map/ppermute | solution.py:691
  12.3 0.1 pack_corners.1
  12.4 1.5 %collective-permute-start.4 = (f32[7,32,128]{2,1,0:T(8,128)S(1)}, f32[7,32,128]{2,1,0:T(8,128)S(1)}, u32[]{:S(2)}, u32[]{:S(2)}) collective-permute-start(f32[7,32,128]{2,1,0:T(8,128)S(1)} %get-tuple-element.51), channel_id=1, source_target_pairs={{0,16},{1,0},{2,18},{3,2},{4,20},{5,4},{6,22},{7,6},{8,24},{9,8},{... | collective-permute-start | bytes 344072 | tf_op jit(solution)/shard_map/ppermute | solution.py:691
  13.9 0.5 collective-permute-start.5
  14.4 0.0 collective-permute-done.2.yf
  14.4 0.0 collective-permute-done.3.yb
  14.4 1.6 %pack_inner.1 = (f32[8,16,24,128]{3,2,1,0:T(8,128)S(1)}, f32[16,24,128]{2,1,0:T(8,128)S(1)}, f32[8,24,128]{2,1,0:T(8,128)S(1)}, f32[8,24,128]{2,1,0:T(8,128)S(1)}, f32[16,16,128]{2,1,0:T(8,128)S(1)}) custom-call(f32[3,16,16,128]{3,2,1,0:T(8,128)S(1)} %get-tuple-element.41.field, f32[4,16,16,128]{3,2,1,0:T(8,128)S(1)} %get-tuple-element.42.scaled, ...), custom_call_target="tpu_custom_call" | custom-call | tf_op jit(solution)/shard_map/pack_inner/pallas_call | solution.py:736
  16.1 2.0 %bulk.1.swept = f32[3,3,16,24,128]{4,3,2,1,0:T(8,128)S(1)} custom-call(f32[8,16,24,128]{3,2,1,0:T(8,128)S(1)} %get-tuple-element.49.whole.inner), custom_call_target="tpu_custom_call" | custom-call | flops 1000000000 | bytes 10000000 | tf_op jit(solution)/shard_map/bulk/pallas_call | solution.py:743
  18.1 0.0 collective-permute-done.4.cf
  18.1 0.6 collective-permute-done.5.cb
  18.7 0.4 pack_outer.1
  19.0 0.0 collective-permute-start.6
  19.1 2.9 %collective-permute-start.7 = (f32[13,24,128]{2,1,0:T(8,128)S(1)}, f32[13,24,128]{2,1,0:T(8,128)S(1)}, u32[]{:S(2)}, u32[]{:S(2)}) collective-permute-start(f32[13,24,128]{2,1,0:T(8,128)S(1)} %get-tuple-element.60), channel_id=1, source_target_pairs={{1,0},{2,1},{3,2},{4,3},{5,4},{6,5},{7,6},{8,7},{9,8},{10,9},{11,1... | collective-permute-start | bytes 479240 | tf_op jit(solution)/shard_map/ppermute | solution.py:697
  22.0 0.2 turn.1.own
  22.2 2.4 %rest_of_bulk.1 = (f32[3,17,24,128]{3,2,1,0:T(8,128)S(1)}, f32[16,16,128]{2,1,0:T(8,128)S(1)}, f32[16,16,128]{2,1,0:T(8,128)S(1)}) custom-call(f32[8,16,24,128]{3,2,1,0:T(8,128)S(1)} %get-tuple-element.49.whole.inner, f32[8,9,24,128]{3,2,1,0:T(8,128)S(1)} %get-tuple-element.55.outer, f32[3,3,16,24,128]{4,3,2,1,0:T(8,128)S(1)} %bulk.1.swept), custom_call_target="tpu_custom_call" | custom-call | flops 1000000000 | bytes 10000000 | tf_op jit(solution)/shard_map/rest_of_bulk/pallas_call | solution.py:757
  24.6 0.4 collective-permute-done.6.below_z
  25.0 0.0 collective-permute-done.7.above_z
  25.0 1.9 %edge.1 = (f32[5,3,32,128]{3,2,1,0:T(8,128)S(1)}, f32[576,128]{1,0:T(8,128)S(1)}, f32[16,16,128]{2,1,0:T(8,128)S(1)}) custom-call(f32[5,128,128]{2,1,0:T(8,128)S(1)} %turn.1.own, f32[13,24,128]{2,1,0:T(8,128)S(1)} %collective-permute-done.6.below_z, f32[13,24,128]{2,1,0:T(8,128)S(1)} %collective-permute-done.7.above_z, ...), custom_call_target="tpu_custom_call" | custom-call | tf_op jit(solution)/shard_map/edge/pallas_call | solution.py:773
  26.9 22.6 %all_to_all.5 = f32[576,1,128]{2,1,0:T(1,128)S(1)} all-to-all(f32[576,1,128]{2,1,0:T(1,128)S(1)} %bitcast.8), channel_id=1, replica_groups=mesh['gx'=8,'gy'=4,'gz'=16] {'gy','gz'}, dimensions={0} | all-to-all | bytes 589824 | tf_op jit(solution)/shard_map/all_to_all | solution.py:788
  49.5 0.5 warm.1
  50.1 3.2 %collective-permute-start.8 = (f32[16,128]{1,0:T(8,128)S(1)}, f32[16,128]{1,0:T(8,128)S(1)}, u32[]{:S(2)}, u32[]{:S(2)}) collective-permute-start(f32[16,128]{1,0:T(8,128)S(1)} %get-tuple-element.75), channel_id=1, source_target_pairs={{0,64},{1,0},{2,66},{3,2},{4,68},{5,4},{6,70},{7,6},{8,72},{9,8},{... | collective-permute-start | bytes 24584 | tf_op jit(solution)/shard_map/ppermute | solution.py:691
  53.3 0.0 collective-permute-start.9
  53.3 1.6 %collective-permute-start.10 = (f32[16,128]{1,0:T(8,128)S(1)}, f32[16,128]{1,0:T(8,128)S(1)}, u32[]{:S(2)}, u32[]{:S(2)}) collective-permute-start(f32[16,128]{1,0:T(8,128)S(1)} %get-tuple-element.77), channel_id=1, source_target_pairs={{0,16},{1,0},{2,18},{3,2},{4,20},{5,4},{6,22},{7,6},{8,24},{9,8},{... | collective-permute-start | bytes 24584 | tf_op jit(solution)/shard_map/ppermute | solution.py:691
  54.9 0.4 collective-permute-start.11
  55.3 1.9 %merge.1 = (f32[3,16,16,128]{3,2,1,0:T(8,128)}, f32[16,16,128]{2,1,0:T(8,128)S(1)}, f32[16,16,128]{2,1,0:T(8,128)S(1)}) custom-call(f32[3,17,24,128]{3,2,1,0:T(8,128)S(1)} %get-tuple-element.56.final, f32[5,3,32,128]{3,2,1,0:T(8,128)S(1)} %get-tuple-element.67.near, f32[576,128]{1,0:T(8,128)S(1)} %bitcast.7, f32[16,16,128]{2,1,0:T(8,128)S(1)} %get-tuple-element.69.beside, ...), custom_call_target="tpu_custom_call" | custom-call | flops 1000000000 | bytes 1000000 | tf_op jit(solution)/shard_map/merge/pallas_call | solution.py:796
  57.3 0.0 collective-permute-done.8.xf
  57.3 0.0 collective-permute-done.9.xb
  57.3 0.0 collective-permute-done.10.yf
  57.3 1.3 %collective-permute-done.11.yb = f32[16,128]{1,0:T(8,128)S(1)} collective-permute-done((f32[16,128]{1,0:T(8,128)S(1)}, f32[16,128]{1,0:T(8,128)S(1)}, u32[]{:S(2)}, u32[]{:S(2)}) %collective-permute-start.11) | collective-permute-done | bytes 8224 | tf_op jit(solution)/shard_map/ppermute | solution.py:691
  58.5 0.7 %finish.1 = f32[16,16,128]{2,1,0:T(8,128)} custom-call(f32[16,16,128]{2,1,0:T(8,128)S(1)} %get-tuple-element.74.rest, f32[16,16,128]{2,1,0:T(8,128)S(1)} %get-tuple-element.44.storage, f32[16,128]{1,0:T(8,128)S(1)} %collective-permute-done.8.xf, f32[16,128]{1,0:T(8,128)S(1)} %collective-permute-done.9.xb, f32[16,128]{1,0:T(8,128)S(1)} %collective-permute-done.10.yf, ...), custom_call_target="tpu_custom_call" | custom-call | tf_op jit(solution)/shard_map/finish/pallas_call | solution.py:803
  (1 shorter events, 0.0 us)
Async XLA Ops:
  0.6 5.9 %copy-start.1 = (s32[1,1,1,256]{3,2,1,0:T(1,128)S(1)}, s32[1,1,1,256]{3,2,1,0:T(1,128)}, u32[]{:S(2)}) copy-start(s32[1,1,1,256]{3,2,1,0:T(1,128)} %param.13) | copy-start | bytes 3076
  0.6 5.9 %copy-start = (s32[1,1,1,256,1]{3,4,2,1,0:T(1,128)S(1)}, s32[1,1,1,256,1]{3,4,2,1,0:T(1,128)}, u32[]{:S(2)}) copy-start(s32[1,1,1,256,1]{3,4,2,1,0:T(1,128)} %param.12) | copy-start | bytes 3076
  2.2 7.7 %collective-permute-start = (f32[30,16,128]{2,1,0:T(8,128)S(1)}, f32[30,16,128]{2,1,0:T(8,128)S(1)}, u32[]{:S(2)}, u32[]{:S(2)}) collective-permute-start(f32[30,16,128]{2,1,0:T(8,128)S(1)} %get-tuple-element.45), channel_id=1, source_target_pairs={{0,64},{1,0},{2,66},{3,2},{4,68},{5,4},{6,70},{7,6},{8,72},{9,8},{... | collective-permute-start | bytes 737288 | tf_op jit(solution)/shard_map/ppermute | solution.py:691
  4.5 7.8 %collective-permute-start.1 = (f32[30,16,128]{2,1,0:T(8,128)S(1)}, f32[30,16,128]{2,1,0:T(8,128)S(1)}, u32[]{:S(2)}, u32[]{:S(2)}) collective-permute-start(f32[30,16,128]{2,1,0:T(8,128)S(1)} %get-tuple-element.46), channel_id=1, source_target_pairs={{64,0},{0,1},{66,2},{2,3},{68,4},{4,5},{70,6},{6,7},{72,8},{8,9},{... | collective-permute-start | bytes 737288 | tf_op jit(solution)/shard_map/ppermute | solution.py:691
  4.5 9.9 %collective-permute-start.2 = (f32[16,32,128]{2,1,0:T(8,128)S(1)}, f32[16,32,128]{2,1,0:T(8,128)S(1)}, u32[]{:S(2)}, u32[]{:S(2)}) collective-permute-start(f32[16,32,128]{2,1,0:T(8,128)S(1)} %get-tuple-element.47), channel_id=1, source_target_pairs={{0,16},{1,0},{2,18},{3,2},{4,20},{5,4},{6,22},{7,6},{8,24},{9,8},{... | collective-permute-start | bytes 786440 | tf_op jit(solution)/shard_map/ppermute | solution.py:691
  6.0 8.4 %collective-permute-start.3 = (f32[16,32,128]{2,1,0:T(8,128)S(1)}, f32[16,32,128]{2,1,0:T(8,128)S(1)}, u32[]{:S(2)}, u32[]{:S(2)}) collective-permute-start(f32[16,32,128]{2,1,0:T(8,128)S(1)} %get-tuple-element.48), channel_id=1, source_target_pairs={{16,0},{0,1},{18,2},{2,3},{20,4},{4,5},{22,6},{6,7},{24,8},{8,9},{... | collective-permute-start | bytes 786440 | tf_op jit(solution)/shard_map/ppermute | solution.py:691
  12.4 5.7 %collective-permute-start.4 = (f32[7,32,128]{2,1,0:T(8,128)S(1)}, f32[7,32,128]{2,1,0:T(8,128)S(1)}, u32[]{:S(2)}, u32[]{:S(2)}) collective-permute-start(f32[7,32,128]{2,1,0:T(8,128)S(1)} %get-tuple-element.51), channel_id=1, source_target_pairs={{0,16},{1,0},{2,18},{3,2},{4,20},{5,4},{6,22},{7,6},{8,24},{9,8},{... | collective-permute-start | bytes 344072 | tf_op jit(solution)/shard_map/ppermute | solution.py:691
  13.9 4.8 %collective-permute-start.5 = (f32[7,32,128]{2,1,0:T(8,128)S(1)}, f32[7,32,128]{2,1,0:T(8,128)S(1)}, u32[]{:S(2)}, u32[]{:S(2)}) collective-permute-start(f32[7,32,128]{2,1,0:T(8,128)S(1)} %get-tuple-element.52), channel_id=1, source_target_pairs={{16,0},{0,1},{18,2},{2,3},{20,4},{4,5},{22,6},{6,7},{24,8},{8,9},{... | collective-permute-start | bytes 344072 | tf_op jit(solution)/shard_map/ppermute | solution.py:691
  19.0 5.9 %collective-permute-start.6 = (f32[13,24,128]{2,1,0:T(8,128)S(1)}, f32[13,24,128]{2,1,0:T(8,128)S(1)}, u32[]{:S(2)}, u32[]{:S(2)}) collective-permute-start(f32[13,24,128]{2,1,0:T(8,128)S(1)} %get-tuple-element.59), channel_id=1, source_target_pairs={{0,1},{1,2},{2,3},{3,4},{4,5},{5,6},{6,7},{7,8},{8,9},{9,10},{10,1... | collective-permute-start | bytes 479240 | tf_op jit(solution)/shard_map/ppermute | solution.py:697
  19.1 5.9 %collective-permute-start.7 = (f32[13,24,128]{2,1,0:T(8,128)S(1)}, f32[13,24,128]{2,1,0:T(8,128)S(1)}, u32[]{:S(2)}, u32[]{:S(2)}) collective-permute-start(f32[13,24,128]{2,1,0:T(8,128)S(1)} %get-tuple-element.60), channel_id=1, source_target_pairs={{1,0},{2,1},{3,2},{4,3},{5,4},{6,5},{7,6},{8,7},{9,8},{10,9},{11,1... | collective-permute-start | bytes 479240 | tf_op jit(solution)/shard_map/ppermute | solution.py:697
  50.1 7.2 %collective-permute-start.8 = (f32[16,128]{1,0:T(8,128)S(1)}, f32[16,128]{1,0:T(8,128)S(1)}, u32[]{:S(2)}, u32[]{:S(2)}) collective-permute-start(f32[16,128]{1,0:T(8,128)S(1)} %get-tuple-element.75), channel_id=1, source_target_pairs={{0,64},{1,0},{2,66},{3,2},{4,68},{5,4},{6,70},{7,6},{8,72},{9,8},{... | collective-permute-start | bytes 24584 | tf_op jit(solution)/shard_map/ppermute | solution.py:691
  53.3 4.0 %collective-permute-start.9 = (f32[16,128]{1,0:T(8,128)S(1)}, f32[16,128]{1,0:T(8,128)S(1)}, u32[]{:S(2)}, u32[]{:S(2)}) collective-permute-start(f32[16,128]{1,0:T(8,128)S(1)} %get-tuple-element.76), channel_id=1, source_target_pairs={{64,0},{0,1},{66,2},{2,3},{68,4},{4,5},{70,6},{6,7},{72,8},{8,9},{... | collective-permute-start | bytes 24584 | tf_op jit(solution)/shard_map/ppermute | solution.py:691
  53.3 4.0 %collective-permute-start.10 = (f32[16,128]{1,0:T(8,128)S(1)}, f32[16,128]{1,0:T(8,128)S(1)}, u32[]{:S(2)}, u32[]{:S(2)}) collective-permute-start(f32[16,128]{1,0:T(8,128)S(1)} %get-tuple-element.77), channel_id=1, source_target_pairs={{0,16},{1,0},{2,18},{3,2},{4,20},{5,4},{6,22},{7,6},{8,24},{9,8},{... | collective-permute-start | bytes 24584 | tf_op jit(solution)/shard_map/ppermute | solution.py:691
  54.9 3.7 %collective-permute-start.11 = (f32[16,128]{1,0:T(8,128)S(1)}, f32[16,128]{1,0:T(8,128)S(1)}, u32[]{:S(2)}, u32[]{:S(2)}) collective-permute-start(f32[16,128]{1,0:T(8,128)S(1)} %get-tuple-element.78), channel_id=1, source_target_pairs={{16,0},{0,1},{18,2},{2,3},{20,4},{4,5},{22,6},{6,7},{24,8},{8,9},{... | collective-permute-start | bytes 24584 | tf_op jit(solution)/shard_map/ppermute | solution.py:691
